TPU v7x, 256 devices: a whole 4x4x8 slice. The times are simulated.
256 devices in a mesh: grp: 8 (over x, z_lo), dev: 32 (over z_hi, y, core).
Axes of the slice: x: 4, y: 4, z: 8 (z_hi: 4, z_lo: 2; z = z_hi * 2 + z_lo), core: 2. Of those that a mesh axis runs over, the one named last changes fastest.
Arguments:
- image_emb: float32 [32768, 1152], P(('grp', 'dev')), may hold values from -0.18 to 0.18
- text_emb: float32 [32768, 1152], P(('grp', 'dev')), may hold values from -0.18 to 0.18
- temp: float32 [], replicated, may hold values from 6 to 12
- bias: float32 [], replicated, may hold values from -4 to -2
Outputs:
- grad_image: float32 [32768, 1152], P(('grp', 'dev'))
- grad_text: float32 [32768, 1152], P(('grp', 'dev'))
All inputs are finite; a program needn't handle non-finite values.
Results may differ from a plain program's by a relative error of at most 0.0053.
Values may be sent and summed in bfloat16 or wider, within the bound.
No kernel may reach another device: no remote copies, remote signals or barrier semaphores. Data moves between devices by JAX's collectives and lax.ppermute only.
A program may use at most 128 MiB of HBM per device.

v0:
```python
import jax
import jax.numpy as jnp
from jax import lax
from jax.sharding import PartitionSpec as P


def passed_along(block, axis, distance):
    devices = range(lax.axis_size(axis))
    route = [((i - distance) % len(devices), i) for i in devices]
    return lax.ppermute(block, axis, route)


def unit_rows(values):
    inverse = lax.rsqrt(jnp.sum(values * values, axis=1, keepdims=True) + 1e-06)
    return (values * inverse, inverse)


def back_rows(unit, inverse, upstream):
    return inverse * (upstream - unit * jnp.sum(unit * upstream, axis=1, keepdims=True))


def local(image_emb, text_emb, temp, bias):
    own_rows = image_emb.shape[0]
    hop_count = min(3, lax.axis_size("grp") - 1)
    img_unit, img_inv = unit_rows(image_emb)
    txt_unit, txt_inv = unit_rows(text_emb)
    img_low = img_unit.astype(jnp.bfloat16)
    txt_low = txt_unit.astype(jnp.bfloat16)
    forward = 1
    group_stay = lax.all_gather(img_low, "dev", axis=0, tiled=True)
    moved_list = [txt_low]
    for offset in range(1, hop_count + 1):
        moved_list.append(passed_along(moved_list[-1], "grp", forward))
    row_ids = lax.broadcasted_iota(jnp.int32, (group_stay.shape[0], own_rows), 0)
    col_ids = lax.broadcasted_iota(jnp.int32, (group_stay.shape[0], own_rows), 1)
    target = (row_ids == lax.axis_index("dev") * own_rows + col_ids).astype(jnp.float32)
    slope_list = []
    moved_terms = []
    for offset in range(hop_count + 1):
        logits = (
            temp
            * lax.dot_general(
                group_stay,
                moved_list[offset],
                (((1,), (1,)), ((), ())),
                preferred_element_type=jnp.float32,
            )
            + bias
        )
        if offset == 0:
            slopes = (temp * (jax.nn.sigmoid(logits) - target)).astype(jnp.bfloat16)
        else:
            slopes = (temp * jax.nn.sigmoid(logits)).astype(jnp.bfloat16)
        slope_list.append(slopes)
        moved_terms.append(
            lax.dot_general(
                slopes, group_stay, (((0,), (0,)), ((), ())), preferred_element_type=jnp.float32
            )
        )
    slope_stack = jnp.stack(slope_list, axis=0)
    moved_stack = jnp.stack(moved_list, axis=0)
    grad_stay = lax.psum_scatter(
        jnp.einsum("kgb,kbd->gd", slope_stack, moved_stack, preferred_element_type=jnp.float32),
        "dev",
        scatter_dimension=0,
        tiled=True,
    )
    carried = moved_terms[hop_count]
    for offset in range(hop_count - 1, -1, -1):
        carried = passed_along(carried, "grp", -forward) + moved_terms[offset]
    return (back_rows(img_unit, img_inv, grad_stay), back_rows(txt_unit, txt_inv, carried))


def solution(mesh):
    return jax.shard_map(
        local,
        mesh=mesh,
        in_specs=(P(("grp", "dev"), None), P(("grp", "dev"), None), P(), P()),
        out_specs=(P(("grp", "dev"), None), P(("grp", "dev"), None)),
        check_vma=False,
    )
```

profile of v0, /device:TPU:24, one launch (start us, length us, event | category | flops | bytes accessed | tf_op | source)
XLA Modules:
  0.0 314.3 jit_solution(14519070335029241809)
XLA Ops:
  7.2 1.2 multiply_reduce_fusion.3
  8.5 1.9 multiply_convert_fusion.1
  10.7 2.0 collective-permute-start
  12.7 9.2 %collective-permute-done = bf16[128,1152]{1,0:T(8,128)(2,1)S(1)} collective-permute-done((bf16[128,1152]{1,0:T(8,128)(2,1)S(1)}, bf16[128,1152]{1,0:T(8,128)(2,1)S(1)}, u32[]{:S(2)}, u32[]{:S(2)}) %collective-permute-start) | collective-permute-done | bytes 294944 | tf_op jit(solution)/shard_map/ppermute | solution.py:10
  23.3 11.6 %collective-permute-done.1 = bf16[128,1152]{1,0:T(8,128)(2,1)} collective-permute-done((bf16[128,1152]{1,0:T(8,128)(2,1)S(1)}, bf16[128,1152]{1,0:T(8,128)(2,1)}, u32[]{:S(2)}, u32[]{:S(2)}) %collective-permute-start.1) | collective-permute-done | bytes 294944 | tf_op jit(solution)/shard_map/ppermute | solution.py:10
  35.0 65.0 %all-gather.2.cloned.1.call-done = bf16[4096,1152]{1,0:T(8,128)(2,1)} async-done(((bf16[128,1152]{1,0:T(8,128)(2,1)}), bf16[4096,1152]{1,0:T(8,128)(2,1)}) %all-gather.2.cloned.1.call-update) | async-done | bytes 9437200 | tf_op jit(solution)/shard_map/all_gather | solution.py:30
  99.9 6.6 %fusion.21 = bf16[4096,128]{1,0:T(8,128)(2,1)S(1)} fusion(bf16[4096,1152]{1,0:T(8,128)(2,1)} %all-gather.2.cloned.1.call-done, bf16[128,1152]{1,0:T(8,128)(2,1)} %collective-permute-done.1, f32[]{:T(128)S(6)} %copy.7, f32[]{:T(128)S(6)} %copy.6), kind=kOutput, calls=%fused_computation.26 | convolution fusion | flops 1211629568 | bytes 10780680 | tf_op jit(solution)/shard_map/dot_general | solution.py:42
  106.5 3.1 fusion.28
  109.6 2.8 fusion.24
  112.4 4.0 %fusion.18 = bf16[4096,128]{1,0:T(8,128)(2,1)S(1)} fusion(bf16[4096,1152]{1,0:T(8,128)(2,1)S(1)} %copy-done, bf16[128,1152]{1,0:T(8,128)(2,1)} %collective-permute-done.2, f32[]{:T(128)S(6)} %copy.7, f32[]{:T(128)S(6)} %copy.6), kind=kOutput, calls=%fused_computation.23 | convolution fusion | flops 1211629568 | bytes 10780680 | tf_op jit(solution)/shard_map/dot_general | solution.py:42
  117.5 10.3 %convolution_bitcast_fusion = f32[4096,1152]{1,0:T(8,128)} fusion(bf16[1,4096,128]{2,1,0:T(8,128)(2,1)S(1)} %bitcast.32, bf16[1,4096,128]{2,1,0:T(8,128)(2,1)S(1)} %bitcast.29, bf16[1,4096,128]{2,1,0:T(8,128)(2,1)S(1)} %bitcast.31, bf16[1,4096,128]{2,1,0:T(8,128)(2,1)S(1)} %bitcast.30, bf16[1,128,1152]{2,1,0:T(8,128)(2,1)} %bitcast.7, ...), kind=kOutput, calls=%fused_computation | convolution fusion | flops 4839899136 | bytes 24248320 | tf_op jit(solution)/shard_map/kgb,kbd->gd/dot_general | solution.py:63
  127.9 5.7 %fusion.44 = f32[128,1152]{1,0:T(8,128)S(1)} fusion(bf16[4096,128]{1,0:T(8,128)(2,1)} %copy-done.5, bf16[4096,1152]{1,0:T(8,128)(2,1)} %all-gather.2.cloned.1.call-done), kind=kOutput, calls=%fused_computation.62 | convolution fusion | flops 1207959552 | bytes 11075584 | tf_op jit(solution)/shard_map/dot_general | solution.py:56
  133.6 3.1 collective-permute-start.3
  136.8 13.0 %collective-permute-done.3 = f32[128,1152]{1,0:T(8,128)S(1)} collective-permute-done((f32[128,1152]{1,0:T(8,128)S(1)}, f32[128,1152]{1,0:T(8,128)S(1)}, u32[]{:S(2)}, u32[]{:S(2)}) %collective-permute-start.3) | collective-permute-done | bytes 589856 | tf_op jit(solution)/shard_map/ppermute | solution.py:10
  149.8 6.3 %convolution_add_fusion = f32[128,1152]{1,0:T(8,128)S(1)} fusion(f32[128,1152]{1,0:T(8,128)S(1)} %collective-permute-done.3, bf16[4096,128]{1,0:T(8,128)(2,1)S(1)} %fusion.21, bf16[4096,1152]{1,0:T(8,128)(2,1)} %all-gather.2.cloned.1.call-done), kind=kOutput, calls=%fused_computation.41 | convolution fusion | flops 1208107008 | bytes 11665408 | tf_op jit(solution)/shard_map/dot_general | solution.py:56
  156.1 4.6 %collective-permute-start.4 = (f32[128,1152]{1,0:T(8,128)S(1)}, f32[128,1152]{1,0:T(8,128)S(1)}, u32[]{:S(2)}, u32[]{:S(2)}) collective-permute-start(f32[128,1152]{1,0:T(8,128)S(1)} %convolution_add_fusion), channel_id=1, source_target_pairs={{32,0},{64,32},{96,64},{128,96},{160,128},{192,160},{224,192},{0,2... | collective-permute-start | bytes 1769480 | tf_op jit(solution)/shard_map/ppermute | solution.py:10
  160.7 1.6 fusion.45
  162.3 10.7 %collective-permute-done.4 = f32[128,1152]{1,0:T(8,128)S(1)} collective-permute-done((f32[128,1152]{1,0:T(8,128)S(1)}, f32[128,1152]{1,0:T(8,128)S(1)}, u32[]{:S(2)}, u32[]{:S(2)}) %collective-permute-start.4) | collective-permute-done | bytes 589856 | tf_op jit(solution)/shard_map/ppermute | solution.py:10
  173.0 4.7 %collective-permute-start.5 = (f32[128,1152]{1,0:T(8,128)S(1)}, f32[128,1152]{1,0:T(8,128)S(1)}, u32[]{:S(2)}, u32[]{:S(2)}) collective-permute-start(f32[128,1152]{1,0:T(8,128)S(1)} %add.78), channel_id=1, source_target_pairs={{32,0},{64,32},{96,64},{128,96},{160,128},{192,160},{224,192},{0,2... | collective-permute-start | bytes 1769480 | tf_op jit(solution)/shard_map/ppermute | solution.py:10
  177.6 1.6 fusion.46
  179.2 28.5 %collective-permute-done.5 = f32[128,1152]{1,0:T(8,128)S(1)} collective-permute-done((f32[128,1152]{1,0:T(8,128)S(1)}, f32[128,1152]{1,0:T(8,128)S(1)}, u32[]{:S(2)}, u32[]{:S(2)}) %collective-permute-start.5) | collective-permute-done | bytes 589856 | tf_op jit(solution)/shard_map/ppermute | solution.py:10
  209.0 95.2 %reduce-scatter.2.cloned.1.call-done = f32[128,1152]{1,0:T(8,128)} async-done(((f32[4096,1152]{1,0:T(8,128)}), f32[128,1152]{1,0:T(8,128)}) %reduce-scatter.2.cloned.1.call-update) | async-done | bytes 589840 | tf_op jit(solution)/shard_map/reduce_scatter | solution.py:62
  304.1 1.3 multiply_reduce_fusion.1
  305.4 2.1 subtract_multiply_fusion.1
  (39 shorter events, 2.8 us)
Async XLA Ops:
  7.2 3.3 %copy-start.1 = (f32[128,1152]{1,0:T(8,128)S(1)}, f32[128,1152]{1,0:T(8,128)}, u32[]{:S(2)}) copy-start(f32[128,1152]{1,0:T(8,128)} %param.5) | copy-start | bytes 1769476
  7.2 92.7 %all-gather.2.cloned.1.call-start = ((), (), s32[]{:S(2)}) async-start(), calls=%async_computation.1 | async-start | bytes 9732096 | tf_op jit(solution)/shard_map/all_gather | solution.py:30
  10.4 293.8 %reduce-scatter.2.cloned.1.call-start = ((), (), s32[]{:S(2)}) async-start(), calls=%async_computation.2 | async-start | bytes 19464192 | tf_op jit(solution)/shard_map/reduce_scatter | solution.py:62
  10.7 11.2 %collective-permute-start = (bf16[128,1152]{1,0:T(8,128)(2,1)S(1)}, bf16[128,1152]{1,0:T(8,128)(2,1)S(1)}, u32[]{:S(2)}, u32[]{:S(2)}) collective-permute-start(bf16[128,1152]{1,0:T(8,128)(2,1)S(1)} %multiply_convert_fusion), channel_id=1, source_target_pairs={{224,0},{0,32},{32,64},{64,96},{96,128},{128,160},{160,192},{192,2... | collective-permute-start | bytes 884744 | tf_op jit(solution)/shard_map/ppermute | solution.py:10
  21.9 78.0 %copy-start.6 = (bf16[128,1152]{1,0:T(8,128)(2,1)}, bf16[128,1152]{1,0:T(8,128)(2,1)S(1)}, u32[]{:S(2)}) copy-start(bf16[128,1152]{1,0:T(8,128)(2,1)S(1)} %collective-permute-done) | copy-start | bytes 884740
  21.9 13.1 %collective-permute-start.1 = (bf16[128,1152]{1,0:T(8,128)(2,1)S(1)}, bf16[128,1152]{1,0:T(8,128)(2,1)}, u32[]{:S(2)}, u32[]{:S(2)}) collective-permute-start(bf16[128,1152]{1,0:T(8,128)(2,1)S(1)} %collective-permute-done), channel_id=1, source_target_pairs={{224,0},{0,32},{32,64},{64,96},{96,128},{128,160},{160,192},{192,2... | collective-permute-start | bytes 884744 | tf_op jit(solution)/shard_map/ppermute | solution.py:10
  34.9 77.5 %collective-permute-start.2 = (bf16[128,1152]{1,0:T(8,128)(2,1)}, bf16[128,1152]{1,0:T(8,128)(2,1)}, u32[]{:S(2)}, u32[]{:S(2)}) collective-permute-start(bf16[128,1152]{1,0:T(8,128)(2,1)} %collective-permute-done.1), channel_id=1, source_target_pairs={{224,0},{0,32},{32,64},{64,96},{96,128},{128,160},{160,192},{192,2... | collective-permute-start | bytes 884744 | tf_op jit(solution)/shard_map/ppermute | solution.py:10
  99.9 6.6 %copy-start = (bf16[4096,1152]{1,0:T(8,128)(2,1)S(1)}, bf16[4096,1152]{1,0:T(8,128)(2,1)}, u32[]{:S(2)}) copy-start(bf16[4096,1152]{1,0:T(8,128)(2,1)} %all-gather.2.cloned.1.call-done) | copy-start | bytes 28311556
  106.5 3.1 copy-start.7
  112.4 4.0 %copy-start.3 = (bf16[4096,128]{1,0:T(8,128)(2,1)}, bf16[4096,128]{1,0:T(8,128)(2,1)S(1)}, u32[]{:S(2)}) copy-start(bf16[4096,128]{1,0:T(8,128)(2,1)S(1)} %fusion.24) | copy-start | bytes 3145732
  116.5 1.1 copy-start.5
  127.9 32.8 %slice-start = ((s8[9437184]{0:T(1024)(128)(4,1)}), s8[4194304]{0:T(1024)(128)(4,1)S(1)}, s32[]{:S(2)}) async-start(s8[9437184]{0:T(1024)(128)(4,1)} %bitcast.27), calls=%async_computation.3 | async-start | bytes 8388608
  127.9 32.8 %slice-start.1 = ((s8[9437184]{0:T(1024)(128)(4,1)}), s8[4194304]{0:T(1024)(128)(4,1)S(1)}, s32[]{:S(2)}) async-start(s8[9437184]{0:T(1024)(128)(4,1)} %bitcast.27), calls=%async_computation.4 | async-start | bytes 8388608
  133.6 27.1 %slice-start.2 = ((s8[9437184]{0:T(1024)(128)(4,1)}), s8[1048576]{0:T(1024)(128)(4,1)S(1)}, s32[]{:S(2)}) async-start(s8[9437184]{0:T(1024)(128)(4,1)} %bitcast.27), calls=%async_computation.5 | async-start | bytes 2097152
  133.6 27.1 %copy-start.4 = (bf16[4096,128]{1,0:T(8,128)(2,1)S(1)}, bf16[4096,128]{1,0:T(8,128)(2,1)}, u32[]{:S(2)}) copy-start(bf16[4096,128]{1,0:T(8,128)(2,1)} %copy-done.3) | copy-start | bytes 3145732
  133.6 16.1 %collective-permute-start.3 = (f32[128,1152]{1,0:T(8,128)S(1)}, f32[128,1152]{1,0:T(8,128)S(1)}, u32[]{:S(2)}, u32[]{:S(2)}) collective-permute-start(f32[128,1152]{1,0:T(8,128)S(1)} %fusion.44), channel_id=1, source_target_pairs={{32,0},{64,32},{96,64},{128,96},{160,128},{192,160},{224,192},{0,2... | collective-permute-start | bytes 1769480 | tf_op jit(solution)/shard_map/ppermute | solution.py:10
  156.1 16.8 %collective-permute-start.4 = (f32[128,1152]{1,0:T(8,128)S(1)}, f32[128,1152]{1,0:T(8,128)S(1)}, u32[]{:S(2)}, u32[]{:S(2)}) collective-permute-start(f32[128,1152]{1,0:T(8,128)S(1)} %convolution_add_fusion), channel_id=1, source_target_pairs={{32,0},{64,32},{96,64},{128,96},{160,128},{192,160},{224,192},{0,2... | collective-permute-start | bytes 1769480 | tf_op jit(solution)/shard_map/ppermute | solution.py:10
  173.0 34.8 %collective-permute-start.5 = (f32[128,1152]{1,0:T(8,128)S(1)}, f32[128,1152]{1,0:T(8,128)S(1)}, u32[]{:S(2)}, u32[]{:S(2)}) collective-permute-start(f32[128,1152]{1,0:T(8,128)S(1)} %add.78), channel_id=1, source_target_pairs={{32,0},{64,32},{96,64},{128,96},{160,128},{192,160},{224,192},{0,2... | collective-permute-start | bytes 1769480 | tf_op jit(solution)/shard_map/ppermute | solution.py:10
  179.2 124.9 %copy-start.2 = (f32[128,1152]{1,0:T(8,128)S(1)}, f32[128,1152]{1,0:T(8,128)}, u32[]{:S(2)}) copy-start(f32[128,1152]{1,0:T(8,128)} %param.4) | copy-start | bytes 1769476
Sparse Core Ops, SparseCore 0:
  11.1 88.7 all-gather.1
  128.0 176.0 reduce-scatter.1
where the time goes:
time: 316 us; the launch traced here: 314 us
  waiting for transfers between devices  233 us (74%)
  matrix products  41.9 us (13%)
  between operations  15.6 us (5%)
  starting transfers between devices  14.5 us (5%)
  other arithmetic  8.05 us (3%)
    reduce_scatter x1, waiting for transfers between devices, local(): lax.psum_scatter(jnp.einsum('kgb,kbd->gd', slope_stack, moved_stack, pref...  95.2 us
    ppermute x6, waiting for transfers between devices, passed_along(): return lax.ppermute(block, axis, route)  73 us
    all_gather x1, waiting for transfers between devices, local(): group_stay = lax.all_gather(img_low, 'dev', axis=0, tiled=True)  65 us
    dot_general x4, matrix products, local(): lax.dot_general(group_stay, moved_list[offset], (((1,), (1,)), ((), ())),...  16.5 us
    dot_general x4, matrix products, local(): lax.dot_general(slopes, group_stay, (((0,), (0,)), ((), ())), preferred_e...  15.1 us
    ppermute x6, starting transfers between devices, passed_along(): return lax.ppermute(block, axis, route)  14.4 us
    dot_general x1, matrix products, local(): jnp.einsum('kgb,kbd->gd', slope_stack, moved_stack, preferred_element_typ...  10.3 us
  transfers between devices with their start and end apart: 8, of which 7 were waited for; matrix products, arithmetic and copies ran while one was open for 9% of the time, Pallas kernels for 0%

commit v1 on v0

v1 whole, which is shorter than its diff:
```python
import functools

import jax
import jax.numpy as jnp
from jax import lax
from jax.experimental import pallas as pl
from jax.experimental.pallas import tpu as pltpu
from jax.sharding import PartitionSpec as P

X, ZL, ZH, Y, CORE = 4, 2, 4, 4, 2
GROUPS, DEVS = X * ZL, ZH * Y * CORE


def to_group(block, step):
    return lax.ppermute(block, "grp", [(i, (i + step) % GROUPS) for i in range(GROUPS)])


def to_dev(block, zh=0, y=0, core=0):
    route = []
    for i in range(DEVS):
        a, b, c = i // (Y * CORE), i // CORE % Y, i % CORE
        target = ((a + zh) % ZH * Y + (b + y) % Y) * CORE + (c + core) % CORE
        route.append((i, target))
    return lax.ppermute(block, "dev", route)


def unit_rows(values):
    inverse = lax.rsqrt(jnp.sum(values * values, axis=1, keepdims=True) + 1e-06)
    return (values * inverse, inverse)


def back_rows(unit, inverse, upstream):
    return inverse * (upstream - unit * jnp.sum(unit * upstream, axis=1, keepdims=True))


TILE = 512


def pair_kernel(own, scalars, img, txt_sib, txt_own, *refs):
    step = pl.program_id(0)
    half_temp, half_bias = scalars[0], scalars[1]
    if own:
        gu_0, gu_n, gu_2, gv_sib, gv_own, acc, coef = refs
        past_sib = past_own = None
    else:
        past_sib, past_own, gu_0, gu_n, gu_2, gv_sib, gv_own, acc, coef = refs

    def tile(txt, gv, past, first_own):
        logits = lax.dot_general(
            img[...], txt[...], (((1,), (1,)), ((), ())), preferred_element_type=jnp.float32
        )
        slopes = half_temp * jnp.tanh(half_temp * logits + half_bias) + half_temp
        coef[...] = slopes.astype(jnp.bfloat16)
        if own and first_own is not None:

            @pl.when(step == first_own)
            def _():
                rows = lax.broadcasted_iota(jnp.int32, (128, 128), 0)
                cols = lax.broadcasted_iota(jnp.int32, (128, 128), 1)
                lowered = slopes[:128, :128] - jnp.where(rows == cols, 2.0 * half_temp, 0.0)
                coef[:128, :128] = lowered.astype(jnp.bfloat16)

        part = jnp.dot(coef[...], txt[...], preferred_element_type=jnp.float32)

        @pl.when(step == 0)
        def _():
            acc[...] = part

        @pl.when(step > 0)
        def _():
            acc[...] += part

        sums = lax.dot_general(
            coef[...], img[...], (((0,), (0,)), ((), ())), preferred_element_type=jnp.float32
        )
        if past is not None:
            sums = sums + past[...]
        gv[...] = sums.astype(gv.dtype)

    half = pl.num_programs(0) // 2

    @pl.when(step < half)
    def _():
        tile(txt_sib, gv_sib, past_sib, None)

    @pl.when(step >= half)
    def _():
        tile(txt_own, gv_own, past_own, half)

    @pl.when(step == pl.num_programs(0) - 1)
    def _():
        gu_0[...] = acc[0:128].astype(gu_0.dtype)
        gu_n[...] = acc[128:384].astype(gu_n.dtype)
        gu_2[...] = acc[384:512].astype(gu_2.dtype)


def pairs(scalars, img, txt_sib, txt_own, past=None):
    own = past is None
    rows, width = img.shape
    count = txt_own.shape[0]
    half = count // TILE
    kind = jnp.float32 if own else jnp.bfloat16
    sib = pl.BlockSpec((TILE, width), lambda i: (jnp.minimum(i, half - 1), 0))
    mine = pl.BlockSpec((TILE, width), lambda i: (jnp.maximum(i - half, 0), 0))

    def whole(n):
        return pl.BlockSpec((n, width), lambda i: (0, 0))

    return pl.pallas_call(
        functools.partial(pair_kernel, own),
        grid=(2 * half,),
        in_specs=[pl.BlockSpec(memory_space=pltpu.SMEM), whole(rows), sib, mine]
        + ([] if own else [sib, mine]),
        out_specs=[whole(128), whole(256), whole(128), sib, mine],
        out_shape=[
            jax.ShapeDtypeStruct((128, width), kind),
            jax.ShapeDtypeStruct((256, width), kind),
            jax.ShapeDtypeStruct((128, width), kind),
            jax.ShapeDtypeStruct((count, width), kind),
            jax.ShapeDtypeStruct((count, width), jnp.float32),
        ],
        scratch_shapes=[
            pltpu.VMEM((rows, width), jnp.float32),
            pltpu.VMEM((rows, TILE), jnp.bfloat16),
        ],
        compiler_params=pltpu.CompilerParams(vmem_limit_bytes=40 * 1024 * 1024),
        cost_estimate=pl.CostEstimate(
            flops=3 * 2 * rows * 2 * count * width,
            bytes_accessed=2 * count * width * 6,
            transcendentals=rows * 2 * count,
        ),
    )(scalars, img, txt_sib, txt_own, *([] if own else past))


def local(image_emb, text_emb, temp, bias):
    f32, low = jnp.float32, jnp.bfloat16
    img_unit, img_inv = unit_rows(image_emb)
    txt_unit, txt_inv = unit_rows(text_emb)
    img_0 = img_unit.astype(low)
    txt_0 = txt_unit.astype(low)
    scalars = jnp.stack([0.5 * temp, 0.5 * bias])

    txt_behind = to_group(txt_0, 1)
    img_up = to_dev(img_0, zh=-1)
    img_down = to_dev(img_0, zh=1)
    img_2 = to_dev(img_0, zh=2)
    ahead_0 = to_group(img_0, -2)
    img_n = jnp.concatenate([img_up, img_down], axis=0)
    ahead_n = to_group(img_n, -2)
    ahead_2 = to_group(img_2, -2)
    txt_pair = jnp.concatenate([txt_0, txt_behind], axis=0)
    txt_up = to_dev(txt_pair, y=-1)
    txt_down = to_dev(txt_pair, y=1)
    txt_2 = to_dev(txt_pair, y=2)
    txt_own = jnp.concatenate([txt_pair, txt_up, txt_down, txt_2], axis=0)
    txt_sib = to_dev(txt_own, core=1)
    img_own = jnp.concatenate([img_0, img_n, img_2], axis=0)
    img_ahead = jnp.concatenate([ahead_0, ahead_n, ahead_2], axis=0)

    gu_0, gu_n, gu_2, past_sib, past_own = pairs(scalars, img_own, txt_sib, txt_own)
    au_0, au_n, au_2, gv_sib, gv_own = pairs(scalars, img_ahead, txt_sib, txt_own, (past_sib, past_own))

    gu_2 = gu_2 + to_group(au_2, 2).astype(f32)
    gu_n = gu_n + to_group(au_n, 2).astype(f32)
    gu_0 = gu_0 + to_group(au_0, 2).astype(f32)
    gu = (
        gu_0
        + to_dev(gu_2.astype(low), zh=2).astype(f32)
        + to_dev(gu_n[:128].astype(low), zh=1).astype(f32)
        + to_dev(gu_n[128:].astype(low), zh=-1).astype(f32)
    )
    gv_own = gv_own + to_dev(gv_sib, core=1).astype(f32)
    gv_pair = (
        gv_own[:256]
        + to_dev(gv_own[768:].astype(low), y=2).astype(f32)
        + to_dev(gv_own[256:512].astype(low), y=1).astype(f32)
        + to_dev(gv_own[512:768].astype(low), y=-1).astype(f32)
    )
    gv = gv_pair[:128] + to_group(gv_pair[128:].astype(low), -1).astype(f32)
    return (back_rows(img_unit, img_inv, gu), back_rows(txt_unit, txt_inv, gv))


def solution(mesh):
    return jax.shard_map(
        local,
        mesh=mesh,
        in_specs=(P(("grp", "dev"), None), P(("grp", "dev"), None), P(), P()),
        out_specs=(P(("grp", "dev"), None), P(("grp", "dev"), None)),
        check_vma=False,
    )
```

time: 316 us -> 202 us (0.64)
  waiting for transfers between devices: 233 us -> 116 us
  matrix products: 41.9 us -> 0 us
  Pallas kernels: 0 us -> 30.3 us
  starting transfers between devices: 14.5 us -> 37.4 us
  between operations: 15.6 us -> 2.12 us
    reduce_scatter x1 -> x0, waiting for transfers between devices: 95.2 us -> none  [local(): lax.psum_scatter(jnp.einsum('kgb,kbd->gd', slope_stack, moved_stack, pref...]
    all_gather x1 -> x0, waiting for transfers between devices: 65 us -> none  [local(): group_stay = lax.all_gather(img_low, 'dev', axis=0, tiled=True)]
    ppermute x6 -> x22, waiting for transfers between devices: 73 us -> 116 us  [the longest x14 62.3 us: to_dev(): return lax.ppermute(block, 'dev', route)]
    dot_general x9 -> x0, matrix products: 41.9 us -> none  [the longest x4 16.5 us: local(): lax.dot_general(group_stay, moved_list[offset], (((1,), (1,)), ((), ())),...]
    pallas_call x0 -> x2, Pallas kernels: none -> 30.3 us  [pairs(): pl.pallas_call(functools.partial(pair_kernel, own), grid=(2 * half,), in_...]
    ppermute x6 -> x22, starting transfers between devices: 14.4 us -> 37.4 us  [the longest x14 26.7 us: to_dev(): return lax.ppermute(block, 'dev', route)]
    concatenate x0 -> x4, other arithmetic: none -> 3.33 us  [the longest x1 1.23 us: local(): img_ahead = jnp.concatenate([ahead_0, ahead_n, ahead_2], axis=0)]
  transfers between devices with their start and end apart: 8 -> 22, of which waited for: 7 -> 15; matrix products, arithmetic and copies ran while one was open for 9% -> 3% of each run, Pallas kernels for 0% -> 0%
where the time goes in v1:
time: 202 us; the launch traced here: 199 us
  waiting for transfers between devices  116 us (57%)
  starting transfers between devices  37.4 us (19%)
  Pallas kernels  30.3 us (15%)
  other arithmetic  9.75 us (5%)
  local copies, waits for them, and re-layouts  2.67 us (1%)
  between operations  2.12 us (1%)
    ppermute x14, waiting for transfers between devices, to_dev(): return lax.ppermute(block, 'dev', route)  62.3 us
    ppermute x8, waiting for transfers between devices, to_group(): lax.ppermute(block, 'grp', [(i, (i + step) % GROUPS) for i in range(GROUP...  53.9 us
    pallas_call x2, Pallas kernels, pairs(): pl.pallas_call(functools.partial(pair_kernel, own), grid=(2 * half,), in_...  30.3 us
    ppermute x14, starting transfers between devices, to_dev(): return lax.ppermute(block, 'dev', route)  26.7 us
    ppermute x8, starting transfers between devices, to_group(): lax.ppermute(block, 'grp', [(i, (i + step) % GROUPS) for i in range(GROUP...  10.7 us
  transfers between devices with their start and end apart: 22, of which 15 were waited for; matrix products, arithmetic and copies ran while one was open for 3% of the time, Pallas kernels for 0%

profile of v1, /device:TPU:24, one launch (start us, length us, event | category | flops | bytes accessed | tf_op | source)
XLA Modules:
  0.0 198.6 jit_solution(10217893336553870411)
XLA Ops:
  5.0 9.2 %collective-permute-done.3 = bf16[128,1152]{1,0:T(8,128)(2,1)S(1)} collective-permute-done((bf16[128,1152]{1,0:T(8,128)(2,1)S(1)}, bf16[128,1152]{1,0:T(8,128)(2,1)S(1)}, u32[]{:S(2)}, u32[]{:S(2)}) %collective-permute-start.3) | collective-permute-done | bytes 294944 | tf_op jit(solution)/shard_map/ppermute | solution.py:15
  15.1 2.5 %collective-permute-start.5 = (bf16[256,1152]{1,0:T(8,128)(2,1)S(1)}, bf16[256,1152]{1,0:T(8,128)(2,1)S(1)}, u32[]{:S(2)}, u32[]{:S(2)}) collective-permute-start(bf16[256,1152]{1,0:T(8,128)(2,1)S(1)} %pad_maximum_fusion.2), channel_id=1, source_target_pairs={{0,2},{1,3},{2,4},{3,5},{4,6},{5,7},{6,0},{7,1},{8,10},{9,11},{10,... | collective-permute-start | bytes 1769480 | tf_op jit(solution)/shard_map/ppermute | solution.py:24
  17.6 25.0 %collective-permute-done.4 = bf16[256,1152]{1,0:T(8,128)(2,1)S(1)} collective-permute-done((bf16[256,1152]{1,0:T(8,128)(2,1)S(1)}, bf16[256,1152]{1,0:T(8,128)(2,1)S(1)}, u32[]{:S(2)}, u32[]{:S(2)}) %collective-permute-start.4) | collective-permute-done | bytes 589856 | tf_op jit(solution)/shard_map/ppermute | solution.py:24
  43.3 3.3 %collective-permute-start.1 = (bf16[128,1152]{1,0:T(8,128)(2,1)S(1)}, bf16[128,1152]{1,0:T(8,128)(2,1)S(1)}, u32[]{:S(2)}, u32[]{:S(2)}) collective-permute-start(bf16[128,1152]{1,0:T(8,128)(2,1)S(1)} %multiply_convert_fusion.1), channel_id=1, source_target_pairs={{0,8},{1,9},{2,10},{3,11},{4,12},{5,13},{6,14},{7,15},{8,16},{9,17... | collective-permute-start | bytes 884744 | tf_op jit(solution)/shard_map/ppermute | solution.py:24
  46.6 2.6 %collective-permute-start = (bf16[128,1152]{1,0:T(8,128)(2,1)S(1)}, bf16[128,1152]{1,0:T(8,128)(2,1)S(1)}, u32[]{:S(2)}, u32[]{:S(2)}) collective-permute-start(bf16[128,1152]{1,0:T(8,128)(2,1)S(1)} %multiply_convert_fusion.1), channel_id=1, source_target_pairs={{0,24},{1,25},{2,26},{3,27},{4,28},{5,29},{6,30},{7,31},{8,0},{9,1... | collective-permute-start | bytes 884744 | tf_op jit(solution)/shard_map/ppermute | solution.py:24
  49.2 4.9 %collective-permute-start.2 = (bf16[128,1152]{1,0:T(8,128)(2,1)S(1)}, bf16[128,1152]{1,0:T(8,128)(2,1)}, u32[]{:S(2)}, u32[]{:S(2)}) collective-permute-start(bf16[128,1152]{1,0:T(8,128)(2,1)S(1)} %multiply_convert_fusion.1), channel_id=1, source_target_pairs={{0,16},{1,17},{2,18},{3,19},{4,20},{5,21},{6,22},{7,23},{8,24},{9,... | collective-permute-start | bytes 884744 | tf_op jit(solution)/shard_map/ppermute | solution.py:24
  54.1 8.5 %collective-permute-done.1 = bf16[128,1152]{1,0:T(8,128)(2,1)S(1)} collective-permute-done((bf16[128,1152]{1,0:T(8,128)(2,1)S(1)}, bf16[128,1152]{1,0:T(8,128)(2,1)S(1)}, u32[]{:S(2)}, u32[]{:S(2)}) %collective-permute-start.1) | collective-permute-done | bytes 294944 | tf_op jit(solution)/shard_map/ppermute | solution.py:24
  62.6 7.8 %collective-permute-done = bf16[128,1152]{1,0:T(8,128)(2,1)S(1)} collective-permute-done((bf16[128,1152]{1,0:T(8,128)(2,1)S(1)}, bf16[128,1152]{1,0:T(8,128)(2,1)S(1)}, u32[]{:S(2)}, u32[]{:S(2)}) %collective-permute-start) | collective-permute-done | bytes 294944 | tf_op jit(solution)/shard_map/ppermute | solution.py:24
  71.4 2.7 %collective-permute-start.9 = (bf16[256,1152]{1,0:T(8,128)(2,1)}, bf16[256,1152]{1,0:T(8,128)(2,1)}, u32[]{:S(2)}, u32[]{:S(2)}) collective-permute-start(bf16[256,1152]{1,0:T(8,128)(2,1)} %pad_maximum_fusion.3), channel_id=1, source_target_pairs={{0,192},{32,224},{64,0},{96,32},{128,64},{160,96},{192,128},{224,1... | collective-permute-start | bytes 1769480 | tf_op jit(solution)/shard_map/ppermute | solution.py:15
  78.7 15.6 %collective-permute-done.8 = bf16[128,1152]{1,0:T(8,128)(2,1)} collective-permute-done((bf16[128,1152]{1,0:T(8,128)(2,1)S(1)}, bf16[128,1152]{1,0:T(8,128)(2,1)}, u32[]{:S(2)}, u32[]{:S(2)}) %collective-permute-start.8) | collective-permute-done | bytes 294944 | tf_op jit(solution)/shard_map/ppermute | solution.py:15
  94.3 5.7 %collective-permute-done.10 = bf16[128,1152]{1,0:T(8,128)(2,1)S(1)} collective-permute-done((bf16[128,1152]{1,0:T(8,128)(2,1)}, bf16[128,1152]{1,0:T(8,128)(2,1)S(1)}, u32[]{:S(2)}, u32[]{:S(2)}) %collective-permute-start.10) | collective-permute-done | bytes 294944 | tf_op jit(solution)/shard_map/ppermute | solution.py:15
  101.2 15.2 %shard_map.59 = (f32[128,1152]{1,0:T(8,128)S(1)}, f32[256,1152]{1,0:T(8,128)S(1)}, f32[128,1152]{1,0:T(8,128)S(1)}, f32[1024,1152]{1,0:T(8,128)S(1)}, f32[1024,1152]{1,0:T(8,128)}) custom-call(f32[2]{0:T(128)S(1)} %pad_maximum_fusion.4.scalars, bf16[512,1152]{1,0:T(8,128)(2,1)S(1)} %pad_maximum_fusion.img, ...), custom_call_target="tpu_custom_call" | custom-call | flops 7247757312 | bytes 14155776 | tf_op jit(solution)/shard_map/pallas_call | solution.py:109
  116.5 2.2 %copy-done = f32[1024,1152]{1,0:T(8,128)} copy-done((f32[1024,1152]{1,0:T(8,128)}, f32[1024,1152]{1,0:T(8,128)S(1)}, u32[]{:S(2)}) %copy-start) | copy-done | bytes 4718616
  118.7 15.1 %shard_map.60 = (bf16[128,1152]{1,0:T(8,128)(2,1)S(1)}, bf16[256,1152]{1,0:T(8,128)(2,1)S(1)}, bf16[128,1152]{1,0:T(8,128)(2,1)S(1)}, bf16[1024,1152]{1,0:T(8,128)(2,1)S(1)}, f32[1024,1152]{1,0:T(8,128)S(1)}) custom-call(f32[2]{0:T(128)S(1)} %pad_maximum_fusion.4.scalars, bf16[512,1152]{1,0:T(8,128)(2,1)S(1)} %pad_maximum_fusion.1.img, ...), custom_call_target="tpu_custom_call" | custom-call | flops 7247757312 | bytes 14155776 | tf_op jit(solution)/shard_map/pallas_call | solution.py:109
  136.5 2.4 %collective-permute-start.11 = (bf16[128,1152]{1,0:T(8,128)(2,1)S(1)}, bf16[128,1152]{1,0:T(8,128)(2,1)S(1)}, u32[]{:S(2)}, u32[]{:S(2)}) collective-permute-start(bf16[128,1152]{1,0:T(8,128)(2,1)S(1)} %get-tuple-element.15), channel_id=1, source_target_pairs={{0,64},{32,96},{64,128},{96,160},{128,192},{160,224},{192,0},{224,... | collective-permute-start | bytes 884744 | tf_op jit(solution)/shard_map/ppermute | solution.py:15
  138.9 6.4 %collective-permute-done.12 = bf16[128,1152]{1,0:T(8,128)(2,1)S(1)} collective-permute-done((bf16[128,1152]{1,0:T(8,128)(2,1)S(1)}, bf16[128,1152]{1,0:T(8,128)(2,1)S(1)}, u32[]{:S(2)}, u32[]{:S(2)}) %collective-permute-start.12) | collective-permute-done | bytes 294944 | tf_op jit(solution)/shard_map/ppermute | solution.py:15
  145.4 4.0 %collective-permute-start.13 = (bf16[128,1152]{1,0:T(8,128)(2,1)S(1)}, bf16[128,1152]{1,0:T(8,128)(2,1)S(1)}, u32[]{:S(2)}, u32[]{:S(2)}) collective-permute-start(bf16[128,1152]{1,0:T(8,128)(2,1)S(1)} %add_convert_fusion.1), channel_id=1, source_target_pairs={{0,16},{1,17},{2,18},{3,19},{4,20},{5,21},{6,22},{7,23},{8,24},{9,... | collective-permute-start | bytes 884744 | tf_op jit(solution)/shard_map/ppermute | solution.py:24
  149.5 8.5 %collective-permute-done.14 = bf16[256,1152]{1,0:T(8,128)(2,1)S(1)} collective-permute-done((bf16[256,1152]{1,0:T(8,128)(2,1)S(1)}, bf16[256,1152]{1,0:T(8,128)(2,1)S(1)}, u32[]{:S(2)}, u32[]{:S(2)}) %collective-permute-start.14) | collective-permute-done | bytes 589856 | tf_op jit(solution)/shard_map/ppermute | solution.py:15
  159.9 2.9 %collective-permute-start.20 = (bf16[256,1152]{1,0:T(8,128)(2,1)S(1)}, bf16[256,1152]{1,0:T(8,128)(2,1)S(1)}, u32[]{:S(2)}, u32[]{:S(2)}) collective-permute-start(bf16[256,1152]{1,0:T(8,128)(2,1)S(1)} %get-tuple-element.27), channel_id=1, source_target_pairs={{0,6},{1,7},{2,0},{3,1},{4,2},{5,3},{6,4},{7,5},{8,14},{9,15},{10,... | collective-permute-start | bytes 1769480 | tf_op jit(solution)/shard_map/ppermute | solution.py:24
  164.1 4.1 %collective-permute-start.15 = (bf16[128,1152]{1,0:T(8,128)(2,1)S(1)}, bf16[128,1152]{1,0:T(8,128)(2,1)S(1)}, u32[]{:S(2)}, u32[]{:S(2)}) collective-permute-start(bf16[128,1152]{1,0:T(8,128)(2,1)S(1)} %get-tuple-element.29), channel_id=1, source_target_pairs={{0,8},{1,9},{2,10},{3,11},{4,12},{5,13},{6,14},{7,15},{8,16},{9,17... | collective-permute-start | bytes 884744 | tf_op jit(solution)/shard_map/ppermute | solution.py:24
  168.2 11.9 %collective-permute-done.15 = bf16[128,1152]{1,0:T(8,128)(2,1)S(1)} collective-permute-done((bf16[128,1152]{1,0:T(8,128)(2,1)S(1)}, bf16[128,1152]{1,0:T(8,128)(2,1)S(1)}, u32[]{:S(2)}, u32[]{:S(2)}) %collective-permute-start.15) | collective-permute-done | bytes 294944 | tf_op jit(solution)/shard_map/ppermute | solution.py:24
  180.1 2.3 %collective-permute-done.16 = bf16[128,1152]{1,0:T(8,128)(2,1)S(1)} collective-permute-done((bf16[128,1152]{1,0:T(8,128)(2,1)S(1)}, bf16[128,1152]{1,0:T(8,128)(2,1)S(1)}, u32[]{:S(2)}, u32[]{:S(2)}) %collective-permute-start.16) | collective-permute-done | bytes 294944 | tf_op jit(solution)/shard_map/ppermute | solution.py:24
  182.7 5.3 %collective-permute-done.20 = bf16[256,1152]{1,0:T(8,128)(2,1)S(1)} collective-permute-done((bf16[256,1152]{1,0:T(8,128)(2,1)S(1)}, bf16[256,1152]{1,0:T(8,128)(2,1)S(1)}, u32[]{:S(2)}, u32[]{:S(2)}) %collective-permute-start.20) | collective-permute-done | bytes 589856 | tf_op jit(solution)/shard_map/ppermute | solution.py:24
  189.7 7.6 %collective-permute-done.21 = bf16[128,1152]{1,0:T(8,128)(2,1)S(1)} collective-permute-done((bf16[128,1152]{1,0:T(8,128)(2,1)S(1)}, bf16[128,1152]{1,0:T(8,128)(2,1)S(1)}, u32[]{:S(2)}, u32[]{:S(2)}) %collective-permute-start.21) | collective-permute-done | bytes 294944 | tf_op jit(solution)/shard_map/ppermute | solution.py:15
  (56 shorter events, 20.6 us)
Async XLA Ops:
  3.0 11.2 %collective-permute-start.3 = (bf16[128,1152]{1,0:T(8,128)(2,1)S(1)}, bf16[128,1152]{1,0:T(8,128)(2,1)S(1)}, u32[]{:S(2)}, u32[]{:S(2)}) collective-permute-start(bf16[128,1152]{1,0:T(8,128)(2,1)S(1)} %get-tuple-element.25), channel_id=1, source_target_pairs={{0,32},{32,64},{64,96},{96,128},{128,160},{160,192},{192,224},{224... | collective-permute-start | bytes 884744 | tf_op jit(solution)/shard_map/ppermute | solution.py:15
  14.3 28.8 %copy-start.2 = (f32[128,1152]{1,0:T(8,128)S(1)}, f32[128,1152]{1,0:T(8,128)}, u32[]{:S(2)}) copy-start(f32[128,1152]{1,0:T(8,128)} %param.4) | copy-start | bytes 1769476
  14.3 28.4 %collective-permute-start.4 = (bf16[256,1152]{1,0:T(8,128)(2,1)S(1)}, bf16[256,1152]{1,0:T(8,128)(2,1)S(1)}, u32[]{:S(2)}, u32[]{:S(2)}) collective-permute-start(bf16[256,1152]{1,0:T(8,128)(2,1)S(1)} %pad_maximum_fusion.2), channel_id=1, source_target_pairs={{0,6},{1,7},{2,0},{3,1},{4,2},{5,3},{6,4},{7,5},{8,14},{9,15},{10,... | collective-permute-start | bytes 1769480 | tf_op jit(solution)/shard_map/ppermute | solution.py:24
  15.1 27.7 %collective-permute-start.5 = (bf16[256,1152]{1,0:T(8,128)(2,1)S(1)}, bf16[256,1152]{1,0:T(8,128)(2,1)S(1)}, u32[]{:S(2)}, u32[]{:S(2)}) collective-permute-start(bf16[256,1152]{1,0:T(8,128)(2,1)S(1)} %pad_maximum_fusion.2), channel_id=1, source_target_pairs={{0,2},{1,3},{2,4},{3,5},{4,6},{5,7},{6,0},{7,1},{8,10},{9,11},{10,... | collective-permute-start | bytes 1769480 | tf_op jit(solution)/shard_map/ppermute | solution.py:24
  17.6 25.3 %collective-permute-start.6 = (bf16[256,1152]{1,0:T(8,128)(2,1)S(1)}, bf16[256,1152]{1,0:T(8,128)(2,1)S(1)}, u32[]{:S(2)}, u32[]{:S(2)}) collective-permute-start(bf16[256,1152]{1,0:T(8,128)(2,1)S(1)} %pad_maximum_fusion.2), channel_id=1, source_target_pairs={{0,4},{1,5},{2,6},{3,7},{4,0},{5,1},{6,2},{7,3},{8,12},{9,13},{10,... | collective-permute-start | bytes 1769480 | tf_op jit(solution)/shard_map/ppermute | solution.py:24
  42.9 58.3 %collective-permute-start.7 = (bf16[1024,1152]{1,0:T(8,128)(2,1)S(1)}, bf16[1024,1152]{1,0:T(8,128)(2,1)}, u32[]{:S(2)}, u32[]{:S(2)}) collective-permute-start(bf16[1024,1152]{1,0:T(8,128)(2,1)S(1)} %constant_dynamic-update-slice_fusion.txt_own), channel_id=1, source_target_pairs={{0,1},{1,0},{2,3},{3,2},{4,5},{5,4},{6,7},{7,6},{8,9},{9,8},{10,11... | collective-permute-start | bytes 7077896 | tf_op jit(solution)/shard_map/ppermute | solution.py:24
  43.3 19.3 %collective-permute-start.1 = (bf16[128,1152]{1,0:T(8,128)(2,1)S(1)}, bf16[128,1152]{1,0:T(8,128)(2,1)S(1)}, u32[]{:S(2)}, u32[]{:S(2)}) collective-permute-start(bf16[128,1152]{1,0:T(8,128)(2,1)S(1)} %multiply_convert_fusion.1), channel_id=1, source_target_pairs={{0,8},{1,9},{2,10},{3,11},{4,12},{5,13},{6,14},{7,15},{8,16},{9,17... | collective-permute-start | bytes 884744 | tf_op jit(solution)/shard_map/ppermute | solution.py:24
  46.6 23.8 %collective-permute-start = (bf16[128,1152]{1,0:T(8,128)(2,1)S(1)}, bf16[128,1152]{1,0:T(8,128)(2,1)S(1)}, u32[]{:S(2)}, u32[]{:S(2)}) collective-permute-start(bf16[128,1152]{1,0:T(8,128)(2,1)S(1)} %multiply_convert_fusion.1), channel_id=1, source_target_pairs={{0,24},{1,25},{2,26},{3,27},{4,28},{5,29},{6,30},{7,31},{8,0},{9,1... | collective-permute-start | bytes 884744 | tf_op jit(solution)/shard_map/ppermute | solution.py:24
  49.2 28.3 %collective-permute-start.2 = (bf16[128,1152]{1,0:T(8,128)(2,1)S(1)}, bf16[128,1152]{1,0:T(8,128)(2,1)}, u32[]{:S(2)}, u32[]{:S(2)}) collective-permute-start(bf16[128,1152]{1,0:T(8,128)(2,1)S(1)} %multiply_convert_fusion.1), channel_id=1, source_target_pairs={{0,16},{1,17},{2,18},{3,19},{4,20},{5,21},{6,22},{7,23},{8,24},{9,... | collective-permute-start | bytes 884744 | tf_op jit(solution)/shard_map/ppermute | solution.py:24
  71.4 28.6 %collective-permute-start.9 = (bf16[256,1152]{1,0:T(8,128)(2,1)}, bf16[256,1152]{1,0:T(8,128)(2,1)}, u32[]{:S(2)}, u32[]{:S(2)}) collective-permute-start(bf16[256,1152]{1,0:T(8,128)(2,1)} %pad_maximum_fusion.3), channel_id=1, source_target_pairs={{0,192},{32,224},{64,0},{96,32},{128,64},{160,96},{192,128},{224,1... | collective-permute-start | bytes 1769480 | tf_op jit(solution)/shard_map/ppermute | solution.py:15
  74.1 20.2 %collective-permute-start.8 = (bf16[128,1152]{1,0:T(8,128)(2,1)S(1)}, bf16[128,1152]{1,0:T(8,128)(2,1)}, u32[]{:S(2)}, u32[]{:S(2)}) collective-permute-start(bf16[128,1152]{1,0:T(8,128)(2,1)S(1)} %multiply_convert_fusion.1), channel_id=1, source_target_pairs={{0,192},{32,224},{64,0},{96,32},{128,64},{160,96},{192,128},{224,1... | collective-permute-start | bytes 884744 | tf_op jit(solution)/shard_map/ppermute | solution.py:15
  77.5 22.5 %collective-permute-start.10 = (bf16[128,1152]{1,0:T(8,128)(2,1)}, bf16[128,1152]{1,0:T(8,128)(2,1)S(1)}, u32[]{:S(2)}, u32[]{:S(2)}) collective-permute-start(bf16[128,1152]{1,0:T(8,128)(2,1)} %collective-permute-done.2), channel_id=1, source_target_pairs={{0,192},{32,224},{64,0},{96,32},{128,64},{160,96},{192,128},{224,1... | collective-permute-start | bytes 884744 | tf_op jit(solution)/shard_map/ppermute | solution.py:15
  133.8 24.4 %collective-permute-start.17 = (bf16[1024,1152]{1,0:T(8,128)(2,1)S(1)}, bf16[1024,1152]{1,0:T(8,128)(2,1)S(1)}, u32[]{:S(2)}, u32[]{:S(2)}) collective-permute-start(bf16[1024,1152]{1,0:T(8,128)(2,1)S(1)} %get-tuple-element.21), channel_id=1, source_target_pairs={{0,1},{1,0},{2,3},{3,2},{4,5},{5,4},{6,7},{7,6},{8,9},{9,8},{10,11... | collective-permute-start | bytes 7077896 | tf_op jit(solution)/shard_map/ppermute | solution.py:24
  133.9 11.5 %collective-permute-start.12 = (bf16[128,1152]{1,0:T(8,128)(2,1)S(1)}, bf16[128,1152]{1,0:T(8,128)(2,1)S(1)}, u32[]{:S(2)}, u32[]{:S(2)}) collective-permute-start(bf16[128,1152]{1,0:T(8,128)(2,1)S(1)} %get-tuple-element.17), channel_id=1, source_target_pairs={{0,64},{32,96},{64,128},{96,160},{128,192},{160,224},{192,0},{224,... | collective-permute-start | bytes 884744 | tf_op jit(solution)/shard_map/ppermute | solution.py:15
  135.1 23.0 %collective-permute-start.14 = (bf16[256,1152]{1,0:T(8,128)(2,1)S(1)}, bf16[256,1152]{1,0:T(8,128)(2,1)S(1)}, u32[]{:S(2)}, u32[]{:S(2)}) collective-permute-start(bf16[256,1152]{1,0:T(8,128)(2,1)S(1)} %get-tuple-element.19), channel_id=1, source_target_pairs={{0,64},{32,96},{64,128},{96,160},{128,192},{160,224},{192,0},{224,... | collective-permute-start | bytes 1769480 | tf_op jit(solution)/shard_map/ppermute | solution.py:15
  136.5 27.5 %collective-permute-start.11 = (bf16[128,1152]{1,0:T(8,128)(2,1)S(1)}, bf16[128,1152]{1,0:T(8,128)(2,1)S(1)}, u32[]{:S(2)}, u32[]{:S(2)}) collective-permute-start(bf16[128,1152]{1,0:T(8,128)(2,1)S(1)} %get-tuple-element.15), channel_id=1, source_target_pairs={{0,64},{32,96},{64,128},{96,160},{128,192},{160,224},{192,0},{224,... | collective-permute-start | bytes 884744 | tf_op jit(solution)/shard_map/ppermute | solution.py:15
  145.4 22.7 %collective-permute-start.13 = (bf16[128,1152]{1,0:T(8,128)(2,1)S(1)}, bf16[128,1152]{1,0:T(8,128)(2,1)S(1)}, u32[]{:S(2)}, u32[]{:S(2)}) collective-permute-start(bf16[128,1152]{1,0:T(8,128)(2,1)S(1)} %add_convert_fusion.1), channel_id=1, source_target_pairs={{0,16},{1,17},{2,18},{3,19},{4,20},{5,21},{6,22},{7,23},{8,24},{9,... | collective-permute-start | bytes 884744 | tf_op jit(solution)/shard_map/ppermute | solution.py:24
  159.0 23.8 %collective-permute-start.18 = (bf16[256,1152]{1,0:T(8,128)(2,1)S(1)}, bf16[256,1152]{1,0:T(8,128)(2,1)S(1)}, u32[]{:S(2)}, u32[]{:S(2)}) collective-permute-start(bf16[256,1152]{1,0:T(8,128)(2,1)S(1)} %get-tuple-element.26), channel_id=1, source_target_pairs={{0,4},{1,5},{2,6},{3,7},{4,0},{5,1},{6,2},{7,3},{8,12},{9,13},{10,... | collective-permute-start | bytes 1769480 | tf_op jit(solution)/shard_map/ppermute | solution.py:24
  159.9 28.1 %collective-permute-start.20 = (bf16[256,1152]{1,0:T(8,128)(2,1)S(1)}, bf16[256,1152]{1,0:T(8,128)(2,1)S(1)}, u32[]{:S(2)}, u32[]{:S(2)}) collective-permute-start(bf16[256,1152]{1,0:T(8,128)(2,1)S(1)} %get-tuple-element.27), channel_id=1, source_target_pairs={{0,6},{1,7},{2,0},{3,1},{4,2},{5,3},{6,4},{7,5},{8,14},{9,15},{10,... | collective-permute-start | bytes 1769480 | tf_op jit(solution)/shard_map/ppermute | solution.py:24
  162.8 25.5 %collective-permute-start.19 = (bf16[256,1152]{1,0:T(8,128)(2,1)S(1)}, bf16[256,1152]{1,0:T(8,128)(2,1)S(1)}, u32[]{:S(2)}, u32[]{:S(2)}) collective-permute-start(bf16[256,1152]{1,0:T(8,128)(2,1)S(1)} %get-tuple-element.28), channel_id=1, source_target_pairs={{0,2},{1,3},{2,4},{3,5},{4,6},{5,7},{6,0},{7,1},{8,10},{9,11},{10,... | collective-permute-start | bytes 1769480 | tf_op jit(solution)/shard_map/ppermute | solution.py:24
  164.1 16.0 %collective-permute-start.15 = (bf16[128,1152]{1,0:T(8,128)(2,1)S(1)}, bf16[128,1152]{1,0:T(8,128)(2,1)S(1)}, u32[]{:S(2)}, u32[]{:S(2)}) collective-permute-start(bf16[128,1152]{1,0:T(8,128)(2,1)S(1)} %get-tuple-element.29), channel_id=1, source_target_pairs={{0,8},{1,9},{2,10},{3,11},{4,12},{5,13},{6,14},{7,15},{8,16},{9,17... | collective-permute-start | bytes 884744 | tf_op jit(solution)/shard_map/ppermute | solution.py:24
  168.2 14.2 %collective-permute-start.16 = (bf16[128,1152]{1,0:T(8,128)(2,1)S(1)}, bf16[128,1152]{1,0:T(8,128)(2,1)S(1)}, u32[]{:S(2)}, u32[]{:S(2)}) collective-permute-start(bf16[128,1152]{1,0:T(8,128)(2,1)S(1)} %get-tuple-element.30), channel_id=1, source_target_pairs={{0,24},{1,25},{2,26},{3,27},{4,28},{5,29},{6,30},{7,31},{8,0},{9,1... | collective-permute-start | bytes 884744 | tf_op jit(solution)/shard_map/ppermute | solution.py:24
  188.5 8.8 %copy-start.1 = (f32[128,1152]{1,0:T(8,128)S(1)}, f32[128,1152]{1,0:T(8,128)}, u32[]{:S(2)}) copy-start(f32[128,1152]{1,0:T(8,128)} %param.5) | copy-start | bytes 1769476
  188.6 8.8 %collective-permute-start.21 = (bf16[128,1152]{1,0:T(8,128)(2,1)S(1)}, bf16[128,1152]{1,0:T(8,128)(2,1)S(1)}, u32[]{:S(2)}, u32[]{:S(2)}) collective-permute-start(bf16[128,1152]{1,0:T(8,128)(2,1)S(1)} %slice.57), channel_id=1, source_target_pairs={{0,224},{32,0},{64,32},{96,64},{128,96},{160,128},{192,160},{224,1... | collective-permute-start | bytes 884744 | tf_op jit(solution)/shard_map/ppermute | solution.py:15
  (2 other events, 3.1 us)

commit v2 on v1

--- a/solution.py
+++ b/solution.py
@@ -22,6 +22,10 @@
         target = ((a + zh) % ZH * Y + (b + y) % Y) * CORE + (c + core) % CORE
         route.append((i, target))
     return lax.ppermute(block, "dev", route)
+
+
+def fence(*arrays):
+    return lax.optimization_barrier(arrays)
 
 
 def unit_rows(values):
@@ -143,40 +147,50 @@
     txt_behind = to_group(txt_0, 1)
     img_up = to_dev(img_0, zh=-1)
     img_down = to_dev(img_0, zh=1)
-    img_2 = to_dev(img_0, zh=2)
     ahead_0 = to_group(img_0, -2)
+    txt_behind, img_up, img_down, ahead_0 = fence(txt_behind, img_up, img_down, ahead_0)
+    txt_pair = jnp.concatenate([txt_0, txt_behind], axis=0)
     img_n = jnp.concatenate([img_up, img_down], axis=0)
-    ahead_n = to_group(img_n, -2)
-    ahead_2 = to_group(img_2, -2)
-    txt_pair = jnp.concatenate([txt_0, txt_behind], axis=0)
     txt_up = to_dev(txt_pair, y=-1)
     txt_down = to_dev(txt_pair, y=1)
-    txt_2 = to_dev(txt_pair, y=2)
-    txt_own = jnp.concatenate([txt_pair, txt_up, txt_down, txt_2], axis=0)
-    txt_sib = to_dev(txt_own, core=1)
+    img_2 = to_dev(img_0, zh=2)
+    ahead_n = to_group(img_n, -2)
+    txt_up, txt_down, img_2, ahead_n = fence(txt_up, txt_down, img_2, ahead_n)
+    txt_far_a = to_dev(txt_up[:128], y=-1)
+    txt_far_b = to_dev(txt_down[128:], y=1)
+    ahead_2 = to_group(img_2, -2)
+    txt_near = jnp.concatenate([txt_pair, txt_up, txt_down], axis=0)
+    sib_near = to_dev(txt_near, core=1)
+    txt_far_a, txt_far_b, ahead_2, sib_near = fence(txt_far_a, txt_far_b, ahead_2, sib_near)
+    txt_far = jnp.concatenate([txt_far_a, txt_far_b], axis=0)
+    sib_far = to_dev(txt_far, core=1)
+    txt_own = jnp.concatenate([txt_near, txt_far], axis=0)
+    txt_sib = jnp.concatenate([sib_near, sib_far], axis=0)
     img_own = jnp.concatenate([img_0, img_n, img_2], axis=0)
     img_ahead = jnp.concatenate([ahead_0, ahead_n, ahead_2], axis=0)
 
     gu_0, gu_n, gu_2, past_sib, past_own = pairs(scalars, img_own, txt_sib, txt_own)
     au_0, au_n, au_2, gv_sib, gv_own = pairs(scalars, img_ahead, txt_sib, txt_own, (past_sib, past_own))
 
-    gu_2 = gu_2 + to_group(au_2, 2).astype(f32)
-    gu_n = gu_n + to_group(au_n, 2).astype(f32)
-    gu_0 = gu_0 + to_group(au_0, 2).astype(f32)
-    gu = (
-        gu_0
-        + to_dev(gu_2.astype(low), zh=2).astype(f32)
-        + to_dev(gu_n[:128].astype(low), zh=1).astype(f32)
-        + to_dev(gu_n[128:].astype(low), zh=-1).astype(f32)
-    )
-    gv_own = gv_own + to_dev(gv_sib, core=1).astype(f32)
-    gv_pair = (
-        gv_own[:256]
-        + to_dev(gv_own[768:].astype(low), y=2).astype(f32)
-        + to_dev(gv_own[256:512].astype(low), y=1).astype(f32)
-        + to_dev(gv_own[512:768].astype(low), y=-1).astype(f32)
-    )
+    back_sib = to_dev(gv_sib, core=1)
+    back_2 = to_group(au_2, 2)
+    back_sib, back_2, au_n = fence(back_sib, back_2, au_n)
+    gv_own = gv_own + back_sib.astype(f32)
+    gu_2 = (gu_2 + back_2.astype(f32)).astype(low)
+    gv_up = to_dev(gv_own[256:512].astype(low), y=1)
+    gv_down = to_dev(gv_own[512:768].astype(low), y=-1)
+    sum_2 = to_dev(gu_2, zh=2)
+    back_n = to_group(au_n, 2)
+    gv_up, gv_down, sum_2, back_n, au_0 = fence(gv_up, gv_down, sum_2, back_n, au_0)
+    gu_n = (gu_n + back_n.astype(f32)).astype(low)
+    gv_2 = to_dev(gv_own[768:].astype(low), y=2)
+    sum_up = to_dev(gu_n[:128], zh=1)
+    sum_down = to_dev(gu_n[128:], zh=-1)
+    back_0 = to_group(au_0, 2)
+    gv_2, sum_up, sum_down, back_0 = fence(gv_2, sum_up, sum_down, back_0)
+    gv_pair = gv_own[:256] + gv_up.astype(f32) + gv_down.astype(f32) + gv_2.astype(f32)
     gv = gv_pair[:128] + to_group(gv_pair[128:].astype(low), -1).astype(f32)
+    gu = gu_0 + back_0.astype(f32) + sum_2.astype(f32) + sum_up.astype(f32) + sum_down.astype(f32)
     return (back_rows(img_unit, img_inv, gu), back_rows(txt_unit, txt_inv, gv))
 
 

time: 202 us -> 169 us (0.84); the launches traced: 199 us -> 168 us
  waiting for transfers between devices: 116 us -> 84.6 us
  local copies, waits for them, and re-layouts: 2.67 us -> 9.83 us
  starting transfers between devices: 37.4 us -> 33.3 us
    ppermute x8, waiting for transfers between devices: 53.9 us -> 19.7 us  [to_group(): lax.ppermute(block, 'grp', [(i, (i + step) % GROUPS) for i in range(GROUP...]
    unnamed x11 -> x39, local copies, waits for them, and re-layouts: 2.38 us -> 8.49 us
    ppermute x8, starting transfers between devices: 10.7 us -> 7.23 us  [to_group(): lax.ppermute(block, 'grp', [(i, (i + step) % GROUPS) for i in range(GROUP...]
    ppermute x14 -> x16, waiting for transfers between devices: 62.3 us -> 64.9 us  [to_dev(): return lax.ppermute(block, 'dev', route)]
    ppermute x14 -> x16, starting transfers between devices: 26.7 us -> 26.1 us  [to_dev(): return lax.ppermute(block, 'dev', route)]
  transfers between devices with their start and end apart: 22 -> 24, of which waited for: 15 -> 12; matrix products, arithmetic and copies ran while one was open for 3% -> 5% of each run, Pallas kernels for 0% -> 0%
where the time goes in v2:
time: 169 us; the launch traced here: 168 us
  waiting for transfers between devices  84.6 us (50%)
  starting transfers between devices  33.3 us (20%)
  Pallas kernels  29.3 us (17%)
  local copies, waits for them, and re-layouts  9.83 us (6%)
  other arithmetic  9.16 us (5%)
  between operations  2.27 us (1%)
    ppermute x16, waiting for transfers between devices, to_dev(): return lax.ppermute(block, 'dev', route)  64.9 us
    pallas_call x2, Pallas kernels, pairs(): pl.pallas_call(functools.partial(pair_kernel, own), grid=(2 * half,), in_...  29.3 us
    ppermute x16, starting transfers between devices, to_dev(): return lax.ppermute(block, 'dev', route)  26.1 us
    ppermute x8, waiting for transfers between devices, to_group(): lax.ppermute(block, 'grp', [(i, (i + step) % GROUPS) for i in range(GROUP...  19.7 us
    unnamed x39, local copies, waits for them, and re-layouts  8.49 us
    ppermute x8, starting transfers between devices, to_group(): lax.ppermute(block, 'grp', [(i, (i + step) % GROUPS) for i in range(GROUP...  7.23 us
  transfers between devices with their start and end apart: 24, of which 12 were waited for; matrix products, arithmetic and copies ran while one was open for 5% of the time, Pallas kernels for 0%

profile of v2, /device:TPU:24, one launch (start us, length us, event | category | flops | bytes accessed | tf_op | source)
XLA Modules:
  0.0 168.5 jit_solution(15379673978747769198)
XLA Ops:
  3.1 2.8 %collective-permute-start.3 = (bf16[128,1152]{1,0:T(8,128)(2,1)S(1)}, bf16[128,1152]{1,0:T(8,128)(2,1)S(1)}, u32[]{:S(2)}, u32[]{:S(2)}) collective-permute-start(bf16[128,1152]{1,0:T(8,128)(2,1)S(1)} %multiply_convert_fusion.1), channel_id=1, source_target_pairs={{0,192},{32,224},{64,0},{96,32},{128,64},{160,96},{192,128},{224,1... | collective-permute-start | bytes 884744 | tf_op jit(solution)/shard_map/ppermute | solution.py:15
  5.9 3.3 %collective-permute-start.2 = (bf16[128,1152]{1,0:T(8,128)(2,1)S(1)}, bf16[128,1152]{1,0:T(8,128)(2,1)S(1)}, u32[]{:S(2)}, u32[]{:S(2)}) collective-permute-start(bf16[128,1152]{1,0:T(8,128)(2,1)S(1)} %multiply_convert_fusion.1), channel_id=1, source_target_pairs={{0,8},{1,9},{2,10},{3,11},{4,12},{5,13},{6,14},{7,15},{8,16},{9,17... | collective-permute-start | bytes 884744 | tf_op jit(solution)/shard_map/ppermute | solution.py:24
  9.2 3.0 %collective-permute-start.1 = (bf16[128,1152]{1,0:T(8,128)(2,1)S(1)}, bf16[128,1152]{1,0:T(8,128)(2,1)S(1)}, u32[]{:S(2)}, u32[]{:S(2)}) collective-permute-start(bf16[128,1152]{1,0:T(8,128)(2,1)S(1)} %multiply_convert_fusion.1), channel_id=1, source_target_pairs={{0,24},{1,25},{2,26},{3,27},{4,28},{5,29},{6,30},{7,31},{8,0},{9,1... | collective-permute-start | bytes 884744 | tf_op jit(solution)/shard_map/ppermute | solution.py:24
  14.6 11.8 %collective-permute-done.2 = bf16[128,1152]{1,0:T(8,128)(2,1)S(1)} collective-permute-done((bf16[128,1152]{1,0:T(8,128)(2,1)S(1)}, bf16[128,1152]{1,0:T(8,128)(2,1)S(1)}, u32[]{:S(2)}, u32[]{:S(2)}) %collective-permute-start.2) | collective-permute-done | bytes 294944 | tf_op jit(solution)/shard_map/ppermute | solution.py:24
  26.4 6.1 %collective-permute-done = bf16[128,1152]{1,0:T(8,128)(2,1)S(1)} collective-permute-done((bf16[128,1152]{1,0:T(8,128)(2,1)S(1)}, bf16[128,1152]{1,0:T(8,128)(2,1)S(1)}, u32[]{:S(2)}, u32[]{:S(2)}) %collective-permute-start) | collective-permute-done | bytes 294944 | tf_op jit(solution)/shard_map/ppermute | solution.py:15
  33.5 1.8 %collective-permute-start.4 = (bf16[256,1152]{1,0:T(8,128)(2,1)S(1)}, bf16[256,1152]{1,0:T(8,128)(2,1)S(1)}, u32[]{:S(2)}, u32[]{:S(2)}) collective-permute-start(bf16[256,1152]{1,0:T(8,128)(2,1)S(1)} %pad_maximum_fusion.3), channel_id=1, source_target_pairs={{0,6},{1,7},{2,0},{3,1},{4,2},{5,3},{6,4},{7,5},{8,14},{9,15},{10,... | collective-permute-start | bytes 1769480 | tf_op jit(solution)/shard_map/ppermute | solution.py:24
  35.3 4.2 %collective-permute-start.6 = (bf16[128,1152]{1,0:T(8,128)(2,1)S(1)}, bf16[128,1152]{1,0:T(8,128)(2,1)S(1)}, u32[]{:S(2)}, u32[]{:S(2)}) collective-permute-start(bf16[128,1152]{1,0:T(8,128)(2,1)S(1)} %multiply_convert_fusion.1), channel_id=1, source_target_pairs={{0,16},{1,17},{2,18},{3,19},{4,20},{5,21},{6,22},{7,23},{8,24},{9,... | collective-permute-start | bytes 884744 | tf_op jit(solution)/shard_map/ppermute | solution.py:24
  39.5 13.4 %collective-permute-done.6 = bf16[128,1152]{1,0:T(8,128)(2,1)S(1)} collective-permute-done((bf16[128,1152]{1,0:T(8,128)(2,1)S(1)}, bf16[128,1152]{1,0:T(8,128)(2,1)S(1)}, u32[]{:S(2)}, u32[]{:S(2)}) %collective-permute-start.6) | collective-permute-done | bytes 294944 | tf_op jit(solution)/shard_map/ppermute | solution.py:24
  59.4 1.6 collective-permute-start.9
  63.5 5.5 %collective-permute-done.9 = bf16[128,1152]{1,0:T(8,128)(2,1)S(1)} collective-permute-done((bf16[128,1152]{1,0:T(8,128)(2,1)S(1)}, bf16[128,1152]{1,0:T(8,128)(2,1)S(1)}, u32[]{:S(2)}, u32[]{:S(2)}) %collective-permute-start.9) | collective-permute-done | bytes 294944 | tf_op jit(solution)/shard_map/ppermute | solution.py:24
  68.9 2.4 %collective-permute-done.8 = bf16[128,1152]{1,0:T(8,128)(2,1)S(1)} collective-permute-done((bf16[128,1152]{1,0:T(8,128)(2,1)S(1)}, bf16[128,1152]{1,0:T(8,128)(2,1)S(1)}, u32[]{:S(2)}, u32[]{:S(2)}) %collective-permute-start.8) | collective-permute-done | bytes 294944 | tf_op jit(solution)/shard_map/ppermute | solution.py:24
  71.9 1.6 constant_dynamic-update-slice_fusion.1
  73.8 14.6 %shard_map.59 = (f32[128,1152]{1,0:T(8,128)S(1)}, f32[256,1152]{1,0:T(8,128)S(1)}, f32[128,1152]{1,0:T(8,128)S(1)}, f32[1024,1152]{1,0:T(8,128)S(1)}, f32[1024,1152]{1,0:T(8,128)}) custom-call(f32[2]{0:T(128)S(1)} %pad_maximum_fusion.6.scalars, bf16[512,1152]{1,0:T(8,128)(2,1)S(1)} %pad_maximum_fusion.1.img, ...), custom_call_target="tpu_custom_call" | custom-call | flops 7247757312 | bytes 14155776 | tf_op jit(solution)/shard_map/pallas_call | solution.py:113
  88.4 2.2 %copy-done = f32[1024,1152]{1,0:T(8,128)} copy-done((f32[1024,1152]{1,0:T(8,128)}, f32[1024,1152]{1,0:T(8,128)S(1)}, u32[]{:S(2)}) %copy-start) | copy-done | bytes 4718616
  90.6 14.7 %shard_map.60 = (bf16[128,1152]{1,0:T(8,128)(2,1)S(1)}, bf16[256,1152]{1,0:T(8,128)(2,1)S(1)}, bf16[128,1152]{1,0:T(8,128)(2,1)S(1)}, bf16[1024,1152]{1,0:T(8,128)(2,1)S(1)}, f32[1024,1152]{1,0:T(8,128)S(1)}) custom-call(f32[2]{0:T(128)S(1)} %pad_maximum_fusion.6.scalars, bf16[512,1152]{1,0:T(8,128)(2,1)S(1)} %pad_maximum_fusion.2.img, ...), custom_call_target="tpu_custom_call" | custom-call | flops 7247757312 | bytes 14155776 | tf_op jit(solution)/shard_map/pallas_call | solution.py:113
  107.2 8.8 %collective-permute-done.14 = bf16[128,1152]{1,0:T(8,128)(2,1)S(1)} collective-permute-done((bf16[128,1152]{1,0:T(8,128)(2,1)S(1)}, bf16[128,1152]{1,0:T(8,128)(2,1)S(1)}, u32[]{:S(2)}, u32[]{:S(2)}) %collective-permute-start.14) | collective-permute-done | bytes 294944 | tf_op jit(solution)/shard_map/ppermute | solution.py:15
  117.2 3.2 %collective-permute-start.16 = (bf16[256,1152]{1,0:T(8,128)(2,1)S(1)}, bf16[256,1152]{1,0:T(8,128)(2,1)S(1)}, u32[]{:S(2)}, u32[]{:S(2)}) collective-permute-start(bf16[256,1152]{1,0:T(8,128)(2,1)S(1)} %get-tuple-element.75), channel_id=1, source_target_pairs={{0,2},{1,3},{2,4},{3,5},{4,6},{5,7},{6,0},{7,1},{8,10},{9,11},{10,... | collective-permute-start | bytes 1769480 | tf_op jit(solution)/shard_map/ppermute | solution.py:24
  120.7 4.1 %collective-permute-start.18 = (bf16[128,1152]{1,0:T(8,128)(2,1)S(1)}, bf16[128,1152]{1,0:T(8,128)(2,1)S(1)}, u32[]{:S(2)}, u32[]{:S(2)}) collective-permute-start(bf16[128,1152]{1,0:T(8,128)(2,1)S(1)} %add_convert_fusion.1), channel_id=1, source_target_pairs={{0,16},{1,17},{2,18},{3,19},{4,20},{5,21},{6,22},{7,23},{8,24},{9,... | collective-permute-start | bytes 884744 | tf_op jit(solution)/shard_map/ppermute | solution.py:24
  125.0 13.4 %collective-permute-done.18 = bf16[128,1152]{1,0:T(8,128)(2,1)S(1)} collective-permute-done((bf16[128,1152]{1,0:T(8,128)(2,1)S(1)}, bf16[128,1152]{1,0:T(8,128)(2,1)S(1)}, u32[]{:S(2)}, u32[]{:S(2)}) %collective-permute-start.18) | collective-permute-done | bytes 294944 | tf_op jit(solution)/shard_map/ppermute | solution.py:24
  138.4 6.5 %collective-permute-done.16 = bf16[256,1152]{1,0:T(8,128)(2,1)S(1)} collective-permute-done((bf16[256,1152]{1,0:T(8,128)(2,1)S(1)}, bf16[256,1152]{1,0:T(8,128)(2,1)S(1)}, u32[]{:S(2)}, u32[]{:S(2)}) %collective-permute-start.16) | collective-permute-done | bytes 589856 | tf_op jit(solution)/shard_map/ppermute | solution.py:24
  145.6 2.5 %collective-permute-start.20 = (bf16[128,1152]{1,0:T(8,128)(2,1)S(1)}, bf16[128,1152]{1,0:T(8,128)(2,1)S(1)}, u32[]{:S(2)}, u32[]{:S(2)}) collective-permute-start(bf16[128,1152]{1,0:T(8,128)(2,1)S(1)} %get-tuple-element.78), channel_id=1, source_target_pairs={{0,8},{1,9},{2,10},{3,11},{4,12},{5,13},{6,14},{7,15},{8,16},{9,17... | collective-permute-start | bytes 884744 | tf_op jit(solution)/shard_map/ppermute | solution.py:24
  148.3 5.7 %collective-permute-done.21 = bf16[128,1152]{1,0:T(8,128)(2,1)S(1)} collective-permute-done((bf16[128,1152]{1,0:T(8,128)(2,1)S(1)}, bf16[128,1152]{1,0:T(8,128)(2,1)S(1)}, u32[]{:S(2)}, u32[]{:S(2)}) %collective-permute-start.21) | collective-permute-done | bytes 294944 | tf_op jit(solution)/shard_map/ppermute | solution.py:24
  154.1 6.1 %collective-permute-done.20 = bf16[128,1152]{1,0:T(8,128)(2,1)S(1)} collective-permute-done((bf16[128,1152]{1,0:T(8,128)(2,1)S(1)}, bf16[128,1152]{1,0:T(8,128)(2,1)S(1)}, u32[]{:S(2)}, u32[]{:S(2)}) %collective-permute-start.20) | collective-permute-done | bytes 294944 | tf_op jit(solution)/shard_map/ppermute | solution.py:24
  162.6 4.7 %collective-permute-done.23 = bf16[128,1152]{1,0:T(8,128)(2,1)S(1)} collective-permute-done((bf16[128,1152]{1,0:T(8,128)(2,1)S(1)}, bf16[128,1152]{1,0:T(8,128)(2,1)S(1)}, u32[]{:S(2)}, u32[]{:S(2)}) %collective-permute-start.23) | collective-permute-done | bytes 294944 | tf_op jit(solution)/shard_map/ppermute | solution.py:15
  (93 shorter events, 22.3 us)
Async XLA Ops:
  3.1 11.6 %collective-permute-start.3 = (bf16[128,1152]{1,0:T(8,128)(2,1)S(1)}, bf16[128,1152]{1,0:T(8,128)(2,1)S(1)}, u32[]{:S(2)}, u32[]{:S(2)}) collective-permute-start(bf16[128,1152]{1,0:T(8,128)(2,1)S(1)} %multiply_convert_fusion.1), channel_id=1, source_target_pairs={{0,192},{32,224},{64,0},{96,32},{128,64},{160,96},{192,128},{224,1... | collective-permute-start | bytes 884744 | tf_op jit(solution)/shard_map/ppermute | solution.py:15
  5.9 20.5 %collective-permute-start.2 = (bf16[128,1152]{1,0:T(8,128)(2,1)S(1)}, bf16[128,1152]{1,0:T(8,128)(2,1)S(1)}, u32[]{:S(2)}, u32[]{:S(2)}) collective-permute-start(bf16[128,1152]{1,0:T(8,128)(2,1)S(1)} %multiply_convert_fusion.1), channel_id=1, source_target_pairs={{0,8},{1,9},{2,10},{3,11},{4,12},{5,13},{6,14},{7,15},{8,16},{9,17... | collective-permute-start | bytes 884744 | tf_op jit(solution)/shard_map/ppermute | solution.py:24
  9.2 17.3 %collective-permute-start.1 = (bf16[128,1152]{1,0:T(8,128)(2,1)S(1)}, bf16[128,1152]{1,0:T(8,128)(2,1)S(1)}, u32[]{:S(2)}, u32[]{:S(2)}) collective-permute-start(bf16[128,1152]{1,0:T(8,128)(2,1)S(1)} %multiply_convert_fusion.1), channel_id=1, source_target_pairs={{0,24},{1,25},{2,26},{3,27},{4,28},{5,29},{6,30},{7,31},{8,0},{9,1... | collective-permute-start | bytes 884744 | tf_op jit(solution)/shard_map/ppermute | solution.py:24
  13.5 19.0 %collective-permute-start = (bf16[128,1152]{1,0:T(8,128)(2,1)S(1)}, bf16[128,1152]{1,0:T(8,128)(2,1)S(1)}, u32[]{:S(2)}, u32[]{:S(2)}) collective-permute-start(bf16[128,1152]{1,0:T(8,128)(2,1)S(1)} %get-tuple-element.73), channel_id=1, source_target_pairs={{0,32},{32,64},{64,96},{96,128},{128,160},{160,192},{192,224},{224... | collective-permute-start | bytes 884744 | tf_op jit(solution)/shard_map/ppermute | solution.py:15
  32.7 20.2 %collective-permute-start.7 = (bf16[256,1152]{1,0:T(8,128)(2,1)S(1)}, bf16[256,1152]{1,0:T(8,128)(2,1)S(1)}, u32[]{:S(2)}, u32[]{:S(2)}) collective-permute-start(bf16[256,1152]{1,0:T(8,128)(2,1)S(1)} %pad_maximum_fusion.4), channel_id=1, source_target_pairs={{0,192},{32,224},{64,0},{96,32},{128,64},{160,96},{192,128},{224,1... | collective-permute-start | bytes 1769480 | tf_op jit(solution)/shard_map/ppermute | solution.py:15
  33.3 19.6 %collective-permute-start.5 = (bf16[256,1152]{1,0:T(8,128)(2,1)S(1)}, bf16[256,1152]{1,0:T(8,128)(2,1)S(1)}, u32[]{:S(2)}, u32[]{:S(2)}) collective-permute-start(bf16[256,1152]{1,0:T(8,128)(2,1)S(1)} %pad_maximum_fusion.3), channel_id=1, source_target_pairs={{0,2},{1,3},{2,4},{3,5},{4,6},{5,7},{6,0},{7,1},{8,10},{9,11},{10,... | collective-permute-start | bytes 1769480 | tf_op jit(solution)/shard_map/ppermute | solution.py:24
  33.5 20.3 %collective-permute-start.4 = (bf16[256,1152]{1,0:T(8,128)(2,1)S(1)}, bf16[256,1152]{1,0:T(8,128)(2,1)S(1)}, u32[]{:S(2)}, u32[]{:S(2)}) collective-permute-start(bf16[256,1152]{1,0:T(8,128)(2,1)S(1)} %pad_maximum_fusion.3), channel_id=1, source_target_pairs={{0,6},{1,7},{2,0},{3,1},{4,2},{5,3},{6,4},{7,5},{8,14},{9,15},{10,... | collective-permute-start | bytes 1769480 | tf_op jit(solution)/shard_map/ppermute | solution.py:24
  35.3 17.5 %collective-permute-start.6 = (bf16[128,1152]{1,0:T(8,128)(2,1)S(1)}, bf16[128,1152]{1,0:T(8,128)(2,1)S(1)}, u32[]{:S(2)}, u32[]{:S(2)}) collective-permute-start(bf16[128,1152]{1,0:T(8,128)(2,1)S(1)} %multiply_convert_fusion.1), channel_id=1, source_target_pairs={{0,16},{1,17},{2,18},{3,19},{4,20},{5,21},{6,22},{7,23},{8,24},{9,... | collective-permute-start | bytes 884744 | tf_op jit(solution)/shard_map/ppermute | solution.py:24
  55.9 15.4 %collective-permute-start.11 = (bf16[768,1152]{1,0:T(8,128)(2,1)}, bf16[768,1152]{1,0:T(8,128)(2,1)}, u32[]{:S(2)}, u32[]{:S(2)}) collective-permute-start(bf16[768,1152]{1,0:T(8,128)(2,1)} %pad_maximum_fusion), channel_id=1, source_target_pairs={{0,1},{1,0},{2,3},{3,2},{4,5},{5,4},{6,7},{7,6},{8,9},{9,8},{10,11... | collective-permute-start | bytes 5308424 | tf_op jit(solution)/shard_map/ppermute | solution.py:24
  59.4 9.5 %collective-permute-start.9 = (bf16[128,1152]{1,0:T(8,128)(2,1)S(1)}, bf16[128,1152]{1,0:T(8,128)(2,1)S(1)}, u32[]{:S(2)}, u32[]{:S(2)}) collective-permute-start(bf16[128,1152]{1,0:T(8,128)(2,1)S(1)} %slice.35), channel_id=1, source_target_pairs={{0,2},{1,3},{2,4},{3,5},{4,6},{5,7},{6,0},{7,1},{8,10},{9,11},{10,... | collective-permute-start | bytes 884744 | tf_op jit(solution)/shard_map/ppermute | solution.py:24
  61.0 10.3 %collective-permute-start.8 = (bf16[128,1152]{1,0:T(8,128)(2,1)S(1)}, bf16[128,1152]{1,0:T(8,128)(2,1)S(1)}, u32[]{:S(2)}, u32[]{:S(2)}) collective-permute-start(bf16[128,1152]{1,0:T(8,128)(2,1)S(1)} %slice.34), channel_id=1, source_target_pairs={{0,6},{1,7},{2,0},{3,1},{4,2},{5,3},{6,4},{7,5},{8,14},{9,15},{10,... | collective-permute-start | bytes 884744 | tf_op jit(solution)/shard_map/ppermute | solution.py:24
  61.6 9.8 %collective-permute-start.10 = (bf16[128,1152]{1,0:T(8,128)(2,1)}, bf16[128,1152]{1,0:T(8,128)(2,1)S(1)}, u32[]{:S(2)}, u32[]{:S(2)}) collective-permute-start(bf16[128,1152]{1,0:T(8,128)(2,1)} %copy-done.15), channel_id=1, source_target_pairs={{0,192},{32,224},{64,0},{96,32},{128,64},{160,96},{192,128},{224,1... | collective-permute-start | bytes 884744 | tf_op jit(solution)/shard_map/ppermute | solution.py:15
  71.5 2.3 %collective-permute-start.12 = (bf16[256,1152]{1,0:T(8,128)(2,1)S(1)}, bf16[256,1152]{1,0:T(8,128)(2,1)S(1)}, u32[]{:S(2)}, u32[]{:S(2)}) collective-permute-start(bf16[256,1152]{1,0:T(8,128)(2,1)S(1)} %pad_maximum_fusion.5), channel_id=1, source_target_pairs={{0,1},{1,0},{2,3},{3,2},{4,5},{5,4},{6,7},{7,6},{8,9},{9,8},{10,11... | collective-permute-start | bytes 1769480 | tf_op jit(solution)/shard_map/ppermute | solution.py:24
  105.3 10.7 %collective-permute-start.13 = (bf16[1024,1152]{1,0:T(8,128)(2,1)S(1)}, bf16[1024,1152]{1,0:T(8,128)(2,1)S(1)}, u32[]{:S(2)}, u32[]{:S(2)}) collective-permute-start(bf16[1024,1152]{1,0:T(8,128)(2,1)S(1)} %get-tuple-element.52), channel_id=1, source_target_pairs={{0,1},{1,0},{2,3},{3,2},{4,5},{5,4},{6,7},{7,6},{8,9},{9,8},{10,11... | collective-permute-start | bytes 7077896 | tf_op jit(solution)/shard_map/ppermute | solution.py:24
  105.7 10.3 %collective-permute-start.14 = (bf16[128,1152]{1,0:T(8,128)(2,1)S(1)}, bf16[128,1152]{1,0:T(8,128)(2,1)S(1)}, u32[]{:S(2)}, u32[]{:S(2)}) collective-permute-start(bf16[128,1152]{1,0:T(8,128)(2,1)S(1)} %get-tuple-element.53), channel_id=1, source_target_pairs={{0,64},{32,96},{64,128},{96,160},{128,192},{160,224},{192,0},{224,... | collective-permute-start | bytes 884744 | tf_op jit(solution)/shard_map/ppermute | solution.py:15
  116.8 21.6 %collective-permute-start.17 = (bf16[256,1152]{1,0:T(8,128)(2,1)S(1)}, bf16[256,1152]{1,0:T(8,128)(2,1)S(1)}, u32[]{:S(2)}, u32[]{:S(2)}) collective-permute-start(bf16[256,1152]{1,0:T(8,128)(2,1)S(1)} %get-tuple-element.74), channel_id=1, source_target_pairs={{0,6},{1,7},{2,0},{3,1},{4,2},{5,3},{6,4},{7,5},{8,14},{9,15},{10,... | collective-permute-start | bytes 1769480 | tf_op jit(solution)/shard_map/ppermute | solution.py:24
  117.2 27.7 %collective-permute-start.16 = (bf16[256,1152]{1,0:T(8,128)(2,1)S(1)}, bf16[256,1152]{1,0:T(8,128)(2,1)S(1)}, u32[]{:S(2)}, u32[]{:S(2)}) collective-permute-start(bf16[256,1152]{1,0:T(8,128)(2,1)S(1)} %get-tuple-element.75), channel_id=1, source_target_pairs={{0,2},{1,3},{2,4},{3,5},{4,6},{5,7},{6,0},{7,1},{8,10},{9,11},{10,... | collective-permute-start | bytes 1769480 | tf_op jit(solution)/shard_map/ppermute | solution.py:24
  120.4 24.5 %collective-permute-start.19 = (bf16[256,1152]{1,0:T(8,128)(2,1)S(1)}, bf16[256,1152]{1,0:T(8,128)(2,1)S(1)}, u32[]{:S(2)}, u32[]{:S(2)}) collective-permute-start(bf16[256,1152]{1,0:T(8,128)(2,1)S(1)} %get-tuple-element.59), channel_id=1, source_target_pairs={{0,64},{32,96},{64,128},{96,160},{128,192},{160,224},{192,0},{224,... | collective-permute-start | bytes 1769480 | tf_op jit(solution)/shard_map/ppermute | solution.py:15
  120.7 17.7 %collective-permute-start.18 = (bf16[128,1152]{1,0:T(8,128)(2,1)S(1)}, bf16[128,1152]{1,0:T(8,128)(2,1)S(1)}, u32[]{:S(2)}, u32[]{:S(2)}) collective-permute-start(bf16[128,1152]{1,0:T(8,128)(2,1)S(1)} %add_convert_fusion.1), channel_id=1, source_target_pairs={{0,16},{1,17},{2,18},{3,19},{4,20},{5,21},{6,22},{7,23},{8,24},{9,... | collective-permute-start | bytes 884744 | tf_op jit(solution)/shard_map/ppermute | solution.py:24
  124.9 23.5 %collective-permute-start.15 = (bf16[256,1152]{1,0:T(8,128)(2,1)S(1)}, bf16[256,1152]{1,0:T(8,128)(2,1)S(1)}, u32[]{:S(2)}, u32[]{:S(2)}) collective-permute-start(bf16[256,1152]{1,0:T(8,128)(2,1)S(1)} %get-tuple-element.76), channel_id=1, source_target_pairs={{0,4},{1,5},{2,6},{3,7},{4,0},{5,1},{6,2},{7,3},{8,12},{9,13},{10,... | collective-permute-start | bytes 1769480 | tf_op jit(solution)/shard_map/ppermute | solution.py:24
  145.1 9.0 %collective-permute-start.21 = (bf16[128,1152]{1,0:T(8,128)(2,1)S(1)}, bf16[128,1152]{1,0:T(8,128)(2,1)S(1)}, u32[]{:S(2)}, u32[]{:S(2)}) collective-permute-start(bf16[128,1152]{1,0:T(8,128)(2,1)S(1)} %get-tuple-element.77), channel_id=1, source_target_pairs={{0,24},{1,25},{2,26},{3,27},{4,28},{5,29},{6,30},{7,31},{8,0},{9,1... | collective-permute-start | bytes 884744 | tf_op jit(solution)/shard_map/ppermute | solution.py:24
  145.6 14.6 %collective-permute-start.20 = (bf16[128,1152]{1,0:T(8,128)(2,1)S(1)}, bf16[128,1152]{1,0:T(8,128)(2,1)S(1)}, u32[]{:S(2)}, u32[]{:S(2)}) collective-permute-start(bf16[128,1152]{1,0:T(8,128)(2,1)S(1)} %get-tuple-element.78), channel_id=1, source_target_pairs={{0,8},{1,9},{2,10},{3,11},{4,12},{5,13},{6,14},{7,15},{8,16},{9,17... | collective-permute-start | bytes 884744 | tf_op jit(solution)/shard_map/ppermute | solution.py:24
  148.1 12.1 %collective-permute-start.22 = (bf16[128,1152]{1,0:T(8,128)(2,1)S(1)}, bf16[128,1152]{1,0:T(8,128)(2,1)S(1)}, u32[]{:S(2)}, u32[]{:S(2)}) collective-permute-start(bf16[128,1152]{1,0:T(8,128)(2,1)S(1)} %get-tuple-element.62), channel_id=1, source_target_pairs={{0,64},{32,96},{64,128},{96,160},{128,192},{160,224},{192,0},{224,... | collective-permute-start | bytes 884744 | tf_op jit(solution)/shard_map/ppermute | solution.py:15
  160.5 6.8 %collective-permute-start.23 = (bf16[128,1152]{1,0:T(8,128)(2,1)S(1)}, bf16[128,1152]{1,0:T(8,128)(2,1)S(1)}, u32[]{:S(2)}, u32[]{:S(2)}) collective-permute-start(bf16[128,1152]{1,0:T(8,128)(2,1)S(1)} %slice.63), channel_id=1, source_target_pairs={{0,224},{32,0},{64,32},{96,64},{128,96},{160,128},{192,160},{224,1... | collective-permute-start | bytes 884744 | tf_op jit(solution)/shard_map/ppermute | solution.py:15
  (17 other events, 197.5 us)

commit v3 on v0

v3 whole, which is shorter than its diff:
```python
import functools

import jax
import jax.numpy as jnp
from jax import lax
from jax.experimental import pallas as pl
from jax.experimental.pallas import tpu as pltpu
from jax.sharding import PartitionSpec as P

X, ZL, ZH, Y, CORE = 4, 2, 4, 4, 2
GROUPS, DEVS = X * ZL, ZH * Y * CORE
F32, LOW = jnp.float32, jnp.bfloat16


def to_group(block, step):
    return lax.ppermute(block, "grp", [(i, (i + step) % GROUPS) for i in range(GROUPS)])


def to_dev(block, zh=0, y=0, core=0):
    route = []
    for i in range(DEVS):
        a, b, c = i // (Y * CORE), i // CORE % Y, i % CORE
        target = ((a + zh) % ZH * Y + (b + y) % Y) * CORE + (c + core) % CORE
        route.append((i, target))
    return lax.ppermute(block, "dev", route)


def fence(*arrays):
    return lax.optimization_barrier(arrays)


VMEM = pl.BlockSpec(memory_space=pltpu.VMEM)
TILE = 512


def whole(kernel, outs, *operands, flops=0, scalars=False, aliases=None, scratch=()):
    first = [pl.BlockSpec(memory_space=pltpu.SMEM)] if scalars else [VMEM]
    size = sum(int(o.size) * o.dtype.itemsize for o in operands)
    return pl.pallas_call(
        kernel,
        in_specs=first + [VMEM] * (len(operands) - 1),
        out_specs=[VMEM] * len(outs),
        out_shape=[jax.ShapeDtypeStruct(shape, kind) for shape, kind in outs],
        input_output_aliases=aliases or {},
        scratch_shapes=list(scratch),
        compiler_params=pltpu.CompilerParams(vmem_limit_bytes=28 * 1024 * 1024),
        cost_estimate=pl.CostEstimate(flops=flops, bytes_accessed=size, transcendentals=0),
    )(*operands)


def inverse_of(values):
    return lax.rsqrt(jnp.sum(values * values, axis=1, keepdims=True) + 1e-06)


def unit_kernel(txt, img, txt_low, img_low):
    for values, low in ((txt, txt_low), (img, img_low)):
        low[...] = (values[...] * inverse_of(values[...])).astype(LOW)


def end_kernel(img, txt, gu_0, *refs):
    *parts, gv_0, up, down, far, behind, grad_img, grad_txt = refs
    gu = gu_0[0:128]
    for part in parts:
        gu = gu + part[...].astype(F32)
    gv = gv_0[0:128]
    for part in (up, down, far, behind):
        gv = gv + part[...].astype(F32)
    for values, sums, grad in ((img, gu, grad_img), (txt, gv, grad_txt)):
        inverse = inverse_of(values[...])
        unit = values[...] * inverse
        grad[...] = inverse * (sums - unit * jnp.sum(unit * sums, axis=1, keepdims=True))


def text_sums_kernel(mine, got, keep, sh_up, sh_down, sh_far, own_up, own_down, own_far):
    def rows(n):
        return mine[pl.ds(n * 128, 128)] + got[pl.ds(n * 128, 128)].astype(F32)

    keep[0:128] = rows(0)
    keep[128:256] = rows(4)
    for n, out in ((1, own_up), (2, own_down), (3, own_far), (5, sh_up), (6, sh_down), (7, sh_far)):
        out[...] = rows(n).astype(LOW)


def pair_kernel(gu_past, gv_past, diagonal, parts, scalars, img, txt, *refs):
    refs = list(refs)
    gu_in = refs.pop(0) if gu_past else None
    gv_in = refs.pop(0) if gv_past else None
    gus = [refs.pop(0) for _ in parts]
    gv = refs.pop(0)
    total = refs.pop(0) if refs else gus[0]
    half_temp, half_bias = scalars[0], scalars[1]
    if gu_past and total is not gus[0]:
        total[...] = gu_in[...]

    @pl.loop(0, txt.shape[0] // TILE)
    def _(n):
        first = pl.multiple_of(n * TILE, TILE)
        span = pl.ds(first, TILE)
        logits = lax.dot_general(
            img[...], txt[span], (((1,), (1,)), ((), ())), preferred_element_type=F32
        )
        slopes = half_temp * jnp.tanh(half_temp * logits + half_bias) + half_temp
        if diagonal:
            rows = lax.broadcasted_iota(jnp.int32, slopes.shape, 0)
            cols = lax.broadcasted_iota(jnp.int32, slopes.shape, 1) + first
            own = jnp.logical_and(rows == cols, rows < 128)
            slopes = slopes - jnp.where(own, 2.0 * half_temp, 0.0)
        coef = slopes.astype(LOW)
        part = jnp.dot(coef, txt[span], preferred_element_type=F32)
        if gu_past:
            total[...] += part
        else:

            @pl.when(n == 0)
            def _():
                total[...] = part

            @pl.when(n > 0)
            def _():
                total[...] += part

        term = lax.dot_general(
            coef, img[...], (((0,), (0,)), ((), ())), preferred_element_type=F32
        )
        if gv_past:
            term = term + gv_in[span]
        gv[span] = term.astype(gv.dtype)

    if total is not gus[0]:
        for (first, size), out in zip(parts, gus):
            out[...] = total[first : first + size].astype(out.dtype)


def pairs(scalars, img, txt, gu_in=None, gv_in=None, gu_parts=None, gv_kind=F32, diagonal=False):
    (rows, width), cols = img.shape, txt.shape[0]
    operands, aliases = [scalars, img, txt], {}
    parts, kind, scratch = gu_parts or [(0, rows)], F32, []
    if gu_parts:
        kind, scratch = LOW, [pltpu.VMEM((rows, width), F32)]
    if gu_in is not None:
        if not gu_parts:
            aliases[len(operands)] = 0
        operands.append(gu_in)
    if gv_in is not None:
        if gv_kind == F32:
            aliases[len(operands)] = len(parts)
        operands.append(gv_in)
    outs = [((size, width), kind) for _, size in parts] + [((cols, width), gv_kind)]
    kernel = functools.partial(pair_kernel, gu_in is not None, gv_in is not None, diagonal, parts)
    return whole(
        kernel,
        outs,
        *operands,
        flops=6 * rows * cols * width,
        scalars=True,
        aliases=aliases,
        scratch=scratch,
    )


def local(image_emb, text_emb, temp, bias):
    rows = image_emb.shape
    txt_0, img_0 = whole(unit_kernel, [(rows, LOW)] * 2, text_emb, image_emb)
    scalars = jnp.stack([0.5 * temp, 0.5 * bias])

    txt_2 = to_dev(txt_0, y=2)
    ahead_0 = to_group(img_0, -2)
    img_up = to_dev(img_0, zh=-1)
    img_down = to_dev(img_0, zh=1)
    behind_0 = to_group(txt_0, 1)
    txt_2, ahead_0, img_up, img_down, behind_0 = fence(txt_2, ahead_0, img_up, img_down, behind_0)
    pair_0 = jnp.concatenate([txt_0, behind_0], axis=0)
    img_n = jnp.concatenate([img_up, img_down], axis=0)
    pair_0, img_n, behind_0, img_0 = fence(pair_0, img_n, behind_0, img_0)
    behind_2 = to_dev(behind_0, y=2)
    pair_up = to_dev(pair_0, y=-1)
    pair_down = to_dev(pair_0, y=1)
    ahead_n = to_group(img_n, -2)
    img_2 = to_dev(img_0, zh=2)
    behind_2, pair_up, pair_down, ahead_n, img_2 = fence(behind_2, pair_up, pair_down, ahead_n, img_2)
    txt_c = jnp.concatenate(
        [txt_0, pair_up[:128], pair_down[:128], txt_2, behind_0, pair_up[128:], pair_down[128:], behind_2],
        axis=0,
    )
    img_own = jnp.concatenate([img_0, img_n, img_2], axis=0)
    txt_s = to_dev(txt_c, core=1)
    ahead_2 = to_group(img_2, -2)
    gu_own, gv_c = pairs(scalars, img_own, txt_c, diagonal=True)
    gu_own, gv_s = pairs(scalars, img_own, txt_s, gu_in=gu_own)
    ahead_2, gu_own, gv_s = fence(ahead_2, gu_own, gv_s)
    img_ahead = jnp.concatenate([ahead_0, ahead_n, ahead_2], axis=0)
    gu_ahead, gv_s = pairs(scalars, img_ahead, txt_s, gv_in=gv_s, gv_kind=LOW)
    got = to_dev(gv_s, core=1)
    au_0, au_n, au_2, gv_c = pairs(
        scalars, img_ahead, txt_c, gu_in=gu_ahead, gv_in=gv_c, gu_parts=[(0, 128), (128, 256), (384, 128)]
    )
    got, gv_c, au_2 = fence(got, gv_c, au_2)
    gv_keep, sh_up, sh_down, sh_far, own_up, own_down, own_far = whole(
        text_sums_kernel, [((256, rows[1]), F32)] + [(rows, LOW)] * 6, gv_c, got
    )
    sh_up = to_dev(sh_up, y=1)
    sh_down = to_dev(sh_down, y=-1)
    back_2 = to_group(au_2, 2)
    sh_up, sh_down, back_2, au_n, sh_far, own_up, own_down = fence(
        sh_up, sh_down, back_2, au_n, sh_far, own_up, own_down
    )
    sum_2 = (gu_own[384:] + back_2.astype(F32)).astype(LOW)
    sum_2, au_n, sh_far, own_up, own_down = fence(sum_2, au_n, sh_far, own_up, own_down)
    sh_far = to_dev(sh_far, y=2)
    own_up = to_dev(own_up, y=1)
    own_down = to_dev(own_down, y=-1)
    back_n = to_group(au_n, 2)
    sum_2 = to_dev(sum_2, zh=2)
    sh_far, own_up, own_down, back_n, sum_2, au_0, own_far = fence(
        sh_far, own_up, own_down, back_n, sum_2, au_0, own_far
    )
    sum_up = (gu_own[128:256] + back_n[:128].astype(F32)).astype(LOW)
    sum_down = (gu_own[256:384] + back_n[128:].astype(F32)).astype(LOW)
    behind = (gv_keep[128:] + sh_up.astype(F32) + sh_down.astype(F32) + sh_far.astype(F32)).astype(LOW)
    sum_up, sum_down, behind, au_0, own_far = fence(sum_up, sum_down, behind, au_0, own_far)
    own_far = to_dev(own_far, y=2)
    back_0 = to_group(au_0, 2)
    behind = to_group(behind, -1)
    sum_up = to_dev(sum_up, zh=1)
    sum_down = to_dev(sum_down, zh=-1)
    return tuple(
        whole(
            end_kernel,
            [(rows, F32)] * 2,
            image_emb,
            text_emb,
            gu_own,
            back_0,
            sum_2,
            sum_up,
            sum_down,
            gv_keep,
            own_up,
            own_down,
            own_far,
            behind,
        )
    )


def solution(mesh):
    return jax.shard_map(
        local,
        mesh=mesh,
        in_specs=(P(("grp", "dev"), None), P(("grp", "dev"), None), P(), P()),
        out_specs=(P(("grp", "dev"), None), P(("grp", "dev"), None)),
        check_vma=False,
    )
```

time: 316 us -> 146 us (0.46)
  the two profiles are of different devices: /device:TPU:24 before, /device:TPU:68 now
where the time goes in v3:
time: 146 us; the launch traced here: 145 us
  waiting for transfers between devices  55.6 us (38%)
  starting transfers between devices  54.5 us (37%)
  Pallas kernels  28.6 us (20%)
  local copies, waits for them, and re-layouts  3.98 us (3%)
  between operations  2.2 us (2%)
    ppermute x18, starting transfers between devices, to_dev(): return lax.ppermute(block, 'dev', route)  43.3 us
    ppermute x18, waiting for transfers between devices, to_dev(): return lax.ppermute(block, 'dev', route)  40.1 us
    pallas_call x7, Pallas kernels, whole(): pl.pallas_call(kernel, in_specs=first + [VMEM] * (len(operands) - 1), out...  28.6 us
    ppermute x8, waiting for transfers between devices, to_group(): lax.ppermute(block, 'grp', [(i, (i + step) % GROUPS) for i in range(GROUP...  15.5 us
    ppermute x8, starting transfers between devices, to_group(): lax.ppermute(block, 'grp', [(i, (i + step) % GROUPS) for i in range(GROUP...  11.2 us
    unnamed x27, local copies, waits for them, and re-layouts  3.88 us
  transfers between devices with their start and end apart: 26, of which 11 were waited for; matrix products, arithmetic and copies ran while one was open for 0% of the time, Pallas kernels for 13%

profile of v3, /device:TPU:68, one launch (start us, length us, event | category | flops | bytes accessed | tf_op | source)
XLA Modules:
  0.0 145.4 jit_solution(3381993296034236794)
XLA Ops:
  2.9 2.0 %collective-permute-start.4 = (bf16[128,1152]{1,0:T(8,128)(2,1)S(1)}, bf16[128,1152]{1,0:T(8,128)(2,1)S(1)}, u32[]{:S(2)}, u32[]{:S(2)}) collective-permute-start(bf16[128,1152]{1,0:T(8,128)(2,1)S(1)} %get-tuple-element.65), channel_id=1, source_target_pairs={{0,32},{32,64},{64,96},{96,128},{128,160},{160,192},{192,224},{224... | collective-permute-start | bytes 884744 | tf_op jit(solution)/shard_map/ppermute | solution.py:16
  4.9 3.2 %collective-permute-start = (bf16[128,1152]{1,0:T(8,128)(2,1)S(1)}, bf16[128,1152]{1,0:T(8,128)(2,1)S(1)}, u32[]{:S(2)}, u32[]{:S(2)}) collective-permute-start(bf16[128,1152]{1,0:T(8,128)(2,1)S(1)} %get-tuple-element.65), channel_id=1, source_target_pairs={{0,4},{1,5},{2,6},{3,7},{4,0},{5,1},{6,2},{7,3},{8,12},{9,13},{10,... | collective-permute-start | bytes 884744 | tf_op jit(solution)/shard_map/ppermute | solution.py:25
  8.1 3.6 %collective-permute-start.3 = (bf16[128,1152]{1,0:T(8,128)(2,1)S(1)}, bf16[128,1152]{1,0:T(8,128)(2,1)S(1)}, u32[]{:S(2)}, u32[]{:S(2)}) collective-permute-start(bf16[128,1152]{1,0:T(8,128)(2,1)S(1)} %get-tuple-element.73), channel_id=1, source_target_pairs={{0,8},{1,9},{2,10},{3,11},{4,12},{5,13},{6,14},{7,15},{8,16},{9,17... | collective-permute-start | bytes 884744 | tf_op jit(solution)/shard_map/ppermute | solution.py:25
  12.2 6.4 %collective-permute-done.4 = bf16[128,1152]{1,0:T(8,128)(2,1)S(1)} collective-permute-done((bf16[128,1152]{1,0:T(8,128)(2,1)S(1)}, bf16[128,1152]{1,0:T(8,128)(2,1)S(1)}, u32[]{:S(2)}, u32[]{:S(2)}) %collective-permute-start.4) | collective-permute-done | bytes 294944 | tf_op jit(solution)/shard_map/ppermute | solution.py:16
  18.7 5.3 %collective-permute-done.3 = bf16[128,1152]{1,0:T(8,128)(2,1)S(1)} collective-permute-done((bf16[128,1152]{1,0:T(8,128)(2,1)S(1)}, bf16[128,1152]{1,0:T(8,128)(2,1)S(1)}, u32[]{:S(2)}, u32[]{:S(2)}) %collective-permute-start.3) | collective-permute-done | bytes 294944 | tf_op jit(solution)/shard_map/ppermute | solution.py:25
  25.7 1.7 %collective-permute-start.6 = (bf16[256,1152]{1,0:T(8,128)(2,1)S(1)}, bf16[256,1152]{1,0:T(8,128)(2,1)S(1)}, u32[]{:S(2)}, u32[]{:S(2)}) collective-permute-start(bf16[256,1152]{1,0:T(8,128)(2,1)S(1)} %get-tuple-element.71), channel_id=1, source_target_pairs={{0,6},{1,7},{2,0},{3,1},{4,2},{5,3},{6,4},{7,5},{8,14},{9,15},{10,... | collective-permute-start | bytes 1769480 | tf_op jit(solution)/shard_map/ppermute | solution.py:25
  28.0 1.9 %collective-permute-start.5 = (bf16[128,1152]{1,0:T(8,128)(2,1)S(1)}, bf16[128,1152]{1,0:T(8,128)(2,1)S(1)}, u32[]{:S(2)}, u32[]{:S(2)}) collective-permute-start(bf16[128,1152]{1,0:T(8,128)(2,1)S(1)} %collective-permute-done.4), channel_id=1, source_target_pairs={{0,4},{1,5},{2,6},{3,7},{4,0},{5,1},{6,2},{7,3},{8,12},{9,13},{10,... | collective-permute-start | bytes 884744 | tf_op jit(solution)/shard_map/ppermute | solution.py:25
  29.9 6.3 %collective-permute-start.9 = (bf16[128,1152]{1,0:T(8,128)(2,1)S(1)}, bf16[128,1152]{1,0:T(8,128)(2,1)S(1)}, u32[]{:S(2)}, u32[]{:S(2)}) collective-permute-start(bf16[128,1152]{1,0:T(8,128)(2,1)S(1)} %get-tuple-element.73), channel_id=1, source_target_pairs={{0,16},{1,17},{2,18},{3,19},{4,20},{5,21},{6,22},{7,23},{8,24},{9,... | collective-permute-start | bytes 884744 | tf_op jit(solution)/shard_map/ppermute | solution.py:25
  36.2 10.9 %collective-permute-done.5 = bf16[128,1152]{1,0:T(8,128)(2,1)S(1)} collective-permute-done((bf16[128,1152]{1,0:T(8,128)(2,1)S(1)}, bf16[128,1152]{1,0:T(8,128)(2,1)S(1)}, u32[]{:S(2)}, u32[]{:S(2)}) %collective-permute-start.5) | collective-permute-done | bytes 294944 | tf_op jit(solution)/shard_map/ppermute | solution.py:25
  50.9 6.5 %shard_map.60 = (f32[512,1152]{1,0:T(8,128)S(1)}, f32[1024,1152]{1,0:T(8,128)S(1)}) custom-call(f32[2]{0:T(128)S(1)} %pad_maximum_fusion.2.scalars, bf16[512,1152]{1,0:T(8,128)(2,1)S(1)} %constant_dynamic-update-slice_fusion.img, bf16[1024,1152]{1,0:T(8,128)(2,1)S(1)} %constant_dynamic-update-slice_fusion.3.txt), custom_call_target="tpu_custom_call" | custom-call | flops 3623878656 | bytes 3538952 | tf_op jit(solution)/shard_map/pallas_call | solution.py:39
  57.4 6.5 %shard_map.61 = (f32[512,1152]{1,0:T(8,128)S(1)}, f32[1024,1152]{1,0:T(8,128)S(1)}) custom-call(f32[2]{0:T(128)S(1)} %pad_maximum_fusion.2.scalars, bf16[512,1152]{1,0:T(8,128)(2,1)S(1)} %constant_dynamic-update-slice_fusion.img, bf16[1024,1152]{1,0:T(8,128)(2,1)} %collective-permute-done.11.txt, ...), custom_call_target="tpu_custom_call", output_to_operand_aliasing={{0}: (3, {})} | custom-call | flops 3623878656 | bytes 5898248 | tf_op jit(solution)/shard_map/pallas_call | solution.py:39
  64.0 7.6 %shard_map.62 = (f32[512,1152]{1,0:T(8,128)S(1)}, bf16[1024,1152]{1,0:T(8,128)(2,1)S(1)}) custom-call(f32[2]{0:T(128)S(1)} %pad_maximum_fusion.2.scalars, bf16[512,1152]{1,0:T(8,128)(2,1)S(1)} %constant_dynamic-update-slice_fusion.7.img, bf16[1024,1152]{1,0:T(8,128)(2,1)} %collective-permute-done.11.txt, f32[1024,1152]{1,0:T(8,128)S(1)} %get-tuple-element.86.refs_0_), custom_call_target="tpu_custom_call" | custom-call | flops 3623878656 | bytes 8257544 | tf_op jit(solution)/shard_map/pallas_call | solution.py:39
  71.8 5.9 %shard_map.63 = (bf16[128,1152]{1,0:T(8,128)(2,1)S(1)}, bf16[256,1152]{1,0:T(8,128)(2,1)S(1)}, bf16[128,1152]{1,0:T(8,128)(2,1)S(1)}, f32[1024,1152]{1,0:T(8,128)S(1)}) custom-call(f32[2]{0:T(128)S(1)} %pad_maximum_fusion.2.scalars, bf16[512,1152]{1,0:T(8,128)(2,1)S(1)} %constant_dynamic-update-slice_fusion.7.img, ...), custom_call_target="tpu_custom_call", output_to_operand_aliasing={{3}: (4, {})} | custom-call | flops 3623878656 | bytes 10616840 | tf_op jit(solution)/shard_map/pallas_call | solution.py:39
  79.4 2.1 %collective-permute-start.14 = (bf16[128,1152]{1,0:T(8,128)(2,1)S(1)}, bf16[128,1152]{1,0:T(8,128)(2,1)S(1)}, u32[]{:S(2)}, u32[]{:S(2)}) collective-permute-start(bf16[128,1152]{1,0:T(8,128)(2,1)S(1)} %get-tuple-element.95), channel_id=1, source_target_pairs={{0,6},{1,7},{2,0},{3,1},{4,2},{5,3},{6,4},{7,5},{8,14},{9,15},{10,... | collective-permute-start | bytes 884744 | tf_op jit(solution)/shard_map/ppermute | solution.py:25
  83.0 5.7 %collective-permute-done.13 = bf16[128,1152]{1,0:T(8,128)(2,1)S(1)} collective-permute-done((bf16[128,1152]{1,0:T(8,128)(2,1)S(1)}, bf16[128,1152]{1,0:T(8,128)(2,1)S(1)}, u32[]{:S(2)}, u32[]{:S(2)}) %collective-permute-start.13) | collective-permute-done | bytes 294944 | tf_op jit(solution)/shard_map/ppermute | solution.py:25
  88.7 2.2 %collective-permute-done.15 = bf16[128,1152]{1,0:T(8,128)(2,1)S(1)} collective-permute-done((bf16[128,1152]{1,0:T(8,128)(2,1)S(1)}, bf16[128,1152]{1,0:T(8,128)(2,1)S(1)}, u32[]{:S(2)}, u32[]{:S(2)}) %collective-permute-start.15) | collective-permute-done | bytes 294944 | tf_op jit(solution)/shard_map/ppermute | solution.py:16
  92.4 1.9 %collective-permute-start.17 = (bf16[128,1152]{1,0:T(8,128)(2,1)S(1)}, bf16[128,1152]{1,0:T(8,128)(2,1)S(1)}, u32[]{:S(2)}, u32[]{:S(2)}) collective-permute-start(bf16[128,1152]{1,0:T(8,128)(2,1)S(1)} %get-tuple-element.107), channel_id=1, source_target_pairs={{0,2},{1,3},{2,4},{3,5},{4,6},{5,7},{6,0},{7,1},{8,10},{9,11},{10,... | collective-permute-start | bytes 884744 | tf_op jit(solution)/shard_map/ppermute | solution.py:25
  95.6 6.4 %collective-permute-start.20 = (bf16[128,1152]{1,0:T(8,128)(2,1)S(1)}, bf16[128,1152]{1,0:T(8,128)(2,1)S(1)}, u32[]{:S(2)}, u32[]{:S(2)}) collective-permute-start(bf16[128,1152]{1,0:T(8,128)(2,1)S(1)} %add_convert_fusion.3), channel_id=1, source_target_pairs={{0,16},{1,17},{2,18},{3,19},{4,20},{5,21},{6,22},{7,23},{8,24},{9,... | collective-permute-start | bytes 884744 | tf_op jit(solution)/shard_map/ppermute | solution.py:25
  103.4 3.9 %collective-permute-done.17.refs_5_ = bf16[128,1152]{1,0:T(8,128)(2,1)S(1)} collective-permute-done((bf16[128,1152]{1,0:T(8,128)(2,1)S(1)}, bf16[128,1152]{1,0:T(8,128)(2,1)S(1)}, u32[]{:S(2)}, u32[]{:S(2)}) %collective-permute-start.17) | collective-permute-done | bytes 294944 | tf_op jit(solution)/shard_map/ppermute | solution.py:25
  108.5 3.9 %collective-permute-start.21 = (bf16[128,1152]{1,0:T(8,128)(2,1)S(1)}, bf16[128,1152]{1,0:T(8,128)(2,1)S(1)}, u32[]{:S(2)}, u32[]{:S(2)}) collective-permute-start(bf16[128,1152]{1,0:T(8,128)(2,1)S(1)} %get-tuple-element.120), channel_id=1, source_target_pairs={{0,64},{32,96},{64,128},{96,160},{128,192},{160,224},{192,0},{224,... | collective-permute-start | bytes 884744 | tf_op jit(solution)/shard_map/ppermute | solution.py:16
  112.3 8.7 %collective-permute-start.22 = (bf16[128,1152]{1,0:T(8,128)(2,1)S(1)}, bf16[128,1152]{1,0:T(8,128)(2,1)S(1)}, u32[]{:S(2)}, u32[]{:S(2)}) collective-permute-start(bf16[128,1152]{1,0:T(8,128)(2,1)S(1)} %get-tuple-element.122), channel_id=1, source_target_pairs={{0,8},{1,9},{2,10},{3,11},{4,12},{5,13},{6,14},{7,15},{8,16},{9,17... | collective-permute-start | bytes 884744 | tf_op jit(solution)/shard_map/ppermute | solution.py:25
  121.8 1.9 %collective-permute-start.24 = (bf16[128,1152]{1,0:T(8,128)(2,1)S(1)}, bf16[128,1152]{1,0:T(8,128)(2,1)S(1)}, u32[]{:S(2)}, u32[]{:S(2)}) collective-permute-start(bf16[128,1152]{1,0:T(8,128)(2,1)S(1)} %get-tuple-element.126), channel_id=1, source_target_pairs={{0,4},{1,5},{2,6},{3,7},{4,0},{5,1},{6,2},{7,3},{8,12},{9,13},{10,... | collective-permute-start | bytes 884744 | tf_op jit(solution)/shard_map/ppermute | solution.py:25
  124.9 10.7 %collective-permute-done.22.refs_2_ = bf16[128,1152]{1,0:T(8,128)(2,1)S(1)} collective-permute-done((bf16[128,1152]{1,0:T(8,128)(2,1)S(1)}, bf16[128,1152]{1,0:T(8,128)(2,1)S(1)}, u32[]{:S(2)}, u32[]{:S(2)}) %collective-permute-start.22) | collective-permute-done | bytes 294944 | tf_op jit(solution)/shard_map/ppermute | solution.py:25
  136.9 6.9 %collective-permute-done.25.refs_8_ = bf16[128,1152]{1,0:T(8,128)(2,1)S(1)} collective-permute-done((bf16[128,1152]{1,0:T(8,128)(2,1)S(1)}, bf16[128,1152]{1,0:T(8,128)(2,1)S(1)}, u32[]{:S(2)}, u32[]{:S(2)}) %collective-permute-start.25) | collective-permute-done | bytes 294944 | tf_op jit(solution)/shard_map/ppermute | solution.py:16
  (70 shorter events, 21.2 us)
Async XLA Ops:
  2.9 15.7 %collective-permute-start.4 = (bf16[128,1152]{1,0:T(8,128)(2,1)S(1)}, bf16[128,1152]{1,0:T(8,128)(2,1)S(1)}, u32[]{:S(2)}, u32[]{:S(2)}) collective-permute-start(bf16[128,1152]{1,0:T(8,128)(2,1)S(1)} %get-tuple-element.65), channel_id=1, source_target_pairs={{0,32},{32,64},{64,96},{96,128},{128,160},{160,192},{192,224},{224... | collective-permute-start | bytes 884744 | tf_op jit(solution)/shard_map/ppermute | solution.py:16
  4.9 13.7 %collective-permute-start = (bf16[128,1152]{1,0:T(8,128)(2,1)S(1)}, bf16[128,1152]{1,0:T(8,128)(2,1)S(1)}, u32[]{:S(2)}, u32[]{:S(2)}) collective-permute-start(bf16[128,1152]{1,0:T(8,128)(2,1)S(1)} %get-tuple-element.65), channel_id=1, source_target_pairs={{0,4},{1,5},{2,6},{3,7},{4,0},{5,1},{6,2},{7,3},{8,12},{9,13},{10,... | collective-permute-start | bytes 884744 | tf_op jit(solution)/shard_map/ppermute | solution.py:25
  8.1 15.9 %collective-permute-start.3 = (bf16[128,1152]{1,0:T(8,128)(2,1)S(1)}, bf16[128,1152]{1,0:T(8,128)(2,1)S(1)}, u32[]{:S(2)}, u32[]{:S(2)}) collective-permute-start(bf16[128,1152]{1,0:T(8,128)(2,1)S(1)} %get-tuple-element.73), channel_id=1, source_target_pairs={{0,8},{1,9},{2,10},{3,11},{4,12},{5,13},{6,14},{7,15},{8,16},{9,17... | collective-permute-start | bytes 884744 | tf_op jit(solution)/shard_map/ppermute | solution.py:25
  11.7 12.3 %collective-permute-start.2 = (bf16[128,1152]{1,0:T(8,128)(2,1)S(1)}, bf16[128,1152]{1,0:T(8,128)(2,1)S(1)}, u32[]{:S(2)}, u32[]{:S(2)}) collective-permute-start(bf16[128,1152]{1,0:T(8,128)(2,1)S(1)} %get-tuple-element.73), channel_id=1, source_target_pairs={{0,24},{1,25},{2,26},{3,27},{4,28},{5,29},{6,30},{7,31},{8,0},{9,1... | collective-permute-start | bytes 884744 | tf_op jit(solution)/shard_map/ppermute | solution.py:25
  11.7 12.3 %collective-permute-start.1 = (bf16[128,1152]{1,0:T(8,128)(2,1)S(1)}, bf16[128,1152]{1,0:T(8,128)(2,1)S(1)}, u32[]{:S(2)}, u32[]{:S(2)}) collective-permute-start(bf16[128,1152]{1,0:T(8,128)(2,1)S(1)} %get-tuple-element.73), channel_id=1, source_target_pairs={{0,192},{32,224},{64,0},{96,32},{128,64},{160,96},{192,128},{224,1... | collective-permute-start | bytes 884744 | tf_op jit(solution)/shard_map/ppermute | solution.py:16
  24.1 23.0 %collective-permute-start.7 = (bf16[256,1152]{1,0:T(8,128)(2,1)S(1)}, bf16[256,1152]{1,0:T(8,128)(2,1)S(1)}, u32[]{:S(2)}, u32[]{:S(2)}) collective-permute-start(bf16[256,1152]{1,0:T(8,128)(2,1)S(1)} %get-tuple-element.71), channel_id=1, source_target_pairs={{0,2},{1,3},{2,4},{3,5},{4,6},{5,7},{6,0},{7,1},{8,10},{9,11},{10,... | collective-permute-start | bytes 1769480 | tf_op jit(solution)/shard_map/ppermute | solution.py:25
  25.7 21.4 %collective-permute-start.6 = (bf16[256,1152]{1,0:T(8,128)(2,1)S(1)}, bf16[256,1152]{1,0:T(8,128)(2,1)S(1)}, u32[]{:S(2)}, u32[]{:S(2)}) collective-permute-start(bf16[256,1152]{1,0:T(8,128)(2,1)S(1)} %get-tuple-element.71), channel_id=1, source_target_pairs={{0,6},{1,7},{2,0},{3,1},{4,2},{5,3},{6,4},{7,5},{8,14},{9,15},{10,... | collective-permute-start | bytes 1769480 | tf_op jit(solution)/shard_map/ppermute | solution.py:25
  27.4 19.7 %collective-permute-start.8 = (bf16[256,1152]{1,0:T(8,128)(2,1)S(1)}, bf16[256,1152]{1,0:T(8,128)(2,1)S(1)}, u32[]{:S(2)}, u32[]{:S(2)}) collective-permute-start(bf16[256,1152]{1,0:T(8,128)(2,1)S(1)} %get-tuple-element.72), channel_id=1, source_target_pairs={{0,192},{32,224},{64,0},{96,32},{128,64},{160,96},{192,128},{224,1... | collective-permute-start | bytes 1769480 | tf_op jit(solution)/shard_map/ppermute | solution.py:16
  28.0 19.1 %collective-permute-start.5 = (bf16[128,1152]{1,0:T(8,128)(2,1)S(1)}, bf16[128,1152]{1,0:T(8,128)(2,1)S(1)}, u32[]{:S(2)}, u32[]{:S(2)}) collective-permute-start(bf16[128,1152]{1,0:T(8,128)(2,1)S(1)} %collective-permute-done.4), channel_id=1, source_target_pairs={{0,4},{1,5},{2,6},{3,7},{4,0},{5,1},{6,2},{7,3},{8,12},{9,13},{10,... | collective-permute-start | bytes 884744 | tf_op jit(solution)/shard_map/ppermute | solution.py:25
  29.9 17.2 %collective-permute-start.9 = (bf16[128,1152]{1,0:T(8,128)(2,1)S(1)}, bf16[128,1152]{1,0:T(8,128)(2,1)S(1)}, u32[]{:S(2)}, u32[]{:S(2)}) collective-permute-start(bf16[128,1152]{1,0:T(8,128)(2,1)S(1)} %get-tuple-element.73), channel_id=1, source_target_pairs={{0,16},{1,17},{2,18},{3,19},{4,20},{5,21},{6,22},{7,23},{8,24},{9,... | collective-permute-start | bytes 884744 | tf_op jit(solution)/shard_map/ppermute | solution.py:25
  48.0 9.4 %collective-permute-start.11 = (bf16[1024,1152]{1,0:T(8,128)(2,1)S(1)}, bf16[1024,1152]{1,0:T(8,128)(2,1)}, u32[]{:S(2)}, u32[]{:S(2)}) collective-permute-start(bf16[1024,1152]{1,0:T(8,128)(2,1)S(1)} %constant_dynamic-update-slice_fusion.3.txt), channel_id=1, source_target_pairs={{0,1},{1,0},{2,3},{3,2},{4,5},{5,4},{6,7},{7,6},{8,9},{9,8},{10,11... | collective-permute-start | bytes 7077896 | tf_op jit(solution)/shard_map/ppermute | solution.py:25
  50.3 13.6 %collective-permute-start.10 = (bf16[128,1152]{1,0:T(8,128)(2,1)S(1)}, bf16[128,1152]{1,0:T(8,128)(2,1)S(1)}, u32[]{:S(2)}, u32[]{:S(2)}) collective-permute-start(bf16[128,1152]{1,0:T(8,128)(2,1)S(1)} %copy-done.7), channel_id=1, source_target_pairs={{0,192},{32,224},{64,0},{96,32},{128,64},{160,96},{192,128},{224,1... | collective-permute-start | bytes 884744 | tf_op jit(solution)/shard_map/ppermute | solution.py:16
  78.2 10.5 %collective-permute-start.13 = (bf16[128,1152]{1,0:T(8,128)(2,1)S(1)}, bf16[128,1152]{1,0:T(8,128)(2,1)S(1)}, u32[]{:S(2)}, u32[]{:S(2)}) collective-permute-start(bf16[128,1152]{1,0:T(8,128)(2,1)S(1)} %get-tuple-element.94), channel_id=1, source_target_pairs={{0,2},{1,3},{2,4},{3,5},{4,6},{5,7},{6,0},{7,1},{8,10},{9,11},{10,... | collective-permute-start | bytes 884744 | tf_op jit(solution)/shard_map/ppermute | solution.py:25
  81.5 9.4 %collective-permute-start.15 = (bf16[128,1152]{1,0:T(8,128)(2,1)S(1)}, bf16[128,1152]{1,0:T(8,128)(2,1)S(1)}, u32[]{:S(2)}, u32[]{:S(2)}) collective-permute-start(bf16[128,1152]{1,0:T(8,128)(2,1)S(1)} %get-tuple-element.96), channel_id=1, source_target_pairs={{0,64},{32,96},{64,128},{96,160},{128,192},{160,224},{192,0},{224,... | collective-permute-start | bytes 884744 | tf_op jit(solution)/shard_map/ppermute | solution.py:16
  90.9 17.2 %collective-permute-start.19 = (bf16[256,1152]{1,0:T(8,128)(2,1)S(1)}, bf16[256,1152]{1,0:T(8,128)(2,1)S(1)}, u32[]{:S(2)}, u32[]{:S(2)}) collective-permute-start(bf16[256,1152]{1,0:T(8,128)(2,1)S(1)} %get-tuple-element.109), channel_id=1, source_target_pairs={{0,64},{32,96},{64,128},{96,160},{128,192},{160,224},{192,0},{224,... | collective-permute-start | bytes 1769480 | tf_op jit(solution)/shard_map/ppermute | solution.py:16
  92.0 11.4 %collective-permute-start.16 = (bf16[128,1152]{1,0:T(8,128)(2,1)S(1)}, bf16[128,1152]{1,0:T(8,128)(2,1)S(1)}, u32[]{:S(2)}, u32[]{:S(2)}) collective-permute-start(bf16[128,1152]{1,0:T(8,128)(2,1)S(1)} %get-tuple-element.106), channel_id=1, source_target_pairs={{0,4},{1,5},{2,6},{3,7},{4,0},{5,1},{6,2},{7,3},{8,12},{9,13},{10,... | collective-permute-start | bytes 884744 | tf_op jit(solution)/shard_map/ppermute | solution.py:25
  92.4 14.9 %collective-permute-start.17 = (bf16[128,1152]{1,0:T(8,128)(2,1)S(1)}, bf16[128,1152]{1,0:T(8,128)(2,1)S(1)}, u32[]{:S(2)}, u32[]{:S(2)}) collective-permute-start(bf16[128,1152]{1,0:T(8,128)(2,1)S(1)} %get-tuple-element.107), channel_id=1, source_target_pairs={{0,2},{1,3},{2,4},{3,5},{4,6},{5,7},{6,0},{7,1},{8,10},{9,11},{10,... | collective-permute-start | bytes 884744 | tf_op jit(solution)/shard_map/ppermute | solution.py:25
  94.3 13.0 %collective-permute-start.18 = (bf16[128,1152]{1,0:T(8,128)(2,1)S(1)}, bf16[128,1152]{1,0:T(8,128)(2,1)S(1)}, u32[]{:S(2)}, u32[]{:S(2)}) collective-permute-start(bf16[128,1152]{1,0:T(8,128)(2,1)S(1)} %get-tuple-element.108), channel_id=1, source_target_pairs={{0,6},{1,7},{2,0},{3,1},{4,2},{5,3},{6,4},{7,5},{8,14},{9,15},{10,... | collective-permute-start | bytes 884744 | tf_op jit(solution)/shard_map/ppermute | solution.py:25
  95.6 12.5 %collective-permute-start.20 = (bf16[128,1152]{1,0:T(8,128)(2,1)S(1)}, bf16[128,1152]{1,0:T(8,128)(2,1)S(1)}, u32[]{:S(2)}, u32[]{:S(2)}) collective-permute-start(bf16[128,1152]{1,0:T(8,128)(2,1)S(1)} %add_convert_fusion.3), channel_id=1, source_target_pairs={{0,16},{1,17},{2,18},{3,19},{4,20},{5,21},{6,22},{7,23},{8,24},{9,... | collective-permute-start | bytes 884744 | tf_op jit(solution)/shard_map/ppermute | solution.py:25
  108.5 16.4 %collective-permute-start.21 = (bf16[128,1152]{1,0:T(8,128)(2,1)S(1)}, bf16[128,1152]{1,0:T(8,128)(2,1)S(1)}, u32[]{:S(2)}, u32[]{:S(2)}) collective-permute-start(bf16[128,1152]{1,0:T(8,128)(2,1)S(1)} %get-tuple-element.120), channel_id=1, source_target_pairs={{0,64},{32,96},{64,128},{96,160},{128,192},{160,224},{192,0},{224,... | collective-permute-start | bytes 884744 | tf_op jit(solution)/shard_map/ppermute | solution.py:16
  112.3 23.3 %collective-permute-start.22 = (bf16[128,1152]{1,0:T(8,128)(2,1)S(1)}, bf16[128,1152]{1,0:T(8,128)(2,1)S(1)}, u32[]{:S(2)}, u32[]{:S(2)}) collective-permute-start(bf16[128,1152]{1,0:T(8,128)(2,1)S(1)} %get-tuple-element.122), channel_id=1, source_target_pairs={{0,8},{1,9},{2,10},{3,11},{4,12},{5,13},{6,14},{7,15},{8,16},{9,17... | collective-permute-start | bytes 884744 | tf_op jit(solution)/shard_map/ppermute | solution.py:25
  121.0 15.9 %collective-permute-start.23 = (bf16[128,1152]{1,0:T(8,128)(2,1)S(1)}, bf16[128,1152]{1,0:T(8,128)(2,1)S(1)}, u32[]{:S(2)}, u32[]{:S(2)}) collective-permute-start(bf16[128,1152]{1,0:T(8,128)(2,1)S(1)} %get-tuple-element.123), channel_id=1, source_target_pairs={{0,24},{1,25},{2,26},{3,27},{4,28},{5,29},{6,30},{7,31},{8,0},{9,1... | collective-permute-start | bytes 884744 | tf_op jit(solution)/shard_map/ppermute | solution.py:25
  121.8 15.1 %collective-permute-start.24 = (bf16[128,1152]{1,0:T(8,128)(2,1)S(1)}, bf16[128,1152]{1,0:T(8,128)(2,1)S(1)}, u32[]{:S(2)}, u32[]{:S(2)}) collective-permute-start(bf16[128,1152]{1,0:T(8,128)(2,1)S(1)} %get-tuple-element.126), channel_id=1, source_target_pairs={{0,4},{1,5},{2,6},{3,7},{4,0},{5,1},{6,2},{7,3},{8,12},{9,13},{10,... | collective-permute-start | bytes 884744 | tf_op jit(solution)/shard_map/ppermute | solution.py:25
  123.7 20.1 %collective-permute-start.25 = (bf16[128,1152]{1,0:T(8,128)(2,1)S(1)}, bf16[128,1152]{1,0:T(8,128)(2,1)S(1)}, u32[]{:S(2)}, u32[]{:S(2)}) collective-permute-start(bf16[128,1152]{1,0:T(8,128)(2,1)S(1)} %add_convert_fusion), channel_id=1, source_target_pairs={{0,224},{32,0},{64,32},{96,64},{128,96},{160,128},{192,160},{224,1... | collective-permute-start | bytes 884744 | tf_op jit(solution)/shard_map/ppermute | solution.py:16
  (10 other events, 127.6 us)

commit v4 on v3

v4 whole, which is shorter than its diff:
```python
import functools

import jax
import jax.numpy as jnp
from jax import lax
from jax.experimental import pallas as pl
from jax.experimental.pallas import tpu as pltpu
from jax.sharding import PartitionSpec as P

X, ZL, ZH, Y, CORE = 4, 2, 4, 4, 2
GROUPS, DEVS = X * ZL, ZH * Y * CORE
F32, LOW = jnp.float32, jnp.bfloat16


def to_group(block, step):
    return lax.ppermute(block, "grp", [(i, (i + step) % GROUPS) for i in range(GROUPS)])


def to_dev(block, zh=0, y=0, core=0):
    route = []
    for i in range(DEVS):
        a, b, c = i // (Y * CORE), i // CORE % Y, i % CORE
        target = ((a + zh) % ZH * Y + (b + y) % Y) * CORE + (c + core) % CORE
        route.append((i, target))
    return lax.ppermute(block, "dev", route)


def fence(*arrays):
    return lax.optimization_barrier(arrays)


VMEM = pl.BlockSpec(memory_space=pltpu.VMEM)


def whole(kernel, outs, *operands, scalars=False, aliases=None, scratch=()):
    first = [pl.BlockSpec(memory_space=pltpu.SMEM)] if scalars else [VMEM]
    return pl.pallas_call(
        kernel,
        in_specs=first + [VMEM] * (len(operands) - 1),
        out_specs=[VMEM] * len(outs),
        out_shape=[jax.ShapeDtypeStruct(shape, kind) for shape, kind in outs],
        input_output_aliases=aliases or {},
        scratch_shapes=list(scratch),
        compiler_params=pltpu.CompilerParams(vmem_limit_bytes=28 * 1024 * 1024),
        cost_estimate=pl.CostEstimate(flops=1, bytes_accessed=1, transcendentals=0),
    )(*operands)


def inverse_of(values):
    return lax.rsqrt(jnp.sum(values * values, axis=1, keepdims=True) + 1e-06)


def each(rows, step):
    def over(body):
        @pl.loop(0, rows // step)
        def _(n):
            body(pl.ds(pl.multiple_of(n * step, step), step))

    return over


def unit_kernel(txt, img, txt_low, img_low):
    for values, low in ((txt, txt_low), (img, img_low)):

        @each(values.shape[0], 32)
        def _(span):
            low[span] = (values[span] * inverse_of(values[span])).astype(LOW)


def end_kernel(img, txt, gu_0, *refs):
    *parts, gv_0, up, down, far, behind, grad_img, grad_txt = refs
    sides = ((img, gu_0, parts, grad_img), (txt, gv_0, (up, down, far, behind), grad_txt))
    for values, own, others, grad in sides:

        @each(values.shape[0], 32)
        def _(span):
            sums = own[span]
            for other in others:
                sums = sums + other[span].astype(F32)
            inverse = inverse_of(values[span])
            unit = values[span] * inverse
            grad[span] = inverse * (sums - unit * jnp.sum(unit * sums, axis=1, keepdims=True))


def text_sums_kernel(mine, got, own_0, sh_0, sh_up, sh_down, sh_far, own_up, own_down, own_far):
    for n, out in enumerate((own_0, own_up, own_down, own_far, sh_0, sh_up, sh_down, sh_far)):

        @each(out.shape[0], 32)
        def _(span):
            there = pl.ds(pl.multiple_of(n * out.shape[0] + span.start, 32), 32)
            out[span] = (mine[there] + got[there].astype(F32)).astype(out.dtype)


def products(scalars, img, txt, mask=None):
    half_temp, half_bias = scalars[0], scalars[1]
    logits = lax.dot_general(img, txt, (((1,), (1,)), ((), ())), preferred_element_type=F32)
    slopes = half_temp * jnp.tanh(half_temp * logits + half_bias) + half_temp
    if mask is not None:
        slopes = slopes - jnp.where(mask, 2.0 * half_temp, 0.0)
    coef = slopes.astype(LOW)
    gu = jnp.dot(coef, txt, preferred_element_type=F32)
    return gu, lax.dot_general(coef, img, (((0,), (0,)), ((), ())), preferred_element_type=F32)


def pair_kernel(gu_past, gv_past, diagonal, parts, scalars, img, txt_c, txt_s, *refs):
    refs = list(refs)
    gu_in = refs.pop(0) if gu_past else None
    gv_in = refs.pop(0) if gv_past else None
    gus = [refs.pop(0) for _ in parts]
    gv, txt = refs[:2]
    total = refs[2] if len(refs) > 2 else gus[0]
    if total is not gus[0] or not gu_past:

        @each(total.shape[0], 32)
        def _(span):
            total[span] = gu_in[span] if gu_past else jnp.zeros((32, total.shape[1]), F32)

    @pl.loop(0, 2)
    def _(n):
        for place, side in enumerate((txt_c, txt_s)):

            @pl.when(n == place)
            def _():
                @each(txt.shape[0], 32)
                def _(span):
                    txt[span] = side[span]

        mask = None
        if diagonal:
            rows = lax.broadcasted_iota(jnp.int32, (img.shape[0], txt.shape[0]), 0)
            cols = lax.broadcasted_iota(jnp.int32, (img.shape[0], txt.shape[0]), 1) + n * img.shape[0]
            mask = jnp.logical_and(rows == cols, rows < 128)
        part, term = products(scalars, img[...], txt[...], mask)
        total[...] += part
        span = pl.ds(pl.multiple_of(n * txt.shape[0], txt.shape[0]), txt.shape[0])
        if gv_past:
            term = term + gv_in[span]
        gv[span] = term

    if total is not gus[0]:
        for (first, size, _), out in zip(parts, gus):

            @each(size, 32)
            def _(span):
                there = pl.ds(pl.multiple_of(first + span.start, 32), 32)
                out[span] = total[there].astype(out.dtype)


def pairs(scalars, img, txt_c, txt_s, gu_in=None, gv_in=None, gu_parts=None, diagonal=False):
    (rows, width), cols = img.shape, txt_c.shape[0]
    operands, aliases = [scalars, img, txt_c, txt_s], {}
    parts = gu_parts or [(0, rows, F32)]
    scratch = [pltpu.VMEM((cols, width), LOW)]
    if gu_parts:
        scratch.append(pltpu.VMEM((rows, width), F32))
    if gu_in is not None:
        if not gu_parts:
            aliases[len(operands)] = 0
        operands.append(gu_in)
    if gv_in is not None:
        aliases[len(operands)] = len(parts)
        operands.append(gv_in)
    outs = [((size, width), kind) for _, size, kind in parts] + [((2 * cols, width), F32)]
    kernel = functools.partial(pair_kernel, gu_in is not None, gv_in is not None, diagonal, parts)
    return whole(
        kernel,
        outs,
        *operands,
        scalars=True,
        aliases=aliases,
        scratch=scratch,
    )


def last_kernel(place, scalars, img, own, sh, gv_own, gv_sh, *refs):
    gu_in, (gu, gv) = (refs[0] if len(refs) > 2 else None), refs[-2:]
    size = own.shape[0]
    total = None if gu_in is None else gu_in[...]
    for n, (txt, past) in enumerate(((own, gv_own), (sh, gv_sh))):
        part, term = products(scalars, img[...], txt[...])
        total = part if total is None else total + part
        gv[n * size : (n + 1) * size] = (term + past[place : place + size]).astype(gv.dtype)
    gu[...] = total.astype(gu.dtype)


def local(image_emb, text_emb, temp, bias):
    rows = image_emb.shape
    txt_0, img_0 = whole(unit_kernel, [(rows, LOW)] * 2, text_emb, image_emb)
    scalars = jnp.stack([0.5 * temp, 0.5 * bias])

    txt_up = to_dev(txt_0, y=-1)
    ahead_0 = to_group(img_0, -2)
    img_up = to_dev(img_0, zh=-1)
    img_down = to_dev(img_0, zh=1)
    behind_0 = to_group(txt_0, 1)
    ahead_0, txt_later = fence(ahead_0, txt_0)
    txt_down = to_dev(txt_later, y=1)
    txt_2 = to_dev(txt_later, y=2)
    txt_up, txt_down, txt_2, img_up, img_down, behind_0 = fence(
        txt_up, txt_down, txt_2, img_up, img_down, behind_0
    )
    own_c = jnp.concatenate([txt_0, txt_up, txt_down, txt_2], axis=0)
    img_n = jnp.concatenate([img_up, img_down], axis=0)
    first = jnp.concatenate([img_0, img_up, img_down, ahead_0], axis=0)
    own_s = to_dev(own_c, core=1)
    behind_up = to_dev(behind_0, y=-1)
    behind_down = to_dev(behind_0, y=1)
    ahead_n = to_group(img_n, -2)
    img_2 = to_dev(img_0, zh=2)
    own_s, behind_later = fence(own_s, behind_0)
    behind_2 = to_dev(behind_later, y=2)
    gu_first, gv_own = pairs(scalars, first, own_c, own_s, diagonal=True)
    behind_up, behind_down, behind_2, ahead_n, img_2, gu_first, gv_own = fence(
        behind_up, behind_down, behind_2, ahead_n, img_2, gu_first, gv_own
    )
    sh_c = jnp.concatenate([behind_0, behind_up, behind_down, behind_2], axis=0)
    second = jnp.concatenate([img_2, ahead_n], axis=0)
    sh_s = to_dev(sh_c, core=1)
    ahead_2 = to_group(img_2, -2)
    gu_second, gv_own = pairs(scalars, second, own_c, own_s, gv_in=gv_own)
    gu_2, au_n, gv_sh = pairs(
        scalars, second, sh_c, sh_s, gu_in=gu_second, gu_parts=[(0, 128, F32), (128, 256, LOW)]
    )
    back_n = to_group(au_n, 2)
    gu_0, gu_up, gu_down, au_0, gv_sh = pairs(
        scalars,
        first,
        sh_c,
        sh_s,
        gu_in=gu_first,
        gv_in=gv_sh,
        gu_parts=[(0, 128, F32), (128, 128, F32), (256, 128, F32), (384, 128, LOW)],
    )
    ahead_2, gv_sh = fence(ahead_2, gv_sh)
    wide = (2 * own_c.shape[0], rows[1])
    gu_last, gv_s = whole(
        functools.partial(last_kernel, own_c.shape[0]),
        [(rows, F32), (wide, LOW)],
        *(scalars, ahead_2, own_s, sh_s, gv_own, gv_sh),
        scalars=True,
    )
    got = to_dev(gv_s, core=1)
    au_2, gv_c = whole(
        functools.partial(last_kernel, 0),
        [(rows, LOW), (wide, F32)],
        *(scalars, ahead_2, own_c, sh_c, gv_own, gv_sh, gu_last),
        scalars=True,
    )
    got, back_n, au_2, gv_c = fence(got, back_n, au_2, gv_c)
    own_sum, sh_sum, sh_up, sh_down, sh_far, own_up, own_down, own_far = whole(
        text_sums_kernel, [(rows, F32)] * 2 + [(rows, LOW)] * 6, gv_c, got
    )
    sum_up = (gu_up + back_n[:128].astype(F32)).astype(LOW)
    sum_down = (gu_down + back_n[128:].astype(F32)).astype(LOW)
    sum_up, sum_down, sh_up, sh_down, au_2 = fence(sum_up, sum_down, sh_up, sh_down, au_2)
    back_2 = to_group(au_2, 2)
    sh_up = to_dev(sh_up, y=1)
    sh_down = to_dev(sh_down, y=-1)
    sum_up = to_dev(sum_up, zh=1)
    sum_down = to_dev(sum_down, zh=-1)
    back_2, sh_far = fence(back_2, sh_far)
    sh_far = to_dev(sh_far, y=2)
    sum_up, sum_down, back_2, sh_up, sh_down, sh_far, au_0, own_up, own_down = fence(
        sum_up, sum_down, back_2, sh_up, sh_down, sh_far, au_0, own_up, own_down
    )
    sum_2 = (gu_2 + back_2.astype(F32)).astype(LOW)
    behind = (sh_sum + sh_up.astype(F32) + sh_down.astype(F32) + sh_far.astype(F32)).astype(LOW)
    sum_2, behind, au_0, own_up, own_down = fence(sum_2, behind, au_0, own_up, own_down)
    back_0 = to_group(au_0, 2)
    own_up = to_dev(own_up, y=1)
    own_down = to_dev(own_down, y=-1)
    behind = to_group(behind, -1)
    sum_2 = to_dev(sum_2, zh=2)
    back_0, own_far = fence(back_0, own_far)
    own_far = to_dev(own_far, y=2)
    return tuple(
        whole(
            end_kernel,
            [(rows, F32)] * 2,
            *(image_emb, text_emb, gu_0, back_0, sum_2, sum_up, sum_down),
            *(own_sum, own_up, own_down, own_far, behind),
        )
    )


def solution(mesh):
    return jax.shard_map(
        local,
        mesh=mesh,
        in_specs=(P(("grp", "dev"), None), P(("grp", "dev"), None), P(), P()),
        out_specs=(P(("grp", "dev"), None), P(("grp", "dev"), None)),
        check_vma=False,
    )
```

time: 146 us -> 145 us (level)
  the two profiles are of different devices: /device:TPU:68 before, /device:TPU:24 now
where the time goes in v4:
time: 145 us; the launch traced here: 144 us
  waiting for transfers between devices  63.2 us (44%)
  starting transfers between devices  39.2 us (27%)
  Pallas kernels  31.9 us (22%)
  local copies, waits for them, and re-layouts  5.94 us (4%)
  between operations  2.3 us (2%)
  other arithmetic  1.46 us (1%)
    ppermute x21, waiting for transfers between devices, to_dev(): return lax.ppermute(block, 'dev', route)  36 us
    pallas_call x9, Pallas kernels, whole(): pl.pallas_call(kernel, in_specs=first + [VMEM] * (len(operands) - 1), out...  31.9 us
    ppermute x21, starting transfers between devices, to_dev(): return lax.ppermute(block, 'dev', route)  29.8 us
    ppermute x8, waiting for transfers between devices, to_group(): lax.ppermute(block, 'grp', [(i, (i + step) % GROUPS) for i in range(GROUP...  27.2 us
    ppermute x8, starting transfers between devices, to_group(): lax.ppermute(block, 'grp', [(i, (i + step) % GROUPS) for i in range(GROUP...  9.42 us
    unnamed x33, local copies, waits for them, and re-layouts  5.78 us
  transfers between devices with their start and end apart: 29, of which 12 were waited for; matrix products, arithmetic and copies ran while one was open for 2% of the time, Pallas kernels for 17%

profile of v4, /device:TPU:24, one launch (start us, length us, event | category | flops | bytes accessed | tf_op | source)
XLA Modules:
  0.0 144.0 jit_solution(14311102173082153875)
XLA Ops:
  4.3 2.8 %collective-permute-start.1 = (bf16[128,1152]{1,0:T(8,128)(2,1)}, bf16[128,1152]{1,0:T(8,128)(2,1)S(1)}, u32[]{:S(2)}, u32[]{:S(2)}) collective-permute-start(bf16[128,1152]{1,0:T(8,128)(2,1)} %get-tuple-element.74), channel_id=1, source_target_pairs={{0,192},{32,224},{64,0},{96,32},{128,64},{160,96},{192,128},{224,1... | collective-permute-start | bytes 884744 | tf_op jit(solution)/shard_map/ppermute | solution.py:16
  9.7 3.3 %collective-permute-start.5 = (bf16[128,1152]{1,0:T(8,128)(2,1)}, bf16[128,1152]{1,0:T(8,128)(2,1)S(1)}, u32[]{:S(2)}, u32[]{:S(2)}) collective-permute-start(bf16[128,1152]{1,0:T(8,128)(2,1)} %get-tuple-element.74), channel_id=1, source_target_pairs={{0,8},{1,9},{2,10},{3,11},{4,12},{5,13},{6,14},{7,15},{8,16},{9,17... | collective-permute-start | bytes 884744 | tf_op jit(solution)/shard_map/ppermute | solution.py:25
  13.0 2.1 %collective-permute-start.4 = (bf16[128,1152]{1,0:T(8,128)(2,1)}, bf16[128,1152]{1,0:T(8,128)(2,1)S(1)}, u32[]{:S(2)}, u32[]{:S(2)}) collective-permute-start(bf16[128,1152]{1,0:T(8,128)(2,1)} %get-tuple-element.74), channel_id=1, source_target_pairs={{0,24},{1,25},{2,26},{3,27},{4,28},{5,29},{6,30},{7,31},{8,0},{9,1... | collective-permute-start | bytes 884744 | tf_op jit(solution)/shard_map/ppermute | solution.py:25
  16.1 8.7 %collective-permute-done.6 = bf16[128,1152]{1,0:T(8,128)(2,1)S(1)} collective-permute-done((bf16[128,1152]{1,0:T(8,128)(2,1)S(1)}, bf16[128,1152]{1,0:T(8,128)(2,1)S(1)}, u32[]{:S(2)}, u32[]{:S(2)}) %collective-permute-start.6) | collective-permute-done | bytes 294944 | tf_op jit(solution)/shard_map/ppermute | solution.py:16
  26.5 6.9 %collective-permute-done.5 = bf16[128,1152]{1,0:T(8,128)(2,1)S(1)} collective-permute-done((bf16[128,1152]{1,0:T(8,128)(2,1)}, bf16[128,1152]{1,0:T(8,128)(2,1)S(1)}, u32[]{:S(2)}, u32[]{:S(2)}) %collective-permute-start.5) | collective-permute-done | bytes 294944 | tf_op jit(solution)/shard_map/ppermute | solution.py:25
  34.3 6.1 %collective-permute-start.12 = (bf16[128,1152]{1,0:T(8,128)(2,1)}, bf16[128,1152]{1,0:T(8,128)(2,1)}, u32[]{:S(2)}, u32[]{:S(2)}) collective-permute-start(bf16[128,1152]{1,0:T(8,128)(2,1)} %get-tuple-element.74), channel_id=1, source_target_pairs={{0,16},{1,17},{2,18},{3,19},{4,20},{5,21},{6,22},{7,23},{8,24},{9,... | collective-permute-start | bytes 884744 | tf_op jit(solution)/shard_map/ppermute | solution.py:25
  46.7 5.8 %shard_map.60 = (f32[512,1152]{1,0:T(8,128)S(1)}, f32[1024,1152]{1,0:T(8,128)S(1)}) custom-call(f32[2]{0:T(128)S(1)} %pad_maximum_fusion.1.scalars, bf16[512,1152]{1,0:T(8,128)(2,1)S(1)} %constant_dynamic-update-slice_fusion.img, bf16[512,1152]{1,0:T(8,128)(2,1)S(1)} %constant_dynamic-update-slice_fusion.4.txt_c.own, ...), custom_call_target="tpu_custom_call" | custom-call | flops 1 | bytes 1 | tf_op jit(solution)/shard_map/pallas_call | solution.py:37
  52.5 7.3 %collective-permute-done.7 = bf16[128,1152]{1,0:T(8,128)(2,1)S(1)} collective-permute-done((bf16[128,1152]{1,0:T(8,128)(2,1)}, bf16[128,1152]{1,0:T(8,128)(2,1)S(1)}, u32[]{:S(2)}, u32[]{:S(2)}) %collective-permute-start.7) | collective-permute-done | bytes 294944 | tf_op jit(solution)/shard_map/ppermute | solution.py:25
  62.9 5.2 %shard_map.61 = (f32[384,1152]{1,0:T(8,128)S(1)}, f32[1024,1152]{1,0:T(8,128)S(1)}) custom-call(f32[2]{0:T(128)S(1)} %pad_maximum_fusion.1.scalars, bf16[384,1152]{1,0:T(8,128)(2,1)S(1)} %constant_dynamic-update-slice_fusion.12.img, bf16[512,1152]{1,0:T(8,128)(2,1)S(1)} %constant_dynamic-update-slice_fusion.4.txt_c.own, ...), custom_call_target="tpu_custom_call", output_to_operand_aliasing={{1}: (4, {})} | custom-call | flops 1 | bytes 1 | tf_op jit(solution)/shard_map/pallas_call | solution.py:37
  68.1 5.0 %shard_map.62 = (f32[128,1152]{1,0:T(8,128)S(1)}, bf16[256,1152]{1,0:T(8,128)(2,1)S(1)}, f32[1024,1152]{1,0:T(8,128)S(1)}) custom-call(f32[2]{0:T(128)S(1)} %pad_maximum_fusion.1.scalars, bf16[384,1152]{1,0:T(8,128)(2,1)S(1)} %constant_dynamic-update-slice_fusion.12.img, bf16[512,1152]{1,0:T(8,128)(2,1)S(1)} %constant_dynamic-update-slice_fusion.8.txt_c.sh, ...), custom_call_target="tpu_custom_call" | custom-call | flops 1 | bytes 1 | tf_op jit(solution)/shard_map/pallas_call | solution.py:37
  73.1 6.3 %shard_map.63 = (f32[128,1152]{1,0:T(8,128)S(1)}, f32[128,1152]{1,0:T(8,128)S(1)}, f32[128,1152]{1,0:T(8,128)S(1)}, bf16[128,1152]{1,0:T(8,128)(2,1)S(1)}, f32[1024,1152]{1,0:T(8,128)S(1)}) custom-call(f32[2]{0:T(128)S(1)} %pad_maximum_fusion.1.scalars, bf16[512,1152]{1,0:T(8,128)(2,1)S(1)} %constant_dynamic-update-slice_fusion.img, ...), custom_call_target="tpu_custom_call", output_to_operand_aliasing={{4}: (5, {})} | custom-call | flops 1 | bytes 1 | tf_op jit(solution)/shard_map/pallas_call | solution.py:37
  79.4 2.6 %shard_map.64 = (f32[128,1152]{1,0:T(8,128)S(1)}, bf16[1024,1152]{1,0:T(8,128)(2,1)S(1)}) custom-call(f32[2]{0:T(128)S(1)} %pad_maximum_fusion.1.scalars, bf16[128,1152]{1,0:T(8,128)(2,1)S(1)} %collective-permute-done.14.img, bf16[512,1152]{1,0:T(8,128)(2,1)S(1)} %collective-permute-done.9.txt_s.own, bf16[512,1152]{1,0:T(8,128)(2,1)S(1)} %collective-permute-done.13.txt_s.sh, ...), custom_call_target="tpu_custom_call" | custom-call | flops 1 | bytes 1 | tf_op jit(solution)/shard_map/pallas_call | solution.py:37
  82.7 2.5 %shard_map.65 = (bf16[128,1152]{1,0:T(8,128)(2,1)S(1)}, f32[1024,1152]{1,0:T(8,128)S(1)}) custom-call(f32[2]{0:T(128)S(1)} %pad_maximum_fusion.1.scalars, bf16[128,1152]{1,0:T(8,128)(2,1)S(1)} %collective-permute-done.14.img, bf16[512,1152]{1,0:T(8,128)(2,1)S(1)} %constant_dynamic-update-slice_fusion.4.txt_c.own, ...), custom_call_target="tpu_custom_call" | custom-call | flops 1 | bytes 1 | tf_op jit(solution)/shard_map/pallas_call | solution.py:37
  85.3 13.7 %collective-permute-done.16 = bf16[256,1152]{1,0:T(8,128)(2,1)S(1)} collective-permute-done((bf16[256,1152]{1,0:T(8,128)(2,1)S(1)}, bf16[256,1152]{1,0:T(8,128)(2,1)S(1)}, u32[]{:S(2)}, u32[]{:S(2)}) %collective-permute-start.16) | collective-permute-done | bytes 589856 | tf_op jit(solution)/shard_map/ppermute | solution.py:16
  101.6 2.7 %collective-permute-start.18 = (bf16[128,1152]{1,0:T(8,128)(2,1)S(1)}, bf16[128,1152]{1,0:T(8,128)(2,1)S(1)}, u32[]{:S(2)}, u32[]{:S(2)}) collective-permute-start(bf16[128,1152]{1,0:T(8,128)(2,1)S(1)} %get-tuple-element.117), channel_id=1, source_target_pairs={{0,24},{1,25},{2,26},{3,27},{4,28},{5,29},{6,30},{7,31},{8,0},{9,1... | collective-permute-start | bytes 884744 | tf_op jit(solution)/shard_map/ppermute | solution.py:25
  104.2 2.6 %collective-permute-start.20 = (bf16[128,1152]{1,0:T(8,128)(2,1)S(1)}, bf16[128,1152]{1,0:T(8,128)(2,1)S(1)}, u32[]{:S(2)}, u32[]{:S(2)}) collective-permute-start(bf16[128,1152]{1,0:T(8,128)(2,1)S(1)} %get-tuple-element.121), channel_id=1, source_target_pairs={{0,2},{1,3},{2,4},{3,5},{4,6},{5,7},{6,0},{7,1},{8,10},{9,11},{10,... | collective-permute-start | bytes 884744 | tf_op jit(solution)/shard_map/ppermute | solution.py:25
  106.9 2.6 %collective-permute-done.19 = bf16[128,1152]{1,0:T(8,128)(2,1)S(1)} collective-permute-done((bf16[128,1152]{1,0:T(8,128)(2,1)S(1)}, bf16[128,1152]{1,0:T(8,128)(2,1)S(1)}, u32[]{:S(2)}, u32[]{:S(2)}) %collective-permute-start.19) | collective-permute-done | bytes 294944 | tf_op jit(solution)/shard_map/ppermute | solution.py:16
  110.7 5.5 %collective-permute-done.17.refs_2_ = bf16[128,1152]{1,0:T(8,128)(2,1)S(1)} collective-permute-done((bf16[128,1152]{1,0:T(8,128)(2,1)S(1)}, bf16[128,1152]{1,0:T(8,128)(2,1)S(1)}, u32[]{:S(2)}, u32[]{:S(2)}) %collective-permute-start.17) | collective-permute-done | bytes 294944 | tf_op jit(solution)/shard_map/ppermute | solution.py:25
  116.4 2.2 %collective-permute-done.20 = bf16[128,1152]{1,0:T(8,128)(2,1)S(1)} collective-permute-done((bf16[128,1152]{1,0:T(8,128)(2,1)S(1)}, bf16[128,1152]{1,0:T(8,128)(2,1)S(1)}, u32[]{:S(2)}, u32[]{:S(2)}) %collective-permute-start.20) | collective-permute-done | bytes 294944 | tf_op jit(solution)/shard_map/ppermute | solution.py:25
  118.6 3.4 %collective-permute-done.21 = bf16[128,1152]{1,0:T(8,128)(2,1)S(1)} collective-permute-done((bf16[128,1152]{1,0:T(8,128)(2,1)S(1)}, bf16[128,1152]{1,0:T(8,128)(2,1)S(1)}, u32[]{:S(2)}, u32[]{:S(2)}) %collective-permute-start.21) | collective-permute-done | bytes 294944 | tf_op jit(solution)/shard_map/ppermute | solution.py:25
  125.7 2.4 %collective-permute-start.28 = (bf16[128,1152]{1,0:T(8,128)(2,1)S(1)}, bf16[128,1152]{1,0:T(8,128)(2,1)S(1)}, u32[]{:S(2)}, u32[]{:S(2)}) collective-permute-start(bf16[128,1152]{1,0:T(8,128)(2,1)S(1)} %add_convert_fusion), channel_id=1, source_target_pairs={{0,224},{32,0},{64,32},{96,64},{128,96},{160,128},{192,160},{224,1... | collective-permute-start | bytes 884744 | tf_op jit(solution)/shard_map/ppermute | solution.py:16
  128.1 2.1 %collective-permute-done.23.refs_0_ = bf16[128,1152]{1,0:T(8,128)(2,1)S(1)} collective-permute-done((bf16[128,1152]{1,0:T(8,128)(2,1)S(1)}, bf16[128,1152]{1,0:T(8,128)(2,1)S(1)}, u32[]{:S(2)}, u32[]{:S(2)}) %collective-permute-start.23) | collective-permute-done | bytes 294944 | tf_op jit(solution)/shard_map/ppermute | solution.py:16
  131.1 10.4 %collective-permute-done.24.refs_1_ = bf16[128,1152]{1,0:T(8,128)(2,1)S(1)} collective-permute-done((bf16[128,1152]{1,0:T(8,128)(2,1)S(1)}, bf16[128,1152]{1,0:T(8,128)(2,1)S(1)}, u32[]{:S(2)}, u32[]{:S(2)}) %collective-permute-start.24) | collective-permute-done | bytes 294944 | tf_op jit(solution)/shard_map/ppermute | solution.py:25
  141.6 2.4 %shard_map.67 = (f32[128,1152]{1,0:T(8,128)}, f32[128,1152]{1,0:T(8,128)}) custom-call(f32[128,1152]{1,0:T(8,128)S(1)} %copy-done.1, f32[128,1152]{1,0:T(8,128)S(1)} %copy-done.3, f32[128,1152]{1,0:T(8,128)S(1)} %get-tuple-element.97.gu_0, bf16[128,1152]{1,0:T(8,128)(2,1)S(1)} %collective-permute-done.23.refs_0_, ...), custom_call_target="tpu_custom_call" | custom-call | flops 1 | bytes 1 | tf_op jit(solution)/shard_map/pallas_call | solution.py:37
  (85 shorter events, 27.1 us)
Async XLA Ops:
  4.3 10.8 %collective-permute-start.1 = (bf16[128,1152]{1,0:T(8,128)(2,1)}, bf16[128,1152]{1,0:T(8,128)(2,1)S(1)}, u32[]{:S(2)}, u32[]{:S(2)}) collective-permute-start(bf16[128,1152]{1,0:T(8,128)(2,1)} %get-tuple-element.74), channel_id=1, source_target_pairs={{0,192},{32,224},{64,0},{96,32},{128,64},{160,96},{192,128},{224,1... | collective-permute-start | bytes 884744 | tf_op jit(solution)/shard_map/ppermute | solution.py:16
  7.0 17.7 %collective-permute-start.6 = (bf16[128,1152]{1,0:T(8,128)(2,1)S(1)}, bf16[128,1152]{1,0:T(8,128)(2,1)S(1)}, u32[]{:S(2)}, u32[]{:S(2)}) collective-permute-start(bf16[128,1152]{1,0:T(8,128)(2,1)S(1)} %get-tuple-element.76), channel_id=1, source_target_pairs={{0,32},{32,64},{64,96},{96,128},{128,160},{160,192},{192,224},{224... | collective-permute-start | bytes 884744 | tf_op jit(solution)/shard_map/ppermute | solution.py:16
  9.0 17.5 %collective-permute-start = (bf16[128,1152]{1,0:T(8,128)(2,1)S(1)}, bf16[128,1152]{1,0:T(8,128)(2,1)S(1)}, u32[]{:S(2)}, u32[]{:S(2)}) collective-permute-start(bf16[128,1152]{1,0:T(8,128)(2,1)S(1)} %get-tuple-element.76), channel_id=1, source_target_pairs={{0,6},{1,7},{2,0},{3,1},{4,2},{5,3},{6,4},{7,5},{8,14},{9,15},{10,... | collective-permute-start | bytes 884744 | tf_op jit(solution)/shard_map/ppermute | solution.py:25
  9.7 23.7 %collective-permute-start.5 = (bf16[128,1152]{1,0:T(8,128)(2,1)}, bf16[128,1152]{1,0:T(8,128)(2,1)S(1)}, u32[]{:S(2)}, u32[]{:S(2)}) collective-permute-start(bf16[128,1152]{1,0:T(8,128)(2,1)} %get-tuple-element.74), channel_id=1, source_target_pairs={{0,8},{1,9},{2,10},{3,11},{4,12},{5,13},{6,14},{7,15},{8,16},{9,17... | collective-permute-start | bytes 884744 | tf_op jit(solution)/shard_map/ppermute | solution.py:25
  13.0 20.5 %collective-permute-start.4 = (bf16[128,1152]{1,0:T(8,128)(2,1)}, bf16[128,1152]{1,0:T(8,128)(2,1)S(1)}, u32[]{:S(2)}, u32[]{:S(2)}) collective-permute-start(bf16[128,1152]{1,0:T(8,128)(2,1)} %get-tuple-element.74), channel_id=1, source_target_pairs={{0,24},{1,25},{2,26},{3,27},{4,28},{5,29},{6,30},{7,31},{8,0},{9,1... | collective-permute-start | bytes 884744 | tf_op jit(solution)/shard_map/ppermute | solution.py:25
  15.1 18.3 %collective-permute-start.3 = (bf16[128,1152]{1,0:T(8,128)(2,1)S(1)}, bf16[128,1152]{1,0:T(8,128)(2,1)S(1)}, u32[]{:S(2)}, u32[]{:S(2)}) collective-permute-start(bf16[128,1152]{1,0:T(8,128)(2,1)S(1)} %get-tuple-element.76), channel_id=1, source_target_pairs={{0,4},{1,5},{2,6},{3,7},{4,0},{5,1},{6,2},{7,3},{8,12},{9,13},{10,... | collective-permute-start | bytes 884744 | tf_op jit(solution)/shard_map/ppermute | solution.py:25
  34.2 10.9 %collective-permute-start.9 = (bf16[512,1152]{1,0:T(8,128)(2,1)S(1)}, bf16[512,1152]{1,0:T(8,128)(2,1)S(1)}, u32[]{:S(2)}, u32[]{:S(2)}) collective-permute-start(bf16[512,1152]{1,0:T(8,128)(2,1)S(1)} %constant_dynamic-update-slice_fusion.4.txt_c.own), channel_id=1, source_target_pairs={{0,1},{1,0},{2,3},{3,2},{4,5},{5,4},{6,7},{7,6},{8,9},{9,8},{10,11... | collective-permute-start | bytes 3538952 | tf_op jit(solution)/shard_map/ppermute | solution.py:25
  34.3 18.2 %collective-permute-start.12 = (bf16[128,1152]{1,0:T(8,128)(2,1)}, bf16[128,1152]{1,0:T(8,128)(2,1)}, u32[]{:S(2)}, u32[]{:S(2)}) collective-permute-start(bf16[128,1152]{1,0:T(8,128)(2,1)} %get-tuple-element.74), channel_id=1, source_target_pairs={{0,16},{1,17},{2,18},{3,19},{4,20},{5,21},{6,22},{7,23},{8,24},{9,... | collective-permute-start | bytes 884744 | tf_op jit(solution)/shard_map/ppermute | solution.py:25
  43.2 16.5 %collective-permute-start.7 = (bf16[128,1152]{1,0:T(8,128)(2,1)}, bf16[128,1152]{1,0:T(8,128)(2,1)S(1)}, u32[]{:S(2)}, u32[]{:S(2)}) collective-permute-start(bf16[128,1152]{1,0:T(8,128)(2,1)} %copy-done.8), channel_id=1, source_target_pairs={{0,6},{1,7},{2,0},{3,1},{4,2},{5,3},{6,4},{7,5},{8,14},{9,15},{10,... | collective-permute-start | bytes 884744 | tf_op jit(solution)/shard_map/ppermute | solution.py:25
  44.9 14.9 %collective-permute-start.11 = (bf16[256,1152]{1,0:T(8,128)(2,1)S(1)}, bf16[256,1152]{1,0:T(8,128)(2,1)S(1)}, u32[]{:S(2)}, u32[]{:S(2)}) collective-permute-start(bf16[256,1152]{1,0:T(8,128)(2,1)S(1)} %pad_maximum_fusion), channel_id=1, source_target_pairs={{0,192},{32,224},{64,0},{96,32},{128,64},{160,96},{192,128},{224,1... | collective-permute-start | bytes 1769480 | tf_op jit(solution)/shard_map/ppermute | solution.py:16
  45.1 14.7 %collective-permute-start.10 = (bf16[128,1152]{1,0:T(8,128)(2,1)S(1)}, bf16[128,1152]{1,0:T(8,128)(2,1)S(1)}, u32[]{:S(2)}, u32[]{:S(2)}) collective-permute-start(bf16[128,1152]{1,0:T(8,128)(2,1)S(1)} %copy-done.9), channel_id=1, source_target_pairs={{0,4},{1,5},{2,6},{3,7},{4,0},{5,1},{6,2},{7,3},{8,12},{9,13},{10,... | collective-permute-start | bytes 884744 | tf_op jit(solution)/shard_map/ppermute | solution.py:25
  60.2 19.2 %collective-permute-start.14 = (bf16[128,1152]{1,0:T(8,128)(2,1)}, bf16[128,1152]{1,0:T(8,128)(2,1)S(1)}, u32[]{:S(2)}, u32[]{:S(2)}) collective-permute-start(bf16[128,1152]{1,0:T(8,128)(2,1)} %collective-permute-done.12), channel_id=1, source_target_pairs={{0,192},{32,224},{64,0},{96,32},{128,64},{160,96},{192,128},{224,1... | collective-permute-start | bytes 884744 | tf_op jit(solution)/shard_map/ppermute | solution.py:16
  81.9 17.0 %collective-permute-start.15 = (bf16[1024,1152]{1,0:T(8,128)(2,1)S(1)}, bf16[1024,1152]{1,0:T(8,128)(2,1)S(1)}, u32[]{:S(2)}, u32[]{:S(2)}) collective-permute-start(bf16[1024,1152]{1,0:T(8,128)(2,1)S(1)} %get-tuple-element.104), channel_id=1, source_target_pairs={{0,1},{1,0},{2,3},{3,2},{4,5},{5,4},{6,7},{7,6},{8,9},{9,8},{10,11... | collective-permute-start | bytes 7077896 | tf_op jit(solution)/shard_map/ppermute | solution.py:25
  82.2 16.8 %collective-permute-start.16 = (bf16[256,1152]{1,0:T(8,128)(2,1)S(1)}, bf16[256,1152]{1,0:T(8,128)(2,1)S(1)}, u32[]{:S(2)}, u32[]{:S(2)}) collective-permute-start(bf16[256,1152]{1,0:T(8,128)(2,1)S(1)} %get-tuple-element.105), channel_id=1, source_target_pairs={{0,64},{32,96},{64,128},{96,160},{128,192},{160,224},{192,0},{224,... | collective-permute-start | bytes 1769480 | tf_op jit(solution)/shard_map/ppermute | solution.py:16
  99.8 16.4 %collective-permute-start.17 = (bf16[128,1152]{1,0:T(8,128)(2,1)S(1)}, bf16[128,1152]{1,0:T(8,128)(2,1)S(1)}, u32[]{:S(2)}, u32[]{:S(2)}) collective-permute-start(bf16[128,1152]{1,0:T(8,128)(2,1)S(1)} %get-tuple-element.116), channel_id=1, source_target_pairs={{0,8},{1,9},{2,10},{3,11},{4,12},{5,13},{6,14},{7,15},{8,16},{9,17... | collective-permute-start | bytes 884744 | tf_op jit(solution)/shard_map/ppermute | solution.py:25
  101.6 14.8 %collective-permute-start.18 = (bf16[128,1152]{1,0:T(8,128)(2,1)S(1)}, bf16[128,1152]{1,0:T(8,128)(2,1)S(1)}, u32[]{:S(2)}, u32[]{:S(2)}) collective-permute-start(bf16[128,1152]{1,0:T(8,128)(2,1)S(1)} %get-tuple-element.117), channel_id=1, source_target_pairs={{0,24},{1,25},{2,26},{3,27},{4,28},{5,29},{6,30},{7,31},{8,0},{9,1... | collective-permute-start | bytes 884744 | tf_op jit(solution)/shard_map/ppermute | solution.py:25
  104.2 14.4 %collective-permute-start.20 = (bf16[128,1152]{1,0:T(8,128)(2,1)S(1)}, bf16[128,1152]{1,0:T(8,128)(2,1)S(1)}, u32[]{:S(2)}, u32[]{:S(2)}) collective-permute-start(bf16[128,1152]{1,0:T(8,128)(2,1)S(1)} %get-tuple-element.121), channel_id=1, source_target_pairs={{0,2},{1,3},{2,4},{3,5},{4,6},{5,7},{6,0},{7,1},{8,10},{9,11},{10,... | collective-permute-start | bytes 884744 | tf_op jit(solution)/shard_map/ppermute | solution.py:25
  106.9 15.2 %collective-permute-start.21 = (bf16[128,1152]{1,0:T(8,128)(2,1)S(1)}, bf16[128,1152]{1,0:T(8,128)(2,1)S(1)}, u32[]{:S(2)}, u32[]{:S(2)}) collective-permute-start(bf16[128,1152]{1,0:T(8,128)(2,1)S(1)} %get-tuple-element.122), channel_id=1, source_target_pairs={{0,6},{1,7},{2,0},{3,1},{4,2},{5,3},{6,4},{7,5},{8,14},{9,15},{10,... | collective-permute-start | bytes 884744 | tf_op jit(solution)/shard_map/ppermute | solution.py:25
  109.5 12.6 %collective-permute-start.22 = (bf16[128,1152]{1,0:T(8,128)(2,1)S(1)}, bf16[128,1152]{1,0:T(8,128)(2,1)S(1)}, u32[]{:S(2)}, u32[]{:S(2)}) collective-permute-start(bf16[128,1152]{1,0:T(8,128)(2,1)S(1)} %get-tuple-element.123), channel_id=1, source_target_pairs={{0,4},{1,5},{2,6},{3,7},{4,0},{5,1},{6,2},{7,3},{8,12},{9,13},{10,... | collective-permute-start | bytes 884744 | tf_op jit(solution)/shard_map/ppermute | solution.py:25
  122.3 19.2 %collective-permute-start.24 = (bf16[128,1152]{1,0:T(8,128)(2,1)S(1)}, bf16[128,1152]{1,0:T(8,128)(2,1)S(1)}, u32[]{:S(2)}, u32[]{:S(2)}) collective-permute-start(bf16[128,1152]{1,0:T(8,128)(2,1)S(1)} %add_convert_fusion.1), channel_id=1, source_target_pairs={{0,16},{1,17},{2,18},{3,19},{4,20},{5,21},{6,22},{7,23},{8,24},{9,... | collective-permute-start | bytes 884744 | tf_op jit(solution)/shard_map/ppermute | solution.py:25
  123.7 17.8 %collective-permute-start.25 = (bf16[128,1152]{1,0:T(8,128)(2,1)S(1)}, bf16[128,1152]{1,0:T(8,128)(2,1)S(1)}, u32[]{:S(2)}, u32[]{:S(2)}) collective-permute-start(bf16[128,1152]{1,0:T(8,128)(2,1)S(1)} %get-tuple-element.142), channel_id=1, source_target_pairs={{0,2},{1,3},{2,4},{3,5},{4,6},{5,7},{6,0},{7,1},{8,10},{9,11},{10,... | collective-permute-start | bytes 884744 | tf_op jit(solution)/shard_map/ppermute | solution.py:25
  124.0 17.6 %collective-permute-start.26 = (bf16[128,1152]{1,0:T(8,128)(2,1)S(1)}, bf16[128,1152]{1,0:T(8,128)(2,1)S(1)}, u32[]{:S(2)}, u32[]{:S(2)}) collective-permute-start(bf16[128,1152]{1,0:T(8,128)(2,1)S(1)} %get-tuple-element.143), channel_id=1, source_target_pairs={{0,6},{1,7},{2,0},{3,1},{4,2},{5,3},{6,4},{7,5},{8,14},{9,15},{10,... | collective-permute-start | bytes 884744 | tf_op jit(solution)/shard_map/ppermute | solution.py:25
  125.7 15.8 %collective-permute-start.28 = (bf16[128,1152]{1,0:T(8,128)(2,1)S(1)}, bf16[128,1152]{1,0:T(8,128)(2,1)S(1)}, u32[]{:S(2)}, u32[]{:S(2)}) collective-permute-start(bf16[128,1152]{1,0:T(8,128)(2,1)S(1)} %add_convert_fusion), channel_id=1, source_target_pairs={{0,224},{32,0},{64,32},{96,64},{128,96},{160,128},{192,160},{224,1... | collective-permute-start | bytes 884744 | tf_op jit(solution)/shard_map/ppermute | solution.py:16
  130.3 11.3 %collective-permute-start.27 = (bf16[128,1152]{1,0:T(8,128)(2,1)S(1)}, bf16[128,1152]{1,0:T(8,128)(2,1)S(1)}, u32[]{:S(2)}, u32[]{:S(2)}) collective-permute-start(bf16[128,1152]{1,0:T(8,128)(2,1)S(1)} %get-tuple-element.144), channel_id=1, source_target_pairs={{0,4},{1,5},{2,6},{3,7},{4,0},{5,1},{6,2},{7,3},{8,12},{9,13},{10,... | collective-permute-start | bytes 884744 | tf_op jit(solution)/shard_map/ppermute | solution.py:25
  (17 other events, 110.8 us)

commit v5 on v4

v5 whole, which is shorter than its diff:
```python
import functools

import jax
import jax.numpy as jnp
from jax import lax
from jax.experimental import pallas as pl
from jax.experimental.pallas import tpu as pltpu
from jax.sharding import PartitionSpec as P

X, ZL, ZH, Y, CORE = 4, 2, 4, 4, 2
GROUPS, DEVS = X * ZL, ZH * Y * CORE
F32, LOW = jnp.float32, jnp.bfloat16


def to_group(block, step):
    return lax.ppermute(block, "grp", [(i, (i + step) % GROUPS) for i in range(GROUPS)])


def to_dev(block, zh=0, y=0, core=0):
    route = []
    for i in range(DEVS):
        a, b, c = i // (Y * CORE), i // CORE % Y, i % CORE
        target = ((a + zh) % ZH * Y + (b + y) % Y) * CORE + (c + core) % CORE
        route.append((i, target))
    return lax.ppermute(block, "dev", route)


def fence(*arrays):
    return lax.optimization_barrier(arrays)


VMEM = pl.BlockSpec(memory_space=pltpu.VMEM)


def whole(kernel, outs, *operands, scalars=False, aliases=None, scratch=()):
    first = [pl.BlockSpec(memory_space=pltpu.SMEM)] if scalars else [VMEM]
    return pl.pallas_call(
        kernel,
        in_specs=first + [VMEM] * (len(operands) - 1),
        out_specs=[VMEM] * len(outs),
        out_shape=[jax.ShapeDtypeStruct(shape, kind) for shape, kind in outs],
        input_output_aliases=aliases or {},
        scratch_shapes=list(scratch),
        compiler_params=pltpu.CompilerParams(vmem_limit_bytes=28 * 1024 * 1024),
        cost_estimate=pl.CostEstimate(flops=1, bytes_accessed=1, transcendentals=0),
    )(*operands)


def inverse_of(values):
    return lax.rsqrt(jnp.sum(values * values, axis=1, keepdims=True) + 1e-06)


def each(rows, step):
    def over(body):
        @pl.loop(0, rows // step)
        def _(n):
            body(pl.ds(pl.multiple_of(n * step, step), step))

    return over


def unit_kernel(txt, img, txt_low, img_low):
    for values, low in ((txt, txt_low), (img, img_low)):

        @each(values.shape[0], 32)
        def _(span):
            low[span] = (values[span] * inverse_of(values[span])).astype(LOW)


def end_kernel(img, txt, gu_0, *refs):
    *parts, gv_0, up, down, far, behind, grad_img, grad_txt = refs
    sides = ((img, gu_0, parts, grad_img), (txt, gv_0, (up, down, far, behind), grad_txt))
    for values, own, others, grad in sides:

        @each(values.shape[0], 32)
        def _(span):
            sums = own[span]
            for other in others:
                sums = sums + other[span].astype(F32)
            inverse = inverse_of(values[span])
            unit = values[span] * inverse
            grad[span] = inverse * (sums - unit * jnp.sum(unit * sums, axis=1, keepdims=True))


def text_sums_kernel(place, mine, got_0, got_1, own, up, down, far):
    for n, out in enumerate((own, up, down, far)):

        @each(128, 32)
        def _(span):
            there = pl.ds(pl.multiple_of(place + n * 128 + span.start, 32), 32)
            inside = pl.ds(pl.multiple_of(n % 2 * 128 + span.start, 32), 32)
            got = (got_0, got_1)[n // 2]
            out[span] = (mine[there] + got[inside].astype(F32)).astype(out.dtype)


def products(scalars, img, txt, mask=None):
    half_temp, half_bias = scalars[0], scalars[1]
    logits = lax.dot_general(img, txt, (((1,), (1,)), ((), ())), preferred_element_type=F32)
    slopes = half_temp * jnp.tanh(half_temp * logits + half_bias) + half_temp
    if mask is not None:
        slopes = slopes - jnp.where(mask, 2.0 * half_temp, 0.0)
    coef = slopes.astype(LOW)
    gu = jnp.dot(coef, txt, preferred_element_type=F32)
    return gu, lax.dot_general(coef, img, (((0,), (0,)), ((), ())), preferred_element_type=F32)


def first_kernel(scalars, img_0, img_n, ahead_0, txt, gu, gv, img):
    for part, first in ((img_0, 0), (img_n, 128), (ahead_0, 384), (ahead_0, 512)):

        @each(part.shape[0], 32)
        def _(span):
            img[pl.ds(pl.multiple_of(first + span.start, 32), 32)] = part[span]

    shape = gu.shape[0], txt.shape[0]
    row, col = lax.broadcasted_iota(jnp.int32, shape, 0), lax.broadcasted_iota(jnp.int32, shape, 1)
    mask = jnp.logical_and(row == col, row < 128)
    gu[...], gv[: shape[1]] = products(scalars, img[0 : shape[0]], txt[...], mask)

    @each(shape[1], 32)
    def _(span):
        there = pl.ds(pl.multiple_of(shape[1] + span.start, 32), 32)
        gv[there] = jnp.zeros((32, gv.shape[1]), F32)


def both_halves(txt):
    size = txt.shape[0] // 2

    def over(body):
        @pl.loop(0, 2)
        def _(n):
            body(n, pl.ds(pl.multiple_of(n * size, size), size))

    return over


def second_kernel(scalars, img, txt, gv_in, gu, gv):
    @each(gu.shape[0], 32)
    def _(span):
        gu[span] = jnp.zeros((32, gu.shape[1]), F32)

    @both_halves(txt)
    def _(n, here):
        part, term = products(scalars, img[...], txt[here])
        gu[...] += part
        gv[here] = term + gv_in[here]


def third_kernel(scalars, img, txt, gu_in, gu_2, gu_n, gv, gu):
    @each(gu.shape[0], 32)
    def _(span):
        gu[span] = gu_in[span]

    @both_halves(txt)
    def _(n, here):
        part, gv[here] = products(scalars, img[...], txt[here])
        gu[...] += part

    gu_2[...] = gu[:128]
    gu_n[:256] = gu[128:].astype(LOW)
    gu_n[256:] = jnp.zeros((16, gu_n.shape[1]), LOW)


def fourth_kernel(scalars, img, txt, gu_in, gv_in, gu, piece_0, piece_1, piece_2, piece_3, gv):
    past = gu_in.shape[0]

    @each(past, 32)
    def _(span):
        gu[span] = gu_in[span]

    @each(gu.shape[0] - past, 32)
    def _(span):
        there = pl.ds(pl.multiple_of(past + span.start, 32), 32)
        gu[there] = jnp.zeros((32, gu.shape[1]), F32)

    @both_halves(txt)
    def _(n, here):
        part, term = products(scalars, img[...], txt[here])
        gu[...] += part
        gv[...] = term + gv_in[here]
        for place, outs in enumerate(((piece_0, piece_1), (piece_2, piece_3))):

            @pl.when(n == place)
            def _():
                for m, out in enumerate(outs):

                    @each(256, 32)
                    def _(span):
                        there = pl.ds(pl.multiple_of(m * 256 + span.start, 32), 32)
                        out[span] = gv[there].astype(LOW)


def fifth_kernel(scalars, img, txt, gu_in, gv_in, gu_0, gu_up, gu_down, au_0, au_2, gv, gu):
    size, past = txt.shape[0] // 2, img.shape[0] - 128
    part, term = products(scalars, img[...], txt[size:])
    gu[...] = gu_in[...] + part
    gv[size:] = term + gv_in[size:]
    part, term = products(scalars, img[past:], txt[0:size])
    gu[past:] += part
    gv[:size] = term + gv_in[:size]
    for n, out in enumerate((gu_0, gu_up, gu_down, au_0, au_2)):

        @each(128, 32)
        def _(span):
            out[span] = gu[pl.ds(pl.multiple_of(n * 128 + span.start, 32), 32)].astype(out.dtype)


def local(image_emb, text_emb, temp, bias):
    rows = image_emb.shape
    txt_0, img_0 = whole(unit_kernel, [(rows, LOW)] * 2, text_emb, image_emb)
    scalars = jnp.stack([0.5 * temp, 0.5 * bias])

    txt_up = to_dev(txt_0, y=-1)
    ahead_0 = to_group(img_0, -2)
    img_up = to_dev(img_0, zh=-1)
    img_down = to_dev(img_0, zh=1)
    behind_0 = to_group(txt_0, 1)
    ahead_0, txt_later = fence(ahead_0, txt_0)
    txt_down = to_dev(txt_later, y=1)
    txt_2 = to_dev(txt_later, y=2)
    txt_up, txt_down, txt_2, img_up, img_down, behind_0 = fence(
        txt_up, txt_down, txt_2, img_up, img_down, behind_0
    )
    width = rows[1]
    own_c = jnp.concatenate([txt_0, txt_up, txt_down, txt_2], axis=0)
    img_n = jnp.concatenate([img_up, img_down], axis=0)
    own_c, img_n, behind_0, img_0 = fence(own_c, img_n, behind_0, img_0)
    behind_up = to_dev(behind_0, y=-1)
    behind_down = to_dev(behind_0, y=1)
    behind_2 = to_dev(behind_0, y=2)
    ahead_n = to_group(img_n, -2)
    img_2 = to_dev(img_0, zh=2)
    half, wide = (own_c.shape[0], width), (2 * own_c.shape[0], width)
    gu_first, sums_c, images = whole(
        first_kernel,
        [(half, F32), (wide, F32), ((640, width), LOW)],
        *(scalars, img_0, img_n, ahead_0, own_c),
        scalars=True,
    )
    behind_up, behind_down, behind_2, ahead_n, img_2, gu_first, sums_c = fence(
        behind_up, behind_down, behind_2, ahead_n, img_2, gu_first, sums_c
    )
    txt_c = jnp.concatenate([own_c, behind_0, behind_up, behind_down, behind_2], axis=0)
    second = jnp.concatenate([img_2, ahead_n], axis=0)
    txt_s = to_dev(txt_c, core=1)
    ahead_2 = to_group(img_2, -2)
    gu_second, sums_c = whole(
        second_kernel,
        [(second.shape, F32), (wide, F32)],
        *(scalars, second, txt_c, sums_c),
        scalars=True,
        aliases={3: 1},
    )
    gu_2, au_n, others = whole(
        third_kernel,
        [(rows, F32), ((272, width), LOW), (wide, F32)],
        *(scalars, second, txt_s, gu_second),
        scalars=True,
        scratch=[pltpu.VMEM(second.shape, F32)],
    )
    back_n = to_group(au_n, 2)
    images = lax.dynamic_update_slice(images, ahead_2, (half[0], 0))
    gu_all, *pieces = whole(
        fourth_kernel,
        [(images.shape, F32)] + [((256, width), LOW)] * 4,
        *(scalars, images, txt_s, gu_first, others),
        scalars=True,
        scratch=[pltpu.VMEM(half, F32)],
    )
    got = [to_dev(piece, core=1) for piece in pieces]
    gu_0, gu_up, gu_down, au_0, au_2, sums_c = whole(
        fifth_kernel,
        [(rows, F32)] * 3 + [(rows, LOW)] * 2 + [(wide, F32)],
        *(scalars, images, txt_c, gu_all, sums_c),
        scalars=True,
        aliases={4: 5},
        scratch=[pltpu.VMEM(images.shape, F32)],
    )
    back_n, *got, au_2, sums_c = fence(back_n, *got, au_2, sums_c)
    sums = [(rows, F32)] + [(rows, LOW)] * 3
    sh_sum, sh_up, sh_down, sh_far = whole(
        functools.partial(text_sums_kernel, half[0]), sums, sums_c, *got[2:]
    )
    sum_up = (gu_up + back_n[:128].astype(F32)).astype(LOW)
    sum_down = (gu_down + back_n[128:256].astype(F32)).astype(LOW)
    sum_up, sum_down, sh_up, sh_down, au_2 = fence(sum_up, sum_down, sh_up, sh_down, au_2)
    back_2 = to_group(au_2, 2)
    sh_up = to_dev(sh_up, y=1)
    sh_down = to_dev(sh_down, y=-1)
    sum_up = to_dev(sum_up, zh=1)
    sum_down = to_dev(sum_down, zh=-1)
    back_2, sh_far = fence(back_2, sh_far)
    sh_far = to_dev(sh_far, y=2)
    own_sum, own_up, own_down, own_far = whole(
        functools.partial(text_sums_kernel, 0), sums, sums_c, *got[:2]
    )
    sum_up, sum_down, back_2, sh_up, sh_down, sh_far, au_0, own_up, own_down = fence(
        sum_up, sum_down, back_2, sh_up, sh_down, sh_far, au_0, own_up, own_down
    )
    sum_2 = (gu_2 + back_2.astype(F32)).astype(LOW)
    behind = (sh_sum + sh_up.astype(F32) + sh_down.astype(F32) + sh_far.astype(F32)).astype(LOW)
    sum_2, behind, au_0, own_up, own_down = fence(sum_2, behind, au_0, own_up, own_down)
    back_0 = to_group(au_0, 2)
    own_up = to_dev(own_up, y=1)
    own_down = to_dev(own_down, y=-1)
    behind = to_group(behind, -1)
    sum_2 = to_dev(sum_2, zh=2)
    back_0, own_far = fence(back_0, own_far)
    own_far = to_dev(own_far, y=2)
    return tuple(
        whole(
            end_kernel,
            [(rows, F32)] * 2,
            *(image_emb, text_emb, gu_0, back_0, sum_2, sum_up, sum_down),
            *(own_sum, own_up, own_down, own_far, behind),
        )
    )


def solution(mesh):
    return jax.shard_map(
        local,
        mesh=mesh,
        in_specs=(P(("grp", "dev"), None), P(("grp", "dev"), None), P(), P()),
        out_specs=(P(("grp", "dev"), None), P(("grp", "dev"), None)),
        check_vma=False,
    )
```

time: 145 us -> 131 us (0.903)
  waiting for transfers between devices: 63.2 us -> 42.1 us
  starting transfers between devices: 39.2 us -> 52.8 us
  local copies, waits for them, and re-layouts: 5.94 us -> 2.48 us
  Pallas kernels: 31.9 us -> 29 us
    ppermute x8, waiting for transfers between devices: 27.2 us -> 13 us  [to_group(): lax.ppermute(block, 'grp', [(i, (i + step) % GROUPS) for i in range(GROUP...]
    ppermute x8, starting transfers between devices: 9.42 us -> 19.5 us  [to_group(): lax.ppermute(block, 'grp', [(i, (i + step) % GROUPS) for i in range(GROUP...]
    ppermute x21 -> x23, waiting for transfers between devices: 36 us -> 29.1 us  [to_dev(): return lax.ppermute(block, 'dev', route)]
    ppermute x21 -> x23, starting transfers between devices: 29.8 us -> 33.2 us  [to_dev(): return lax.ppermute(block, 'dev', route)]
    unnamed x33 -> x13, local copies, waits for them, and re-layouts: 5.78 us -> 2.34 us
    pallas_call x9, Pallas kernels: 31.9 us -> 29 us  [whole(): pl.pallas_call(kernel, in_specs=first + [VMEM] * (len(operands) - 1), out...]
  transfers between devices with their start and end apart: 29 -> 31, of which waited for: 12 -> 10; matrix products, arithmetic and copies ran while one was open for 2% -> 0% of each run, Pallas kernels for 17% -> 20%
where the time goes in v5:
time: 131 us; the launch traced here: 129 us
  starting transfers between devices  52.8 us (40%)
  waiting for transfers between devices  42.1 us (32%)
  Pallas kernels  29 us (22%)
  local copies, waits for them, and re-layouts  2.48 us (2%)
  between operations  2.18 us (2%)
    ppermute x23, starting transfers between devices, to_dev(): return lax.ppermute(block, 'dev', route)  33.2 us
    ppermute x23, waiting for transfers between devices, to_dev(): return lax.ppermute(block, 'dev', route)  29.1 us
    pallas_call x9, Pallas kernels, whole(): pl.pallas_call(kernel, in_specs=first + [VMEM] * (len(operands) - 1), out...  29 us
    ppermute x8, starting transfers between devices, to_group(): lax.ppermute(block, 'grp', [(i, (i + step) % GROUPS) for i in range(GROUP...  19.5 us
    ppermute x8, waiting for transfers between devices, to_group(): lax.ppermute(block, 'grp', [(i, (i + step) % GROUPS) for i in range(GROUP...  13 us
  transfers between devices with their start and end apart: 31, of which 10 were waited for; matrix products, arithmetic and copies ran while one was open for 0% of the time, Pallas kernels for 20%

profile of v5, /device:TPU:24, one launch (start us, length us, event | category | flops | bytes accessed | tf_op | source)
XLA Modules:
  0.0 129.1 jit_solution(662045755915614441)
XLA Ops:
  3.6 2.8 %collective-permute-start.1 = (bf16[128,1152]{1,0:T(8,128)(2,1)S(1)}, bf16[128,1152]{1,0:T(8,128)(2,1)S(1)}, u32[]{:S(2)}, u32[]{:S(2)}) collective-permute-start(bf16[128,1152]{1,0:T(8,128)(2,1)S(1)} %get-tuple-element.89.img_0), channel_id=1, source_target_pairs={{0,192},{32,224},{64,0},{96,32},{128,64},{160,96},{192,128},{224,1... | collective-permute-start | bytes 884744 | tf_op jit(solution)/shard_map/ppermute | solution.py:16
  9.1 3.3 %collective-permute-start.5 = (bf16[128,1152]{1,0:T(8,128)(2,1)S(1)}, bf16[128,1152]{1,0:T(8,128)(2,1)S(1)}, u32[]{:S(2)}, u32[]{:S(2)}) collective-permute-start(bf16[128,1152]{1,0:T(8,128)(2,1)S(1)} %get-tuple-element.89.img_0), channel_id=1, source_target_pairs={{0,8},{1,9},{2,10},{3,11},{4,12},{5,13},{6,14},{7,15},{8,16},{9,17... | collective-permute-start | bytes 884744 | tf_op jit(solution)/shard_map/ppermute | solution.py:25
  15.4 8.9 %collective-permute-done.6 = bf16[128,1152]{1,0:T(8,128)(2,1)S(1)} collective-permute-done((bf16[128,1152]{1,0:T(8,128)(2,1)S(1)}, bf16[128,1152]{1,0:T(8,128)(2,1)S(1)}, u32[]{:S(2)}, u32[]{:S(2)}) %collective-permute-start.6) | collective-permute-done | bytes 294944 | tf_op jit(solution)/shard_map/ppermute | solution.py:16
  25.7 7.1 %collective-permute-done.5 = bf16[128,1152]{1,0:T(8,128)(2,1)S(1)} collective-permute-done((bf16[128,1152]{1,0:T(8,128)(2,1)S(1)}, bf16[128,1152]{1,0:T(8,128)(2,1)S(1)}, u32[]{:S(2)}, u32[]{:S(2)}) %collective-permute-start.5) | collective-permute-done | bytes 294944 | tf_op jit(solution)/shard_map/ppermute | solution.py:25
  35.2 2.2 %collective-permute-start.8 = (bf16[128,1152]{1,0:T(8,128)(2,1)S(1)}, bf16[128,1152]{1,0:T(8,128)(2,1)S(1)}, u32[]{:S(2)}, u32[]{:S(2)}) collective-permute-start(bf16[128,1152]{1,0:T(8,128)(2,1)S(1)} %collective-permute-done.6), channel_id=1, source_target_pairs={{0,2},{1,3},{2,4},{3,5},{4,6},{5,7},{6,0},{7,1},{8,10},{9,11},{10,... | collective-permute-start | bytes 884744 | tf_op jit(solution)/shard_map/ppermute | solution.py:25
  37.4 5.6 %collective-permute-start.11 = (bf16[128,1152]{1,0:T(8,128)(2,1)S(1)}, bf16[128,1152]{1,0:T(8,128)(2,1)S(1)}, u32[]{:S(2)}, u32[]{:S(2)}) collective-permute-start(bf16[128,1152]{1,0:T(8,128)(2,1)S(1)} %get-tuple-element.89.img_0), channel_id=1, source_target_pairs={{0,16},{1,17},{2,18},{3,19},{4,20},{5,21},{6,22},{7,23},{8,24},{9,... | collective-permute-start | bytes 884744 | tf_op jit(solution)/shard_map/ppermute | solution.py:25
  43.1 3.2 %shard_map.60 = (f32[512,1152]{1,0:T(8,128)S(1)}, f32[1024,1152]{1,0:T(8,128)S(1)}, bf16[640,1152]{1,0:T(8,128)(2,1)S(1)}) custom-call(f32[2]{0:T(128)S(1)} %pad_maximum_fusion.2.scalars, bf16[128,1152]{1,0:T(8,128)(2,1)S(1)} %get-tuple-element.89.img_0, bf16[256,1152]{1,0:T(8,128)(2,1)S(1)} %pad_maximum_fusion.1.img_n, ...), custom_call_target="tpu_custom_call" | custom-call | flops 1 | bytes 1 | tf_op jit(solution)/shard_map/pallas_call | solution.py:37
  46.4 3.4 %collective-permute-done.11 = bf16[128,1152]{1,0:T(8,128)(2,1)S(1)} collective-permute-done((bf16[128,1152]{1,0:T(8,128)(2,1)S(1)}, bf16[128,1152]{1,0:T(8,128)(2,1)S(1)}, u32[]{:S(2)}, u32[]{:S(2)}) %collective-permute-start.11) | collective-permute-done | bytes 294944 | tf_op jit(solution)/shard_map/ppermute | solution.py:25
  51.1 4.9 %shard_map.61 = (f32[384,1152]{1,0:T(8,128)S(1)}, f32[1024,1152]{1,0:T(8,128)S(1)}) custom-call(f32[2]{0:T(128)S(1)} %pad_maximum_fusion.2.scalars, bf16[384,1152]{1,0:T(8,128)(2,1)S(1)} %constant_dynamic-update-slice_fusion.5.img, bf16[1024,1152]{1,0:T(8,128)(2,1)S(1)} %constant_dynamic-update-slice_fusion.txt, ...), custom_call_target="tpu_custom_call", output_to_operand_aliasing={{1}: (3, {})} | custom-call | flops 1 | bytes 1 | tf_op jit(solution)/shard_map/pallas_call | solution.py:37
  56.0 4.7 %shard_map.62 = (f32[128,1152]{1,0:T(8,128)S(1)}, bf16[272,1152]{1,0:T(8,128)(2,1)S(1)}, f32[1024,1152]{1,0:T(8,128)S(1)}) custom-call(f32[2]{0:T(128)S(1)} %pad_maximum_fusion.2.scalars, bf16[384,1152]{1,0:T(8,128)(2,1)S(1)} %constant_dynamic-update-slice_fusion.5.img, bf16[1024,1152]{1,0:T(8,128)(2,1)S(1)} %collective-permute-done.13.txt, ...), custom_call_target="tpu_custom_call" | custom-call | flops 1 | bytes 1 | tf_op jit(solution)/shard_map/pallas_call | solution.py:37
  60.7 4.6 %collective-permute-start.14 = (bf16[272,1152]{1,0:T(8,128)(2,1)S(1)}, bf16[272,1152]{1,0:T(8,128)(2,1)S(1)}, u32[]{:S(2)}, u32[]{:S(2)}) collective-permute-start(bf16[272,1152]{1,0:T(8,128)(2,1)S(1)} %get-tuple-element.111), channel_id=1, source_target_pairs={{0,64},{32,96},{64,128},{96,160},{128,192},{160,224},{192,0},{224,... | collective-permute-start | bytes 1880072 | tf_op jit(solution)/shard_map/ppermute | solution.py:16
  65.3 7.1 %shard_map.63 = (f32[640,1152]{1,0:T(8,128)S(1)}, bf16[256,1152]{1,0:T(8,128)(2,1)S(1)}, bf16[256,1152]{1,0:T(8,128)(2,1)S(1)}, bf16[256,1152]{1,0:T(8,128)(2,1)S(1)}, bf16[256,1152]{1,0:T(8,128)(2,1)S(1)}) custom-call(f32[2]{0:T(128)S(1)} %pad_maximum_fusion.2.scalars, bf16[640,1152]{1,0:T(8,128)(2,1)S(1)} %constant_dynamic-update-slice_fusion.7.img, ...), custom_call_target="tpu_custom_call" | custom-call | flops 1 | bytes 1 | tf_op jit(solution)/shard_map/pallas_call | solution.py:37
  73.6 5.3 %shard_map.64 = (f32[128,1152]{1,0:T(8,128)S(1)}, f32[128,1152]{1,0:T(8,128)S(1)}, f32[128,1152]{1,0:T(8,128)S(1)}, bf16[128,1152]{1,0:T(8,128)(2,1)S(1)}, bf16[...) custom-call(f32[2]{0:T(128)S(1)} %pad_maximum_fusion.2.scalars, ...), custom_call_target="tpu_custom_call", output_to_operand_aliasing={{5}: (4, {})} | custom-call | flops 1 | bytes 1 | tf_op jit(solution)/shard_map/pallas_call | solution.py:37
  79.5 2.6 %collective-permute-start.21 = (bf16[128,1152]{1,0:T(8,128)(2,1)S(1)}, bf16[128,1152]{1,0:T(8,128)(2,1)S(1)}, u32[]{:S(2)}, u32[]{:S(2)}) collective-permute-start(bf16[128,1152]{1,0:T(8,128)(2,1)S(1)} %get-tuple-element.128), channel_id=1, source_target_pairs={{0,64},{32,96},{64,128},{96,160},{128,192},{160,224},{192,0},{224,... | collective-permute-start | bytes 884744 | tf_op jit(solution)/shard_map/ppermute | solution.py:16
  84.1 2.9 %collective-permute-start.20 = (bf16[128,1152]{1,0:T(8,128)(2,1)S(1)}, bf16[128,1152]{1,0:T(8,128)(2,1)S(1)}, u32[]{:S(2)}, u32[]{:S(2)}) collective-permute-start(bf16[128,1152]{1,0:T(8,128)(2,1)S(1)} %get-tuple-element.127), channel_id=1, source_target_pairs={{0,24},{1,25},{2,26},{3,27},{4,28},{5,29},{6,30},{7,31},{8,0},{9,1... | collective-permute-start | bytes 884744 | tf_op jit(solution)/shard_map/ppermute | solution.py:25
  87.0 3.0 %collective-permute-start.22 = (bf16[128,1152]{1,0:T(8,128)(2,1)S(1)}, bf16[128,1152]{1,0:T(8,128)(2,1)S(1)}, u32[]{:S(2)}, u32[]{:S(2)}) collective-permute-start(bf16[128,1152]{1,0:T(8,128)(2,1)S(1)} %get-tuple-element.131), channel_id=1, source_target_pairs={{0,2},{1,3},{2,4},{3,5},{4,6},{5,7},{6,0},{7,1},{8,10},{9,11},{10,... | collective-permute-start | bytes 884744 | tf_op jit(solution)/shard_map/ppermute | solution.py:25
  92.4 3.8 %collective-permute-done.19.refs_2_ = bf16[128,1152]{1,0:T(8,128)(2,1)S(1)} collective-permute-done((bf16[128,1152]{1,0:T(8,128)(2,1)S(1)}, bf16[128,1152]{1,0:T(8,128)(2,1)S(1)}, u32[]{:S(2)}, u32[]{:S(2)}) %collective-permute-start.19) | collective-permute-done | bytes 294944 | tf_op jit(solution)/shard_map/ppermute | solution.py:25
  97.5 3.8 %collective-permute-done.22 = bf16[128,1152]{1,0:T(8,128)(2,1)S(1)} collective-permute-done((bf16[128,1152]{1,0:T(8,128)(2,1)S(1)}, bf16[128,1152]{1,0:T(8,128)(2,1)S(1)}, u32[]{:S(2)}, u32[]{:S(2)}) %collective-permute-start.22) | collective-permute-done | bytes 294944 | tf_op jit(solution)/shard_map/ppermute | solution.py:25
  101.3 3.4 %collective-permute-done.23 = bf16[128,1152]{1,0:T(8,128)(2,1)S(1)} collective-permute-done((bf16[128,1152]{1,0:T(8,128)(2,1)S(1)}, bf16[128,1152]{1,0:T(8,128)(2,1)S(1)}, u32[]{:S(2)}, u32[]{:S(2)}) %collective-permute-start.23) | collective-permute-done | bytes 294944 | tf_op jit(solution)/shard_map/ppermute | solution.py:25
  105.5 3.3 %collective-permute-start.26 = (bf16[128,1152]{1,0:T(8,128)(2,1)S(1)}, bf16[128,1152]{1,0:T(8,128)(2,1)S(1)}, u32[]{:S(2)}, u32[]{:S(2)}) collective-permute-start(bf16[128,1152]{1,0:T(8,128)(2,1)S(1)} %get-tuple-element.150), channel_id=1, source_target_pairs={{0,16},{1,17},{2,18},{3,19},{4,20},{5,21},{6,22},{7,23},{8,24},{9,... | collective-permute-start | bytes 884744 | tf_op jit(solution)/shard_map/ppermute | solution.py:25
  110.8 5.1 %collective-permute-start.30 = (bf16[128,1152]{1,0:T(8,128)(2,1)S(1)}, bf16[128,1152]{1,0:T(8,128)(2,1)S(1)}, u32[]{:S(2)}, u32[]{:S(2)}) collective-permute-start(bf16[128,1152]{1,0:T(8,128)(2,1)S(1)} %get-tuple-element.157), channel_id=1, source_target_pairs={{0,224},{32,0},{64,32},{96,64},{128,96},{160,128},{192,160},{224,1... | collective-permute-start | bytes 884744 | tf_op jit(solution)/shard_map/ppermute | solution.py:16
  116.5 6.3 %collective-permute-done.26.refs_1_ = bf16[128,1152]{1,0:T(8,128)(2,1)S(1)} collective-permute-done((bf16[128,1152]{1,0:T(8,128)(2,1)S(1)}, bf16[128,1152]{1,0:T(8,128)(2,1)S(1)}, u32[]{:S(2)}, u32[]{:S(2)}) %collective-permute-start.26) | collective-permute-done | bytes 294944 | tf_op jit(solution)/shard_map/ppermute | solution.py:25
  122.8 3.9 %collective-permute-done.30.refs_8_ = bf16[128,1152]{1,0:T(8,128)(2,1)S(1)} collective-permute-done((bf16[128,1152]{1,0:T(8,128)(2,1)S(1)}, bf16[128,1152]{1,0:T(8,128)(2,1)S(1)}, u32[]{:S(2)}, u32[]{:S(2)}) %collective-permute-start.30) | collective-permute-done | bytes 294944 | tf_op jit(solution)/shard_map/ppermute | solution.py:16
  126.7 2.4 %shard_map.67 = (f32[128,1152]{1,0:T(8,128)}, f32[128,1152]{1,0:T(8,128)}) custom-call(f32[128,1152]{1,0:T(8,128)S(1)} %copy-done.1, f32[128,1152]{1,0:T(8,128)S(1)} %copy-done.3, f32[128,1152]{1,0:T(8,128)S(1)} %get-tuple-element.108.gu_0, bf16[128,1152]{1,0:T(8,128)(2,1)S(1)} %collective-permute-done.25.refs_0_, ...), custom_call_target="tpu_custom_call" | custom-call | flops 1 | bytes 1 | tf_op jit(solution)/shard_map/pallas_call | solution.py:37
  (68 shorter events, 23.3 us)
Async XLA Ops:
  3.6 10.9 %collective-permute-start.1 = (bf16[128,1152]{1,0:T(8,128)(2,1)S(1)}, bf16[128,1152]{1,0:T(8,128)(2,1)S(1)}, u32[]{:S(2)}, u32[]{:S(2)}) collective-permute-start(bf16[128,1152]{1,0:T(8,128)(2,1)S(1)} %get-tuple-element.89.img_0), channel_id=1, source_target_pairs={{0,192},{32,224},{64,0},{96,32},{128,64},{160,96},{192,128},{224,1... | collective-permute-start | bytes 884744 | tf_op jit(solution)/shard_map/ppermute | solution.py:16
  6.4 18.0 %collective-permute-start.6 = (bf16[128,1152]{1,0:T(8,128)(2,1)S(1)}, bf16[128,1152]{1,0:T(8,128)(2,1)S(1)}, u32[]{:S(2)}, u32[]{:S(2)}) collective-permute-start(bf16[128,1152]{1,0:T(8,128)(2,1)S(1)} %get-tuple-element.82), channel_id=1, source_target_pairs={{0,32},{32,64},{64,96},{96,128},{128,160},{160,192},{192,224},{224... | collective-permute-start | bytes 884744 | tf_op jit(solution)/shard_map/ppermute | solution.py:16
  8.3 17.4 %collective-permute-start = (bf16[128,1152]{1,0:T(8,128)(2,1)S(1)}, bf16[128,1152]{1,0:T(8,128)(2,1)S(1)}, u32[]{:S(2)}, u32[]{:S(2)}) collective-permute-start(bf16[128,1152]{1,0:T(8,128)(2,1)S(1)} %get-tuple-element.82), channel_id=1, source_target_pairs={{0,6},{1,7},{2,0},{3,1},{4,2},{5,3},{6,4},{7,5},{8,14},{9,15},{10,... | collective-permute-start | bytes 884744 | tf_op jit(solution)/shard_map/ppermute | solution.py:25
  9.1 23.7 %collective-permute-start.5 = (bf16[128,1152]{1,0:T(8,128)(2,1)S(1)}, bf16[128,1152]{1,0:T(8,128)(2,1)S(1)}, u32[]{:S(2)}, u32[]{:S(2)}) collective-permute-start(bf16[128,1152]{1,0:T(8,128)(2,1)S(1)} %get-tuple-element.89.img_0), channel_id=1, source_target_pairs={{0,8},{1,9},{2,10},{3,11},{4,12},{5,13},{6,14},{7,15},{8,16},{9,17... | collective-permute-start | bytes 884744 | tf_op jit(solution)/shard_map/ppermute | solution.py:25
  12.3 20.5 %collective-permute-start.4 = (bf16[128,1152]{1,0:T(8,128)(2,1)S(1)}, bf16[128,1152]{1,0:T(8,128)(2,1)S(1)}, u32[]{:S(2)}, u32[]{:S(2)}) collective-permute-start(bf16[128,1152]{1,0:T(8,128)(2,1)S(1)} %get-tuple-element.89.img_0), channel_id=1, source_target_pairs={{0,24},{1,25},{2,26},{3,27},{4,28},{5,29},{6,30},{7,31},{8,0},{9,1... | collective-permute-start | bytes 884744 | tf_op jit(solution)/shard_map/ppermute | solution.py:25
  14.5 18.3 %collective-permute-start.3 = (bf16[128,1152]{1,0:T(8,128)(2,1)S(1)}, bf16[128,1152]{1,0:T(8,128)(2,1)S(1)}, u32[]{:S(2)}, u32[]{:S(2)}) collective-permute-start(bf16[128,1152]{1,0:T(8,128)(2,1)S(1)} %get-tuple-element.82), channel_id=1, source_target_pairs={{0,4},{1,5},{2,6},{3,7},{4,0},{5,1},{6,2},{7,3},{8,12},{9,13},{10,... | collective-permute-start | bytes 884744 | tf_op jit(solution)/shard_map/ppermute | solution.py:25
  33.0 16.8 %collective-permute-start.10 = (bf16[256,1152]{1,0:T(8,128)(2,1)S(1)}, bf16[256,1152]{1,0:T(8,128)(2,1)S(1)}, u32[]{:S(2)}, u32[]{:S(2)}) collective-permute-start(bf16[256,1152]{1,0:T(8,128)(2,1)S(1)} %pad_maximum_fusion.1.img_n), channel_id=1, source_target_pairs={{0,192},{32,224},{64,0},{96,32},{128,64},{160,96},{192,128},{224,1... | collective-permute-start | bytes 1769480 | tf_op jit(solution)/shard_map/ppermute | solution.py:16
  34.0 15.8 %collective-permute-start.9 = (bf16[128,1152]{1,0:T(8,128)(2,1)S(1)}, bf16[128,1152]{1,0:T(8,128)(2,1)S(1)}, u32[]{:S(2)}, u32[]{:S(2)}) collective-permute-start(bf16[128,1152]{1,0:T(8,128)(2,1)S(1)} %collective-permute-done.6), channel_id=1, source_target_pairs={{0,4},{1,5},{2,6},{3,7},{4,0},{5,1},{6,2},{7,3},{8,12},{9,13},{10,... | collective-permute-start | bytes 884744 | tf_op jit(solution)/shard_map/ppermute | solution.py:25
  35.2 14.6 %collective-permute-start.8 = (bf16[128,1152]{1,0:T(8,128)(2,1)S(1)}, bf16[128,1152]{1,0:T(8,128)(2,1)S(1)}, u32[]{:S(2)}, u32[]{:S(2)}) collective-permute-start(bf16[128,1152]{1,0:T(8,128)(2,1)S(1)} %collective-permute-done.6), channel_id=1, source_target_pairs={{0,2},{1,3},{2,4},{3,5},{4,6},{5,7},{6,0},{7,1},{8,10},{9,11},{10,... | collective-permute-start | bytes 884744 | tf_op jit(solution)/shard_map/ppermute | solution.py:25
  37.4 12.4 %collective-permute-start.7 = (bf16[128,1152]{1,0:T(8,128)(2,1)S(1)}, bf16[128,1152]{1,0:T(8,128)(2,1)S(1)}, u32[]{:S(2)}, u32[]{:S(2)}) collective-permute-start(bf16[128,1152]{1,0:T(8,128)(2,1)S(1)} %collective-permute-done.6), channel_id=1, source_target_pairs={{0,6},{1,7},{2,0},{3,1},{4,2},{5,3},{6,4},{7,5},{8,14},{9,15},{10,... | collective-permute-start | bytes 884744 | tf_op jit(solution)/shard_map/ppermute | solution.py:25
  37.4 12.4 %collective-permute-start.11 = (bf16[128,1152]{1,0:T(8,128)(2,1)S(1)}, bf16[128,1152]{1,0:T(8,128)(2,1)S(1)}, u32[]{:S(2)}, u32[]{:S(2)}) collective-permute-start(bf16[128,1152]{1,0:T(8,128)(2,1)S(1)} %get-tuple-element.89.img_0), channel_id=1, source_target_pairs={{0,16},{1,17},{2,18},{3,19},{4,20},{5,21},{6,22},{7,23},{8,24},{9,... | collective-permute-start | bytes 884744 | tf_op jit(solution)/shard_map/ppermute | solution.py:25
  50.0 15.3 %collective-permute-start.12 = (bf16[128,1152]{1,0:T(8,128)(2,1)S(1)}, bf16[128,1152]{1,0:T(8,128)(2,1)S(1)}, u32[]{:S(2)}, u32[]{:S(2)}) collective-permute-start(bf16[128,1152]{1,0:T(8,128)(2,1)S(1)} %collective-permute-done.11), channel_id=1, source_target_pairs={{0,192},{32,224},{64,0},{96,32},{128,64},{160,96},{192,128},{224,1... | collective-permute-start | bytes 884744 | tf_op jit(solution)/shard_map/ppermute | solution.py:16
  60.7 18.4 %collective-permute-start.14 = (bf16[272,1152]{1,0:T(8,128)(2,1)S(1)}, bf16[272,1152]{1,0:T(8,128)(2,1)S(1)}, u32[]{:S(2)}, u32[]{:S(2)}) collective-permute-start(bf16[272,1152]{1,0:T(8,128)(2,1)S(1)} %get-tuple-element.111), channel_id=1, source_target_pairs={{0,64},{32,96},{64,128},{96,160},{128,192},{160,224},{192,0},{224,... | collective-permute-start | bytes 1880072 | tf_op jit(solution)/shard_map/ppermute | solution.py:16
  82.1 14.1 %collective-permute-start.19 = (bf16[128,1152]{1,0:T(8,128)(2,1)S(1)}, bf16[128,1152]{1,0:T(8,128)(2,1)S(1)}, u32[]{:S(2)}, u32[]{:S(2)}) collective-permute-start(bf16[128,1152]{1,0:T(8,128)(2,1)S(1)} %get-tuple-element.126), channel_id=1, source_target_pairs={{0,8},{1,9},{2,10},{3,11},{4,12},{5,13},{6,14},{7,15},{8,16},{9,17... | collective-permute-start | bytes 884744 | tf_op jit(solution)/shard_map/ppermute | solution.py:25
  84.1 13.3 %collective-permute-start.20 = (bf16[128,1152]{1,0:T(8,128)(2,1)S(1)}, bf16[128,1152]{1,0:T(8,128)(2,1)S(1)}, u32[]{:S(2)}, u32[]{:S(2)}) collective-permute-start(bf16[128,1152]{1,0:T(8,128)(2,1)S(1)} %get-tuple-element.127), channel_id=1, source_target_pairs={{0,24},{1,25},{2,26},{3,27},{4,28},{5,29},{6,30},{7,31},{8,0},{9,1... | collective-permute-start | bytes 884744 | tf_op jit(solution)/shard_map/ppermute | solution.py:25
  87.0 14.3 %collective-permute-start.22 = (bf16[128,1152]{1,0:T(8,128)(2,1)S(1)}, bf16[128,1152]{1,0:T(8,128)(2,1)S(1)}, u32[]{:S(2)}, u32[]{:S(2)}) collective-permute-start(bf16[128,1152]{1,0:T(8,128)(2,1)S(1)} %get-tuple-element.131), channel_id=1, source_target_pairs={{0,2},{1,3},{2,4},{3,5},{4,6},{5,7},{6,0},{7,1},{8,10},{9,11},{10,... | collective-permute-start | bytes 884744 | tf_op jit(solution)/shard_map/ppermute | solution.py:25
  90.0 14.7 %collective-permute-start.23 = (bf16[128,1152]{1,0:T(8,128)(2,1)S(1)}, bf16[128,1152]{1,0:T(8,128)(2,1)S(1)}, u32[]{:S(2)}, u32[]{:S(2)}) collective-permute-start(bf16[128,1152]{1,0:T(8,128)(2,1)S(1)} %get-tuple-element.132), channel_id=1, source_target_pairs={{0,6},{1,7},{2,0},{3,1},{4,2},{5,3},{6,4},{7,5},{8,14},{9,15},{10,... | collective-permute-start | bytes 884744 | tf_op jit(solution)/shard_map/ppermute | solution.py:25
  90.0 14.7 %collective-permute-start.24 = (bf16[128,1152]{1,0:T(8,128)(2,1)S(1)}, bf16[128,1152]{1,0:T(8,128)(2,1)S(1)}, u32[]{:S(2)}, u32[]{:S(2)}) collective-permute-start(bf16[128,1152]{1,0:T(8,128)(2,1)S(1)} %get-tuple-element.133), channel_id=1, source_target_pairs={{0,4},{1,5},{2,6},{3,7},{4,0},{5,1},{6,2},{7,3},{8,12},{9,13},{10,... | collective-permute-start | bytes 884744 | tf_op jit(solution)/shard_map/ppermute | solution.py:25
  104.9 11.0 %collective-permute-start.25 = (bf16[128,1152]{1,0:T(8,128)(2,1)S(1)}, bf16[128,1152]{1,0:T(8,128)(2,1)S(1)}, u32[]{:S(2)}, u32[]{:S(2)}) collective-permute-start(bf16[128,1152]{1,0:T(8,128)(2,1)S(1)} %get-tuple-element.147), channel_id=1, source_target_pairs={{0,64},{32,96},{64,128},{96,160},{128,192},{160,224},{192,0},{224,... | collective-permute-start | bytes 884744 | tf_op jit(solution)/shard_map/ppermute | solution.py:16
  105.5 17.2 %collective-permute-start.26 = (bf16[128,1152]{1,0:T(8,128)(2,1)S(1)}, bf16[128,1152]{1,0:T(8,128)(2,1)S(1)}, u32[]{:S(2)}, u32[]{:S(2)}) collective-permute-start(bf16[128,1152]{1,0:T(8,128)(2,1)S(1)} %get-tuple-element.150), channel_id=1, source_target_pairs={{0,16},{1,17},{2,18},{3,19},{4,20},{5,21},{6,22},{7,23},{8,24},{9,... | collective-permute-start | bytes 884744 | tf_op jit(solution)/shard_map/ppermute | solution.py:25
  108.8 14.0 %collective-permute-start.27 = (bf16[128,1152]{1,0:T(8,128)(2,1)S(1)}, bf16[128,1152]{1,0:T(8,128)(2,1)S(1)}, u32[]{:S(2)}, u32[]{:S(2)}) collective-permute-start(bf16[128,1152]{1,0:T(8,128)(2,1)S(1)} %get-tuple-element.154), channel_id=1, source_target_pairs={{0,2},{1,3},{2,4},{3,5},{4,6},{5,7},{6,0},{7,1},{8,10},{9,11},{10,... | collective-permute-start | bytes 884744 | tf_op jit(solution)/shard_map/ppermute | solution.py:25
  109.1 13.7 %collective-permute-start.28 = (bf16[128,1152]{1,0:T(8,128)(2,1)S(1)}, bf16[128,1152]{1,0:T(8,128)(2,1)S(1)}, u32[]{:S(2)}, u32[]{:S(2)}) collective-permute-start(bf16[128,1152]{1,0:T(8,128)(2,1)S(1)} %get-tuple-element.155), channel_id=1, source_target_pairs={{0,6},{1,7},{2,0},{3,1},{4,2},{5,3},{6,4},{7,5},{8,14},{9,15},{10,... | collective-permute-start | bytes 884744 | tf_op jit(solution)/shard_map/ppermute | solution.py:25
  110.8 15.8 %collective-permute-start.30 = (bf16[128,1152]{1,0:T(8,128)(2,1)S(1)}, bf16[128,1152]{1,0:T(8,128)(2,1)S(1)}, u32[]{:S(2)}, u32[]{:S(2)}) collective-permute-start(bf16[128,1152]{1,0:T(8,128)(2,1)S(1)} %get-tuple-element.157), channel_id=1, source_target_pairs={{0,224},{32,0},{64,32},{96,64},{128,96},{160,128},{192,160},{224,1... | collective-permute-start | bytes 884744 | tf_op jit(solution)/shard_map/ppermute | solution.py:16
  115.9 10.8 %collective-permute-start.29 = (bf16[128,1152]{1,0:T(8,128)(2,1)S(1)}, bf16[128,1152]{1,0:T(8,128)(2,1)S(1)}, u32[]{:S(2)}, u32[]{:S(2)}) collective-permute-start(bf16[128,1152]{1,0:T(8,128)(2,1)S(1)} %get-tuple-element.156), channel_id=1, source_target_pairs={{0,4},{1,5},{2,6},{3,7},{4,0},{5,1},{6,2},{7,3},{8,12},{9,13},{10,... | collective-permute-start | bytes 884744 | tf_op jit(solution)/shard_map/ppermute | solution.py:25
  (11 other events, 120.1 us)

commit v6 on v5

v6 whole, which is shorter than its diff:
```python
import functools

import jax
import jax.numpy as jnp
from jax import lax
from jax.experimental import pallas as pl
from jax.experimental.pallas import tpu as pltpu
from jax.sharding import PartitionSpec as P

X, ZL, ZH, Y, CORE = 4, 2, 4, 4, 2
GROUPS, DEVS = X * ZL, ZH * Y * CORE
F32, LOW = jnp.float32, jnp.bfloat16


def to_group(block, step):
    return lax.ppermute(block, "grp", [(i, (i + step) % GROUPS) for i in range(GROUPS)])


def to_dev(block, zh=0, y=0, core=0):
    route = []
    for i in range(DEVS):
        a, b, c = i // (Y * CORE), i // CORE % Y, i % CORE
        target = ((a + zh) % ZH * Y + (b + y) % Y) * CORE + (c + core) % CORE
        route.append((i, target))
    return lax.ppermute(block, "dev", route)


def fence(*arrays):
    return lax.optimization_barrier(arrays)


VMEM = pl.BlockSpec(memory_space=pltpu.VMEM)


def whole(kernel, outs, *operands, scalars=False, aliases=None, scratch=(), place=pltpu.VMEM, room=28):
    spec = pl.BlockSpec(memory_space=place)
    first = [pl.BlockSpec(memory_space=pltpu.SMEM)] if scalars else [spec]
    return pl.pallas_call(
        kernel,
        in_specs=first + [spec] * (len(operands) - 1),
        out_specs=[VMEM] * len(outs),
        out_shape=[jax.ShapeDtypeStruct(shape, kind) for shape, kind in outs],
        input_output_aliases=aliases or {},
        scratch_shapes=list(scratch),
        compiler_params=pltpu.CompilerParams(vmem_limit_bytes=room * 1024 * 1024),
        cost_estimate=pl.CostEstimate(flops=1, bytes_accessed=1, transcendentals=0),
    )(*operands)


def inverse_of(values):
    return lax.rsqrt(jnp.sum(values * values, axis=1, keepdims=True) + 1e-06)


def each(rows, step):
    def over(body):
        @pl.loop(0, rows // step)
        def _(n):
            body(pl.ds(pl.multiple_of(n * step, step), step))

    return over


def unit_kernel(txt, img, txt_low, img_low, txt_here, img_here, arrived):
    copies = []
    for n, (there, here) in enumerate(((txt, txt_here), (img, img_here))):
        copies.append(pltpu.make_async_copy(there, here, arrived.at[n]))
        copies[-1].start()
    for copy, values, low in ((copies[0], txt_here, txt_low), (copies[1], img_here, img_low)):
        copy.wait()

        @each(values.shape[0], 64)
        def _(span):
            low[span] = (values[span] * inverse_of(values[span])).astype(LOW)


def end_kernel(values, own, *refs):
    *others, grad = refs

    @each(values.shape[0], 64)
    def _(span):
        sums = own[span]
        for other in others:
            sums = sums + other[span].astype(F32)
        inverse = inverse_of(values[span])
        unit = values[span] * inverse
        grad[span] = inverse * (sums - unit * jnp.sum(unit * sums, axis=1, keepdims=True))


def join_kernel(txt_0, txt_up, txt_down, txt_2, img_0, img_up, img_down, own_c, img_n, img_again):
    places = (
        *((own_c, 128 * n, part) for n, part in enumerate((txt_0, txt_up, txt_down, txt_2))),
        *((img_n, 128 * n, part) for n, part in enumerate((img_up, img_down))),
        (img_again, 0, img_0),
    )
    for out, first, part in places:

        @each(128, 64)
        def _(span):
            out[pl.ds(pl.multiple_of(first + span.start, 64), 64)] = part[span]


def text_sums_kernel(place, mine, got_0, got_1, own, up, down, far):
    for n, out in enumerate((own, up, down, far)):

        @each(128, 32)
        def _(span):
            there = pl.ds(pl.multiple_of(place + n * 128 + span.start, 32), 32)
            inside = pl.ds(pl.multiple_of(n % 2 * 128 + span.start, 32), 32)
            got = (got_0, got_1)[n // 2]
            out[span] = (mine[there] + got[inside].astype(F32)).astype(out.dtype)


def products(scalars, img, txt, mask=None):
    half_temp, half_bias = scalars[0], scalars[1]
    logits = lax.dot_general(img, txt, (((1,), (1,)), ((), ())), preferred_element_type=F32)
    slopes = half_temp * jnp.tanh(half_temp * logits + half_bias) + half_temp
    if mask is not None:
        slopes = slopes - jnp.where(mask, 2.0 * half_temp, 0.0)
    coef = slopes.astype(LOW)
    gu = jnp.dot(coef, txt, preferred_element_type=F32)
    return gu, lax.dot_general(coef, img, (((0,), (0,)), ((), ())), preferred_element_type=F32)


def first_kernel(scalars, img_0, img_n, ahead_0, txt, gu, gv, img):
    for part, first in ((img_0, 0), (img_n, 128), (ahead_0, 384)):

        @each(part.shape[0], 32)
        def _(span):
            img[pl.ds(pl.multiple_of(first + span.start, 32), 32)] = part[span]

    shape = gu.shape[0], txt.shape[0]
    row, col = lax.broadcasted_iota(jnp.int32, shape, 0), lax.broadcasted_iota(jnp.int32, shape, 1)
    mask = jnp.logical_and(row == col, row < 128)
    gu[...], gv[: shape[1]] = products(scalars, img[0 : shape[0]], txt[...], mask)

    @each(shape[1], 32)
    def _(span):
        there = pl.ds(pl.multiple_of(shape[1] + span.start, 32), 32)
        gv[there] = jnp.zeros((32, gv.shape[1]), F32)


def both_halves(txt):
    size = txt.shape[0] // 2

    def over(body):
        @pl.loop(0, 2)
        def _(n):
            body(n, pl.ds(pl.multiple_of(n * size, size), size))

    return over


def second_kernel(scalars, img, txt, gv_in, gu, gv):
    @each(gu.shape[0], 32)
    def _(span):
        gu[span] = jnp.zeros((32, gu.shape[1]), F32)

    @both_halves(txt)
    def _(n, here):
        part, term = products(scalars, img[...], txt[here])
        gu[...] += part
        gv[here] = term + gv_in[here]


def third_kernel(scalars, img, txt, gu_in, gu_n, gv, gu):
    @each(gu.shape[0], 32)
    def _(span):
        gu[span] = gu_in[span]

    @both_halves(txt)
    def _(n, here):
        part, gv[here] = products(scalars, img[...], txt[here])
        gu[...] += part

    gu_n[:256] = gu[...].astype(LOW)
    gu_n[256:] = jnp.zeros((16, gu_n.shape[1]), LOW)


def fourth_kernel(scalars, img, txt, gu_in, gv_in, gu, piece_0, piece_1, piece_2, piece_3, gv):
    past = gu_in.shape[0]

    @each(past, 32)
    def _(span):
        gu[span] = gu_in[span]

    @each(gu.shape[0] - past, 32)
    def _(span):
        there = pl.ds(pl.multiple_of(past + span.start, 32), 32)
        gu[there] = jnp.zeros((32, gu.shape[1]), F32)

    @both_halves(txt)
    def _(n, here):
        part, term = products(scalars, img[...], txt[here])
        gu[...] += part
        gv[...] = term + gv_in[here]
        for place, outs in enumerate(((piece_0, piece_1), (piece_2, piece_3))):

            @pl.when(n == place)
            def _():
                for m, out in enumerate(outs):

                    @each(256, 32)
                    def _(span):
                        there = pl.ds(pl.multiple_of(m * 256 + span.start, 32), 32)
                        out[span] = gv[there].astype(LOW)


def fifth_kernel(scalars, img, txt, gu_in, gv_in, gu_0, gu_up, gu_down, gu_2, au, gv, gu):
    size, past = txt.shape[0] // 2, img.shape[0] - 256
    part, term = products(scalars, img[...], txt[size:])
    gu[...] = gu_in[...] + part
    gv[size:] = term + gv_in[size:]
    part, term = products(scalars, img[past:], txt[0:size])
    gu[past:] += part
    gv[:size] = term + gv_in[:size]
    places = (gu_0, 0), (gu_up, 0), (gu_down, 0), (au, 0), (gu_2, 0), (au, 128)
    for n, (out, first) in enumerate(places):

        @each(128, 32)
        def _(span):
            rows = gu[pl.ds(pl.multiple_of(n * 128 + span.start, 32), 32)]
            out[pl.ds(pl.multiple_of(first + span.start, 32), 32)] = rows.astype(out.dtype)


def local(image_emb, text_emb, temp, bias):
    rows = image_emb.shape
    width = rows[1]
    pair, half, wide = (256, width), (512, width), (1024, width)
    here = [pltpu.VMEM(rows, F32)] * 2 + [pltpu.SemaphoreType.DMA((2,))]
    txt_0, img_0 = whole(unit_kernel, [(rows, LOW)] * 2, text_emb, image_emb, place=pltpu.HBM, scratch=here, room=62)
    scalars = jnp.stack([0.5 * temp, 0.5 * bias])

    txt_up = to_dev(txt_0, y=-1)
    ahead_0 = to_group(img_0, -2)
    img_up = to_dev(img_0, zh=-1)
    img_down = to_dev(img_0, zh=1)
    behind_0 = to_group(txt_0, 1)
    ahead_0, txt_later = fence(ahead_0, txt_0)
    txt_down = to_dev(txt_later, y=1)
    txt_2 = to_dev(txt_later, y=2)
    txt_up, txt_down, txt_2, behind_0, img_up, img_down = fence(
        txt_up, txt_down, txt_2, behind_0, img_up, img_down
    )
    own_c, img_n, img_again = whole(
        join_kernel,
        [(half, LOW), (pair, LOW), (rows, LOW)],
        *(txt_0, txt_up, txt_down, txt_2, img_0, img_up, img_down),
    )
    own_c, img_n, behind_0, img_again = fence(own_c, img_n, behind_0, img_again)
    behind_up = to_dev(behind_0, y=-1)
    behind_down = to_dev(behind_0, y=1)
    behind_2 = to_dev(behind_0, y=2)
    ahead_n = to_group(img_n, -2)
    img_2 = to_dev(img_again, zh=2)
    gu_first, sums_c, images = whole(
        first_kernel,
        [(half, F32), (wide, F32), ((768, width), LOW)],
        *(scalars, img_again, img_n, ahead_0, own_c),
        scalars=True,
    )
    behind_up, behind_down, behind_2, ahead_n, img_2, gu_first, sums_c = fence(
        behind_up, behind_down, behind_2, ahead_n, img_2, gu_first, sums_c
    )
    txt_c = jnp.concatenate([own_c, behind_0, behind_up, behind_down, behind_2], axis=0)
    txt_s = to_dev(txt_c, core=1)
    ahead_2 = to_group(img_2, -2)
    gu_n, sums_c = whole(
        second_kernel,
        [(pair, F32), (wide, F32)],
        *(scalars, ahead_n, txt_c, sums_c),
        scalars=True,
        aliases={3: 1},
    )
    au_n, others = whole(
        third_kernel,
        [((272, width), LOW), (wide, F32)],
        *(scalars, ahead_n, txt_s, gu_n),
        scalars=True,
        scratch=[pltpu.VMEM(pair, F32)],
    )
    back_n = to_group(au_n, 2)
    images = lax.dynamic_update_slice(images, jnp.concatenate([img_2, ahead_2], axis=0), (512, 0))
    gu_all, *pieces = whole(
        fourth_kernel,
        [(images.shape, F32)] + [(pair, LOW)] * 4,
        *(scalars, images, txt_s, gu_first, others),
        scalars=True,
        scratch=[pltpu.VMEM(half, F32)],
    )
    got = [to_dev(piece, core=1) for piece in pieces]
    gu_0, gu_up, gu_down, gu_2, au, sums_c = whole(
        fifth_kernel,
        [(rows, F32)] * 4 + [(pair, LOW), (wide, F32)],
        *(scalars, images, txt_c, gu_all, sums_c),
        scalars=True,
        aliases={4: 5},
        scratch=[pltpu.VMEM(images.shape, F32)],
    )
    back_n, *got, au, sums_c = fence(back_n, *got, au, sums_c)
    sums = [(rows, F32)] + [(rows, LOW)] * 3
    sh_sum, sh_up, sh_down, sh_far = whole(
        functools.partial(text_sums_kernel, 512), sums, sums_c, *got[2:]
    )
    sum_up = (gu_up + back_n[:128].astype(F32)).astype(LOW)
    sum_down = (gu_down + back_n[128:256].astype(F32)).astype(LOW)
    sum_up, sum_down, sh_up, sh_down, au = fence(sum_up, sum_down, sh_up, sh_down, au)
    sh_up = to_dev(sh_up, y=1)
    sum_up = to_dev(sum_up, zh=1)
    sum_down = to_dev(sum_down, zh=-1)
    sh_down = to_dev(sh_down, y=-1)
    back = to_group(au, 2)
    sh_up, sh_far = fence(sh_up, sh_far)
    sh_far = to_dev(sh_far, y=2)
    own_sum, own_up, own_down, own_far = whole(
        functools.partial(text_sums_kernel, 0), sums, sums_c, *got[:2]
    )
    sh_up, sum_up, sum_down, sh_down, back, sh_far, own_up, own_down, own_far = fence(
        sh_up, sum_up, sum_down, sh_down, back, sh_far, own_up, own_down, own_far
    )
    back_0, sum_2 = back[:128], (gu_2 + back[128:].astype(F32)).astype(LOW)
    behind = (sh_sum + sh_up.astype(F32) + sh_down.astype(F32) + sh_far.astype(F32)).astype(LOW)
    sum_2, behind, own_up, own_down, own_far = fence(sum_2, behind, own_up, own_down, own_far)
    sum_2 = to_dev(sum_2, zh=2)
    behind = to_group(behind, -1)
    own_up = to_dev(own_up, y=1)
    own_down = to_dev(own_down, y=-1)
    own_far = to_dev(own_far, y=2)
    (grad_image,) = whole(end_kernel, [(rows, F32)], image_emb, gu_0, sum_2, sum_up, sum_down, back_0)
    (grad_text,) = whole(end_kernel, [(rows, F32)], text_emb, own_sum, behind, own_up, own_down, own_far)
    return grad_image, grad_text


def solution(mesh):
    return jax.shard_map(
        local,
        mesh=mesh,
        in_specs=(P(("grp", "dev"), None), P(("grp", "dev"), None), P(), P()),
        out_specs=(P(("grp", "dev"), None), P(("grp", "dev"), None)),
        check_vma=False,
    )
```

time: 131 us -> 129 us (0.985); the launches traced: 129 us -> 128 us
  starting transfers between devices: 52.8 us -> 48.3 us
  waiting for transfers between devices: 42.1 us -> 45.5 us
    ppermute x8 -> x7, starting transfers between devices: 19.5 us -> 14.4 us  [to_group(): lax.ppermute(block, 'grp', [(i, (i + step) % GROUPS) for i in range(GROUP...]
    ppermute x23, waiting for transfers between devices: 29.1 us -> 32.3 us  [to_dev(): return lax.ppermute(block, 'dev', route)]
    pallas_call x9 -> x11, Pallas kernels: 29 us -> 29.8 us  [whole(): pl.pallas_call(kernel, in_specs=first + [spec] * (len(operands) - 1), out...]
    ppermute x8 -> x7, waiting for transfers between devices: 13 us -> 13.2 us  [to_group(): lax.ppermute(block, 'grp', [(i, (i + step) % GROUPS) for i in range(GROUP...]
  transfers between devices with their start and end apart: 31 -> 30, of which waited for: 10 -> 10; matrix products, arithmetic and copies ran while one was open for 0% -> 0% of each run, Pallas kernels for 20% -> 20%
where the time goes in v6:
time: 129 us; the launch traced here: 128 us
  starting transfers between devices  48.3 us (37%)
  waiting for transfers between devices  45.5 us (35%)
  Pallas kernels  29.8 us (23%)
  between operations  2.18 us (2%)
  local copies, waits for them, and re-layouts  2.17 us (2%)
    ppermute x23, starting transfers between devices, to_dev(): return lax.ppermute(block, 'dev', route)  33.9 us
    ppermute x23, waiting for transfers between devices, to_dev(): return lax.ppermute(block, 'dev', route)  32.3 us
    pallas_call x11, Pallas kernels, whole(): pl.pallas_call(kernel, in_specs=first + [spec] * (len(operands) - 1), out...  29.8 us
    ppermute x7, starting transfers between devices, to_group(): lax.ppermute(block, 'grp', [(i, (i + step) % GROUPS) for i in range(GROUP...  14.4 us
    ppermute x7, waiting for transfers between devices, to_group(): lax.ppermute(block, 'grp', [(i, (i + step) % GROUPS) for i in range(GROUP...  13.2 us
  transfers between devices with their start and end apart: 30, of which 10 were waited for; matrix products, arithmetic and copies ran while one was open for 0% of the time, Pallas kernels for 20%

profile of v6, /device:TPU:24, one launch (start us, length us, event | category | flops | bytes accessed | tf_op | source)
XLA Modules:
  0.0 128.4 jit_solution(12182047581395238406)
XLA Ops:
  0.6 2.3 %shard_map.59 = (bf16[128,1152]{1,0:T(8,128)(2,1)}, bf16[128,1152]{1,0:T(8,128)(2,1)}) custom-call(f32[128,1152]{1,0:T(8,128)} %values.3, f32[128,1152]{1,0:T(8,128)} %values.2), custom_call_target="tpu_custom_call" | custom-call | flops 1 | bytes 1 | tf_op jit(solution)/shard_map/pallas_call | solution.py:38
  2.9 2.8 %collective-permute-start.1 = (bf16[128,1152]{1,0:T(8,128)(2,1)}, bf16[128,1152]{1,0:T(8,128)(2,1)S(1)}, u32[]{:S(2)}, u32[]{:S(2)}) collective-permute-start(bf16[128,1152]{1,0:T(8,128)(2,1)} %get-tuple-element.81.img_0), channel_id=1, source_target_pairs={{0,192},{32,224},{64,0},{96,32},{128,64},{160,96},{192,128},{224,1... | collective-permute-start | bytes 884744 | tf_op jit(solution)/shard_map/ppermute | solution.py:16
  8.4 3.3 %collective-permute-start.6 = (bf16[128,1152]{1,0:T(8,128)(2,1)}, bf16[128,1152]{1,0:T(8,128)(2,1)S(1)}, u32[]{:S(2)}, u32[]{:S(2)}) collective-permute-start(bf16[128,1152]{1,0:T(8,128)(2,1)} %get-tuple-element.81.img_0), channel_id=1, source_target_pairs={{0,8},{1,9},{2,10},{3,11},{4,12},{5,13},{6,14},{7,15},{8,16},{9,17... | collective-permute-start | bytes 884744 | tf_op jit(solution)/shard_map/ppermute | solution.py:25
  11.7 2.1 %collective-permute-start.5 = (bf16[128,1152]{1,0:T(8,128)(2,1)}, bf16[128,1152]{1,0:T(8,128)(2,1)S(1)}, u32[]{:S(2)}, u32[]{:S(2)}) collective-permute-start(bf16[128,1152]{1,0:T(8,128)(2,1)} %get-tuple-element.81.img_0), channel_id=1, source_target_pairs={{0,24},{1,25},{2,26},{3,27},{4,28},{5,29},{6,30},{7,31},{8,0},{9,1... | collective-permute-start | bytes 884744 | tf_op jit(solution)/shard_map/ppermute | solution.py:25
  14.7 9.1 %collective-permute-done.4 = bf16[128,1152]{1,0:T(8,128)(2,1)S(1)} collective-permute-done((bf16[128,1152]{1,0:T(8,128)(2,1)}, bf16[128,1152]{1,0:T(8,128)(2,1)S(1)}, u32[]{:S(2)}, u32[]{:S(2)}) %collective-permute-start.4) | collective-permute-done | bytes 294944 | tf_op jit(solution)/shard_map/ppermute | solution.py:16
  25.2 7.2 %collective-permute-done.6.img_down = bf16[128,1152]{1,0:T(8,128)(2,1)S(1)} collective-permute-done((bf16[128,1152]{1,0:T(8,128)(2,1)}, bf16[128,1152]{1,0:T(8,128)(2,1)S(1)}, u32[]{:S(2)}, u32[]{:S(2)}) %collective-permute-start.6) | collective-permute-done | bytes 294944 | tf_op jit(solution)/shard_map/ppermute | solution.py:25
  36.7 2.2 %collective-permute-start.8 = (bf16[128,1152]{1,0:T(8,128)(2,1)S(1)}, bf16[128,1152]{1,0:T(8,128)(2,1)S(1)}, u32[]{:S(2)}, u32[]{:S(2)}) collective-permute-start(bf16[128,1152]{1,0:T(8,128)(2,1)S(1)} %collective-permute-done.4), channel_id=1, source_target_pairs={{0,2},{1,3},{2,4},{3,5},{4,6},{5,7},{6,0},{7,1},{8,10},{9,11},{10,... | collective-permute-start | bytes 884744 | tf_op jit(solution)/shard_map/ppermute | solution.py:25
  38.9 5.8 %collective-permute-start.11 = (bf16[128,1152]{1,0:T(8,128)(2,1)S(1)}, bf16[128,1152]{1,0:T(8,128)(2,1)S(1)}, u32[]{:S(2)}, u32[]{:S(2)}) collective-permute-start(bf16[128,1152]{1,0:T(8,128)(2,1)S(1)} %get-tuple-element.92.img_0), channel_id=1, source_target_pairs={{0,16},{1,17},{2,18},{3,19},{4,20},{5,21},{6,22},{7,23},{8,24},{9,... | collective-permute-start | bytes 884744 | tf_op jit(solution)/shard_map/ppermute | solution.py:25
  44.8 3.2 %shard_map.61 = (f32[512,1152]{1,0:T(8,128)S(1)}, f32[1024,1152]{1,0:T(8,128)S(1)}, bf16[768,1152]{1,0:T(8,128)(2,1)S(1)}) custom-call(f32[2]{0:T(128)S(1)} %pad_maximum_fusion.scalars, bf16[128,1152]{1,0:T(8,128)(2,1)S(1)} %get-tuple-element.92.img_0, bf16[256,1152]{1,0:T(8,128)(2,1)S(1)} %get-tuple-element.93.img_n, ...), custom_call_target="tpu_custom_call" | custom-call | flops 1 | bytes 1 | tf_op jit(solution)/shard_map/pallas_call | solution.py:38
  48.1 5.9 %collective-permute-done.11 = bf16[128,1152]{1,0:T(8,128)(2,1)S(1)} collective-permute-done((bf16[128,1152]{1,0:T(8,128)(2,1)S(1)}, bf16[128,1152]{1,0:T(8,128)(2,1)S(1)}, u32[]{:S(2)}, u32[]{:S(2)}) %collective-permute-start.11) | collective-permute-done | bytes 294944 | tf_op jit(solution)/shard_map/ppermute | solution.py:25
  54.5 3.7 %shard_map.62 = (f32[256,1152]{1,0:T(8,128)S(1)}, f32[1024,1152]{1,0:T(8,128)S(1)}) custom-call(f32[2]{0:T(128)S(1)} %pad_maximum_fusion.scalars, bf16[256,1152]{1,0:T(8,128)(2,1)S(1)} %collective-permute-done.10.img, bf16[1024,1152]{1,0:T(8,128)(2,1)S(1)} %constant_dynamic-update-slice_fusion.txt, ...), custom_call_target="tpu_custom_call", output_to_operand_aliasing={{1}: (3, {})} | custom-call | flops 1 | bytes 1 | tf_op jit(solution)/shard_map/pallas_call | solution.py:38
  58.7 3.4 %shard_map.63 = (bf16[272,1152]{1,0:T(8,128)(2,1)S(1)}, f32[1024,1152]{1,0:T(8,128)S(1)}) custom-call(f32[2]{0:T(128)S(1)} %pad_maximum_fusion.scalars, bf16[256,1152]{1,0:T(8,128)(2,1)S(1)} %collective-permute-done.10.img, bf16[1024,1152]{1,0:T(8,128)(2,1)S(1)} %collective-permute-done.13.txt, f32[256,1152]{1,0:T(8,128)S(1)} %get-tuple-element.107.gu_in), custom_call_target="tpu_custom_call" | custom-call | flops 1 | bytes 1 | tf_op jit(solution)/shard_map/pallas_call | solution.py:38
  62.1 2.5 %collective-permute-start.14 = (bf16[272,1152]{1,0:T(8,128)(2,1)S(1)}, bf16[272,1152]{1,0:T(8,128)(2,1)S(1)}, u32[]{:S(2)}, u32[]{:S(2)}) collective-permute-start(bf16[272,1152]{1,0:T(8,128)(2,1)S(1)} %get-tuple-element.114), channel_id=1, source_target_pairs={{0,64},{32,96},{64,128},{96,160},{128,192},{160,224},{192,0},{224,... | collective-permute-start | bytes 1880072 | tf_op jit(solution)/shard_map/ppermute | solution.py:16
  64.7 8.2 %shard_map.64 = (f32[768,1152]{1,0:T(8,128)S(1)}, bf16[256,1152]{1,0:T(8,128)(2,1)S(1)}, bf16[256,1152]{1,0:T(8,128)(2,1)S(1)}, bf16[256,1152]{1,0:T(8,128)(2,1)S(1)}, bf16[256,1152]{1,0:T(8,128)(2,1)S(1)}) custom-call(f32[2]{0:T(128)S(1)} %pad_maximum_fusion.scalars, bf16[768,1152]{1,0:T(8,128)(2,1)S(1)} %maximum_dynamic-update-slice_fusion.img, ...), custom_call_target="tpu_custom_call" | custom-call | flops 1 | bytes 1 | tf_op jit(solution)/shard_map/pallas_call | solution.py:38
  74.0 5.8 %shard_map.65 = (f32[128,1152]{1,0:T(8,128)S(1)}, f32[128,1152]{1,0:T(8,128)S(1)}, f32[128,1152]{1,0:T(8,128)S(1)}, f32[128,1152]{1,0:T(8,128)S(1)}, bf16[256,11...) custom-call(f32[2]{0:T(128)S(1)} %pad_maximum_fusion.scalars, ...), custom_call_target="tpu_custom_call", output_to_operand_aliasing={{5}: (4, {})} | custom-call | flops 1 | bytes 1 | tf_op jit(solution)/shard_map/pallas_call | solution.py:38
  80.3 2.9 %collective-permute-start.19 = (bf16[128,1152]{1,0:T(8,128)(2,1)S(1)}, bf16[128,1152]{1,0:T(8,128)(2,1)S(1)}, u32[]{:S(2)}, u32[]{:S(2)}) collective-permute-start(bf16[128,1152]{1,0:T(8,128)(2,1)S(1)} %get-tuple-element.129), channel_id=1, source_target_pairs={{0,2},{1,3},{2,4},{3,5},{4,6},{5,7},{6,0},{7,1},{8,10},{9,11},{10,... | collective-permute-start | bytes 884744 | tf_op jit(solution)/shard_map/ppermute | solution.py:25
  86.2 2.8 %collective-permute-start.21 = (bf16[128,1152]{1,0:T(8,128)(2,1)S(1)}, bf16[128,1152]{1,0:T(8,128)(2,1)S(1)}, u32[]{:S(2)}, u32[]{:S(2)}) collective-permute-start(bf16[128,1152]{1,0:T(8,128)(2,1)S(1)} %get-tuple-element.133), channel_id=1, source_target_pairs={{0,24},{1,25},{2,26},{3,27},{4,28},{5,29},{6,30},{7,31},{8,0},{9,1... | collective-permute-start | bytes 884744 | tf_op jit(solution)/shard_map/ppermute | solution.py:25
  89.7 2.2 %collective-permute-start.24 = (bf16[128,1152]{1,0:T(8,128)(2,1)S(1)}, bf16[128,1152]{1,0:T(8,128)(2,1)S(1)}, u32[]{:S(2)}, u32[]{:S(2)}) collective-permute-start(bf16[128,1152]{1,0:T(8,128)(2,1)S(1)} %get-tuple-element.136), channel_id=1, source_target_pairs={{0,4},{1,5},{2,6},{3,7},{4,0},{5,1},{6,2},{7,3},{8,12},{9,13},{10,... | collective-permute-start | bytes 884744 | tf_op jit(solution)/shard_map/ppermute | solution.py:25
  92.2 6.1 %collective-permute-done.20.refs_1_ = bf16[128,1152]{1,0:T(8,128)(2,1)S(1)} collective-permute-done((bf16[128,1152]{1,0:T(8,128)(2,1)S(1)}, bf16[128,1152]{1,0:T(8,128)(2,1)S(1)}, u32[]{:S(2)}, u32[]{:S(2)}) %collective-permute-start.20) | collective-permute-done | bytes 294944 | tf_op jit(solution)/shard_map/ppermute | solution.py:25
  99.8 4.5 %collective-permute-done.22 = bf16[128,1152]{1,0:T(8,128)(2,1)S(1)} collective-permute-done((bf16[128,1152]{1,0:T(8,128)(2,1)S(1)}, bf16[128,1152]{1,0:T(8,128)(2,1)S(1)}, u32[]{:S(2)}, u32[]{:S(2)}) %collective-permute-start.22) | collective-permute-done | bytes 294944 | tf_op jit(solution)/shard_map/ppermute | solution.py:25
  104.5 4.3 %collective-permute-start.25 = (bf16[128,1152]{1,0:T(8,128)(2,1)S(1)}, bf16[128,1152]{1,0:T(8,128)(2,1)S(1)}, u32[]{:S(2)}, u32[]{:S(2)}) collective-permute-start(bf16[128,1152]{1,0:T(8,128)(2,1)S(1)} %get-tuple-element.150), channel_id=1, source_target_pairs={{0,16},{1,17},{2,18},{3,19},{4,20},{5,21},{6,22},{7,23},{8,24},{9,... | collective-permute-start | bytes 884744 | tf_op jit(solution)/shard_map/ppermute | solution.py:25
  108.8 4.6 %collective-permute-start.26 = (bf16[128,1152]{1,0:T(8,128)(2,1)S(1)}, bf16[128,1152]{1,0:T(8,128)(2,1)S(1)}, u32[]{:S(2)}, u32[]{:S(2)}) collective-permute-start(bf16[128,1152]{1,0:T(8,128)(2,1)S(1)} %get-tuple-element.154), channel_id=1, source_target_pairs={{0,224},{32,0},{64,32},{96,64},{128,96},{160,128},{192,160},{224,1... | collective-permute-start | bytes 884744 | tf_op jit(solution)/shard_map/ppermute | solution.py:16
  116.0 5.9 %collective-permute-done.25.refs_0_ = bf16[128,1152]{1,0:T(8,128)(2,1)S(1)} collective-permute-done((bf16[128,1152]{1,0:T(8,128)(2,1)S(1)}, bf16[128,1152]{1,0:T(8,128)(2,1)S(1)}, u32[]{:S(2)}, u32[]{:S(2)}) %collective-permute-start.25) | collective-permute-done | bytes 294944 | tf_op jit(solution)/shard_map/ppermute | solution.py:25
  123.1 4.0 %collective-permute-done.26.refs_0_ = bf16[128,1152]{1,0:T(8,128)(2,1)S(1)} collective-permute-done((bf16[128,1152]{1,0:T(8,128)(2,1)S(1)}, bf16[128,1152]{1,0:T(8,128)(2,1)S(1)}, u32[]{:S(2)}, u32[]{:S(2)}) %collective-permute-start.26) | collective-permute-done | bytes 294944 | tf_op jit(solution)/shard_map/ppermute | solution.py:16
  (65 shorter events, 21.7 us)
Async XLA Ops:
  2.9 10.9 %collective-permute-start.1 = (bf16[128,1152]{1,0:T(8,128)(2,1)}, bf16[128,1152]{1,0:T(8,128)(2,1)S(1)}, u32[]{:S(2)}, u32[]{:S(2)}) collective-permute-start(bf16[128,1152]{1,0:T(8,128)(2,1)} %get-tuple-element.81.img_0), channel_id=1, source_target_pairs={{0,192},{32,224},{64,0},{96,32},{128,64},{160,96},{192,128},{224,1... | collective-permute-start | bytes 884744 | tf_op jit(solution)/shard_map/ppermute | solution.py:16
  5.7 18.1 %collective-permute-start.4 = (bf16[128,1152]{1,0:T(8,128)(2,1)}, bf16[128,1152]{1,0:T(8,128)(2,1)S(1)}, u32[]{:S(2)}, u32[]{:S(2)}) collective-permute-start(bf16[128,1152]{1,0:T(8,128)(2,1)} %get-tuple-element.82.txt_0), channel_id=1, source_target_pairs={{0,32},{32,64},{64,96},{96,128},{128,160},{160,192},{192,224},{224... | collective-permute-start | bytes 884744 | tf_op jit(solution)/shard_map/ppermute | solution.py:16
  7.6 17.5 %collective-permute-start = (bf16[128,1152]{1,0:T(8,128)(2,1)}, bf16[128,1152]{1,0:T(8,128)(2,1)S(1)}, u32[]{:S(2)}, u32[]{:S(2)}) collective-permute-start(bf16[128,1152]{1,0:T(8,128)(2,1)} %get-tuple-element.82.txt_0), channel_id=1, source_target_pairs={{0,6},{1,7},{2,0},{3,1},{4,2},{5,3},{6,4},{7,5},{8,14},{9,15},{10,... | collective-permute-start | bytes 884744 | tf_op jit(solution)/shard_map/ppermute | solution.py:25
  8.4 23.9 %collective-permute-start.6 = (bf16[128,1152]{1,0:T(8,128)(2,1)}, bf16[128,1152]{1,0:T(8,128)(2,1)S(1)}, u32[]{:S(2)}, u32[]{:S(2)}) collective-permute-start(bf16[128,1152]{1,0:T(8,128)(2,1)} %get-tuple-element.81.img_0), channel_id=1, source_target_pairs={{0,8},{1,9},{2,10},{3,11},{4,12},{5,13},{6,14},{7,15},{8,16},{9,17... | collective-permute-start | bytes 884744 | tf_op jit(solution)/shard_map/ppermute | solution.py:25
  11.7 20.7 %collective-permute-start.5 = (bf16[128,1152]{1,0:T(8,128)(2,1)}, bf16[128,1152]{1,0:T(8,128)(2,1)S(1)}, u32[]{:S(2)}, u32[]{:S(2)}) collective-permute-start(bf16[128,1152]{1,0:T(8,128)(2,1)} %get-tuple-element.81.img_0), channel_id=1, source_target_pairs={{0,24},{1,25},{2,26},{3,27},{4,28},{5,29},{6,30},{7,31},{8,0},{9,1... | collective-permute-start | bytes 884744 | tf_op jit(solution)/shard_map/ppermute | solution.py:25
  13.8 18.5 %collective-permute-start.3 = (bf16[128,1152]{1,0:T(8,128)(2,1)}, bf16[128,1152]{1,0:T(8,128)(2,1)S(1)}, u32[]{:S(2)}, u32[]{:S(2)}) collective-permute-start(bf16[128,1152]{1,0:T(8,128)(2,1)} %get-tuple-element.82.txt_0), channel_id=1, source_target_pairs={{0,4},{1,5},{2,6},{3,7},{4,0},{5,1},{6,2},{7,3},{8,12},{9,13},{10,... | collective-permute-start | bytes 884744 | tf_op jit(solution)/shard_map/ppermute | solution.py:25
  34.5 19.5 %collective-permute-start.10 = (bf16[256,1152]{1,0:T(8,128)(2,1)S(1)}, bf16[256,1152]{1,0:T(8,128)(2,1)S(1)}, u32[]{:S(2)}, u32[]{:S(2)}) collective-permute-start(bf16[256,1152]{1,0:T(8,128)(2,1)S(1)} %get-tuple-element.93.img_n), channel_id=1, source_target_pairs={{0,192},{32,224},{64,0},{96,32},{128,64},{160,96},{192,128},{224,1... | collective-permute-start | bytes 1769480 | tf_op jit(solution)/shard_map/ppermute | solution.py:16
  35.5 18.5 %collective-permute-start.9 = (bf16[128,1152]{1,0:T(8,128)(2,1)S(1)}, bf16[128,1152]{1,0:T(8,128)(2,1)S(1)}, u32[]{:S(2)}, u32[]{:S(2)}) collective-permute-start(bf16[128,1152]{1,0:T(8,128)(2,1)S(1)} %collective-permute-done.4), channel_id=1, source_target_pairs={{0,4},{1,5},{2,6},{3,7},{4,0},{5,1},{6,2},{7,3},{8,12},{9,13},{10,... | collective-permute-start | bytes 884744 | tf_op jit(solution)/shard_map/ppermute | solution.py:25
  36.7 17.3 %collective-permute-start.8 = (bf16[128,1152]{1,0:T(8,128)(2,1)S(1)}, bf16[128,1152]{1,0:T(8,128)(2,1)S(1)}, u32[]{:S(2)}, u32[]{:S(2)}) collective-permute-start(bf16[128,1152]{1,0:T(8,128)(2,1)S(1)} %collective-permute-done.4), channel_id=1, source_target_pairs={{0,2},{1,3},{2,4},{3,5},{4,6},{5,7},{6,0},{7,1},{8,10},{9,11},{10,... | collective-permute-start | bytes 884744 | tf_op jit(solution)/shard_map/ppermute | solution.py:25
  38.9 15.1 %collective-permute-start.7 = (bf16[128,1152]{1,0:T(8,128)(2,1)S(1)}, bf16[128,1152]{1,0:T(8,128)(2,1)S(1)}, u32[]{:S(2)}, u32[]{:S(2)}) collective-permute-start(bf16[128,1152]{1,0:T(8,128)(2,1)S(1)} %collective-permute-done.4), channel_id=1, source_target_pairs={{0,6},{1,7},{2,0},{3,1},{4,2},{5,3},{6,4},{7,5},{8,14},{9,15},{10,... | collective-permute-start | bytes 884744 | tf_op jit(solution)/shard_map/ppermute | solution.py:25
  38.9 15.1 %collective-permute-start.11 = (bf16[128,1152]{1,0:T(8,128)(2,1)S(1)}, bf16[128,1152]{1,0:T(8,128)(2,1)S(1)}, u32[]{:S(2)}, u32[]{:S(2)}) collective-permute-start(bf16[128,1152]{1,0:T(8,128)(2,1)S(1)} %get-tuple-element.92.img_0), channel_id=1, source_target_pairs={{0,16},{1,17},{2,18},{3,19},{4,20},{5,21},{6,22},{7,23},{8,24},{9,... | collective-permute-start | bytes 884744 | tf_op jit(solution)/shard_map/ppermute | solution.py:25
  54.2 10.4 %collective-permute-start.12 = (bf16[128,1152]{1,0:T(8,128)(2,1)S(1)}, bf16[128,1152]{1,0:T(8,128)(2,1)S(1)}, u32[]{:S(2)}, u32[]{:S(2)}) collective-permute-start(bf16[128,1152]{1,0:T(8,128)(2,1)S(1)} %collective-permute-done.11), channel_id=1, source_target_pairs={{0,192},{32,224},{64,0},{96,32},{128,64},{160,96},{192,128},{224,1... | collective-permute-start | bytes 884744 | tf_op jit(solution)/shard_map/ppermute | solution.py:16
  62.1 17.7 %collective-permute-start.14 = (bf16[272,1152]{1,0:T(8,128)(2,1)S(1)}, bf16[272,1152]{1,0:T(8,128)(2,1)S(1)}, u32[]{:S(2)}, u32[]{:S(2)}) collective-permute-start(bf16[272,1152]{1,0:T(8,128)(2,1)S(1)} %get-tuple-element.114), channel_id=1, source_target_pairs={{0,64},{32,96},{64,128},{96,160},{128,192},{160,224},{192,0},{224,... | collective-permute-start | bytes 1880072 | tf_op jit(solution)/shard_map/ppermute | solution.py:16
  80.3 9.4 %collective-permute-start.19 = (bf16[128,1152]{1,0:T(8,128)(2,1)S(1)}, bf16[128,1152]{1,0:T(8,128)(2,1)S(1)}, u32[]{:S(2)}, u32[]{:S(2)}) collective-permute-start(bf16[128,1152]{1,0:T(8,128)(2,1)S(1)} %get-tuple-element.129), channel_id=1, source_target_pairs={{0,2},{1,3},{2,4},{3,5},{4,6},{5,7},{6,0},{7,1},{8,10},{9,11},{10,... | collective-permute-start | bytes 884744 | tf_op jit(solution)/shard_map/ppermute | solution.py:25
  83.2 21.1 %collective-permute-start.23 = (bf16[256,1152]{1,0:T(8,128)(2,1)S(1)}, bf16[256,1152]{1,0:T(8,128)(2,1)S(1)}, u32[]{:S(2)}, u32[]{:S(2)}) collective-permute-start(bf16[256,1152]{1,0:T(8,128)(2,1)S(1)} %get-tuple-element.135), channel_id=1, source_target_pairs={{0,64},{32,96},{64,128},{96,160},{128,192},{160,224},{192,0},{224,... | collective-permute-start | bytes 1769480 | tf_op jit(solution)/shard_map/ppermute | solution.py:16
  84.6 13.7 %collective-permute-start.20 = (bf16[128,1152]{1,0:T(8,128)(2,1)S(1)}, bf16[128,1152]{1,0:T(8,128)(2,1)S(1)}, u32[]{:S(2)}, u32[]{:S(2)}) collective-permute-start(bf16[128,1152]{1,0:T(8,128)(2,1)S(1)} %get-tuple-element.132), channel_id=1, source_target_pairs={{0,8},{1,9},{2,10},{3,11},{4,12},{5,13},{6,14},{7,15},{8,16},{9,17... | collective-permute-start | bytes 884744 | tf_op jit(solution)/shard_map/ppermute | solution.py:25
  86.2 13.6 %collective-permute-start.21 = (bf16[128,1152]{1,0:T(8,128)(2,1)S(1)}, bf16[128,1152]{1,0:T(8,128)(2,1)S(1)}, u32[]{:S(2)}, u32[]{:S(2)}) collective-permute-start(bf16[128,1152]{1,0:T(8,128)(2,1)S(1)} %get-tuple-element.133), channel_id=1, source_target_pairs={{0,24},{1,25},{2,26},{3,27},{4,28},{5,29},{6,30},{7,31},{8,0},{9,1... | collective-permute-start | bytes 884744 | tf_op jit(solution)/shard_map/ppermute | solution.py:25
  89.0 15.3 %collective-permute-start.22 = (bf16[128,1152]{1,0:T(8,128)(2,1)S(1)}, bf16[128,1152]{1,0:T(8,128)(2,1)S(1)}, u32[]{:S(2)}, u32[]{:S(2)}) collective-permute-start(bf16[128,1152]{1,0:T(8,128)(2,1)S(1)} %get-tuple-element.134), channel_id=1, source_target_pairs={{0,6},{1,7},{2,0},{3,1},{4,2},{5,3},{6,4},{7,5},{8,14},{9,15},{10,... | collective-permute-start | bytes 884744 | tf_op jit(solution)/shard_map/ppermute | solution.py:25
  89.7 14.6 %collective-permute-start.24 = (bf16[128,1152]{1,0:T(8,128)(2,1)S(1)}, bf16[128,1152]{1,0:T(8,128)(2,1)S(1)}, u32[]{:S(2)}, u32[]{:S(2)}) collective-permute-start(bf16[128,1152]{1,0:T(8,128)(2,1)S(1)} %get-tuple-element.136), channel_id=1, source_target_pairs={{0,4},{1,5},{2,6},{3,7},{4,0},{5,1},{6,2},{7,3},{8,12},{9,13},{10,... | collective-permute-start | bytes 884744 | tf_op jit(solution)/shard_map/ppermute | solution.py:25
  104.5 17.4 %collective-permute-start.25 = (bf16[128,1152]{1,0:T(8,128)(2,1)S(1)}, bf16[128,1152]{1,0:T(8,128)(2,1)S(1)}, u32[]{:S(2)}, u32[]{:S(2)}) collective-permute-start(bf16[128,1152]{1,0:T(8,128)(2,1)S(1)} %get-tuple-element.150), channel_id=1, source_target_pairs={{0,16},{1,17},{2,18},{3,19},{4,20},{5,21},{6,22},{7,23},{8,24},{9,... | collective-permute-start | bytes 884744 | tf_op jit(solution)/shard_map/ppermute | solution.py:25
  108.8 18.4 %collective-permute-start.26 = (bf16[128,1152]{1,0:T(8,128)(2,1)S(1)}, bf16[128,1152]{1,0:T(8,128)(2,1)S(1)}, u32[]{:S(2)}, u32[]{:S(2)}) collective-permute-start(bf16[128,1152]{1,0:T(8,128)(2,1)S(1)} %get-tuple-element.154), channel_id=1, source_target_pairs={{0,224},{32,0},{64,32},{96,64},{128,96},{160,128},{192,160},{224,1... | collective-permute-start | bytes 884744 | tf_op jit(solution)/shard_map/ppermute | solution.py:16
  113.4 13.8 %collective-permute-start.27 = (bf16[128,1152]{1,0:T(8,128)(2,1)S(1)}, bf16[128,1152]{1,0:T(8,128)(2,1)S(1)}, u32[]{:S(2)}, u32[]{:S(2)}) collective-permute-start(bf16[128,1152]{1,0:T(8,128)(2,1)S(1)} %get-tuple-element.155), channel_id=1, source_target_pairs={{0,2},{1,3},{2,4},{3,5},{4,6},{5,7},{6,0},{7,1},{8,10},{9,11},{10,... | collective-permute-start | bytes 884744 | tf_op jit(solution)/shard_map/ppermute | solution.py:25
  113.4 13.8 %collective-permute-start.28 = (bf16[128,1152]{1,0:T(8,128)(2,1)S(1)}, bf16[128,1152]{1,0:T(8,128)(2,1)S(1)}, u32[]{:S(2)}, u32[]{:S(2)}) collective-permute-start(bf16[128,1152]{1,0:T(8,128)(2,1)S(1)} %get-tuple-element.156), channel_id=1, source_target_pairs={{0,6},{1,7},{2,0},{3,1},{4,2},{5,3},{6,4},{7,5},{8,14},{9,15},{10,... | collective-permute-start | bytes 884744 | tf_op jit(solution)/shard_map/ppermute | solution.py:25
  115.4 11.8 %collective-permute-start.29 = (bf16[128,1152]{1,0:T(8,128)(2,1)S(1)}, bf16[128,1152]{1,0:T(8,128)(2,1)S(1)}, u32[]{:S(2)}, u32[]{:S(2)}) collective-permute-start(bf16[128,1152]{1,0:T(8,128)(2,1)S(1)} %get-tuple-element.157), channel_id=1, source_target_pairs={{0,4},{1,5},{2,6},{3,7},{4,0},{5,1},{6,2},{7,3},{8,12},{9,13},{10,... | collective-permute-start | bytes 884744 | tf_op jit(solution)/shard_map/ppermute | solution.py:25
  (10 other events, 93.8 us)

commit v7 on v6

--- a/solution.py
+++ b/solution.py
@@ -32,17 +32,16 @@
 VMEM = pl.BlockSpec(memory_space=pltpu.VMEM)
 
 
-def whole(kernel, outs, *operands, scalars=False, aliases=None, scratch=(), place=pltpu.VMEM, room=28):
-    spec = pl.BlockSpec(memory_space=place)
-    first = [pl.BlockSpec(memory_space=pltpu.SMEM)] if scalars else [spec]
+def whole(kernel, outs, *operands, scalars=False, aliases=None, scratch=()):
+    first = [pl.BlockSpec(memory_space=pltpu.SMEM)] if scalars else [VMEM]
     return pl.pallas_call(
         kernel,
-        in_specs=first + [spec] * (len(operands) - 1),
+        in_specs=first + [VMEM] * (len(operands) - 1),
         out_specs=[VMEM] * len(outs),
         out_shape=[jax.ShapeDtypeStruct(shape, kind) for shape, kind in outs],
         input_output_aliases=aliases or {},
         scratch_shapes=list(scratch),
-        compiler_params=pltpu.CompilerParams(vmem_limit_bytes=room * 1024 * 1024),
+        compiler_params=pltpu.CompilerParams(vmem_limit_bytes=28 * 1024 * 1024),
         cost_estimate=pl.CostEstimate(flops=1, bytes_accessed=1, transcendentals=0),
     )(*operands)
 
@@ -60,17 +59,10 @@
     return over
 
 
-def unit_kernel(txt, img, txt_low, img_low, txt_here, img_here, arrived):
-    copies = []
-    for n, (there, here) in enumerate(((txt, txt_here), (img, img_here))):
-        copies.append(pltpu.make_async_copy(there, here, arrived.at[n]))
-        copies[-1].start()
-    for copy, values, low in ((copies[0], txt_here, txt_low), (copies[1], img_here, img_low)):
-        copy.wait()
-
-        @each(values.shape[0], 64)
-        def _(span):
-            low[span] = (values[span] * inverse_of(values[span])).astype(LOW)
+def unit_kernel(values, low):
+    @each(values.shape[0], 64)
+    def _(span):
+        low[span] = (values[span] * inverse_of(values[span])).astype(LOW)
 
 
 def end_kernel(values, own, *refs):
@@ -226,8 +218,8 @@
     rows = image_emb.shape
     width = rows[1]
     pair, half, wide = (256, width), (512, width), (1024, width)
-    here = [pltpu.VMEM(rows, F32)] * 2 + [pltpu.SemaphoreType.DMA((2,))]
-    txt_0, img_0 = whole(unit_kernel, [(rows, LOW)] * 2, text_emb, image_emb, place=pltpu.HBM, scratch=here, room=62)
+    (img_0,) = whole(unit_kernel, [(rows, LOW)], image_emb)
+    (txt_0,) = whole(unit_kernel, [(rows, LOW)], text_emb)
     scalars = jnp.stack([0.5 * temp, 0.5 * bias])
 
     txt_up = to_dev(txt_0, y=-1)
@@ -304,23 +296,23 @@
     sum_up = (gu_up + back_n[:128].astype(F32)).astype(LOW)
     sum_down = (gu_down + back_n[128:256].astype(F32)).astype(LOW)
     sum_up, sum_down, sh_up, sh_down, au = fence(sum_up, sum_down, sh_up, sh_down, au)
+    back = to_group(au, 2)
     sh_up = to_dev(sh_up, y=1)
     sum_up = to_dev(sum_up, zh=1)
     sum_down = to_dev(sum_down, zh=-1)
     sh_down = to_dev(sh_down, y=-1)
-    back = to_group(au, 2)
     sh_up, sh_far = fence(sh_up, sh_far)
     sh_far = to_dev(sh_far, y=2)
     own_sum, own_up, own_down, own_far = whole(
         functools.partial(text_sums_kernel, 0), sums, sums_c, *got[:2]
     )
-    sh_up, sum_up, sum_down, sh_down, back, sh_far, own_up, own_down, own_far = fence(
-        sh_up, sum_up, sum_down, sh_down, back, sh_far, own_up, own_down, own_far
-    )
     back_0, sum_2 = back[:128], (gu_2 + back[128:].astype(F32)).astype(LOW)
+    sum_2 = to_dev(jnp.pad(sum_2, ((0, 16), (0, 0))), zh=2)
+    sh_up, sum_up, sum_down, sh_down, sh_far, own_up, own_down, own_far = fence(
+        sh_up, sum_up, sum_down, sh_down, sh_far, own_up, own_down, own_far
+    )
     behind = (sh_sum + sh_up.astype(F32) + sh_down.astype(F32) + sh_far.astype(F32)).astype(LOW)
-    sum_2, behind, own_up, own_down, own_far = fence(sum_2, behind, own_up, own_down, own_far)
-    sum_2 = to_dev(sum_2, zh=2)
+    behind, own_up, own_down, own_far = fence(behind, own_up, own_down, own_far)
     behind = to_group(behind, -1)
     own_up = to_dev(own_up, y=1)
     own_down = to_dev(own_down, y=-1)

time: 129 us -> 130 us (level)
  the two profiles are of different devices: /device:TPU:24 before, /device:TPU:164 now
where the time goes in v7:
time: 130 us
  starting transfers between devices  49.6 us (38%)
  waiting for transfers between devices  47 us (36%)
  Pallas kernels  28 us (22%)
  local copies, waits for them, and re-layouts  2.4 us (2%)
  between operations  2.19 us (2%)
    ppermute x23, starting transfers between devices, to_dev(): return lax.ppermute(block, 'dev', route)  43.5 us
    ppermute x23, waiting for transfers between devices, to_dev(): return lax.ppermute(block, 'dev', route)  35 us
    pallas_call x12, Pallas kernels, whole(): pl.pallas_call(kernel, in_specs=first + [VMEM] * (len(operands) - 1), out...  28 us
    ppermute x7, waiting for transfers between devices, to_group(): lax.ppermute(block, 'grp', [(i, (i + step) % GROUPS) for i in range(GROUP...  11.9 us
    ppermute x7, starting transfers between devices, to_group(): lax.ppermute(block, 'grp', [(i, (i + step) % GROUPS) for i in range(GROUP...  6.16 us
  transfers between devices with their start and end apart: 30, of which 13 were waited for; matrix products, arithmetic and copies ran while one was open for 0% of the time, Pallas kernels for 20%

profile of v7, /device:TPU:164, one launch (start us, length us, event | category | flops | bytes accessed | tf_op | source)
XLA Modules:
  0.0 129.7 jit_solution(3710618048900544535)
XLA Ops:
  3.8 2.0 %collective-permute-start.4 = (bf16[128,1152]{1,0:T(8,128)(2,1)S(1)}, bf16[128,1152]{1,0:T(8,128)(2,1)S(1)}, u32[]{:S(2)}, u32[]{:S(2)}) collective-permute-start(bf16[128,1152]{1,0:T(8,128)(2,1)S(1)} %shard_map.59.txt_0), channel_id=1, source_target_pairs={{0,32},{32,64},{64,96},{96,128},{128,160},{160,192},{192,224},{224... | collective-permute-start | bytes 884744 | tf_op jit(solution)/shard_map/ppermute | solution.py:16
  5.8 3.0 %collective-permute-start = (bf16[128,1152]{1,0:T(8,128)(2,1)S(1)}, bf16[128,1152]{1,0:T(8,128)(2,1)S(1)}, u32[]{:S(2)}, u32[]{:S(2)}) collective-permute-start(bf16[128,1152]{1,0:T(8,128)(2,1)S(1)} %shard_map.59.txt_0), channel_id=1, source_target_pairs={{0,6},{1,7},{2,0},{3,1},{4,2},{5,3},{6,4},{7,5},{8,14},{9,15},{10,... | collective-permute-start | bytes 884744 | tf_op jit(solution)/shard_map/ppermute | solution.py:25
  10.3 2.7 %collective-permute-start.5 = (bf16[128,1152]{1,0:T(8,128)(2,1)S(1)}, bf16[128,1152]{1,0:T(8,128)(2,1)S(1)}, u32[]{:S(2)}, u32[]{:S(2)}) collective-permute-start(bf16[128,1152]{1,0:T(8,128)(2,1)S(1)} %shard_map.60.img_0), channel_id=1, source_target_pairs={{0,24},{1,25},{2,26},{3,27},{4,28},{5,29},{6,30},{7,31},{8,0},{9,1... | collective-permute-start | bytes 884744 | tf_op jit(solution)/shard_map/ppermute | solution.py:25
  13.9 6.2 %collective-permute-done.4 = bf16[128,1152]{1,0:T(8,128)(2,1)S(1)} collective-permute-done((bf16[128,1152]{1,0:T(8,128)(2,1)S(1)}, bf16[128,1152]{1,0:T(8,128)(2,1)S(1)}, u32[]{:S(2)}, u32[]{:S(2)}) %collective-permute-start.4) | collective-permute-done | bytes 294944 | tf_op jit(solution)/shard_map/ppermute | solution.py:16
  23.1 3.3 %collective-permute-done.5.img_up = bf16[128,1152]{1,0:T(8,128)(2,1)S(1)} collective-permute-done((bf16[128,1152]{1,0:T(8,128)(2,1)S(1)}, bf16[128,1152]{1,0:T(8,128)(2,1)S(1)}, u32[]{:S(2)}, u32[]{:S(2)}) %collective-permute-start.5) | collective-permute-done | bytes 294944 | tf_op jit(solution)/shard_map/ppermute | solution.py:25
  26.4 1.8 %collective-permute-done.2.txt_down = bf16[128,1152]{1,0:T(8,128)(2,1)S(1)} collective-permute-done((bf16[128,1152]{1,0:T(8,128)(2,1)S(1)}, bf16[128,1152]{1,0:T(8,128)(2,1)S(1)}, u32[]{:S(2)}, u32[]{:S(2)}) %collective-permute-start.2) | collective-permute-done | bytes 294944 | tf_op jit(solution)/shard_map/ppermute | solution.py:25
  29.1 1.9 %collective-permute-start.9 = (bf16[128,1152]{1,0:T(8,128)(2,1)S(1)}, bf16[128,1152]{1,0:T(8,128)(2,1)S(1)}, u32[]{:S(2)}, u32[]{:S(2)}) collective-permute-start(bf16[128,1152]{1,0:T(8,128)(2,1)S(1)} %collective-permute-done.4), channel_id=1, source_target_pairs={{0,4},{1,5},{2,6},{3,7},{4,0},{5,1},{6,2},{7,3},{8,12},{9,13},{10,... | collective-permute-start | bytes 884744 | tf_op jit(solution)/shard_map/ppermute | solution.py:25
  31.7 2.6 %collective-permute-start.7 = (bf16[128,1152]{1,0:T(8,128)(2,1)S(1)}, bf16[128,1152]{1,0:T(8,128)(2,1)S(1)}, u32[]{:S(2)}, u32[]{:S(2)}) collective-permute-start(bf16[128,1152]{1,0:T(8,128)(2,1)S(1)} %collective-permute-done.4), channel_id=1, source_target_pairs={{0,6},{1,7},{2,0},{3,1},{4,2},{5,3},{6,4},{7,5},{8,14},{9,15},{10,... | collective-permute-start | bytes 884744 | tf_op jit(solution)/shard_map/ppermute | solution.py:25
  34.4 3.2 %shard_map.62 = (f32[512,1152]{1,0:T(8,128)S(1)}, f32[1024,1152]{1,0:T(8,128)S(1)}, bf16[768,1152]{1,0:T(8,128)(2,1)S(1)}) custom-call(f32[2]{0:T(128)S(1)} %pad_maximum_fusion.scalars, bf16[128,1152]{1,0:T(8,128)(2,1)S(1)} %get-tuple-element.86.img_0, bf16[256,1152]{1,0:T(8,128)(2,1)S(1)} %get-tuple-element.87.img_n, ...), custom_call_target="tpu_custom_call" | custom-call | flops 1 | bytes 1 | tf_op jit(solution)/shard_map/pallas_call | solution.py:37
  37.6 12.3 %collective-permute-done.11 = bf16[128,1152]{1,0:T(8,128)(2,1)S(1)} collective-permute-done((bf16[128,1152]{1,0:T(8,128)(2,1)S(1)}, bf16[128,1152]{1,0:T(8,128)(2,1)S(1)}, u32[]{:S(2)}, u32[]{:S(2)}) %collective-permute-start.11) | collective-permute-done | bytes 294944 | tf_op jit(solution)/shard_map/ppermute | solution.py:25
  50.4 3.7 %shard_map.63 = (f32[256,1152]{1,0:T(8,128)S(1)}, f32[1024,1152]{1,0:T(8,128)S(1)}) custom-call(f32[2]{0:T(128)S(1)} %pad_maximum_fusion.scalars, bf16[256,1152]{1,0:T(8,128)(2,1)S(1)} %collective-permute-done.10.img, bf16[1024,1152]{1,0:T(8,128)(2,1)S(1)} %constant_dynamic-update-slice_fusion.txt, ...), custom_call_target="tpu_custom_call", output_to_operand_aliasing={{1}: (3, {})} | custom-call | flops 1 | bytes 1 | tf_op jit(solution)/shard_map/pallas_call | solution.py:37
  54.7 3.4 %shard_map.64 = (bf16[272,1152]{1,0:T(8,128)(2,1)S(1)}, f32[1024,1152]{1,0:T(8,128)S(1)}) custom-call(f32[2]{0:T(128)S(1)} %pad_maximum_fusion.scalars, bf16[256,1152]{1,0:T(8,128)(2,1)S(1)} %collective-permute-done.10.img, bf16[1024,1152]{1,0:T(8,128)(2,1)S(1)} %collective-permute-done.13.txt, f32[256,1152]{1,0:T(8,128)S(1)} %get-tuple-element.101.gu_in), custom_call_target="tpu_custom_call" | custom-call | flops 1 | bytes 1 | tf_op jit(solution)/shard_map/pallas_call | solution.py:37
  59.7 8.2 %shard_map.65 = (f32[768,1152]{1,0:T(8,128)S(1)}, bf16[256,1152]{1,0:T(8,128)(2,1)S(1)}, bf16[256,1152]{1,0:T(8,128)(2,1)S(1)}, bf16[256,1152]{1,0:T(8,128)(2,1)S(1)}, bf16[256,1152]{1,0:T(8,128)(2,1)S(1)}) custom-call(f32[2]{0:T(128)S(1)} %pad_maximum_fusion.scalars, bf16[768,1152]{1,0:T(8,128)(2,1)S(1)} %maximum_dynamic-update-slice_fusion.img, ...), custom_call_target="tpu_custom_call" | custom-call | flops 1 | bytes 1 | tf_op jit(solution)/shard_map/pallas_call | solution.py:37
  69.0 5.8 %shard_map.66 = (f32[128,1152]{1,0:T(8,128)S(1)}, f32[128,1152]{1,0:T(8,128)S(1)}, f32[128,1152]{1,0:T(8,128)S(1)}, f32[128,1152]{1,0:T(8,128)S(1)}, bf16[256,11...) custom-call(f32[2]{0:T(128)S(1)} %pad_maximum_fusion.scalars, ...), custom_call_target="tpu_custom_call", output_to_operand_aliasing={{5}: (4, {})} | custom-call | flops 1 | bytes 1 | tf_op jit(solution)/shard_map/pallas_call | solution.py:37
  76.1 3.6 %collective-permute-start.22 = (bf16[128,1152]{1,0:T(8,128)(2,1)S(1)}, bf16[128,1152]{1,0:T(8,128)(2,1)S(1)}, u32[]{:S(2)}, u32[]{:S(2)}) collective-permute-start(bf16[128,1152]{1,0:T(8,128)(2,1)S(1)} %get-tuple-element.127), channel_id=1, source_target_pairs={{0,8},{1,9},{2,10},{3,11},{4,12},{5,13},{6,14},{7,15},{8,16},{9,17... | collective-permute-start | bytes 884744 | tf_op jit(solution)/shard_map/ppermute | solution.py:25
  79.7 2.7 %collective-permute-start.23 = (bf16[128,1152]{1,0:T(8,128)(2,1)S(1)}, bf16[128,1152]{1,0:T(8,128)(2,1)S(1)}, u32[]{:S(2)}, u32[]{:S(2)}) collective-permute-start(bf16[128,1152]{1,0:T(8,128)(2,1)S(1)} %get-tuple-element.128), channel_id=1, source_target_pairs={{0,24},{1,25},{2,26},{3,27},{4,28},{5,29},{6,30},{7,31},{8,0},{9,1... | collective-permute-start | bytes 884744 | tf_op jit(solution)/shard_map/ppermute | solution.py:25
  82.4 3.2 %collective-permute-start.24 = (bf16[128,1152]{1,0:T(8,128)(2,1)S(1)}, bf16[128,1152]{1,0:T(8,128)(2,1)S(1)}, u32[]{:S(2)}, u32[]{:S(2)}) collective-permute-start(bf16[128,1152]{1,0:T(8,128)(2,1)S(1)} %get-tuple-element.129), channel_id=1, source_target_pairs={{0,6},{1,7},{2,0},{3,1},{4,2},{5,3},{6,4},{7,5},{8,14},{9,15},{10,... | collective-permute-start | bytes 884744 | tf_op jit(solution)/shard_map/ppermute | solution.py:25
  87.5 3.2 %collective-permute-done.19 = bf16[256,1152]{1,0:T(8,128)(2,1)S(1)} collective-permute-done((bf16[256,1152]{1,0:T(8,128)(2,1)S(1)}, bf16[256,1152]{1,0:T(8,128)(2,1)S(1)}, u32[]{:S(2)}, u32[]{:S(2)}) %collective-permute-start.19) | collective-permute-done | bytes 589856 | tf_op jit(solution)/shard_map/ppermute | solution.py:16
  90.9 4.4 %collective-permute-done.22.refs_1_ = bf16[128,1152]{1,0:T(8,128)(2,1)S(1)} collective-permute-done((bf16[128,1152]{1,0:T(8,128)(2,1)S(1)}, bf16[128,1152]{1,0:T(8,128)(2,1)S(1)}, u32[]{:S(2)}, u32[]{:S(2)}) %collective-permute-start.22) | collective-permute-done | bytes 294944 | tf_op jit(solution)/shard_map/ppermute | solution.py:25
  99.6 13.3 %collective-permute-start.28 = (bf16[128,1152]{1,0:T(8,128)(2,1)S(1)}, bf16[128,1152]{1,0:T(8,128)(2,1)S(1)}, u32[]{:S(2)}, u32[]{:S(2)}) collective-permute-start(bf16[128,1152]{1,0:T(8,128)(2,1)S(1)} %get-tuple-element.148), channel_id=1, source_target_pairs={{0,6},{1,7},{2,0},{3,1},{4,2},{5,3},{6,4},{7,5},{8,14},{9,15},{10,... | collective-permute-start | bytes 884744 | tf_op jit(solution)/shard_map/ppermute | solution.py:25
  114.4 2.5 %collective-permute-done.26.refs_0_ = bf16[128,1152]{1,0:T(8,128)(2,1)S(1)} collective-permute-done((bf16[128,1152]{1,0:T(8,128)(2,1)S(1)}, bf16[128,1152]{1,0:T(8,128)(2,1)S(1)}, u32[]{:S(2)}, u32[]{:S(2)}) %collective-permute-start.26) | collective-permute-done | bytes 294944 | tf_op jit(solution)/shard_map/ppermute | solution.py:16
  116.9 3.0 %collective-permute-done.27.refs_1_ = bf16[128,1152]{1,0:T(8,128)(2,1)S(1)} collective-permute-done((bf16[128,1152]{1,0:T(8,128)(2,1)S(1)}, bf16[128,1152]{1,0:T(8,128)(2,1)S(1)}, u32[]{:S(2)}, u32[]{:S(2)}) %collective-permute-start.27) | collective-permute-done | bytes 294944 | tf_op jit(solution)/shard_map/ppermute | solution.py:25
  119.9 5.3 %collective-permute-done.28.refs_2_ = bf16[128,1152]{1,0:T(8,128)(2,1)S(1)} collective-permute-done((bf16[128,1152]{1,0:T(8,128)(2,1)S(1)}, bf16[128,1152]{1,0:T(8,128)(2,1)S(1)}, u32[]{:S(2)}, u32[]{:S(2)}) %collective-permute-start.28) | collective-permute-done | bytes 294944 | tf_op jit(solution)/shard_map/ppermute | solution.py:25
  125.2 1.9 %collective-permute-done.29.refs_3_ = bf16[128,1152]{1,0:T(8,128)(2,1)S(1)} collective-permute-done((bf16[128,1152]{1,0:T(8,128)(2,1)S(1)}, bf16[128,1152]{1,0:T(8,128)(2,1)S(1)}, u32[]{:S(2)}, u32[]{:S(2)}) %collective-permute-start.29) | collective-permute-done | bytes 294944 | tf_op jit(solution)/shard_map/ppermute | solution.py:25
  (68 shorter events, 24.3 us)
Async XLA Ops:
  1.9 11.1 %collective-permute-start.1 = (bf16[128,1152]{1,0:T(8,128)(2,1)S(1)}, bf16[128,1152]{1,0:T(8,128)(2,1)S(1)}, u32[]{:S(2)}, u32[]{:S(2)}) collective-permute-start(bf16[128,1152]{1,0:T(8,128)(2,1)S(1)} %shard_map.60.img_0), channel_id=1, source_target_pairs={{0,192},{32,224},{64,0},{96,32},{128,64},{160,96},{192,128},{224,1... | collective-permute-start | bytes 884744 | tf_op jit(solution)/shard_map/ppermute | solution.py:16
  3.8 16.3 %collective-permute-start.4 = (bf16[128,1152]{1,0:T(8,128)(2,1)S(1)}, bf16[128,1152]{1,0:T(8,128)(2,1)S(1)}, u32[]{:S(2)}, u32[]{:S(2)}) collective-permute-start(bf16[128,1152]{1,0:T(8,128)(2,1)S(1)} %shard_map.59.txt_0), channel_id=1, source_target_pairs={{0,32},{32,64},{64,96},{96,128},{128,160},{160,192},{192,224},{224... | collective-permute-start | bytes 884744 | tf_op jit(solution)/shard_map/ppermute | solution.py:16
  5.8 17.2 %collective-permute-start = (bf16[128,1152]{1,0:T(8,128)(2,1)S(1)}, bf16[128,1152]{1,0:T(8,128)(2,1)S(1)}, u32[]{:S(2)}, u32[]{:S(2)}) collective-permute-start(bf16[128,1152]{1,0:T(8,128)(2,1)S(1)} %shard_map.59.txt_0), channel_id=1, source_target_pairs={{0,6},{1,7},{2,0},{3,1},{4,2},{5,3},{6,4},{7,5},{8,14},{9,15},{10,... | collective-permute-start | bytes 884744 | tf_op jit(solution)/shard_map/ppermute | solution.py:25
  8.9 14.2 %collective-permute-start.6 = (bf16[128,1152]{1,0:T(8,128)(2,1)S(1)}, bf16[128,1152]{1,0:T(8,128)(2,1)S(1)}, u32[]{:S(2)}, u32[]{:S(2)}) collective-permute-start(bf16[128,1152]{1,0:T(8,128)(2,1)S(1)} %shard_map.60.img_0), channel_id=1, source_target_pairs={{0,8},{1,9},{2,10},{3,11},{4,12},{5,13},{6,14},{7,15},{8,16},{9,17... | collective-permute-start | bytes 884744 | tf_op jit(solution)/shard_map/ppermute | solution.py:25
  10.3 16.1 %collective-permute-start.5 = (bf16[128,1152]{1,0:T(8,128)(2,1)S(1)}, bf16[128,1152]{1,0:T(8,128)(2,1)S(1)}, u32[]{:S(2)}, u32[]{:S(2)}) collective-permute-start(bf16[128,1152]{1,0:T(8,128)(2,1)S(1)} %shard_map.60.img_0), channel_id=1, source_target_pairs={{0,24},{1,25},{2,26},{3,27},{4,28},{5,29},{6,30},{7,31},{8,0},{9,1... | collective-permute-start | bytes 884744 | tf_op jit(solution)/shard_map/ppermute | solution.py:25
  13.0 13.4 %collective-permute-start.3 = (bf16[128,1152]{1,0:T(8,128)(2,1)S(1)}, bf16[128,1152]{1,0:T(8,128)(2,1)S(1)}, u32[]{:S(2)}, u32[]{:S(2)}) collective-permute-start(bf16[128,1152]{1,0:T(8,128)(2,1)S(1)} %shard_map.59.txt_0), channel_id=1, source_target_pairs={{0,4},{1,5},{2,6},{3,7},{4,0},{5,1},{6,2},{7,3},{8,12},{9,13},{10,... | collective-permute-start | bytes 884744 | tf_op jit(solution)/shard_map/ppermute | solution.py:25
  28.4 21.6 %collective-permute-start.10 = (bf16[256,1152]{1,0:T(8,128)(2,1)S(1)}, bf16[256,1152]{1,0:T(8,128)(2,1)S(1)}, u32[]{:S(2)}, u32[]{:S(2)}) collective-permute-start(bf16[256,1152]{1,0:T(8,128)(2,1)S(1)} %get-tuple-element.87.img_n), channel_id=1, source_target_pairs={{0,192},{32,224},{64,0},{96,32},{128,64},{160,96},{192,128},{224,1... | collective-permute-start | bytes 1769480 | tf_op jit(solution)/shard_map/ppermute | solution.py:16
  29.1 20.9 %collective-permute-start.9 = (bf16[128,1152]{1,0:T(8,128)(2,1)S(1)}, bf16[128,1152]{1,0:T(8,128)(2,1)S(1)}, u32[]{:S(2)}, u32[]{:S(2)}) collective-permute-start(bf16[128,1152]{1,0:T(8,128)(2,1)S(1)} %collective-permute-done.4), channel_id=1, source_target_pairs={{0,4},{1,5},{2,6},{3,7},{4,0},{5,1},{6,2},{7,3},{8,12},{9,13},{10,... | collective-permute-start | bytes 884744 | tf_op jit(solution)/shard_map/ppermute | solution.py:25
  31.0 19.0 %collective-permute-start.8 = (bf16[128,1152]{1,0:T(8,128)(2,1)S(1)}, bf16[128,1152]{1,0:T(8,128)(2,1)S(1)}, u32[]{:S(2)}, u32[]{:S(2)}) collective-permute-start(bf16[128,1152]{1,0:T(8,128)(2,1)S(1)} %collective-permute-done.4), channel_id=1, source_target_pairs={{0,2},{1,3},{2,4},{3,5},{4,6},{5,7},{6,0},{7,1},{8,10},{9,11},{10,... | collective-permute-start | bytes 884744 | tf_op jit(solution)/shard_map/ppermute | solution.py:25
  31.7 18.3 %collective-permute-start.7 = (bf16[128,1152]{1,0:T(8,128)(2,1)S(1)}, bf16[128,1152]{1,0:T(8,128)(2,1)S(1)}, u32[]{:S(2)}, u32[]{:S(2)}) collective-permute-start(bf16[128,1152]{1,0:T(8,128)(2,1)S(1)} %collective-permute-done.4), channel_id=1, source_target_pairs={{0,6},{1,7},{2,0},{3,1},{4,2},{5,3},{6,4},{7,5},{8,14},{9,15},{10,... | collective-permute-start | bytes 884744 | tf_op jit(solution)/shard_map/ppermute | solution.py:25
  34.2 15.7 %collective-permute-start.11 = (bf16[128,1152]{1,0:T(8,128)(2,1)S(1)}, bf16[128,1152]{1,0:T(8,128)(2,1)S(1)}, u32[]{:S(2)}, u32[]{:S(2)}) collective-permute-start(bf16[128,1152]{1,0:T(8,128)(2,1)S(1)} %get-tuple-element.86.img_0), channel_id=1, source_target_pairs={{0,16},{1,17},{2,18},{3,19},{4,20},{5,21},{6,22},{7,23},{8,24},{9,... | collective-permute-start | bytes 884744 | tf_op jit(solution)/shard_map/ppermute | solution.py:25
  50.2 9.4 %collective-permute-start.12 = (bf16[128,1152]{1,0:T(8,128)(2,1)S(1)}, bf16[128,1152]{1,0:T(8,128)(2,1)S(1)}, u32[]{:S(2)}, u32[]{:S(2)}) collective-permute-start(bf16[128,1152]{1,0:T(8,128)(2,1)S(1)} %collective-permute-done.11), channel_id=1, source_target_pairs={{0,192},{32,224},{64,0},{96,32},{128,64},{160,96},{192,128},{224,1... | collective-permute-start | bytes 884744 | tf_op jit(solution)/shard_map/ppermute | solution.py:16
  58.1 16.7 %collective-permute-start.14 = (bf16[272,1152]{1,0:T(8,128)(2,1)S(1)}, bf16[272,1152]{1,0:T(8,128)(2,1)S(1)}, u32[]{:S(2)}, u32[]{:S(2)}) collective-permute-start(bf16[272,1152]{1,0:T(8,128)(2,1)S(1)} %get-tuple-element.108), channel_id=1, source_target_pairs={{0,64},{32,96},{64,128},{96,160},{128,192},{160,224},{192,0},{224,... | collective-permute-start | bytes 1880072 | tf_op jit(solution)/shard_map/ppermute | solution.py:16
  75.3 15.4 %collective-permute-start.19 = (bf16[256,1152]{1,0:T(8,128)(2,1)S(1)}, bf16[256,1152]{1,0:T(8,128)(2,1)S(1)}, u32[]{:S(2)}, u32[]{:S(2)}) collective-permute-start(bf16[256,1152]{1,0:T(8,128)(2,1)S(1)} %get-tuple-element.123), channel_id=1, source_target_pairs={{0,64},{32,96},{64,128},{96,160},{128,192},{160,224},{192,0},{224,... | collective-permute-start | bytes 1769480 | tf_op jit(solution)/shard_map/ppermute | solution.py:16
  76.1 9.8 %collective-permute-start.21 = (bf16[128,1152]{1,0:T(8,128)(2,1)S(1)}, bf16[128,1152]{1,0:T(8,128)(2,1)S(1)}, u32[]{:S(2)}, u32[]{:S(2)}) collective-permute-start(bf16[128,1152]{1,0:T(8,128)(2,1)S(1)} %get-tuple-element.124), channel_id=1, source_target_pairs={{0,2},{1,3},{2,4},{3,5},{4,6},{5,7},{6,0},{7,1},{8,10},{9,11},{10,... | collective-permute-start | bytes 884744 | tf_op jit(solution)/shard_map/ppermute | solution.py:25
  76.1 19.1 %collective-permute-start.22 = (bf16[128,1152]{1,0:T(8,128)(2,1)S(1)}, bf16[128,1152]{1,0:T(8,128)(2,1)S(1)}, u32[]{:S(2)}, u32[]{:S(2)}) collective-permute-start(bf16[128,1152]{1,0:T(8,128)(2,1)S(1)} %get-tuple-element.127), channel_id=1, source_target_pairs={{0,8},{1,9},{2,10},{3,11},{4,12},{5,13},{6,14},{7,15},{8,16},{9,17... | collective-permute-start | bytes 884744 | tf_op jit(solution)/shard_map/ppermute | solution.py:25
  79.7 16.3 %collective-permute-start.23 = (bf16[128,1152]{1,0:T(8,128)(2,1)S(1)}, bf16[128,1152]{1,0:T(8,128)(2,1)S(1)}, u32[]{:S(2)}, u32[]{:S(2)}) collective-permute-start(bf16[128,1152]{1,0:T(8,128)(2,1)S(1)} %get-tuple-element.128), channel_id=1, source_target_pairs={{0,24},{1,25},{2,26},{3,27},{4,28},{5,29},{6,30},{7,31},{8,0},{9,1... | collective-permute-start | bytes 884744 | tf_op jit(solution)/shard_map/ppermute | solution.py:25
  82.4 15.2 %collective-permute-start.24 = (bf16[128,1152]{1,0:T(8,128)(2,1)S(1)}, bf16[128,1152]{1,0:T(8,128)(2,1)S(1)}, u32[]{:S(2)}, u32[]{:S(2)}) collective-permute-start(bf16[128,1152]{1,0:T(8,128)(2,1)S(1)} %get-tuple-element.129), channel_id=1, source_target_pairs={{0,6},{1,7},{2,0},{3,1},{4,2},{5,3},{6,4},{7,5},{8,14},{9,15},{10,... | collective-permute-start | bytes 884744 | tf_op jit(solution)/shard_map/ppermute | solution.py:25
  85.9 11.7 %collective-permute-start.25 = (bf16[128,1152]{1,0:T(8,128)(2,1)S(1)}, bf16[128,1152]{1,0:T(8,128)(2,1)S(1)}, u32[]{:S(2)}, u32[]{:S(2)}) collective-permute-start(bf16[128,1152]{1,0:T(8,128)(2,1)S(1)} %get-tuple-element.130), channel_id=1, source_target_pairs={{0,4},{1,5},{2,6},{3,7},{4,0},{5,1},{6,2},{7,3},{8,12},{9,13},{10,... | collective-permute-start | bytes 884744 | tf_op jit(solution)/shard_map/ppermute | solution.py:25
  90.8 37.6 %collective-permute-start.20 = (bf16[144,1152]{1,0:T(8,128)(2,1)S(1)}, bf16[144,1152]{1,0:T(8,128)(2,1)S(1)}, u32[]{:S(2)}, u32[]{:S(2)}) collective-permute-start(bf16[144,1152]{1,0:T(8,128)(2,1)S(1)} %pad.4), channel_id=1, source_target_pairs={{0,16},{1,17},{2,18},{3,19},{4,20},{5,21},{6,22},{7,23},{8,24},{9,... | collective-permute-start | bytes 995336 | tf_op jit(solution)/shard_map/ppermute | solution.py:25
  97.8 19.1 %collective-permute-start.26 = (bf16[128,1152]{1,0:T(8,128)(2,1)S(1)}, bf16[128,1152]{1,0:T(8,128)(2,1)S(1)}, u32[]{:S(2)}, u32[]{:S(2)}) collective-permute-start(bf16[128,1152]{1,0:T(8,128)(2,1)S(1)} %add_convert_fusion), channel_id=1, source_target_pairs={{0,224},{32,0},{64,32},{96,64},{128,96},{160,128},{192,160},{224,1... | collective-permute-start | bytes 884744 | tf_op jit(solution)/shard_map/ppermute | solution.py:16
  98.1 21.8 %collective-permute-start.27 = (bf16[128,1152]{1,0:T(8,128)(2,1)S(1)}, bf16[128,1152]{1,0:T(8,128)(2,1)S(1)}, u32[]{:S(2)}, u32[]{:S(2)}) collective-permute-start(bf16[128,1152]{1,0:T(8,128)(2,1)S(1)} %get-tuple-element.147), channel_id=1, source_target_pairs={{0,2},{1,3},{2,4},{3,5},{4,6},{5,7},{6,0},{7,1},{8,10},{9,11},{10,... | collective-permute-start | bytes 884744 | tf_op jit(solution)/shard_map/ppermute | solution.py:25
  99.6 25.7 %collective-permute-start.28 = (bf16[128,1152]{1,0:T(8,128)(2,1)S(1)}, bf16[128,1152]{1,0:T(8,128)(2,1)S(1)}, u32[]{:S(2)}, u32[]{:S(2)}) collective-permute-start(bf16[128,1152]{1,0:T(8,128)(2,1)S(1)} %get-tuple-element.148), channel_id=1, source_target_pairs={{0,6},{1,7},{2,0},{3,1},{4,2},{5,3},{6,4},{7,5},{8,14},{9,15},{10,... | collective-permute-start | bytes 884744 | tf_op jit(solution)/shard_map/ppermute | solution.py:25
  112.9 14.3 %collective-permute-start.29 = (bf16[128,1152]{1,0:T(8,128)(2,1)S(1)}, bf16[128,1152]{1,0:T(8,128)(2,1)S(1)}, u32[]{:S(2)}, u32[]{:S(2)}) collective-permute-start(bf16[128,1152]{1,0:T(8,128)(2,1)S(1)} %get-tuple-element.149), channel_id=1, source_target_pairs={{0,4},{1,5},{2,6},{3,7},{4,0},{5,1},{6,2},{7,3},{8,12},{9,13},{10,... | collective-permute-start | bytes 884744 | tf_op jit(solution)/shard_map/ppermute | solution.py:25
  (10 other events, 113.2 us)

commit v8 on v7

--- a/solution.py
+++ b/solution.py
@@ -68,7 +68,7 @@
 def end_kernel(values, own, *refs):
     *others, grad = refs
 
-    @each(values.shape[0], 64)
+    @each(values.shape[0], 128)
     def _(span):
         sums = own[span]
         for other in others:
@@ -243,7 +243,7 @@
     behind_down = to_dev(behind_0, y=1)
     behind_2 = to_dev(behind_0, y=2)
     ahead_n = to_group(img_n, -2)
-    img_2 = to_dev(img_again, zh=2)
+    img_2 = to_dev(img_0, zh=2)
     gu_first, sums_c, images = whole(
         first_kernel,
         [(half, F32), (wide, F32), ((768, width), LOW)],
@@ -306,13 +306,13 @@
     own_sum, own_up, own_down, own_far = whole(
         functools.partial(text_sums_kernel, 0), sums, sums_c, *got[:2]
     )
+    sh_up, sum_up, sum_down, sh_down, back, sh_far, own_up, own_down, own_far = fence(
+        sh_up, sum_up, sum_down, sh_down, back, sh_far, own_up, own_down, own_far
+    )
     back_0, sum_2 = back[:128], (gu_2 + back[128:].astype(F32)).astype(LOW)
-    sum_2 = to_dev(jnp.pad(sum_2, ((0, 16), (0, 0))), zh=2)
-    sh_up, sum_up, sum_down, sh_down, sh_far, own_up, own_down, own_far = fence(
-        sh_up, sum_up, sum_down, sh_down, sh_far, own_up, own_down, own_far
-    )
     behind = (sh_sum + sh_up.astype(F32) + sh_down.astype(F32) + sh_far.astype(F32)).astype(LOW)
-    behind, own_up, own_down, own_far = fence(behind, own_up, own_down, own_far)
+    sum_2, behind, own_up, own_down, own_far = fence(sum_2, behind, own_up, own_down, own_far)
+    sum_2 = to_dev(sum_2, zh=2)
     behind = to_group(behind, -1)
     own_up = to_dev(own_up, y=1)
     own_down = to_dev(own_down, y=-1)

time: 130 us -> 122 us (0.938)
  the two profiles are of different devices: /device:TPU:164 before, /device:TPU:24 now
where the time goes in v8:
time: 122 us; the launch traced here: 121 us
  starting transfers between devices  46.1 us (38%)
  waiting for transfers between devices  41.7 us (34%)
  Pallas kernels  27.8 us (23%)
  local copies, waits for them, and re-layouts  2.37 us (2%)
  between operations  2.17 us (2%)
    ppermute x23, starting transfers between devices, to_dev(): return lax.ppermute(block, 'dev', route)  37.5 us
    ppermute x23, waiting for transfers between devices, to_dev(): return lax.ppermute(block, 'dev', route)  29.8 us
    pallas_call x12, Pallas kernels, whole(): pl.pallas_call(kernel, in_specs=first + [VMEM] * (len(operands) - 1), out...  27.8 us
    ppermute x7, waiting for transfers between devices, to_group(): lax.ppermute(block, 'grp', [(i, (i + step) % GROUPS) for i in range(GROUP...  11.9 us
    ppermute x7, starting transfers between devices, to_group(): lax.ppermute(block, 'grp', [(i, (i + step) % GROUPS) for i in range(GROUP...  8.69 us
  transfers between devices with their start and end apart: 30, of which 12 were waited for; matrix products, arithmetic and copies ran while one was open for 0% of the time, Pallas kernels for 22%

profile of v8, /device:TPU:24, one launch (start us, length us, event | category | flops | bytes accessed | tf_op | source)
XLA Modules:
  0.0 120.6 jit_solution(15832100825837984234)
XLA Ops:
  1.9 2.8 %collective-permute-start.1 = (bf16[128,1152]{1,0:T(8,128)(2,1)S(1)}, bf16[128,1152]{1,0:T(8,128)(2,1)S(1)}, u32[]{:S(2)}, u32[]{:S(2)}) collective-permute-start(bf16[128,1152]{1,0:T(8,128)(2,1)S(1)} %shard_map.60.img_0), channel_id=1, source_target_pairs={{0,192},{32,224},{64,0},{96,32},{128,64},{160,96},{192,128},{224,1... | collective-permute-start | bytes 884744 | tf_op jit(solution)/shard_map/ppermute | solution.py:16
  6.1 2.0 %collective-permute-start.4 = (bf16[128,1152]{1,0:T(8,128)(2,1)S(1)}, bf16[128,1152]{1,0:T(8,128)(2,1)S(1)}, u32[]{:S(2)}, u32[]{:S(2)}) collective-permute-start(bf16[128,1152]{1,0:T(8,128)(2,1)S(1)} %shard_map.59.txt_0), channel_id=1, source_target_pairs={{0,32},{32,64},{64,96},{96,128},{128,160},{160,192},{192,224},{224... | collective-permute-start | bytes 884744 | tf_op jit(solution)/shard_map/ppermute | solution.py:16
  8.8 3.3 %collective-permute-start.6 = (bf16[128,1152]{1,0:T(8,128)(2,1)S(1)}, bf16[128,1152]{1,0:T(8,128)(2,1)S(1)}, u32[]{:S(2)}, u32[]{:S(2)}) collective-permute-start(bf16[128,1152]{1,0:T(8,128)(2,1)S(1)} %shard_map.60.img_0), channel_id=1, source_target_pairs={{0,8},{1,9},{2,10},{3,11},{4,12},{5,13},{6,14},{7,15},{8,16},{9,17... | collective-permute-start | bytes 884744 | tf_op jit(solution)/shard_map/ppermute | solution.py:25
  12.1 2.1 %collective-permute-start.5 = (bf16[128,1152]{1,0:T(8,128)(2,1)S(1)}, bf16[128,1152]{1,0:T(8,128)(2,1)S(1)}, u32[]{:S(2)}, u32[]{:S(2)}) collective-permute-start(bf16[128,1152]{1,0:T(8,128)(2,1)S(1)} %shard_map.60.img_0), channel_id=1, source_target_pairs={{0,24},{1,25},{2,26},{3,27},{4,28},{5,29},{6,30},{7,31},{8,0},{9,1... | collective-permute-start | bytes 884744 | tf_op jit(solution)/shard_map/ppermute | solution.py:25
  15.1 9.0 %collective-permute-done.4 = bf16[128,1152]{1,0:T(8,128)(2,1)S(1)} collective-permute-done((bf16[128,1152]{1,0:T(8,128)(2,1)S(1)}, bf16[128,1152]{1,0:T(8,128)(2,1)S(1)}, u32[]{:S(2)}, u32[]{:S(2)}) %collective-permute-start.4) | collective-permute-done | bytes 294944 | tf_op jit(solution)/shard_map/ppermute | solution.py:16
  25.4 7.9 %collective-permute-start.11 = (bf16[128,1152]{1,0:T(8,128)(2,1)S(1)}, bf16[128,1152]{1,0:T(8,128)(2,1)S(1)}, u32[]{:S(2)}, u32[]{:S(2)}) collective-permute-start(bf16[128,1152]{1,0:T(8,128)(2,1)S(1)} %shard_map.60.img_0), channel_id=1, source_target_pairs={{0,16},{1,17},{2,18},{3,19},{4,20},{5,21},{6,22},{7,23},{8,24},{9,... | collective-permute-start | bytes 884744 | tf_op jit(solution)/shard_map/ppermute | solution.py:25
  33.3 2.7 %collective-permute-done.6.img_down = bf16[128,1152]{1,0:T(8,128)(2,1)S(1)} collective-permute-done((bf16[128,1152]{1,0:T(8,128)(2,1)S(1)}, bf16[128,1152]{1,0:T(8,128)(2,1)S(1)}, u32[]{:S(2)}, u32[]{:S(2)}) %collective-permute-start.6) | collective-permute-done | bytes 294944 | tf_op jit(solution)/shard_map/ppermute | solution.py:25
  36.4 2.1 %collective-permute-start.9 = (bf16[128,1152]{1,0:T(8,128)(2,1)S(1)}, bf16[128,1152]{1,0:T(8,128)(2,1)S(1)}, u32[]{:S(2)}, u32[]{:S(2)}) collective-permute-start(bf16[128,1152]{1,0:T(8,128)(2,1)S(1)} %collective-permute-done.4), channel_id=1, source_target_pairs={{0,4},{1,5},{2,6},{3,7},{4,0},{5,1},{6,2},{7,3},{8,12},{9,13},{10,... | collective-permute-start | bytes 884744 | tf_op jit(solution)/shard_map/ppermute | solution.py:25
  38.5 2.1 %collective-permute-start.8 = (bf16[128,1152]{1,0:T(8,128)(2,1)S(1)}, bf16[128,1152]{1,0:T(8,128)(2,1)S(1)}, u32[]{:S(2)}, u32[]{:S(2)}) collective-permute-start(bf16[128,1152]{1,0:T(8,128)(2,1)S(1)} %collective-permute-done.4), channel_id=1, source_target_pairs={{0,2},{1,3},{2,4},{3,5},{4,6},{5,7},{6,0},{7,1},{8,10},{9,11},{10,... | collective-permute-start | bytes 884744 | tf_op jit(solution)/shard_map/ppermute | solution.py:25
  40.7 3.2 %shard_map.62 = (f32[512,1152]{1,0:T(8,128)S(1)}, f32[1024,1152]{1,0:T(8,128)S(1)}, bf16[768,1152]{1,0:T(8,128)(2,1)S(1)}) custom-call(f32[2]{0:T(128)S(1)} %pad_maximum_fusion.scalars, bf16[128,1152]{1,0:T(8,128)(2,1)S(1)} %get-tuple-element.88.img_0, bf16[256,1152]{1,0:T(8,128)(2,1)S(1)} %get-tuple-element.89.img_n, ...), custom_call_target="tpu_custom_call" | custom-call | flops 1 | bytes 1 | tf_op jit(solution)/shard_map/pallas_call | solution.py:37
  43.9 1.8 %collective-permute-done.9 = bf16[128,1152]{1,0:T(8,128)(2,1)S(1)} collective-permute-done((bf16[128,1152]{1,0:T(8,128)(2,1)S(1)}, bf16[128,1152]{1,0:T(8,128)(2,1)S(1)}, u32[]{:S(2)}, u32[]{:S(2)}) %collective-permute-start.9) | collective-permute-done | bytes 294944 | tf_op jit(solution)/shard_map/ppermute | solution.py:25
  46.4 2.4 %collective-permute-done.7 = bf16[128,1152]{1,0:T(8,128)(2,1)S(1)} collective-permute-done((bf16[128,1152]{1,0:T(8,128)(2,1)S(1)}, bf16[128,1152]{1,0:T(8,128)(2,1)S(1)}, u32[]{:S(2)}, u32[]{:S(2)}) %collective-permute-start.7) | collective-permute-done | bytes 294944 | tf_op jit(solution)/shard_map/ppermute | solution.py:25
  49.9 3.7 %shard_map.63 = (f32[256,1152]{1,0:T(8,128)S(1)}, f32[1024,1152]{1,0:T(8,128)S(1)}) custom-call(f32[2]{0:T(128)S(1)} %pad_maximum_fusion.scalars, bf16[256,1152]{1,0:T(8,128)(2,1)S(1)} %collective-permute-done.10.img, bf16[1024,1152]{1,0:T(8,128)(2,1)S(1)} %constant_dynamic-update-slice_fusion.txt, ...), custom_call_target="tpu_custom_call", output_to_operand_aliasing={{1}: (3, {})} | custom-call | flops 1 | bytes 1 | tf_op jit(solution)/shard_map/pallas_call | solution.py:37
  53.6 3.4 %shard_map.64 = (bf16[272,1152]{1,0:T(8,128)(2,1)S(1)}, f32[1024,1152]{1,0:T(8,128)S(1)}) custom-call(f32[2]{0:T(128)S(1)} %pad_maximum_fusion.scalars, bf16[256,1152]{1,0:T(8,128)(2,1)S(1)} %collective-permute-done.10.img, bf16[1024,1152]{1,0:T(8,128)(2,1)S(1)} %collective-permute-done.13.txt, f32[256,1152]{1,0:T(8,128)S(1)} %get-tuple-element.103.gu_in), custom_call_target="tpu_custom_call" | custom-call | flops 1 | bytes 1 | tf_op jit(solution)/shard_map/pallas_call | solution.py:37
  57.0 1.8 %collective-permute-start.14 = (bf16[272,1152]{1,0:T(8,128)(2,1)S(1)}, bf16[272,1152]{1,0:T(8,128)(2,1)S(1)}, u32[]{:S(2)}, u32[]{:S(2)}) collective-permute-start(bf16[272,1152]{1,0:T(8,128)(2,1)S(1)} %get-tuple-element.110), channel_id=1, source_target_pairs={{0,64},{32,96},{64,128},{96,160},{128,192},{160,224},{192,0},{224,... | collective-permute-start | bytes 1880072 | tf_op jit(solution)/shard_map/ppermute | solution.py:16
  58.8 8.2 %shard_map.65 = (f32[768,1152]{1,0:T(8,128)S(1)}, bf16[256,1152]{1,0:T(8,128)(2,1)S(1)}, bf16[256,1152]{1,0:T(8,128)(2,1)S(1)}, bf16[256,1152]{1,0:T(8,128)(2,1)S(1)}, bf16[256,1152]{1,0:T(8,128)(2,1)S(1)}) custom-call(f32[2]{0:T(128)S(1)} %pad_maximum_fusion.scalars, bf16[768,1152]{1,0:T(8,128)(2,1)S(1)} %maximum_dynamic-update-slice_fusion.img, ...), custom_call_target="tpu_custom_call" | custom-call | flops 1 | bytes 1 | tf_op jit(solution)/shard_map/pallas_call | solution.py:37
  68.1 5.8 %shard_map.66 = (f32[128,1152]{1,0:T(8,128)S(1)}, f32[128,1152]{1,0:T(8,128)S(1)}, f32[128,1152]{1,0:T(8,128)S(1)}, f32[128,1152]{1,0:T(8,128)S(1)}, bf16[256,11...) custom-call(f32[2]{0:T(128)S(1)} %pad_maximum_fusion.scalars, ...), custom_call_target="tpu_custom_call", output_to_operand_aliasing={{5}: (4, {})} | custom-call | flops 1 | bytes 1 | tf_op jit(solution)/shard_map/pallas_call | solution.py:37
  76.0 7.5 %collective-permute-start.20 = (bf16[128,1152]{1,0:T(8,128)(2,1)S(1)}, bf16[128,1152]{1,0:T(8,128)(2,1)S(1)}, u32[]{:S(2)}, u32[]{:S(2)}) collective-permute-start(bf16[128,1152]{1,0:T(8,128)(2,1)S(1)} %get-tuple-element.128), channel_id=1, source_target_pairs={{0,8},{1,9},{2,10},{3,11},{4,12},{5,13},{6,14},{7,15},{8,16},{9,17... | collective-permute-start | bytes 884744 | tf_op jit(solution)/shard_map/ppermute | solution.py:25
  85.4 8.1 %collective-permute-done.20.refs_1_ = bf16[128,1152]{1,0:T(8,128)(2,1)S(1)} collective-permute-done((bf16[128,1152]{1,0:T(8,128)(2,1)S(1)}, bf16[128,1152]{1,0:T(8,128)(2,1)S(1)}, u32[]{:S(2)}, u32[]{:S(2)}) %collective-permute-start.20) | collective-permute-done | bytes 294944 | tf_op jit(solution)/shard_map/ppermute | solution.py:25
  94.3 4.9 %collective-permute-done.22 = bf16[128,1152]{1,0:T(8,128)(2,1)S(1)} collective-permute-done((bf16[128,1152]{1,0:T(8,128)(2,1)S(1)}, bf16[128,1152]{1,0:T(8,128)(2,1)S(1)}, u32[]{:S(2)}, u32[]{:S(2)}) %collective-permute-start.22) | collective-permute-done | bytes 294944 | tf_op jit(solution)/shard_map/ppermute | solution.py:25
  99.5 3.7 %collective-permute-start.25 = (bf16[128,1152]{1,0:T(8,128)(2,1)S(1)}, bf16[128,1152]{1,0:T(8,128)(2,1)S(1)}, u32[]{:S(2)}, u32[]{:S(2)}) collective-permute-start(bf16[128,1152]{1,0:T(8,128)(2,1)S(1)} %get-tuple-element.146), channel_id=1, source_target_pairs={{0,16},{1,17},{2,18},{3,19},{4,20},{5,21},{6,22},{7,23},{8,24},{9,... | collective-permute-start | bytes 884744 | tf_op jit(solution)/shard_map/ppermute | solution.py:25
  103.8 2.0 %collective-permute-start.28 = (bf16[128,1152]{1,0:T(8,128)(2,1)S(1)}, bf16[128,1152]{1,0:T(8,128)(2,1)S(1)}, u32[]{:S(2)}, u32[]{:S(2)}) collective-permute-start(bf16[128,1152]{1,0:T(8,128)(2,1)S(1)} %get-tuple-element.152), channel_id=1, source_target_pairs={{0,6},{1,7},{2,0},{3,1},{4,2},{5,3},{6,4},{7,5},{8,14},{9,15},{10,... | collective-permute-start | bytes 884744 | tf_op jit(solution)/shard_map/ppermute | solution.py:25
  107.6 8.3 %collective-permute-done.25.refs_0_ = bf16[128,1152]{1,0:T(8,128)(2,1)S(1)} collective-permute-done((bf16[128,1152]{1,0:T(8,128)(2,1)S(1)}, bf16[128,1152]{1,0:T(8,128)(2,1)S(1)}, u32[]{:S(2)}, u32[]{:S(2)}) %collective-permute-start.25) | collective-permute-done | bytes 294944 | tf_op jit(solution)/shard_map/ppermute | solution.py:25
  117.0 2.5 %collective-permute-done.26.refs_0_ = bf16[128,1152]{1,0:T(8,128)(2,1)S(1)} collective-permute-done((bf16[128,1152]{1,0:T(8,128)(2,1)S(1)}, bf16[128,1152]{1,0:T(8,128)(2,1)S(1)}, u32[]{:S(2)}, u32[]{:S(2)}) %collective-permute-start.26) | collective-permute-done | bytes 294944 | tf_op jit(solution)/shard_map/ppermute | solution.py:16
  (66 shorter events, 17.3 us)
Async XLA Ops:
  1.9 12.3 %collective-permute-start.1 = (bf16[128,1152]{1,0:T(8,128)(2,1)S(1)}, bf16[128,1152]{1,0:T(8,128)(2,1)S(1)}, u32[]{:S(2)}, u32[]{:S(2)}) collective-permute-start(bf16[128,1152]{1,0:T(8,128)(2,1)S(1)} %shard_map.60.img_0), channel_id=1, source_target_pairs={{0,192},{32,224},{64,0},{96,32},{128,64},{160,96},{192,128},{224,1... | collective-permute-start | bytes 884744 | tf_op jit(solution)/shard_map/ppermute | solution.py:16
  6.1 18.0 %collective-permute-start.4 = (bf16[128,1152]{1,0:T(8,128)(2,1)S(1)}, bf16[128,1152]{1,0:T(8,128)(2,1)S(1)}, u32[]{:S(2)}, u32[]{:S(2)}) collective-permute-start(bf16[128,1152]{1,0:T(8,128)(2,1)S(1)} %shard_map.59.txt_0), channel_id=1, source_target_pairs={{0,32},{32,64},{64,96},{96,128},{128,160},{160,192},{192,224},{224... | collective-permute-start | bytes 884744 | tf_op jit(solution)/shard_map/ppermute | solution.py:16
  8.1 17.4 %collective-permute-start = (bf16[128,1152]{1,0:T(8,128)(2,1)S(1)}, bf16[128,1152]{1,0:T(8,128)(2,1)S(1)}, u32[]{:S(2)}, u32[]{:S(2)}) collective-permute-start(bf16[128,1152]{1,0:T(8,128)(2,1)S(1)} %shard_map.59.txt_0), channel_id=1, source_target_pairs={{0,6},{1,7},{2,0},{3,1},{4,2},{5,3},{6,4},{7,5},{8,14},{9,15},{10,... | collective-permute-start | bytes 884744 | tf_op jit(solution)/shard_map/ppermute | solution.py:25
  8.8 27.2 %collective-permute-start.6 = (bf16[128,1152]{1,0:T(8,128)(2,1)S(1)}, bf16[128,1152]{1,0:T(8,128)(2,1)S(1)}, u32[]{:S(2)}, u32[]{:S(2)}) collective-permute-start(bf16[128,1152]{1,0:T(8,128)(2,1)S(1)} %shard_map.60.img_0), channel_id=1, source_target_pairs={{0,8},{1,9},{2,10},{3,11},{4,12},{5,13},{6,14},{7,15},{8,16},{9,17... | collective-permute-start | bytes 884744 | tf_op jit(solution)/shard_map/ppermute | solution.py:25
  12.1 23.9 %collective-permute-start.5 = (bf16[128,1152]{1,0:T(8,128)(2,1)S(1)}, bf16[128,1152]{1,0:T(8,128)(2,1)S(1)}, u32[]{:S(2)}, u32[]{:S(2)}) collective-permute-start(bf16[128,1152]{1,0:T(8,128)(2,1)S(1)} %shard_map.60.img_0), channel_id=1, source_target_pairs={{0,24},{1,25},{2,26},{3,27},{4,28},{5,29},{6,30},{7,31},{8,0},{9,1... | collective-permute-start | bytes 884744 | tf_op jit(solution)/shard_map/ppermute | solution.py:25
  14.2 21.8 %collective-permute-start.3 = (bf16[128,1152]{1,0:T(8,128)(2,1)S(1)}, bf16[128,1152]{1,0:T(8,128)(2,1)S(1)}, u32[]{:S(2)}, u32[]{:S(2)}) collective-permute-start(bf16[128,1152]{1,0:T(8,128)(2,1)S(1)} %shard_map.59.txt_0), channel_id=1, source_target_pairs={{0,4},{1,5},{2,6},{3,7},{4,0},{5,1},{6,2},{7,3},{8,12},{9,13},{10,... | collective-permute-start | bytes 884744 | tf_op jit(solution)/shard_map/ppermute | solution.py:25
  24.1 11.9 %collective-permute-start.2 = (bf16[128,1152]{1,0:T(8,128)(2,1)S(1)}, bf16[128,1152]{1,0:T(8,128)(2,1)S(1)}, u32[]{:S(2)}, u32[]{:S(2)}) collective-permute-start(bf16[128,1152]{1,0:T(8,128)(2,1)S(1)} %shard_map.59.txt_0), channel_id=1, source_target_pairs={{0,2},{1,3},{2,4},{3,5},{4,6},{5,7},{6,0},{7,1},{8,10},{9,11},{10,... | collective-permute-start | bytes 884744 | tf_op jit(solution)/shard_map/ppermute | solution.py:25
  25.4 18.5 %collective-permute-start.11 = (bf16[128,1152]{1,0:T(8,128)(2,1)S(1)}, bf16[128,1152]{1,0:T(8,128)(2,1)S(1)}, u32[]{:S(2)}, u32[]{:S(2)}) collective-permute-start(bf16[128,1152]{1,0:T(8,128)(2,1)S(1)} %shard_map.60.img_0), channel_id=1, source_target_pairs={{0,16},{1,17},{2,18},{3,19},{4,20},{5,21},{6,22},{7,23},{8,24},{9,... | collective-permute-start | bytes 884744 | tf_op jit(solution)/shard_map/ppermute | solution.py:25
  36.2 12.6 %collective-permute-start.10 = (bf16[256,1152]{1,0:T(8,128)(2,1)S(1)}, bf16[256,1152]{1,0:T(8,128)(2,1)S(1)}, u32[]{:S(2)}, u32[]{:S(2)}) collective-permute-start(bf16[256,1152]{1,0:T(8,128)(2,1)S(1)} %get-tuple-element.89.img_n), channel_id=1, source_target_pairs={{0,192},{32,224},{64,0},{96,32},{128,64},{160,96},{192,128},{224,1... | collective-permute-start | bytes 1769480 | tf_op jit(solution)/shard_map/ppermute | solution.py:16
  36.4 9.3 %collective-permute-start.9 = (bf16[128,1152]{1,0:T(8,128)(2,1)S(1)}, bf16[128,1152]{1,0:T(8,128)(2,1)S(1)}, u32[]{:S(2)}, u32[]{:S(2)}) collective-permute-start(bf16[128,1152]{1,0:T(8,128)(2,1)S(1)} %collective-permute-done.4), channel_id=1, source_target_pairs={{0,4},{1,5},{2,6},{3,7},{4,0},{5,1},{6,2},{7,3},{8,12},{9,13},{10,... | collective-permute-start | bytes 884744 | tf_op jit(solution)/shard_map/ppermute | solution.py:25
  40.6 8.3 %collective-permute-start.7 = (bf16[128,1152]{1,0:T(8,128)(2,1)S(1)}, bf16[128,1152]{1,0:T(8,128)(2,1)S(1)}, u32[]{:S(2)}, u32[]{:S(2)}) collective-permute-start(bf16[128,1152]{1,0:T(8,128)(2,1)S(1)} %collective-permute-done.4), channel_id=1, source_target_pairs={{0,6},{1,7},{2,0},{3,1},{4,2},{5,3},{6,4},{7,5},{8,14},{9,15},{10,... | collective-permute-start | bytes 884744 | tf_op jit(solution)/shard_map/ppermute | solution.py:25
  49.1 9.7 %collective-permute-start.12 = (bf16[128,1152]{1,0:T(8,128)(2,1)S(1)}, bf16[128,1152]{1,0:T(8,128)(2,1)S(1)}, u32[]{:S(2)}, u32[]{:S(2)}) collective-permute-start(bf16[128,1152]{1,0:T(8,128)(2,1)S(1)} %collective-permute-done.11), channel_id=1, source_target_pairs={{0,192},{32,224},{64,0},{96,32},{128,64},{160,96},{192,128},{224,1... | collective-permute-start | bytes 884744 | tf_op jit(solution)/shard_map/ppermute | solution.py:16
  57.0 17.4 %collective-permute-start.14 = (bf16[272,1152]{1,0:T(8,128)(2,1)S(1)}, bf16[272,1152]{1,0:T(8,128)(2,1)S(1)}, u32[]{:S(2)}, u32[]{:S(2)}) collective-permute-start(bf16[272,1152]{1,0:T(8,128)(2,1)S(1)} %get-tuple-element.110), channel_id=1, source_target_pairs={{0,64},{32,96},{64,128},{96,160},{128,192},{160,224},{192,0},{224,... | collective-permute-start | bytes 1880072 | tf_op jit(solution)/shard_map/ppermute | solution.py:16
  74.9 8.7 %collective-permute-start.19 = (bf16[128,1152]{1,0:T(8,128)(2,1)S(1)}, bf16[128,1152]{1,0:T(8,128)(2,1)S(1)}, u32[]{:S(2)}, u32[]{:S(2)}) collective-permute-start(bf16[128,1152]{1,0:T(8,128)(2,1)S(1)} %get-tuple-element.125), channel_id=1, source_target_pairs={{0,2},{1,3},{2,4},{3,5},{4,6},{5,7},{6,0},{7,1},{8,10},{9,11},{10,... | collective-permute-start | bytes 884744 | tf_op jit(solution)/shard_map/ppermute | solution.py:25
  75.5 23.7 %collective-permute-start.23 = (bf16[256,1152]{1,0:T(8,128)(2,1)S(1)}, bf16[256,1152]{1,0:T(8,128)(2,1)S(1)}, u32[]{:S(2)}, u32[]{:S(2)}) collective-permute-start(bf16[256,1152]{1,0:T(8,128)(2,1)S(1)} %get-tuple-element.131), channel_id=1, source_target_pairs={{0,64},{32,96},{64,128},{96,160},{128,192},{160,224},{192,0},{224,... | collective-permute-start | bytes 1769480 | tf_op jit(solution)/shard_map/ppermute | solution.py:16
  76.0 17.5 %collective-permute-start.20 = (bf16[128,1152]{1,0:T(8,128)(2,1)S(1)}, bf16[128,1152]{1,0:T(8,128)(2,1)S(1)}, u32[]{:S(2)}, u32[]{:S(2)}) collective-permute-start(bf16[128,1152]{1,0:T(8,128)(2,1)S(1)} %get-tuple-element.128), channel_id=1, source_target_pairs={{0,8},{1,9},{2,10},{3,11},{4,12},{5,13},{6,14},{7,15},{8,16},{9,17... | collective-permute-start | bytes 884744 | tf_op jit(solution)/shard_map/ppermute | solution.py:25
  83.5 10.8 %collective-permute-start.21 = (bf16[128,1152]{1,0:T(8,128)(2,1)S(1)}, bf16[128,1152]{1,0:T(8,128)(2,1)S(1)}, u32[]{:S(2)}, u32[]{:S(2)}) collective-permute-start(bf16[128,1152]{1,0:T(8,128)(2,1)S(1)} %get-tuple-element.129), channel_id=1, source_target_pairs={{0,24},{1,25},{2,26},{3,27},{4,28},{5,29},{6,30},{7,31},{8,0},{9,1... | collective-permute-start | bytes 884744 | tf_op jit(solution)/shard_map/ppermute | solution.py:25
  83.5 15.7 %collective-permute-start.22 = (bf16[128,1152]{1,0:T(8,128)(2,1)S(1)}, bf16[128,1152]{1,0:T(8,128)(2,1)S(1)}, u32[]{:S(2)}, u32[]{:S(2)}) collective-permute-start(bf16[128,1152]{1,0:T(8,128)(2,1)S(1)} %get-tuple-element.130), channel_id=1, source_target_pairs={{0,6},{1,7},{2,0},{3,1},{4,2},{5,3},{6,4},{7,5},{8,14},{9,15},{10,... | collective-permute-start | bytes 884744 | tf_op jit(solution)/shard_map/ppermute | solution.py:25
  83.5 15.7 %collective-permute-start.24 = (bf16[128,1152]{1,0:T(8,128)(2,1)S(1)}, bf16[128,1152]{1,0:T(8,128)(2,1)S(1)}, u32[]{:S(2)}, u32[]{:S(2)}) collective-permute-start(bf16[128,1152]{1,0:T(8,128)(2,1)S(1)} %get-tuple-element.132), channel_id=1, source_target_pairs={{0,4},{1,5},{2,6},{3,7},{4,0},{5,1},{6,2},{7,3},{8,12},{9,13},{10,... | collective-permute-start | bytes 884744 | tf_op jit(solution)/shard_map/ppermute | solution.py:25
  99.5 16.4 %collective-permute-start.25 = (bf16[128,1152]{1,0:T(8,128)(2,1)S(1)}, bf16[128,1152]{1,0:T(8,128)(2,1)S(1)}, u32[]{:S(2)}, u32[]{:S(2)}) collective-permute-start(bf16[128,1152]{1,0:T(8,128)(2,1)S(1)} %get-tuple-element.146), channel_id=1, source_target_pairs={{0,16},{1,17},{2,18},{3,19},{4,20},{5,21},{6,22},{7,23},{8,24},{9,... | collective-permute-start | bytes 884744 | tf_op jit(solution)/shard_map/ppermute | solution.py:25
  103.1 16.3 %collective-permute-start.26 = (bf16[128,1152]{1,0:T(8,128)(2,1)S(1)}, bf16[128,1152]{1,0:T(8,128)(2,1)S(1)}, u32[]{:S(2)}, u32[]{:S(2)}) collective-permute-start(bf16[128,1152]{1,0:T(8,128)(2,1)S(1)} %get-tuple-element.150), channel_id=1, source_target_pairs={{0,224},{32,0},{64,32},{96,64},{128,96},{160,128},{192,160},{224,1... | collective-permute-start | bytes 884744 | tf_op jit(solution)/shard_map/ppermute | solution.py:16
  103.8 15.6 %collective-permute-start.27 = (bf16[128,1152]{1,0:T(8,128)(2,1)S(1)}, bf16[128,1152]{1,0:T(8,128)(2,1)S(1)}, u32[]{:S(2)}, u32[]{:S(2)}) collective-permute-start(bf16[128,1152]{1,0:T(8,128)(2,1)S(1)} %get-tuple-element.151), channel_id=1, source_target_pairs={{0,2},{1,3},{2,4},{3,5},{4,6},{5,7},{6,0},{7,1},{8,10},{9,11},{10,... | collective-permute-start | bytes 884744 | tf_op jit(solution)/shard_map/ppermute | solution.py:25
  103.8 15.6 %collective-permute-start.28 = (bf16[128,1152]{1,0:T(8,128)(2,1)S(1)}, bf16[128,1152]{1,0:T(8,128)(2,1)S(1)}, u32[]{:S(2)}, u32[]{:S(2)}) collective-permute-start(bf16[128,1152]{1,0:T(8,128)(2,1)S(1)} %get-tuple-element.152), channel_id=1, source_target_pairs={{0,6},{1,7},{2,0},{3,1},{4,2},{5,3},{6,4},{7,5},{8,14},{9,15},{10,... | collective-permute-start | bytes 884744 | tf_op jit(solution)/shard_map/ppermute | solution.py:25
  105.9 13.6 %collective-permute-start.29 = (bf16[128,1152]{1,0:T(8,128)(2,1)S(1)}, bf16[128,1152]{1,0:T(8,128)(2,1)S(1)}, u32[]{:S(2)}, u32[]{:S(2)}) collective-permute-start(bf16[128,1152]{1,0:T(8,128)(2,1)S(1)} %get-tuple-element.153), channel_id=1, source_target_pairs={{0,4},{1,5},{2,6},{3,7},{4,0},{5,1},{6,2},{7,3},{8,12},{9,13},{10,... | collective-permute-start | bytes 884744 | tf_op jit(solution)/shard_map/ppermute | solution.py:25
  (10 other events, 91.5 us)

commit v9 on v8

--- a/solution.py
+++ b/solution.py
@@ -120,10 +120,15 @@
         def _(span):
             img[pl.ds(pl.multiple_of(first + span.start, 32), 32)] = part[span]
 
-    shape = gu.shape[0], txt.shape[0]
+    shape = gu.shape[0] - 256, txt.shape[0]
     row, col = lax.broadcasted_iota(jnp.int32, shape, 0), lax.broadcasted_iota(jnp.int32, shape, 1)
     mask = jnp.logical_and(row == col, row < 128)
-    gu[...], gv[: shape[1]] = products(scalars, img[0 : shape[0]], txt[...], mask)
+    gu[: shape[0]], gv[: shape[1]] = products(scalars, img[0 : shape[0]], txt[...], mask)
+
+    @each(256, 32)
+    def _(span):
+        there = pl.ds(pl.multiple_of(shape[0] + span.start, 32), 32)
+        gu[there] = jnp.zeros((32, gu.shape[1]), F32)
 
     @each(shape[1], 32)
     def _(span):
@@ -131,10 +136,15 @@
         gv[there] = jnp.zeros((32, gv.shape[1]), F32)
 
 
-def both_halves(txt):
+def both_halves(txt, unrolled=False):
     size = txt.shape[0] // 2
 
     def over(body):
+        if unrolled:
+            for n in (0, 1):
+                body(n, slice(n * size, (n + 1) * size))
+            return
+
         @pl.loop(0, 2)
         def _(n):
             body(n, pl.ds(pl.multiple_of(n * size, size), size))
@@ -147,7 +157,7 @@
     def _(span):
         gu[span] = jnp.zeros((32, gu.shape[1]), F32)
 
-    @both_halves(txt)
+    @both_halves(txt, unrolled=True)
     def _(n, here):
         part, term = products(scalars, img[...], txt[here])
         gu[...] += part
@@ -159,7 +169,7 @@
     def _(span):
         gu[span] = gu_in[span]
 
-    @both_halves(txt)
+    @both_halves(txt, unrolled=True)
     def _(n, here):
         part, gv[here] = products(scalars, img[...], txt[here])
         gu[...] += part
@@ -169,17 +179,6 @@
 
 
 def fourth_kernel(scalars, img, txt, gu_in, gv_in, gu, piece_0, piece_1, piece_2, piece_3, gv):
-    past = gu_in.shape[0]
-
-    @each(past, 32)
-    def _(span):
-        gu[span] = gu_in[span]
-
-    @each(gu.shape[0] - past, 32)
-    def _(span):
-        there = pl.ds(pl.multiple_of(past + span.start, 32), 32)
-        gu[there] = jnp.zeros((32, gu.shape[1]), F32)
-
     @both_halves(txt)
     def _(n, here):
         part, term = products(scalars, img[...], txt[here])
@@ -197,21 +196,18 @@
                         out[span] = gv[there].astype(LOW)
 
 
-def fifth_kernel(scalars, img, txt, gu_in, gv_in, gu_0, gu_up, gu_down, gu_2, au, gv, gu):
+def fifth_kernel(scalars, img, txt, gu_in, gv_in, gu_0, gu_up, gu_down, gu_2, au, gv):
     size, past = txt.shape[0] // 2, img.shape[0] - 256
     part, term = products(scalars, img[...], txt[size:])
-    gu[...] = gu_in[...] + part
     gv[size:] = term + gv_in[size:]
-    part, term = products(scalars, img[past:], txt[0:size])
-    gu[past:] += part
+    last, term = products(scalars, img[past:], txt[0:size])
     gv[:size] = term + gv_in[:size]
-    places = (gu_0, 0), (gu_up, 0), (gu_down, 0), (au, 0), (gu_2, 0), (au, 128)
-    for n, (out, first) in enumerate(places):
-
-        @each(128, 32)
-        def _(span):
-            rows = gu[pl.ds(pl.multiple_of(n * 128 + span.start, 32), 32)]
-            out[pl.ds(pl.multiple_of(first + span.start, 32), 32)] = rows.astype(out.dtype)
+    for first, out in ((0, gu_0), (128, gu_up), (256, gu_down)):
+        out[...] = gu_in[first : first + 128] + part[first : first + 128]
+    au[:128] = (gu_in[384:past] + part[384:past]).astype(LOW)
+    last = last + gu_in[past:] + part[past:]
+    gu_2[...] = last[:128]
+    au[128:] = last[128:].astype(LOW)
 
 
 def local(image_emb, text_emb, temp, bias):
@@ -246,7 +242,7 @@
     img_2 = to_dev(img_0, zh=2)
     gu_first, sums_c, images = whole(
         first_kernel,
-        [(half, F32), (wide, F32), ((768, width), LOW)],
+        [((768, width), F32), (wide, F32), ((768, width), LOW)],
         *(scalars, img_again, img_n, ahead_0, own_c),
         scalars=True,
     )
@@ -277,6 +273,7 @@
         [(images.shape, F32)] + [(pair, LOW)] * 4,
         *(scalars, images, txt_s, gu_first, others),
         scalars=True,
+        aliases={3: 0},
         scratch=[pltpu.VMEM(half, F32)],
     )
     got = [to_dev(piece, core=1) for piece in pieces]
@@ -286,7 +283,6 @@
         *(scalars, images, txt_c, gu_all, sums_c),
         scalars=True,
         aliases={4: 5},
-        scratch=[pltpu.VMEM(images.shape, F32)],
     )
     back_n, *got, au, sums_c = fence(back_n, *got, au, sums_c)
     sums = [(rows, F32)] + [(rows, LOW)] * 3

time: 122 us -> 122 us (level)
  transfers between devices with their start and end apart: 30 -> 30, of which waited for: 12 -> 12; matrix products, arithmetic and copies ran while one was open for 0% -> 0% of each run, Pallas kernels for 22% -> 21%
where the time goes in v9:
time: 122 us; the launch traced here: 120 us
  starting transfers between devices  46.8 us (38%)
  waiting for transfers between devices  41 us (34%)
  Pallas kernels  27.2 us (22%)
  local copies, waits for them, and re-layouts  2.37 us (2%)
  between operations  2.18 us (2%)
    ppermute x23, starting transfers between devices, to_dev(): return lax.ppermute(block, 'dev', route)  38.4 us
    ppermute x23, waiting for transfers between devices, to_dev(): return lax.ppermute(block, 'dev', route)  28.8 us
    pallas_call x12, Pallas kernels, whole(): pl.pallas_call(kernel, in_specs=first + [VMEM] * (len(operands) - 1), out...  27.2 us
    ppermute x7, waiting for transfers between devices, to_group(): lax.ppermute(block, 'grp', [(i, (i + step) % GROUPS) for i in range(GROUP...  12.2 us
    ppermute x7, starting transfers between devices, to_group(): lax.ppermute(block, 'grp', [(i, (i + step) % GROUPS) for i in range(GROUP...  8.46 us
  transfers between devices with their start and end apart: 30, of which 12 were waited for; matrix products, arithmetic and copies ran while one was open for 0% of the time, Pallas kernels for 21%

profile of v9, /device:TPU:24, one launch (start us, length us, event | category | flops | bytes accessed | tf_op | source)
XLA Modules:
  0.0 120.1 jit_solution(2986306340790456900)
XLA Ops:
  1.9 2.8 %collective-permute-start.1 = (bf16[128,1152]{1,0:T(8,128)(2,1)S(1)}, bf16[128,1152]{1,0:T(8,128)(2,1)S(1)}, u32[]{:S(2)}, u32[]{:S(2)}) collective-permute-start(bf16[128,1152]{1,0:T(8,128)(2,1)S(1)} %shard_map.60.img_0), channel_id=1, source_target_pairs={{0,192},{32,224},{64,0},{96,32},{128,64},{160,96},{192,128},{224,1... | collective-permute-start | bytes 884744 | tf_op jit(solution)/shard_map/ppermute | solution.py:16
  6.1 2.0 %collective-permute-start.4 = (bf16[128,1152]{1,0:T(8,128)(2,1)S(1)}, bf16[128,1152]{1,0:T(8,128)(2,1)S(1)}, u32[]{:S(2)}, u32[]{:S(2)}) collective-permute-start(bf16[128,1152]{1,0:T(8,128)(2,1)S(1)} %shard_map.59.txt_0), channel_id=1, source_target_pairs={{0,32},{32,64},{64,96},{96,128},{128,160},{160,192},{192,224},{224... | collective-permute-start | bytes 884744 | tf_op jit(solution)/shard_map/ppermute | solution.py:16
  8.8 3.3 %collective-permute-start.6 = (bf16[128,1152]{1,0:T(8,128)(2,1)S(1)}, bf16[128,1152]{1,0:T(8,128)(2,1)S(1)}, u32[]{:S(2)}, u32[]{:S(2)}) collective-permute-start(bf16[128,1152]{1,0:T(8,128)(2,1)S(1)} %shard_map.60.img_0), channel_id=1, source_target_pairs={{0,8},{1,9},{2,10},{3,11},{4,12},{5,13},{6,14},{7,15},{8,16},{9,17... | collective-permute-start | bytes 884744 | tf_op jit(solution)/shard_map/ppermute | solution.py:25
  12.1 2.1 %collective-permute-start.5 = (bf16[128,1152]{1,0:T(8,128)(2,1)S(1)}, bf16[128,1152]{1,0:T(8,128)(2,1)S(1)}, u32[]{:S(2)}, u32[]{:S(2)}) collective-permute-start(bf16[128,1152]{1,0:T(8,128)(2,1)S(1)} %shard_map.60.img_0), channel_id=1, source_target_pairs={{0,24},{1,25},{2,26},{3,27},{4,28},{5,29},{6,30},{7,31},{8,0},{9,1... | collective-permute-start | bytes 884744 | tf_op jit(solution)/shard_map/ppermute | solution.py:25
  15.1 9.0 %collective-permute-done.4 = bf16[128,1152]{1,0:T(8,128)(2,1)S(1)} collective-permute-done((bf16[128,1152]{1,0:T(8,128)(2,1)S(1)}, bf16[128,1152]{1,0:T(8,128)(2,1)S(1)}, u32[]{:S(2)}, u32[]{:S(2)}) %collective-permute-start.4) | collective-permute-done | bytes 294944 | tf_op jit(solution)/shard_map/ppermute | solution.py:16
  25.4 7.9 %collective-permute-start.11 = (bf16[128,1152]{1,0:T(8,128)(2,1)S(1)}, bf16[128,1152]{1,0:T(8,128)(2,1)S(1)}, u32[]{:S(2)}, u32[]{:S(2)}) collective-permute-start(bf16[128,1152]{1,0:T(8,128)(2,1)S(1)} %shard_map.60.img_0), channel_id=1, source_target_pairs={{0,16},{1,17},{2,18},{3,19},{4,20},{5,21},{6,22},{7,23},{8,24},{9,... | collective-permute-start | bytes 884744 | tf_op jit(solution)/shard_map/ppermute | solution.py:25
  33.3 2.7 %collective-permute-done.6.img_down = bf16[128,1152]{1,0:T(8,128)(2,1)S(1)} collective-permute-done((bf16[128,1152]{1,0:T(8,128)(2,1)S(1)}, bf16[128,1152]{1,0:T(8,128)(2,1)S(1)}, u32[]{:S(2)}, u32[]{:S(2)}) %collective-permute-start.6) | collective-permute-done | bytes 294944 | tf_op jit(solution)/shard_map/ppermute | solution.py:25
  36.4 2.1 %collective-permute-start.9 = (bf16[128,1152]{1,0:T(8,128)(2,1)S(1)}, bf16[128,1152]{1,0:T(8,128)(2,1)S(1)}, u32[]{:S(2)}, u32[]{:S(2)}) collective-permute-start(bf16[128,1152]{1,0:T(8,128)(2,1)S(1)} %collective-permute-done.4), channel_id=1, source_target_pairs={{0,4},{1,5},{2,6},{3,7},{4,0},{5,1},{6,2},{7,3},{8,12},{9,13},{10,... | collective-permute-start | bytes 884744 | tf_op jit(solution)/shard_map/ppermute | solution.py:25
  38.5 2.1 %collective-permute-start.8 = (bf16[128,1152]{1,0:T(8,128)(2,1)S(1)}, bf16[128,1152]{1,0:T(8,128)(2,1)S(1)}, u32[]{:S(2)}, u32[]{:S(2)}) collective-permute-start(bf16[128,1152]{1,0:T(8,128)(2,1)S(1)} %collective-permute-done.4), channel_id=1, source_target_pairs={{0,2},{1,3},{2,4},{3,5},{4,6},{5,7},{6,0},{7,1},{8,10},{9,11},{10,... | collective-permute-start | bytes 884744 | tf_op jit(solution)/shard_map/ppermute | solution.py:25
  40.7 3.3 %shard_map.62 = (f32[768,1152]{1,0:T(8,128)S(1)}, f32[1024,1152]{1,0:T(8,128)S(1)}, bf16[768,1152]{1,0:T(8,128)(2,1)S(1)}) custom-call(f32[2]{0:T(128)S(1)} %pad_maximum_fusion.scalars, bf16[128,1152]{1,0:T(8,128)(2,1)S(1)} %get-tuple-element.88.img_0, bf16[256,1152]{1,0:T(8,128)(2,1)S(1)} %get-tuple-element.89.img_n, ...), custom_call_target="tpu_custom_call" | custom-call | flops 1 | bytes 1 | tf_op jit(solution)/shard_map/pallas_call | solution.py:37
  44.0 1.7 %collective-permute-done.9 = bf16[128,1152]{1,0:T(8,128)(2,1)S(1)} collective-permute-done((bf16[128,1152]{1,0:T(8,128)(2,1)S(1)}, bf16[128,1152]{1,0:T(8,128)(2,1)S(1)}, u32[]{:S(2)}, u32[]{:S(2)}) %collective-permute-start.9) | collective-permute-done | bytes 294944 | tf_op jit(solution)/shard_map/ppermute | solution.py:25
  46.4 2.4 %collective-permute-done.7 = bf16[128,1152]{1,0:T(8,128)(2,1)S(1)} collective-permute-done((bf16[128,1152]{1,0:T(8,128)(2,1)S(1)}, bf16[128,1152]{1,0:T(8,128)(2,1)S(1)}, u32[]{:S(2)}, u32[]{:S(2)}) %collective-permute-start.7) | collective-permute-done | bytes 294944 | tf_op jit(solution)/shard_map/ppermute | solution.py:25
  49.9 3.8 %shard_map.63 = (f32[256,1152]{1,0:T(8,128)S(1)}, f32[1024,1152]{1,0:T(8,128)S(1)}) custom-call(f32[2]{0:T(128)S(1)} %pad_maximum_fusion.scalars, bf16[256,1152]{1,0:T(8,128)(2,1)S(1)} %collective-permute-done.10.img, bf16[1024,1152]{1,0:T(8,128)(2,1)S(1)} %constant_dynamic-update-slice_fusion.txt, ...), custom_call_target="tpu_custom_call", output_to_operand_aliasing={{1}: (3, {})} | custom-call | flops 1 | bytes 1 | tf_op jit(solution)/shard_map/pallas_call | solution.py:37
  53.7 3.0 %shard_map.64 = (bf16[272,1152]{1,0:T(8,128)(2,1)S(1)}, f32[1024,1152]{1,0:T(8,128)S(1)}) custom-call(f32[2]{0:T(128)S(1)} %pad_maximum_fusion.scalars, bf16[256,1152]{1,0:T(8,128)(2,1)S(1)} %collective-permute-done.10.img, bf16[1024,1152]{1,0:T(8,128)(2,1)S(1)} %collective-permute-done.13.txt, f32[256,1152]{1,0:T(8,128)S(1)} %get-tuple-element.103.gu_in), custom_call_target="tpu_custom_call" | custom-call | flops 1 | bytes 1 | tf_op jit(solution)/shard_map/pallas_call | solution.py:37
  58.6 7.8 %shard_map.65 = (f32[768,1152]{1,0:T(8,128)S(1)}, bf16[256,1152]{1,0:T(8,128)(2,1)S(1)}, bf16[256,1152]{1,0:T(8,128)(2,1)S(1)}, bf16[256,1152]{1,0:T(8,128)(2,1)S(1)}, bf16[256,1152]{1,0:T(8,128)(2,1)S(1)}) custom-call(f32[2]{0:T(128)S(1)} %pad_maximum_fusion.scalars, ...), custom_call_target="tpu_custom_call", output_to_operand_aliasing={{0}: (3, {})} | custom-call | flops 1 | bytes 1 | tf_op jit(solution)/shard_map/pallas_call | solution.py:37
  67.5 5.6 %shard_map.66 = (f32[128,1152]{1,0:T(8,128)S(1)}, f32[128,1152]{1,0:T(8,128)S(1)}, f32[128,1152]{1,0:T(8,128)S(1)}, f32[128,1152]{1,0:T(8,128)S(1)}, bf16[256,11...) custom-call(f32[2]{0:T(128)S(1)} %pad_maximum_fusion.scalars, ...), custom_call_target="tpu_custom_call", output_to_operand_aliasing={{5}: (4, {})} | custom-call | flops 1 | bytes 1 | tf_op jit(solution)/shard_map/pallas_call | solution.py:37
  75.5 7.5 %collective-permute-start.20 = (bf16[128,1152]{1,0:T(8,128)(2,1)S(1)}, bf16[128,1152]{1,0:T(8,128)(2,1)S(1)}, u32[]{:S(2)}, u32[]{:S(2)}) collective-permute-start(bf16[128,1152]{1,0:T(8,128)(2,1)S(1)} %get-tuple-element.128), channel_id=1, source_target_pairs={{0,8},{1,9},{2,10},{3,11},{4,12},{5,13},{6,14},{7,15},{8,16},{9,17... | collective-permute-start | bytes 884744 | tf_op jit(solution)/shard_map/ppermute | solution.py:25
  84.8 8.3 %collective-permute-done.20.refs_1_ = bf16[128,1152]{1,0:T(8,128)(2,1)S(1)} collective-permute-done((bf16[128,1152]{1,0:T(8,128)(2,1)S(1)}, bf16[128,1152]{1,0:T(8,128)(2,1)S(1)}, u32[]{:S(2)}, u32[]{:S(2)}) %collective-permute-start.20) | collective-permute-done | bytes 294944 | tf_op jit(solution)/shard_map/ppermute | solution.py:25
  93.8 4.8 %collective-permute-done.22 = bf16[128,1152]{1,0:T(8,128)(2,1)S(1)} collective-permute-done((bf16[128,1152]{1,0:T(8,128)(2,1)S(1)}, bf16[128,1152]{1,0:T(8,128)(2,1)S(1)}, u32[]{:S(2)}, u32[]{:S(2)}) %collective-permute-start.22) | collective-permute-done | bytes 294944 | tf_op jit(solution)/shard_map/ppermute | solution.py:25
  98.9 3.7 %collective-permute-start.25 = (bf16[128,1152]{1,0:T(8,128)(2,1)S(1)}, bf16[128,1152]{1,0:T(8,128)(2,1)S(1)}, u32[]{:S(2)}, u32[]{:S(2)}) collective-permute-start(bf16[128,1152]{1,0:T(8,128)(2,1)S(1)} %get-tuple-element.146), channel_id=1, source_target_pairs={{0,16},{1,17},{2,18},{3,19},{4,20},{5,21},{6,22},{7,23},{8,24},{9,... | collective-permute-start | bytes 884744 | tf_op jit(solution)/shard_map/ppermute | solution.py:25
  103.4 2.6 %collective-permute-start.28 = (bf16[128,1152]{1,0:T(8,128)(2,1)S(1)}, bf16[128,1152]{1,0:T(8,128)(2,1)S(1)}, u32[]{:S(2)}, u32[]{:S(2)}) collective-permute-start(bf16[128,1152]{1,0:T(8,128)(2,1)S(1)} %get-tuple-element.152), channel_id=1, source_target_pairs={{0,6},{1,7},{2,0},{3,1},{4,2},{5,3},{6,4},{7,5},{8,14},{9,15},{10,... | collective-permute-start | bytes 884744 | tf_op jit(solution)/shard_map/ppermute | solution.py:25
  106.0 2.1 %collective-permute-start.29 = (bf16[128,1152]{1,0:T(8,128)(2,1)S(1)}, bf16[128,1152]{1,0:T(8,128)(2,1)S(1)}, u32[]{:S(2)}, u32[]{:S(2)}) collective-permute-start(bf16[128,1152]{1,0:T(8,128)(2,1)S(1)} %get-tuple-element.153), channel_id=1, source_target_pairs={{0,4},{1,5},{2,6},{3,7},{4,0},{5,1},{6,2},{7,3},{8,12},{9,13},{10,... | collective-permute-start | bytes 884744 | tf_op jit(solution)/shard_map/ppermute | solution.py:25
  108.0 7.4 %collective-permute-done.25.refs_0_ = bf16[128,1152]{1,0:T(8,128)(2,1)S(1)} collective-permute-done((bf16[128,1152]{1,0:T(8,128)(2,1)S(1)}, bf16[128,1152]{1,0:T(8,128)(2,1)S(1)}, u32[]{:S(2)}, u32[]{:S(2)}) %collective-permute-start.25) | collective-permute-done | bytes 294944 | tf_op jit(solution)/shard_map/ppermute | solution.py:25
  116.6 2.3 %collective-permute-done.26.refs_0_ = bf16[128,1152]{1,0:T(8,128)(2,1)S(1)} collective-permute-done((bf16[128,1152]{1,0:T(8,128)(2,1)S(1)}, bf16[128,1152]{1,0:T(8,128)(2,1)S(1)}, u32[]{:S(2)}, u32[]{:S(2)}) %collective-permute-start.26) | collective-permute-done | bytes 294944 | tf_op jit(solution)/shard_map/ppermute | solution.py:16
  (66 shorter events, 17.5 us)
Async XLA Ops:
  1.9 12.3 %collective-permute-start.1 = (bf16[128,1152]{1,0:T(8,128)(2,1)S(1)}, bf16[128,1152]{1,0:T(8,128)(2,1)S(1)}, u32[]{:S(2)}, u32[]{:S(2)}) collective-permute-start(bf16[128,1152]{1,0:T(8,128)(2,1)S(1)} %shard_map.60.img_0), channel_id=1, source_target_pairs={{0,192},{32,224},{64,0},{96,32},{128,64},{160,96},{192,128},{224,1... | collective-permute-start | bytes 884744 | tf_op jit(solution)/shard_map/ppermute | solution.py:16
  6.1 18.0 %collective-permute-start.4 = (bf16[128,1152]{1,0:T(8,128)(2,1)S(1)}, bf16[128,1152]{1,0:T(8,128)(2,1)S(1)}, u32[]{:S(2)}, u32[]{:S(2)}) collective-permute-start(bf16[128,1152]{1,0:T(8,128)(2,1)S(1)} %shard_map.59.txt_0), channel_id=1, source_target_pairs={{0,32},{32,64},{64,96},{96,128},{128,160},{160,192},{192,224},{224... | collective-permute-start | bytes 884744 | tf_op jit(solution)/shard_map/ppermute | solution.py:16
  8.1 17.4 %collective-permute-start = (bf16[128,1152]{1,0:T(8,128)(2,1)S(1)}, bf16[128,1152]{1,0:T(8,128)(2,1)S(1)}, u32[]{:S(2)}, u32[]{:S(2)}) collective-permute-start(bf16[128,1152]{1,0:T(8,128)(2,1)S(1)} %shard_map.59.txt_0), channel_id=1, source_target_pairs={{0,6},{1,7},{2,0},{3,1},{4,2},{5,3},{6,4},{7,5},{8,14},{9,15},{10,... | collective-permute-start | bytes 884744 | tf_op jit(solution)/shard_map/ppermute | solution.py:25
  8.8 27.2 %collective-permute-start.6 = (bf16[128,1152]{1,0:T(8,128)(2,1)S(1)}, bf16[128,1152]{1,0:T(8,128)(2,1)S(1)}, u32[]{:S(2)}, u32[]{:S(2)}) collective-permute-start(bf16[128,1152]{1,0:T(8,128)(2,1)S(1)} %shard_map.60.img_0), channel_id=1, source_target_pairs={{0,8},{1,9},{2,10},{3,11},{4,12},{5,13},{6,14},{7,15},{8,16},{9,17... | collective-permute-start | bytes 884744 | tf_op jit(solution)/shard_map/ppermute | solution.py:25
  12.1 23.9 %collective-permute-start.5 = (bf16[128,1152]{1,0:T(8,128)(2,1)S(1)}, bf16[128,1152]{1,0:T(8,128)(2,1)S(1)}, u32[]{:S(2)}, u32[]{:S(2)}) collective-permute-start(bf16[128,1152]{1,0:T(8,128)(2,1)S(1)} %shard_map.60.img_0), channel_id=1, source_target_pairs={{0,24},{1,25},{2,26},{3,27},{4,28},{5,29},{6,30},{7,31},{8,0},{9,1... | collective-permute-start | bytes 884744 | tf_op jit(solution)/shard_map/ppermute | solution.py:25
  14.2 21.8 %collective-permute-start.3 = (bf16[128,1152]{1,0:T(8,128)(2,1)S(1)}, bf16[128,1152]{1,0:T(8,128)(2,1)S(1)}, u32[]{:S(2)}, u32[]{:S(2)}) collective-permute-start(bf16[128,1152]{1,0:T(8,128)(2,1)S(1)} %shard_map.59.txt_0), channel_id=1, source_target_pairs={{0,4},{1,5},{2,6},{3,7},{4,0},{5,1},{6,2},{7,3},{8,12},{9,13},{10,... | collective-permute-start | bytes 884744 | tf_op jit(solution)/shard_map/ppermute | solution.py:25
  24.1 11.9 %collective-permute-start.2 = (bf16[128,1152]{1,0:T(8,128)(2,1)S(1)}, bf16[128,1152]{1,0:T(8,128)(2,1)S(1)}, u32[]{:S(2)}, u32[]{:S(2)}) collective-permute-start(bf16[128,1152]{1,0:T(8,128)(2,1)S(1)} %shard_map.59.txt_0), channel_id=1, source_target_pairs={{0,2},{1,3},{2,4},{3,5},{4,6},{5,7},{6,0},{7,1},{8,10},{9,11},{10,... | collective-permute-start | bytes 884744 | tf_op jit(solution)/shard_map/ppermute | solution.py:25
  25.4 18.6 %collective-permute-start.11 = (bf16[128,1152]{1,0:T(8,128)(2,1)S(1)}, bf16[128,1152]{1,0:T(8,128)(2,1)S(1)}, u32[]{:S(2)}, u32[]{:S(2)}) collective-permute-start(bf16[128,1152]{1,0:T(8,128)(2,1)S(1)} %shard_map.60.img_0), channel_id=1, source_target_pairs={{0,16},{1,17},{2,18},{3,19},{4,20},{5,21},{6,22},{7,23},{8,24},{9,... | collective-permute-start | bytes 884744 | tf_op jit(solution)/shard_map/ppermute | solution.py:25
  36.2 12.6 %collective-permute-start.10 = (bf16[256,1152]{1,0:T(8,128)(2,1)S(1)}, bf16[256,1152]{1,0:T(8,128)(2,1)S(1)}, u32[]{:S(2)}, u32[]{:S(2)}) collective-permute-start(bf16[256,1152]{1,0:T(8,128)(2,1)S(1)} %get-tuple-element.89.img_n), channel_id=1, source_target_pairs={{0,192},{32,224},{64,0},{96,32},{128,64},{160,96},{192,128},{224,1... | collective-permute-start | bytes 1769480 | tf_op jit(solution)/shard_map/ppermute | solution.py:16
  36.4 9.3 %collective-permute-start.9 = (bf16[128,1152]{1,0:T(8,128)(2,1)S(1)}, bf16[128,1152]{1,0:T(8,128)(2,1)S(1)}, u32[]{:S(2)}, u32[]{:S(2)}) collective-permute-start(bf16[128,1152]{1,0:T(8,128)(2,1)S(1)} %collective-permute-done.4), channel_id=1, source_target_pairs={{0,4},{1,5},{2,6},{3,7},{4,0},{5,1},{6,2},{7,3},{8,12},{9,13},{10,... | collective-permute-start | bytes 884744 | tf_op jit(solution)/shard_map/ppermute | solution.py:25
  40.6 8.3 %collective-permute-start.7 = (bf16[128,1152]{1,0:T(8,128)(2,1)S(1)}, bf16[128,1152]{1,0:T(8,128)(2,1)S(1)}, u32[]{:S(2)}, u32[]{:S(2)}) collective-permute-start(bf16[128,1152]{1,0:T(8,128)(2,1)S(1)} %collective-permute-done.4), channel_id=1, source_target_pairs={{0,6},{1,7},{2,0},{3,1},{4,2},{5,3},{6,4},{7,5},{8,14},{9,15},{10,... | collective-permute-start | bytes 884744 | tf_op jit(solution)/shard_map/ppermute | solution.py:25
  49.1 9.4 %collective-permute-start.12 = (bf16[128,1152]{1,0:T(8,128)(2,1)S(1)}, bf16[128,1152]{1,0:T(8,128)(2,1)S(1)}, u32[]{:S(2)}, u32[]{:S(2)}) collective-permute-start(bf16[128,1152]{1,0:T(8,128)(2,1)S(1)} %collective-permute-done.11), channel_id=1, source_target_pairs={{0,192},{32,224},{64,0},{96,32},{128,64},{160,96},{192,128},{224,1... | collective-permute-start | bytes 884744 | tf_op jit(solution)/shard_map/ppermute | solution.py:16
  56.8 17.3 %collective-permute-start.14 = (bf16[272,1152]{1,0:T(8,128)(2,1)S(1)}, bf16[272,1152]{1,0:T(8,128)(2,1)S(1)}, u32[]{:S(2)}, u32[]{:S(2)}) collective-permute-start(bf16[272,1152]{1,0:T(8,128)(2,1)S(1)} %get-tuple-element.110), channel_id=1, source_target_pairs={{0,64},{32,96},{64,128},{96,160},{128,192},{160,224},{192,0},{224,... | collective-permute-start | bytes 1880072 | tf_op jit(solution)/shard_map/ppermute | solution.py:16
  74.5 8.5 %collective-permute-start.19 = (bf16[128,1152]{1,0:T(8,128)(2,1)S(1)}, bf16[128,1152]{1,0:T(8,128)(2,1)S(1)}, u32[]{:S(2)}, u32[]{:S(2)}) collective-permute-start(bf16[128,1152]{1,0:T(8,128)(2,1)S(1)} %get-tuple-element.125), channel_id=1, source_target_pairs={{0,2},{1,3},{2,4},{3,5},{4,6},{5,7},{6,0},{7,1},{8,10},{9,11},{10,... | collective-permute-start | bytes 884744 | tf_op jit(solution)/shard_map/ppermute | solution.py:25
  75.1 23.5 %collective-permute-start.23 = (bf16[256,1152]{1,0:T(8,128)(2,1)S(1)}, bf16[256,1152]{1,0:T(8,128)(2,1)S(1)}, u32[]{:S(2)}, u32[]{:S(2)}) collective-permute-start(bf16[256,1152]{1,0:T(8,128)(2,1)S(1)} %get-tuple-element.131), channel_id=1, source_target_pairs={{0,64},{32,96},{64,128},{96,160},{128,192},{160,224},{192,0},{224,... | collective-permute-start | bytes 1769480 | tf_op jit(solution)/shard_map/ppermute | solution.py:16
  75.5 17.7 %collective-permute-start.20 = (bf16[128,1152]{1,0:T(8,128)(2,1)S(1)}, bf16[128,1152]{1,0:T(8,128)(2,1)S(1)}, u32[]{:S(2)}, u32[]{:S(2)}) collective-permute-start(bf16[128,1152]{1,0:T(8,128)(2,1)S(1)} %get-tuple-element.128), channel_id=1, source_target_pairs={{0,8},{1,9},{2,10},{3,11},{4,12},{5,13},{6,14},{7,15},{8,16},{9,17... | collective-permute-start | bytes 884744 | tf_op jit(solution)/shard_map/ppermute | solution.py:25
  82.9 10.9 %collective-permute-start.21 = (bf16[128,1152]{1,0:T(8,128)(2,1)S(1)}, bf16[128,1152]{1,0:T(8,128)(2,1)S(1)}, u32[]{:S(2)}, u32[]{:S(2)}) collective-permute-start(bf16[128,1152]{1,0:T(8,128)(2,1)S(1)} %get-tuple-element.129), channel_id=1, source_target_pairs={{0,24},{1,25},{2,26},{3,27},{4,28},{5,29},{6,30},{7,31},{8,0},{9,1... | collective-permute-start | bytes 884744 | tf_op jit(solution)/shard_map/ppermute | solution.py:25
  82.9 15.7 %collective-permute-start.22 = (bf16[128,1152]{1,0:T(8,128)(2,1)S(1)}, bf16[128,1152]{1,0:T(8,128)(2,1)S(1)}, u32[]{:S(2)}, u32[]{:S(2)}) collective-permute-start(bf16[128,1152]{1,0:T(8,128)(2,1)S(1)} %get-tuple-element.130), channel_id=1, source_target_pairs={{0,6},{1,7},{2,0},{3,1},{4,2},{5,3},{6,4},{7,5},{8,14},{9,15},{10,... | collective-permute-start | bytes 884744 | tf_op jit(solution)/shard_map/ppermute | solution.py:25
  83.0 15.7 %collective-permute-start.24 = (bf16[128,1152]{1,0:T(8,128)(2,1)S(1)}, bf16[128,1152]{1,0:T(8,128)(2,1)S(1)}, u32[]{:S(2)}, u32[]{:S(2)}) collective-permute-start(bf16[128,1152]{1,0:T(8,128)(2,1)S(1)} %get-tuple-element.132), channel_id=1, source_target_pairs={{0,4},{1,5},{2,6},{3,7},{4,0},{5,1},{6,2},{7,3},{8,12},{9,13},{10,... | collective-permute-start | bytes 884744 | tf_op jit(solution)/shard_map/ppermute | solution.py:25
  98.9 16.6 %collective-permute-start.25 = (bf16[128,1152]{1,0:T(8,128)(2,1)S(1)}, bf16[128,1152]{1,0:T(8,128)(2,1)S(1)}, u32[]{:S(2)}, u32[]{:S(2)}) collective-permute-start(bf16[128,1152]{1,0:T(8,128)(2,1)S(1)} %get-tuple-element.146), channel_id=1, source_target_pairs={{0,16},{1,17},{2,18},{3,19},{4,20},{5,21},{6,22},{7,23},{8,24},{9,... | collective-permute-start | bytes 884744 | tf_op jit(solution)/shard_map/ppermute | solution.py:25
  102.6 16.3 %collective-permute-start.26 = (bf16[128,1152]{1,0:T(8,128)(2,1)S(1)}, bf16[128,1152]{1,0:T(8,128)(2,1)S(1)}, u32[]{:S(2)}, u32[]{:S(2)}) collective-permute-start(bf16[128,1152]{1,0:T(8,128)(2,1)S(1)} %get-tuple-element.150), channel_id=1, source_target_pairs={{0,224},{32,0},{64,32},{96,64},{128,96},{160,128},{192,160},{224,1... | collective-permute-start | bytes 884744 | tf_op jit(solution)/shard_map/ppermute | solution.py:16
  103.4 15.5 %collective-permute-start.27 = (bf16[128,1152]{1,0:T(8,128)(2,1)S(1)}, bf16[128,1152]{1,0:T(8,128)(2,1)S(1)}, u32[]{:S(2)}, u32[]{:S(2)}) collective-permute-start(bf16[128,1152]{1,0:T(8,128)(2,1)S(1)} %get-tuple-element.151), channel_id=1, source_target_pairs={{0,2},{1,3},{2,4},{3,5},{4,6},{5,7},{6,0},{7,1},{8,10},{9,11},{10,... | collective-permute-start | bytes 884744 | tf_op jit(solution)/shard_map/ppermute | solution.py:25
  103.4 15.5 %collective-permute-start.28 = (bf16[128,1152]{1,0:T(8,128)(2,1)S(1)}, bf16[128,1152]{1,0:T(8,128)(2,1)S(1)}, u32[]{:S(2)}, u32[]{:S(2)}) collective-permute-start(bf16[128,1152]{1,0:T(8,128)(2,1)S(1)} %get-tuple-element.152), channel_id=1, source_target_pairs={{0,6},{1,7},{2,0},{3,1},{4,2},{5,3},{6,4},{7,5},{8,14},{9,15},{10,... | collective-permute-start | bytes 884744 | tf_op jit(solution)/shard_map/ppermute | solution.py:25
  106.0 12.9 %collective-permute-start.29 = (bf16[128,1152]{1,0:T(8,128)(2,1)S(1)}, bf16[128,1152]{1,0:T(8,128)(2,1)S(1)}, u32[]{:S(2)}, u32[]{:S(2)}) collective-permute-start(bf16[128,1152]{1,0:T(8,128)(2,1)S(1)} %get-tuple-element.153), channel_id=1, source_target_pairs={{0,4},{1,5},{2,6},{3,7},{4,0},{5,1},{6,2},{7,3},{8,12},{9,13},{10,... | collective-permute-start | bytes 884744 | tf_op jit(solution)/shard_map/ppermute | solution.py:25
  (10 other events, 91.1 us)

commit v10 on v9

--- a/solution.py
+++ b/solution.py
@@ -136,15 +136,10 @@
         gv[there] = jnp.zeros((32, gv.shape[1]), F32)
 
 
-def both_halves(txt, unrolled=False):
+def both_halves(txt):
     size = txt.shape[0] // 2
 
     def over(body):
-        if unrolled:
-            for n in (0, 1):
-                body(n, slice(n * size, (n + 1) * size))
-            return
-
         @pl.loop(0, 2)
         def _(n):
             body(n, pl.ds(pl.multiple_of(n * size, size), size))
@@ -153,28 +148,18 @@
 
 
 def second_kernel(scalars, img, txt, gv_in, gu, gv):
-    @each(gu.shape[0], 32)
-    def _(span):
-        gu[span] = jnp.zeros((32, gu.shape[1]), F32)
-
-    @both_halves(txt, unrolled=True)
-    def _(n, here):
-        part, term = products(scalars, img[...], txt[here])
-        gu[...] += part
-        gv[here] = term + gv_in[here]
-
-
-def third_kernel(scalars, img, txt, gu_in, gu_n, gv, gu):
-    @each(gu.shape[0], 32)
-    def _(span):
-        gu[span] = gu_in[span]
-
-    @both_halves(txt, unrolled=True)
-    def _(n, here):
-        part, gv[here] = products(scalars, img[...], txt[here])
-        gu[...] += part
-
-    gu_n[:256] = gu[...].astype(LOW)
+    size = txt.shape[0] // 2
+    for n in (0, size):
+        part, term = products(scalars, img[...], txt[n : n + size])
+        gu[...] = part if n == 0 else gu[...] + part
+        gv[n : n + size] = term + gv_in[n : n + size]
+
+
+def third_kernel(scalars, img, txt, gu_in, gu_n, gv):
+    size = txt.shape[0] // 2
+    first, gv[:size] = products(scalars, img[...], txt[:size])
+    second, gv[size:] = products(scalars, img[...], txt[size:])
+    gu_n[:256] = (gu_in[...] + first + second).astype(LOW)
     gu_n[256:] = jnp.zeros((16, gu_n.shape[1]), LOW)
 
 
@@ -264,7 +249,6 @@
         [((272, width), LOW), (wide, F32)],
         *(scalars, ahead_n, txt_s, gu_n),
         scalars=True,
-        scratch=[pltpu.VMEM(pair, F32)],
     )
     back_n = to_group(au_n, 2)
     images = lax.dynamic_update_slice(images, jnp.concatenate([img_2, ahead_2], axis=0), (512, 0))

time: 122 us -> 122 us (level)
  no operation moved by 1% of the time
where the time goes in v10:
time: 122 us; the launch traced here: 120 us
  starting transfers between devices  46 us (38%)
  waiting for transfers between devices  42 us (34%)
  Pallas kernels  27 us (22%)
  local copies, waits for them, and re-layouts  2.37 us (2%)
  between operations  2.18 us (2%)
    ppermute x23, starting transfers between devices, to_dev(): return lax.ppermute(block, 'dev', route)  37.5 us
    ppermute x23, waiting for transfers between devices, to_dev(): return lax.ppermute(block, 'dev', route)  29.7 us
    pallas_call x12, Pallas kernels, whole(): pl.pallas_call(kernel, in_specs=first + [VMEM] * (len(operands) - 1), out...  27 us
    ppermute x7, waiting for transfers between devices, to_group(): lax.ppermute(block, 'grp', [(i, (i + step) % GROUPS) for i in range(GROUP...  12.3 us
    ppermute x7, starting transfers between devices, to_group(): lax.ppermute(block, 'grp', [(i, (i + step) % GROUPS) for i in range(GROUP...  8.58 us
  transfers between devices with their start and end apart: 30, of which 12 were waited for; matrix products, arithmetic and copies ran while one was open for 0% of the time, Pallas kernels for 21%

profile of v10, /device:TPU:24, one launch (start us, length us, event | category | flops | bytes accessed | tf_op | source)
XLA Modules:
  0.0 120.1 jit_solution(17414527333804643960)
XLA Ops:
  1.9 2.8 %collective-permute-start.1 = (bf16[128,1152]{1,0:T(8,128)(2,1)S(1)}, bf16[128,1152]{1,0:T(8,128)(2,1)S(1)}, u32[]{:S(2)}, u32[]{:S(2)}) collective-permute-start(bf16[128,1152]{1,0:T(8,128)(2,1)S(1)} %shard_map.60.img_0), channel_id=1, source_target_pairs={{0,192},{32,224},{64,0},{96,32},{128,64},{160,96},{192,128},{224,1... | collective-permute-start | bytes 884744 | tf_op jit(solution)/shard_map/ppermute | solution.py:16
  6.1 2.0 %collective-permute-start.4 = (bf16[128,1152]{1,0:T(8,128)(2,1)S(1)}, bf16[128,1152]{1,0:T(8,128)(2,1)S(1)}, u32[]{:S(2)}, u32[]{:S(2)}) collective-permute-start(bf16[128,1152]{1,0:T(8,128)(2,1)S(1)} %shard_map.59.txt_0), channel_id=1, source_target_pairs={{0,32},{32,64},{64,96},{96,128},{128,160},{160,192},{192,224},{224... | collective-permute-start | bytes 884744 | tf_op jit(solution)/shard_map/ppermute | solution.py:16
  8.8 3.3 %collective-permute-start.6 = (bf16[128,1152]{1,0:T(8,128)(2,1)S(1)}, bf16[128,1152]{1,0:T(8,128)(2,1)S(1)}, u32[]{:S(2)}, u32[]{:S(2)}) collective-permute-start(bf16[128,1152]{1,0:T(8,128)(2,1)S(1)} %shard_map.60.img_0), channel_id=1, source_target_pairs={{0,8},{1,9},{2,10},{3,11},{4,12},{5,13},{6,14},{7,15},{8,16},{9,17... | collective-permute-start | bytes 884744 | tf_op jit(solution)/shard_map/ppermute | solution.py:25
  12.1 2.1 %collective-permute-start.5 = (bf16[128,1152]{1,0:T(8,128)(2,1)S(1)}, bf16[128,1152]{1,0:T(8,128)(2,1)S(1)}, u32[]{:S(2)}, u32[]{:S(2)}) collective-permute-start(bf16[128,1152]{1,0:T(8,128)(2,1)S(1)} %shard_map.60.img_0), channel_id=1, source_target_pairs={{0,24},{1,25},{2,26},{3,27},{4,28},{5,29},{6,30},{7,31},{8,0},{9,1... | collective-permute-start | bytes 884744 | tf_op jit(solution)/shard_map/ppermute | solution.py:25
  15.1 9.0 %collective-permute-done.4 = bf16[128,1152]{1,0:T(8,128)(2,1)S(1)} collective-permute-done((bf16[128,1152]{1,0:T(8,128)(2,1)S(1)}, bf16[128,1152]{1,0:T(8,128)(2,1)S(1)}, u32[]{:S(2)}, u32[]{:S(2)}) %collective-permute-start.4) | collective-permute-done | bytes 294944 | tf_op jit(solution)/shard_map/ppermute | solution.py:16
  25.4 7.9 %collective-permute-start.11 = (bf16[128,1152]{1,0:T(8,128)(2,1)S(1)}, bf16[128,1152]{1,0:T(8,128)(2,1)S(1)}, u32[]{:S(2)}, u32[]{:S(2)}) collective-permute-start(bf16[128,1152]{1,0:T(8,128)(2,1)S(1)} %shard_map.60.img_0), channel_id=1, source_target_pairs={{0,16},{1,17},{2,18},{3,19},{4,20},{5,21},{6,22},{7,23},{8,24},{9,... | collective-permute-start | bytes 884744 | tf_op jit(solution)/shard_map/ppermute | solution.py:25
  33.3 2.7 %collective-permute-done.6.img_down = bf16[128,1152]{1,0:T(8,128)(2,1)S(1)} collective-permute-done((bf16[128,1152]{1,0:T(8,128)(2,1)S(1)}, bf16[128,1152]{1,0:T(8,128)(2,1)S(1)}, u32[]{:S(2)}, u32[]{:S(2)}) %collective-permute-start.6) | collective-permute-done | bytes 294944 | tf_op jit(solution)/shard_map/ppermute | solution.py:25
  36.4 2.1 %collective-permute-start.9 = (bf16[128,1152]{1,0:T(8,128)(2,1)S(1)}, bf16[128,1152]{1,0:T(8,128)(2,1)S(1)}, u32[]{:S(2)}, u32[]{:S(2)}) collective-permute-start(bf16[128,1152]{1,0:T(8,128)(2,1)S(1)} %collective-permute-done.4), channel_id=1, source_target_pairs={{0,4},{1,5},{2,6},{3,7},{4,0},{5,1},{6,2},{7,3},{8,12},{9,13},{10,... | collective-permute-start | bytes 884744 | tf_op jit(solution)/shard_map/ppermute | solution.py:25
  38.5 2.1 %collective-permute-start.8 = (bf16[128,1152]{1,0:T(8,128)(2,1)S(1)}, bf16[128,1152]{1,0:T(8,128)(2,1)S(1)}, u32[]{:S(2)}, u32[]{:S(2)}) collective-permute-start(bf16[128,1152]{1,0:T(8,128)(2,1)S(1)} %collective-permute-done.4), channel_id=1, source_target_pairs={{0,2},{1,3},{2,4},{3,5},{4,6},{5,7},{6,0},{7,1},{8,10},{9,11},{10,... | collective-permute-start | bytes 884744 | tf_op jit(solution)/shard_map/ppermute | solution.py:25
  40.7 3.3 %shard_map.62 = (f32[768,1152]{1,0:T(8,128)S(1)}, f32[1024,1152]{1,0:T(8,128)S(1)}, bf16[768,1152]{1,0:T(8,128)(2,1)S(1)}) custom-call(f32[2]{0:T(128)S(1)} %pad_maximum_fusion.scalars, bf16[128,1152]{1,0:T(8,128)(2,1)S(1)} %get-tuple-element.88.img_0, bf16[256,1152]{1,0:T(8,128)(2,1)S(1)} %get-tuple-element.89.img_n, ...), custom_call_target="tpu_custom_call" | custom-call | flops 1 | bytes 1 | tf_op jit(solution)/shard_map/pallas_call | solution.py:37
  46.4 2.4 %collective-permute-done.7 = bf16[128,1152]{1,0:T(8,128)(2,1)S(1)} collective-permute-done((bf16[128,1152]{1,0:T(8,128)(2,1)S(1)}, bf16[128,1152]{1,0:T(8,128)(2,1)S(1)}, u32[]{:S(2)}, u32[]{:S(2)}) %collective-permute-start.7) | collective-permute-done | bytes 294944 | tf_op jit(solution)/shard_map/ppermute | solution.py:25
  49.9 3.8 %shard_map.63 = (f32[256,1152]{1,0:T(8,128)S(1)}, f32[1024,1152]{1,0:T(8,128)S(1)}) custom-call(f32[2]{0:T(128)S(1)} %pad_maximum_fusion.scalars, bf16[256,1152]{1,0:T(8,128)(2,1)S(1)} %collective-permute-done.10.img, bf16[1024,1152]{1,0:T(8,128)(2,1)S(1)} %constant_dynamic-update-slice_fusion.txt, ...), custom_call_target="tpu_custom_call", output_to_operand_aliasing={{1}: (3, {})} | custom-call | flops 1 | bytes 1 | tf_op jit(solution)/shard_map/pallas_call | solution.py:37
  53.6 2.9 %shard_map.64 = (bf16[272,1152]{1,0:T(8,128)(2,1)S(1)}, f32[1024,1152]{1,0:T(8,128)S(1)}) custom-call(f32[2]{0:T(128)S(1)} %pad_maximum_fusion.scalars, bf16[256,1152]{1,0:T(8,128)(2,1)S(1)} %collective-permute-done.10.img, bf16[1024,1152]{1,0:T(8,128)(2,1)S(1)} %collective-permute-done.13.txt, f32[256,1152]{1,0:T(8,128)S(1)} %get-tuple-element.103.gu_in), custom_call_target="tpu_custom_call" | custom-call | flops 1 | bytes 1 | tf_op jit(solution)/shard_map/pallas_call | solution.py:37
  56.6 1.7 %collective-permute-start.14 = (bf16[272,1152]{1,0:T(8,128)(2,1)S(1)}, bf16[272,1152]{1,0:T(8,128)(2,1)S(1)}, u32[]{:S(2)}, u32[]{:S(2)}) collective-permute-start(bf16[272,1152]{1,0:T(8,128)(2,1)S(1)} %get-tuple-element.110), channel_id=1, source_target_pairs={{0,64},{32,96},{64,128},{96,160},{128,192},{160,224},{192,0},{224,... | collective-permute-start | bytes 1880072 | tf_op jit(solution)/shard_map/ppermute | solution.py:16
  58.6 7.8 %shard_map.65 = (f32[768,1152]{1,0:T(8,128)S(1)}, bf16[256,1152]{1,0:T(8,128)(2,1)S(1)}, bf16[256,1152]{1,0:T(8,128)(2,1)S(1)}, bf16[256,1152]{1,0:T(8,128)(2,1)S(1)}, bf16[256,1152]{1,0:T(8,128)(2,1)S(1)}) custom-call(f32[2]{0:T(128)S(1)} %pad_maximum_fusion.scalars, ...), custom_call_target="tpu_custom_call", output_to_operand_aliasing={{0}: (3, {})} | custom-call | flops 1 | bytes 1 | tf_op jit(solution)/shard_map/pallas_call | solution.py:37
  67.5 5.6 %shard_map.66 = (f32[128,1152]{1,0:T(8,128)S(1)}, f32[128,1152]{1,0:T(8,128)S(1)}, f32[128,1152]{1,0:T(8,128)S(1)}, f32[128,1152]{1,0:T(8,128)S(1)}, bf16[256,11...) custom-call(f32[2]{0:T(128)S(1)} %pad_maximum_fusion.scalars, ...), custom_call_target="tpu_custom_call", output_to_operand_aliasing={{5}: (4, {})} | custom-call | flops 1 | bytes 1 | tf_op jit(solution)/shard_map/pallas_call | solution.py:37
  75.5 7.5 %collective-permute-start.20 = (bf16[128,1152]{1,0:T(8,128)(2,1)S(1)}, bf16[128,1152]{1,0:T(8,128)(2,1)S(1)}, u32[]{:S(2)}, u32[]{:S(2)}) collective-permute-start(bf16[128,1152]{1,0:T(8,128)(2,1)S(1)} %get-tuple-element.128), channel_id=1, source_target_pairs={{0,8},{1,9},{2,10},{3,11},{4,12},{5,13},{6,14},{7,15},{8,16},{9,17... | collective-permute-start | bytes 884744 | tf_op jit(solution)/shard_map/ppermute | solution.py:25
  84.8 8.1 %collective-permute-done.20.refs_1_ = bf16[128,1152]{1,0:T(8,128)(2,1)S(1)} collective-permute-done((bf16[128,1152]{1,0:T(8,128)(2,1)S(1)}, bf16[128,1152]{1,0:T(8,128)(2,1)S(1)}, u32[]{:S(2)}, u32[]{:S(2)}) %collective-permute-start.20) | collective-permute-done | bytes 294944 | tf_op jit(solution)/shard_map/ppermute | solution.py:25
  93.7 4.9 %collective-permute-done.22 = bf16[128,1152]{1,0:T(8,128)(2,1)S(1)} collective-permute-done((bf16[128,1152]{1,0:T(8,128)(2,1)S(1)}, bf16[128,1152]{1,0:T(8,128)(2,1)S(1)}, u32[]{:S(2)}, u32[]{:S(2)}) %collective-permute-start.22) | collective-permute-done | bytes 294944 | tf_op jit(solution)/shard_map/ppermute | solution.py:25
  98.9 3.7 %collective-permute-start.25 = (bf16[128,1152]{1,0:T(8,128)(2,1)S(1)}, bf16[128,1152]{1,0:T(8,128)(2,1)S(1)}, u32[]{:S(2)}, u32[]{:S(2)}) collective-permute-start(bf16[128,1152]{1,0:T(8,128)(2,1)S(1)} %get-tuple-element.146), channel_id=1, source_target_pairs={{0,16},{1,17},{2,18},{3,19},{4,20},{5,21},{6,22},{7,23},{8,24},{9,... | collective-permute-start | bytes 884744 | tf_op jit(solution)/shard_map/ppermute | solution.py:25
  103.3 2.0 %collective-permute-start.28 = (bf16[128,1152]{1,0:T(8,128)(2,1)S(1)}, bf16[128,1152]{1,0:T(8,128)(2,1)S(1)}, u32[]{:S(2)}, u32[]{:S(2)}) collective-permute-start(bf16[128,1152]{1,0:T(8,128)(2,1)S(1)} %get-tuple-element.152), channel_id=1, source_target_pairs={{0,6},{1,7},{2,0},{3,1},{4,2},{5,3},{6,4},{7,5},{8,14},{9,15},{10,... | collective-permute-start | bytes 884744 | tf_op jit(solution)/shard_map/ppermute | solution.py:25
  105.3 1.7 %collective-permute-start.29 = (bf16[128,1152]{1,0:T(8,128)(2,1)S(1)}, bf16[128,1152]{1,0:T(8,128)(2,1)S(1)}, u32[]{:S(2)}, u32[]{:S(2)}) collective-permute-start(bf16[128,1152]{1,0:T(8,128)(2,1)S(1)} %get-tuple-element.153), channel_id=1, source_target_pairs={{0,4},{1,5},{2,6},{3,7},{4,0},{5,1},{6,2},{7,3},{8,12},{9,13},{10,... | collective-permute-start | bytes 884744 | tf_op jit(solution)/shard_map/ppermute | solution.py:25
  107.0 8.3 %collective-permute-done.25.refs_0_ = bf16[128,1152]{1,0:T(8,128)(2,1)S(1)} collective-permute-done((bf16[128,1152]{1,0:T(8,128)(2,1)S(1)}, bf16[128,1152]{1,0:T(8,128)(2,1)S(1)}, u32[]{:S(2)}, u32[]{:S(2)}) %collective-permute-start.25) | collective-permute-done | bytes 294944 | tf_op jit(solution)/shard_map/ppermute | solution.py:25
  116.5 2.4 %collective-permute-done.26.refs_0_ = bf16[128,1152]{1,0:T(8,128)(2,1)S(1)} collective-permute-done((bf16[128,1152]{1,0:T(8,128)(2,1)S(1)}, bf16[128,1152]{1,0:T(8,128)(2,1)S(1)}, u32[]{:S(2)}, u32[]{:S(2)}) %collective-permute-start.26) | collective-permute-done | bytes 294944 | tf_op jit(solution)/shard_map/ppermute | solution.py:16
  (66 shorter events, 17.7 us)
Async XLA Ops:
  1.9 12.3 %collective-permute-start.1 = (bf16[128,1152]{1,0:T(8,128)(2,1)S(1)}, bf16[128,1152]{1,0:T(8,128)(2,1)S(1)}, u32[]{:S(2)}, u32[]{:S(2)}) collective-permute-start(bf16[128,1152]{1,0:T(8,128)(2,1)S(1)} %shard_map.60.img_0), channel_id=1, source_target_pairs={{0,192},{32,224},{64,0},{96,32},{128,64},{160,96},{192,128},{224,1... | collective-permute-start | bytes 884744 | tf_op jit(solution)/shard_map/ppermute | solution.py:16
  6.1 18.0 %collective-permute-start.4 = (bf16[128,1152]{1,0:T(8,128)(2,1)S(1)}, bf16[128,1152]{1,0:T(8,128)(2,1)S(1)}, u32[]{:S(2)}, u32[]{:S(2)}) collective-permute-start(bf16[128,1152]{1,0:T(8,128)(2,1)S(1)} %shard_map.59.txt_0), channel_id=1, source_target_pairs={{0,32},{32,64},{64,96},{96,128},{128,160},{160,192},{192,224},{224... | collective-permute-start | bytes 884744 | tf_op jit(solution)/shard_map/ppermute | solution.py:16
  8.1 17.4 %collective-permute-start = (bf16[128,1152]{1,0:T(8,128)(2,1)S(1)}, bf16[128,1152]{1,0:T(8,128)(2,1)S(1)}, u32[]{:S(2)}, u32[]{:S(2)}) collective-permute-start(bf16[128,1152]{1,0:T(8,128)(2,1)S(1)} %shard_map.59.txt_0), channel_id=1, source_target_pairs={{0,6},{1,7},{2,0},{3,1},{4,2},{5,3},{6,4},{7,5},{8,14},{9,15},{10,... | collective-permute-start | bytes 884744 | tf_op jit(solution)/shard_map/ppermute | solution.py:25
  8.8 27.2 %collective-permute-start.6 = (bf16[128,1152]{1,0:T(8,128)(2,1)S(1)}, bf16[128,1152]{1,0:T(8,128)(2,1)S(1)}, u32[]{:S(2)}, u32[]{:S(2)}) collective-permute-start(bf16[128,1152]{1,0:T(8,128)(2,1)S(1)} %shard_map.60.img_0), channel_id=1, source_target_pairs={{0,8},{1,9},{2,10},{3,11},{4,12},{5,13},{6,14},{7,15},{8,16},{9,17... | collective-permute-start | bytes 884744 | tf_op jit(solution)/shard_map/ppermute | solution.py:25
  12.1 23.9 %collective-permute-start.5 = (bf16[128,1152]{1,0:T(8,128)(2,1)S(1)}, bf16[128,1152]{1,0:T(8,128)(2,1)S(1)}, u32[]{:S(2)}, u32[]{:S(2)}) collective-permute-start(bf16[128,1152]{1,0:T(8,128)(2,1)S(1)} %shard_map.60.img_0), channel_id=1, source_target_pairs={{0,24},{1,25},{2,26},{3,27},{4,28},{5,29},{6,30},{7,31},{8,0},{9,1... | collective-permute-start | bytes 884744 | tf_op jit(solution)/shard_map/ppermute | solution.py:25
  14.2 21.8 %collective-permute-start.3 = (bf16[128,1152]{1,0:T(8,128)(2,1)S(1)}, bf16[128,1152]{1,0:T(8,128)(2,1)S(1)}, u32[]{:S(2)}, u32[]{:S(2)}) collective-permute-start(bf16[128,1152]{1,0:T(8,128)(2,1)S(1)} %shard_map.59.txt_0), channel_id=1, source_target_pairs={{0,4},{1,5},{2,6},{3,7},{4,0},{5,1},{6,2},{7,3},{8,12},{9,13},{10,... | collective-permute-start | bytes 884744 | tf_op jit(solution)/shard_map/ppermute | solution.py:25
  24.1 11.9 %collective-permute-start.2 = (bf16[128,1152]{1,0:T(8,128)(2,1)S(1)}, bf16[128,1152]{1,0:T(8,128)(2,1)S(1)}, u32[]{:S(2)}, u32[]{:S(2)}) collective-permute-start(bf16[128,1152]{1,0:T(8,128)(2,1)S(1)} %shard_map.59.txt_0), channel_id=1, source_target_pairs={{0,2},{1,3},{2,4},{3,5},{4,6},{5,7},{6,0},{7,1},{8,10},{9,11},{10,... | collective-permute-start | bytes 884744 | tf_op jit(solution)/shard_map/ppermute | solution.py:25
  25.4 18.6 %collective-permute-start.11 = (bf16[128,1152]{1,0:T(8,128)(2,1)S(1)}, bf16[128,1152]{1,0:T(8,128)(2,1)S(1)}, u32[]{:S(2)}, u32[]{:S(2)}) collective-permute-start(bf16[128,1152]{1,0:T(8,128)(2,1)S(1)} %shard_map.60.img_0), channel_id=1, source_target_pairs={{0,16},{1,17},{2,18},{3,19},{4,20},{5,21},{6,22},{7,23},{8,24},{9,... | collective-permute-start | bytes 884744 | tf_op jit(solution)/shard_map/ppermute | solution.py:25
  36.2 12.6 %collective-permute-start.10 = (bf16[256,1152]{1,0:T(8,128)(2,1)S(1)}, bf16[256,1152]{1,0:T(8,128)(2,1)S(1)}, u32[]{:S(2)}, u32[]{:S(2)}) collective-permute-start(bf16[256,1152]{1,0:T(8,128)(2,1)S(1)} %get-tuple-element.89.img_n), channel_id=1, source_target_pairs={{0,192},{32,224},{64,0},{96,32},{128,64},{160,96},{192,128},{224,1... | collective-permute-start | bytes 1769480 | tf_op jit(solution)/shard_map/ppermute | solution.py:16
  36.4 9.3 %collective-permute-start.9 = (bf16[128,1152]{1,0:T(8,128)(2,1)S(1)}, bf16[128,1152]{1,0:T(8,128)(2,1)S(1)}, u32[]{:S(2)}, u32[]{:S(2)}) collective-permute-start(bf16[128,1152]{1,0:T(8,128)(2,1)S(1)} %collective-permute-done.4), channel_id=1, source_target_pairs={{0,4},{1,5},{2,6},{3,7},{4,0},{5,1},{6,2},{7,3},{8,12},{9,13},{10,... | collective-permute-start | bytes 884744 | tf_op jit(solution)/shard_map/ppermute | solution.py:25
  40.6 8.3 %collective-permute-start.7 = (bf16[128,1152]{1,0:T(8,128)(2,1)S(1)}, bf16[128,1152]{1,0:T(8,128)(2,1)S(1)}, u32[]{:S(2)}, u32[]{:S(2)}) collective-permute-start(bf16[128,1152]{1,0:T(8,128)(2,1)S(1)} %collective-permute-done.4), channel_id=1, source_target_pairs={{0,6},{1,7},{2,0},{3,1},{4,2},{5,3},{6,4},{7,5},{8,14},{9,15},{10,... | collective-permute-start | bytes 884744 | tf_op jit(solution)/shard_map/ppermute | solution.py:25
  49.1 9.4 %collective-permute-start.12 = (bf16[128,1152]{1,0:T(8,128)(2,1)S(1)}, bf16[128,1152]{1,0:T(8,128)(2,1)S(1)}, u32[]{:S(2)}, u32[]{:S(2)}) collective-permute-start(bf16[128,1152]{1,0:T(8,128)(2,1)S(1)} %collective-permute-done.11), channel_id=1, source_target_pairs={{0,192},{32,224},{64,0},{96,32},{128,64},{160,96},{192,128},{224,1... | collective-permute-start | bytes 884744 | tf_op jit(solution)/shard_map/ppermute | solution.py:16
  56.6 17.4 %collective-permute-start.14 = (bf16[272,1152]{1,0:T(8,128)(2,1)S(1)}, bf16[272,1152]{1,0:T(8,128)(2,1)S(1)}, u32[]{:S(2)}, u32[]{:S(2)}) collective-permute-start(bf16[272,1152]{1,0:T(8,128)(2,1)S(1)} %get-tuple-element.110), channel_id=1, source_target_pairs={{0,64},{32,96},{64,128},{96,160},{128,192},{160,224},{192,0},{224,... | collective-permute-start | bytes 1880072 | tf_op jit(solution)/shard_map/ppermute | solution.py:16
  74.4 8.6 %collective-permute-start.19 = (bf16[128,1152]{1,0:T(8,128)(2,1)S(1)}, bf16[128,1152]{1,0:T(8,128)(2,1)S(1)}, u32[]{:S(2)}, u32[]{:S(2)}) collective-permute-start(bf16[128,1152]{1,0:T(8,128)(2,1)S(1)} %get-tuple-element.125), channel_id=1, source_target_pairs={{0,2},{1,3},{2,4},{3,5},{4,6},{5,7},{6,0},{7,1},{8,10},{9,11},{10,... | collective-permute-start | bytes 884744 | tf_op jit(solution)/shard_map/ppermute | solution.py:25
  75.0 23.6 %collective-permute-start.23 = (bf16[256,1152]{1,0:T(8,128)(2,1)S(1)}, bf16[256,1152]{1,0:T(8,128)(2,1)S(1)}, u32[]{:S(2)}, u32[]{:S(2)}) collective-permute-start(bf16[256,1152]{1,0:T(8,128)(2,1)S(1)} %get-tuple-element.131), channel_id=1, source_target_pairs={{0,64},{32,96},{64,128},{96,160},{128,192},{160,224},{192,0},{224,... | collective-permute-start | bytes 1769480 | tf_op jit(solution)/shard_map/ppermute | solution.py:16
  75.5 17.5 %collective-permute-start.20 = (bf16[128,1152]{1,0:T(8,128)(2,1)S(1)}, bf16[128,1152]{1,0:T(8,128)(2,1)S(1)}, u32[]{:S(2)}, u32[]{:S(2)}) collective-permute-start(bf16[128,1152]{1,0:T(8,128)(2,1)S(1)} %get-tuple-element.128), channel_id=1, source_target_pairs={{0,8},{1,9},{2,10},{3,11},{4,12},{5,13},{6,14},{7,15},{8,16},{9,17... | collective-permute-start | bytes 884744 | tf_op jit(solution)/shard_map/ppermute | solution.py:25
  82.9 10.8 %collective-permute-start.21 = (bf16[128,1152]{1,0:T(8,128)(2,1)S(1)}, bf16[128,1152]{1,0:T(8,128)(2,1)S(1)}, u32[]{:S(2)}, u32[]{:S(2)}) collective-permute-start(bf16[128,1152]{1,0:T(8,128)(2,1)S(1)} %get-tuple-element.129), channel_id=1, source_target_pairs={{0,24},{1,25},{2,26},{3,27},{4,28},{5,29},{6,30},{7,31},{8,0},{9,1... | collective-permute-start | bytes 884744 | tf_op jit(solution)/shard_map/ppermute | solution.py:25
  82.9 15.7 %collective-permute-start.22 = (bf16[128,1152]{1,0:T(8,128)(2,1)S(1)}, bf16[128,1152]{1,0:T(8,128)(2,1)S(1)}, u32[]{:S(2)}, u32[]{:S(2)}) collective-permute-start(bf16[128,1152]{1,0:T(8,128)(2,1)S(1)} %get-tuple-element.130), channel_id=1, source_target_pairs={{0,6},{1,7},{2,0},{3,1},{4,2},{5,3},{6,4},{7,5},{8,14},{9,15},{10,... | collective-permute-start | bytes 884744 | tf_op jit(solution)/shard_map/ppermute | solution.py:25
  83.0 15.7 %collective-permute-start.24 = (bf16[128,1152]{1,0:T(8,128)(2,1)S(1)}, bf16[128,1152]{1,0:T(8,128)(2,1)S(1)}, u32[]{:S(2)}, u32[]{:S(2)}) collective-permute-start(bf16[128,1152]{1,0:T(8,128)(2,1)S(1)} %get-tuple-element.132), channel_id=1, source_target_pairs={{0,4},{1,5},{2,6},{3,7},{4,0},{5,1},{6,2},{7,3},{8,12},{9,13},{10,... | collective-permute-start | bytes 884744 | tf_op jit(solution)/shard_map/ppermute | solution.py:25
  98.9 16.4 %collective-permute-start.25 = (bf16[128,1152]{1,0:T(8,128)(2,1)S(1)}, bf16[128,1152]{1,0:T(8,128)(2,1)S(1)}, u32[]{:S(2)}, u32[]{:S(2)}) collective-permute-start(bf16[128,1152]{1,0:T(8,128)(2,1)S(1)} %get-tuple-element.146), channel_id=1, source_target_pairs={{0,16},{1,17},{2,18},{3,19},{4,20},{5,21},{6,22},{7,23},{8,24},{9,... | collective-permute-start | bytes 884744 | tf_op jit(solution)/shard_map/ppermute | solution.py:25
  102.6 16.3 %collective-permute-start.26 = (bf16[128,1152]{1,0:T(8,128)(2,1)S(1)}, bf16[128,1152]{1,0:T(8,128)(2,1)S(1)}, u32[]{:S(2)}, u32[]{:S(2)}) collective-permute-start(bf16[128,1152]{1,0:T(8,128)(2,1)S(1)} %get-tuple-element.150), channel_id=1, source_target_pairs={{0,224},{32,0},{64,32},{96,64},{128,96},{160,128},{192,160},{224,1... | collective-permute-start | bytes 884744 | tf_op jit(solution)/shard_map/ppermute | solution.py:16
  103.3 15.6 %collective-permute-start.27 = (bf16[128,1152]{1,0:T(8,128)(2,1)S(1)}, bf16[128,1152]{1,0:T(8,128)(2,1)S(1)}, u32[]{:S(2)}, u32[]{:S(2)}) collective-permute-start(bf16[128,1152]{1,0:T(8,128)(2,1)S(1)} %get-tuple-element.151), channel_id=1, source_target_pairs={{0,2},{1,3},{2,4},{3,5},{4,6},{5,7},{6,0},{7,1},{8,10},{9,11},{10,... | collective-permute-start | bytes 884744 | tf_op jit(solution)/shard_map/ppermute | solution.py:25
  103.3 15.6 %collective-permute-start.28 = (bf16[128,1152]{1,0:T(8,128)(2,1)S(1)}, bf16[128,1152]{1,0:T(8,128)(2,1)S(1)}, u32[]{:S(2)}, u32[]{:S(2)}) collective-permute-start(bf16[128,1152]{1,0:T(8,128)(2,1)S(1)} %get-tuple-element.152), channel_id=1, source_target_pairs={{0,6},{1,7},{2,0},{3,1},{4,2},{5,3},{6,4},{7,5},{8,14},{9,15},{10,... | collective-permute-start | bytes 884744 | tf_op jit(solution)/shard_map/ppermute | solution.py:25
  105.3 13.6 %collective-permute-start.29 = (bf16[128,1152]{1,0:T(8,128)(2,1)S(1)}, bf16[128,1152]{1,0:T(8,128)(2,1)S(1)}, u32[]{:S(2)}, u32[]{:S(2)}) collective-permute-start(bf16[128,1152]{1,0:T(8,128)(2,1)S(1)} %get-tuple-element.153), channel_id=1, source_target_pairs={{0,4},{1,5},{2,6},{3,7},{4,0},{5,1},{6,2},{7,3},{8,12},{9,13},{10,... | collective-permute-start | bytes 884744 | tf_op jit(solution)/shard_map/ppermute | solution.py:25
  (10 other events, 90.9 us)
